TPU v7x, 32 devices: a whole 2x2x4 slice. The times are simulated.
32 devices in a mesh: dp: 4 (over z), member: 8 (over y, x, core).
Axes of the slice: x: 2, y: 2, z: 4, core: 2. Of those that a mesh axis runs over, the one named last changes fastest.
Arguments:
- objects: bfloat16 [16384, 512], P(('dp', 'member'))
- counts: int32 [32], P(('dp', 'member')), may hold values from 1 to 512, as said below
- cotangent: float32 [16384], P(('dp', 'member')), may hold values from -6 to 6
- matrix: float32 [512, 512], P(('dp', 'member'))
- matrix_first: float32 [512, 512], P(('dp', 'member'))
- matrix_second: float32 [512, 512], P(('dp', 'member')), may hold values from 16 to 64
- adapters: float32 [3, 32, 512], P(None, None, ('dp', 'member'))
- adapter_first: float32 [3, 32, 512], P(None, None, ('dp', 'member'))
- adapter_second: float32 [3, 32, 512], P(None, None, ('dp', 'member')), may hold values from 0.125 to 0.5
- head_weights: float32 [32, 512], P('member')
- head_first: float32 [32, 512], P('member')
- head_second: float32 [32, 512], P('member'), may hold values from 4 to 16
Outputs:
- predictions: float32 [16384], P(('dp', 'member'))
- input_grad: float32 [16384, 512], P(('dp', 'member'))
- new_matrix: float32 [512, 512], P(('dp', 'member'))
- new_matrix_first: float32 [512, 512], P(('dp', 'member'))
- new_matrix_second: float32 [512, 512], P(('dp', 'member'))
- new_adapters: float32 [3, 32, 512], P(None, None, ('dp', 'member'))
- new_adapter_first: float32 [3, 32, 512], P(None, None, ('dp', 'member'))
- new_adapter_second: float32 [3, 32, 512], P(None, None, ('dp', 'member'))
- new_heads: float32 [32, 512], P('member')
- new_head_first: float32 [32, 512], P('member')
- new_head_second: float32 [32, 512], P('member')
- norm_pairs: float32 [5, 2], replicated
Inputs may be any that keep to these rules, and one draw needn't show every extreme that they name: `counts`: the last device's count is always the full 512.
All inputs are finite; a program needn't handle non-finite values.
Results may differ from a plain program's by a relative error of at most 0.0095.
Values may be sent and summed in bfloat16 or wider, within the bound.
No kernel may reach another device: no remote copies, remote signals or barrier semaphores. Data moves between devices by JAX's collectives and lax.ppermute only.
A program may use at most 192 MiB of HBM per device.

v0:
```python
import jax
import jax.numpy as jnp
from jax import lax
from jax.sharding import PartitionSpec as P

STEP = 10


beta_one = 0.5
beta_two = 0.5
epsilon = 1e-06
weight_decay = 0.01
learn_rate = 0.25


def direction(weight, first_old, second_old, gradient):
    first_new = beta_one * first_old + (1.0 - beta_one) * gradient
    second_new = beta_two * second_old + (1.0 - beta_two) * gradient * gradient
    fix_one = 1.0 - beta_one**STEP
    fix_two = 1.0 - beta_two**STEP
    update = (
        first_new / fix_one / (jnp.sqrt(second_new / fix_two) + epsilon) + weight_decay * weight
    )
    return (first_new, second_new, update)


def squares(matrix, adapters, head_weights, spread):
    return jnp.concatenate(
        [
            jnp.sum(matrix * matrix)[None],
            jnp.sum(adapters * adapters, axis=(1, 2)),
            (jnp.sum(head_weights * head_weights) / spread)[None],
        ]
    )


def shards(
    objects,
    counts,
    cotangent,
    matrix,
    matrix_first,
    matrix_second,
    adapters,
    adapter_first,
    adapter_second,
    head_weights,
    head_first,
    head_second,
):
    row_count = objects.shape[0]
    feat_count = objects.shape[1]
    member_count = adapters.shape[1]
    spread = float(lax.axis_size("dp"))
    weight_sums = lax.psum(squares(matrix, adapters, head_weights, spread), ("dp", "member"))
    matrix_low, adapt_low = (
        lax.all_gather(matrix.astype(jnp.bfloat16), ("dp", "member"), axis=0, tiled=True),
        lax.all_gather(adapters.astype(jnp.bfloat16), ("dp", "member"), axis=2, tiled=True),
    )
    adapt_full = adapt_low.astype(jnp.float32)
    scale_in = adapt_full[0]
    scale_out = adapt_full[1]
    shift_vec = adapt_full[2]
    valid_rows = (jnp.arange(row_count, dtype=jnp.int32) < counts[0]).astype(jnp.float32)
    inputs = objects.astype(jnp.float32)
    mixed_rows = (inputs[:, None, :] * scale_in[None]).astype(jnp.bfloat16)
    flat_mixed = mixed_rows.reshape(row_count * member_count, feat_count)
    inner_sum = jnp.dot(flat_mixed, matrix_low, preferred_element_type=jnp.float32).reshape(
        row_count, member_count, feat_count
    )
    pre_act = inner_sum * scale_out[None] + shift_vec[None]
    active, silu_back = jax.vjp(jax.nn.silu, pre_act)
    active_low = active.astype(jnp.bfloat16)
    weighted = cotangent * valid_rows / member_count
    heads_low = head_weights.astype(jnp.bfloat16)
    regrouped = lax.all_to_all(active_low, "member", split_axis=1, concat_axis=0, tiled=True)
    head_terms = jnp.einsum("rkd,kd->r", regrouped, heads_low, preferred_element_type=jnp.float32)
    predictions = (
        lax.psum_scatter(head_terms, "member", scatter_dimension=0, tiled=True)
        * valid_rows
        / member_count
    )
    weighted_all = lax.all_gather(weighted, "member", axis=0, tiled=True)
    head_grad = jnp.einsum("r,rkd->kd", weighted_all, regrouped, preferred_element_type=jnp.float32)
    back_rows = (weighted_all[:, None, None] * heads_low.astype(jnp.float32)[None]).astype(
        jnp.bfloat16
    )
    returned = lax.all_to_all(back_rows, "member", split_axis=0, concat_axis=1, tiled=True)
    head_grad = lax.psum(head_grad, "dp")
    grad_pre = silu_back(returned.astype(jnp.float32))[0]
    grad_scale_out = jnp.sum(grad_pre * inner_sum, axis=0)
    grad_shift = jnp.sum(grad_pre, axis=0)
    grad_inner = (
        (grad_pre * scale_out[None])
        .astype(jnp.bfloat16)
        .reshape(row_count * member_count, feat_count)
    )
    grad_matrix = lax.dot_general(
        flat_mixed, grad_inner, (((0,), (0,)), ((), ())), preferred_element_type=jnp.float32
    )
    grad_mixed = lax.dot_general(
        grad_inner, matrix_low, (((1,), (1,)), ((), ())), preferred_element_type=jnp.float32
    ).reshape(row_count, member_count, feat_count)
    grad_scale_in = jnp.sum(grad_mixed * inputs[:, None, :], axis=0)
    input_grad = jnp.sum(grad_mixed * scale_in[None], axis=1)
    grad_adapt = jnp.stack([grad_scale_in, grad_scale_out, grad_shift])
    grad_matrix, grad_adapt = (
        lax.psum_scatter(grad_matrix, ("dp", "member"), scatter_dimension=0, tiled=True),
        lax.psum_scatter(grad_adapt, ("dp", "member"), scatter_dimension=2, tiled=True),
    )
    m_first, m_second, m_update = direction(matrix, matrix_first, matrix_second, grad_matrix)
    a_first, a_second, a_update = direction(adapters, adapter_first, adapter_second, grad_adapt)
    h_first, h_second, h_update = direction(head_weights, head_first, head_second, head_grad)
    update_sq = squares(m_update, a_update, h_update, spread)
    update_sums = lax.psum(update_sq, ("dp", "member"))
    weight_norm = jnp.sqrt(weight_sums)
    update_norm = jnp.sqrt(update_sums)
    trust_ratio = weight_norm / update_norm
    new_matrix = matrix - learn_rate * trust_ratio[0] * m_update
    new_adapters = adapters - learn_rate * trust_ratio[1:4][:, None, None] * a_update
    new_heads = head_weights - learn_rate * trust_ratio[4] * h_update
    norm_pairs = jnp.stack([weight_norm, update_norm], axis=1)
    return (
        predictions,
        input_grad,
        new_matrix,
        m_first,
        m_second,
        new_adapters,
        a_first,
        a_second,
        new_heads,
        h_first,
        h_second,
        norm_pairs,
    )


def solution(mesh):
    return jax.shard_map(
        shards,
        mesh=mesh,
        in_specs=(
            P(("dp", "member"), None),
            P(("dp", "member")),
            P(("dp", "member")),
            P(("dp", "member"), None),
            P(("dp", "member"), None),
            P(("dp", "member"), None),
            P(None, None, ("dp", "member")),
            P(None, None, ("dp", "member")),
            P(None, None, ("dp", "member")),
            P("member", None),
            P("member", None),
            P("member", None),
        ),
        out_specs=(
            P(("dp", "member")),
            P(("dp", "member"), None),
            P(("dp", "member"), None),
            P(("dp", "member"), None),
            P(("dp", "member"), None),
            P(None, None, ("dp", "member")),
            P(None, None, ("dp", "member")),
            P(None, None, ("dp", "member")),
            P("member", None),
            P("member", None),
            P("member", None),
            P(),
        ),
        check_vma=False,
    )
```

profile of v0, /device:TPU:0, one launch (start us, length us, event | category | flops | bytes accessed | tf_op | source)
XLA Modules:
  0.0 775.7 jit_solution(5899362582160477262)
XLA Ops:
  8.6 10.3 %all-gather = f32[8,1,512]{2,1,0:T(1,128)S(1)} all-gather(f32[1,1,512]{2,1,0:T(1,128)S(1)} %bitcast.77), channel_id=1, replica_groups=mesh['dp'=4,'member'=8] {'member'}, dimensions={0}, use_global_device_ids=true | all-gather | bytes 18432 | tf_op jit(solution)/shard_map/all_gather | solution.py:83
  18.9 1.4 multiply_reduce_fusion.8
  20.3 13.5 %multiply_convert_fusion.1 = bf16[4096,4,512]{2,1,0:T(4,128)(2,1)} fusion(f32[4,512]{1,0:T(4,128)S(1)} %get-tuple-element.62, f32[4096]{0:T(1024)S(1)} %bitcast.69), kind=kLoop, calls=%fused_computation.10 | loop fusion | flops 16777216 | bytes 16801792 | tf_op jit(solution)/shard_map/convert_element_type | solution.py:85
  33.8 5.8 all-to-all-start.1
  39.6 217.3 %all_gather.9 = bf16[3,32,512]{1,2,0:T(8,128)(2,1)S(1)} all-gather(bf16[3,32,16]{1,2,0:T(8,128)(2,1)S(1)} %convert_element_type.46), channel_id=1, replica_groups=mesh['dp'=4,'member'=8] {'dp','member'}, dimensions={2}, use_global_device_ids=true | all-gather | bytes 101376 | tf_op jit(solution)/shard_map/all_gather | solution.py:58
  257.5 38.1 %all_gather.10 = bf16[512,512]{1,0:T(8,128)(2,1)S(1)} all-gather(bf16[16,512]{1,0:T(8,128)(2,1)S(1)} %convert_element_type.49), channel_id=1, replica_groups=mesh['dp'=4,'member'=8] {'dp','member'}, dimensions={0}, use_global_device_ids=true | all-gather | bytes 540672 | tf_op jit(solution)/shard_map/all_gather | solution.py:57
  295.6 16.2 %copy.66 = bf16[4096,4,512]{2,0,1:T(8,128)(2,1)} copy(bf16[4096,4,512]{2,1,0:T(4,128)(2,1)} %all-to-all-done.1) | data formatting | bytes 33554432 | tf_op jit(solution)/shard_map/all_to_all | solution.py:88
  311.7 9.9 %convert_bitcast_fusion = f32[512,8,4,512]{3,0,1,2:T(8,128)S(1)} fusion(bf16[8,512,4,512]{3,1,0,2:T(8,128)(2,1)} %bitcast.67), kind=kLoop, calls=%fused_computation.3 | loop fusion | flops 8388608 | bytes 50331648 | tf_op jit(solution)/shard_map/convert_element_type | solution.py:90
  321.6 11.2 %copy.67 = f32[512,8,4,512]{3,0,2,1:T(8,128)} copy(f32[512,8,4,512]{3,0,1,2:T(8,128)S(1)} %convert_bitcast_fusion) | data formatting | bytes 67108864 | tf_op jit(solution)/shard_map/convert_element_type | solution.py:90
  332.8 36.0 %multiply_reduce_fusion = (f32[32,512]{1,0:T(8,128)S(1)}, f32[32,512]{1,0:T(8,128)S(1)}, f32[512,32,512]{2,0,1:T(8,128)}, bf16[512,32,512]{2,0,1:T(8,128)(2,1)}) fusion(f32[32,512]{1,0:T(8,128)S(1)} %copy.64, f32[32,512]{1,0:T(8,128)S(1)} %copy.63, f32[512,8,4,512]{3,0,2,1:T(8,128)} %copy.67, bf16[512,512]{1,0:T(8,128)(2,1)S(1)} %all_gather.10, ...), kind=kOutput, calls=%fused_computation.6 | convolution fusion | flops 8740896768 | bytes 85786624 | tf_op jit(solution)/shard_map/dot_general | solution.py:68
  368.8 5.7 all-to-all-start
  374.8 18.4 %multiply_reduce_fusion.1 = (f32[32,512]{1,0:T(8,128)S(1)}, f32[512,512]{1,0:T(8,128)}) fusion(f32[512,512]{1,0:T(8,128)S(1)} %convert_element_type.45, f32[32,512]{1,0:T(8,128)S(1)} %copy.62, bf16[512,512]{1,0:T(8,128)(2,1)S(1)} %all_gather.10, f32[512,32,512]{2,0,1:T(8,128)} %get-tuple-element.50, f32[32,512]{1,0:T(8,128)S(1)} %copy.63), kind=kOutput, calls=%fused_computation.7 | convolution fusion | flops 8639987712 | bytes 36372480 | tf_op jit(solution)/shard_map/dot_general | solution.py:101
  394.8 16.1 %fusion.9 = f32[512,512]{1,0:T(8,128)} fusion(f32[512,32,512]{2,0,1:T(8,128)} %get-tuple-element.50, f32[32,512]{1,0:T(8,128)S(1)} %copy.63, f32[32,512]{1,0:T(8,128)S(1)} %copy.62, f32[512,512]{1,0:T(8,128)S(1)} %convert_element_type.45), kind=kOutput, calls=%fused_computation.22 | convolution fusion | flops 8623489024 | bytes 35782656 | tf_op jit(solution)/shard_map/dot_general | solution.py:98
  412.8 114.9 %reduce-scatter.7.cloned.1.call-done = f32[16,96]{1,0:T(8,128)} async-done(((f32[512,96]{1,0:T(8,128)}), f32[16,96]{1,0:T(8,128)}) %reduce-scatter.7.cloned.1.call-update) | async-done | bytes 6160
  528.6 132.6 %reduce-scatter.5.cloned.1.call-done = f32[16,512]{1,0:T(8,128)} async-done(((f32[512,512]{1,0:T(8,128)}), f32[16,512]{1,0:T(8,128)}) %reduce-scatter.5.cloned.1.call-update) | async-done | bytes 32784 | tf_op jit(solution)/shard_map/reduce_scatter | solution.py:108
  661.3 1.4 multiply_reduce_fusion.4
  662.7 8.1 %copy.65 = bf16[512,8,4,512]{3,0,1,2:T(8,128)(2,1)S(1)} copy(bf16[512,8,4,512]{3,0,2,1:T(8,128)(2,1)} %bitcast.5) | data formatting | bytes 33554432 | tf_op jit(solution)/shard_map/all_to_all | solution.py:76
  670.9 5.7 copy-done
  676.6 2.3 fusion.23
  678.8 8.5 %psum.22 = f32[4,512]{1,0:T(4,128)S(1)} all-reduce(f32[4,512]{1,0:T(4,128)S(1)} %bitcast.76), channel_id=1, replica_groups=mesh['dp'=4,'member'=8] {'dp'}, use_global_device_ids=true, to_apply=%region_13.14 | all-reduce | flops 2048 | bytes 16384 | tf_op jit(solution)/shard_map/psum | solution.py:89
  689.2 1.4 pad_maximum_fusion.2
  690.6 39.8 %all-reduce.1 = (f32[5]{0:T(128)S(1)}, f32[5]{0:T(128)S(1)}) all-reduce(f32[5]{0:T(128)S(1)} %get-tuple-element.69, f32[5]{0:T(128)S(1)} %get-tuple-element.68), channel_id=1, replica_groups=mesh['dp'=4,'member'=8] {'dp','member'}, use_global_device_ids=true, to_apply=%region_15.16 | all-reduce | flops 10 | bytes 80 | tf_op jit(solution)/shard_map/psum | solution.py:115
  733.0 10.2 %fusion.15 = f32[1,4096,1]{1,0,2:T(1,128)S(1)} fusion(bf16[4096,4,512]{2,0,1:T(8,128)(2,1)} %bitcast.66, bf16[4,512,1]{1,0,2:T(4,128)(2,1)S(1)} %get-tuple-element.60), kind=kOutput, calls=%fused_computation.47 | convolution fusion | flops 16777216 | bytes 16797696 | tf_op jit(solution)/shard_map/rkd,kd->r/dot_general | solution.py:77
  743.2 23.1 %all-reduce = f32[4096]{0:T(1024)S(1)} all-reduce(f32[4096]{0:T(1024)S(1)} %bitcast.72), channel_id=2, replica_groups=mesh['dp'=4,'member'=8] {'member'}, use_global_device_ids=true, to_apply=%region_0.0.clone | all-reduce | flops 4096 | bytes 32768
  (70 shorter events, 9.7 us)
Async XLA Ops:
  7.2 32.4 %copy-start.4 = (f32[3,32,16]{1,2,0:T(8,128)S(1)}, f32[3,32,16]{1,2,0:T(8,128)}, u32[]{:S(2)}) copy-start(f32[3,32,16]{1,2,0:T(8,128)} %param.18) | copy-start | bytes 18436
  7.2 250.1 %copy-start.1 = (bf16[512,512]{1,0:T(8,128)(2,1)S(1)}, bf16[512,512]{1,0:T(8,128)(2,1)}, u32[]{:S(2)}) copy-start(bf16[512,512]{1,0:T(8,128)(2,1)} %param.12) | copy-start | bytes 1572868
  7.2 250.3 %copy-start.2 = (f32[16,512]{1,0:T(8,128)S(1)}, f32[16,512]{1,0:T(8,128)}, u32[]{:S(2)}) copy-start(f32[16,512]{1,0:T(8,128)} %param.15) | copy-start | bytes 98308
  18.9 237.9 %copy-start.6 = (f32[8,1,512]{2,1,0:T(1,128)}, f32[8,1,512]{2,1,0:T(1,128)S(1)}, u32[]{:S(2)}) copy-start(f32[8,1,512]{2,1,0:T(1,128)S(1)} %all-gather) | copy-start | bytes 49156
  33.8 261.7 %all-to-all-start.1 = ((bf16[4096,4,512]{2,1,0:T(4,128)(2,1)}), bf16[4096,4,512]{2,1,0:T(4,128)(2,1)}, u32[]{:S(2)}, u32[]{:S(2)}) async-start(bf16[4096,4,512]{2,1,0:T(4,128)(2,1)} %multiply_convert_fusion.1), calls=%async_computation.1 | async-start | bytes 33554432 | tf_op jit(solution)/shard_map/all_to_all | solution.py:88
  368.8 293.9 %all-to-all-start = ((bf16[512,32,512]{2,0,1:T(8,128)(2,1)}), bf16[512,32,512]{2,0,1:T(8,128)(2,1)}, u32[]{:S(2)}, u32[]{:S(2)}) async-start(bf16[512,32,512]{2,0,1:T(8,128)(2,1)} %get-tuple-element.55), calls=%async_computation | async-start | bytes 33554432 | tf_op jit(solution)/shard_map/all_to_all | solution.py:76
  374.5 153.2 %reduce-scatter.7.cloned.1.call-start = ((), (), s32[]{:S(2)}) async-start(), calls=%async_computation.5 | async-start | bytes 270336
  393.1 18.4 %copy-start.19 = (u32[32]{0:T(128)S(1)}, u32[32]{0:T(128)}, u32[]{:S(2)}) copy-start(u32[32]{0:T(128)} %constant.54) | copy-start | bytes 388
  393.1 135.3 %copy-start.5 = (f32[3,32,16]{1,2,0:T(8,128)S(1)}, f32[3,32,16]{1,2,0:T(8,128)}, u32[]{:S(2)}) copy-start(f32[3,32,16]{1,2,0:T(8,128)} %param.18) | copy-start | bytes 18436
  393.1 135.3 %copy-start.15 = (f32[3,32,16]{1,2,0:T(8,128)S(1)}, f32[3,32,16]{1,2,0:T(8,128)}, u32[]{:S(2)}) copy-start(f32[3,32,16]{1,2,0:T(8,128)} %param.19) | copy-start | bytes 18436
  393.1 135.4 %copy-start.16 = (f32[3,32,16]{1,2,0:T(8,128)S(1)}, f32[3,32,16]{1,2,0:T(8,128)}, u32[]{:S(2)}) copy-start(f32[3,32,16]{1,2,0:T(8,128)} %param.20) | copy-start | bytes 18436
  393.1 268.2 %copy-start.3 = (f32[16,512]{1,0:T(8,128)S(1)}, f32[16,512]{1,0:T(8,128)}, u32[]{:S(2)}) copy-start(f32[16,512]{1,0:T(8,128)} %param.15) | copy-start | bytes 98308
  393.1 268.2 %copy-start.13 = (f32[16,512]{1,0:T(8,128)S(1)}, f32[16,512]{1,0:T(8,128)}, u32[]{:S(2)}) copy-start(f32[16,512]{1,0:T(8,128)} %param.16) | copy-start | bytes 98308
  393.2 268.1 %copy-start.14 = (f32[16,512]{1,0:T(8,128)S(1)}, f32[16,512]{1,0:T(8,128)}, u32[]{:S(2)}) copy-start(f32[16,512]{1,0:T(8,128)} %param.17) | copy-start | bytes 98308
  394.7 281.9 %copy-start.7 = (f32[8,1,512]{2,1,0:T(1,128)S(1)}, f32[8,1,512]{2,1,0:T(1,128)}, u32[]{:S(2)}) copy-start(f32[8,1,512]{2,1,0:T(1,128)} %copy-done.6) | copy-start | bytes 49156
  394.7 266.6 %reduce-scatter.5.cloned.1.call-start = ((), (), s32[]{:S(2)}) async-start(), calls=%async_computation.4 | async-start | bytes 1081344 | tf_op jit(solution)/shard_map/reduce_scatter | solution.py:108
  410.9 276.5 %copy-start.12 = (f32[4,512]{1,0:T(4,128)S(1)}, f32[4,512]{1,0:T(4,128)}, u32[]{:S(2)}) copy-start(f32[4,512]{1,0:T(4,128)} %param.21) | copy-start | bytes 24580
  410.9 276.5 %copy-start.17 = (f32[4,512]{1,0:T(4,128)S(1)}, f32[4,512]{1,0:T(4,128)}, u32[]{:S(2)}) copy-start(f32[4,512]{1,0:T(4,128)} %param.22) | copy-start | bytes 24580
  410.9 276.5 %copy-start.18 = (f32[4,512]{1,0:T(4,128)S(1)}, f32[4,512]{1,0:T(4,128)}, u32[]{:S(2)}) copy-start(f32[4,512]{1,0:T(4,128)} %param.23) | copy-start | bytes 24580
  528.6 238.2 %copy-start.10 = (f32[3,32,16]{1,2,0:T(8,128)}, f32[3,32,16]{1,2,0:T(8,128)S(1)}, u32[]{:S(2)}) copy-start(f32[3,32,16]{1,2,0:T(8,128)S(1)} %get-tuple-element.48) | copy-start | bytes 18436
  528.6 238.2 %copy-start.11 = (f32[3,32,16]{1,2,0:T(8,128)}, f32[3,32,16]{1,2,0:T(8,128)S(1)}, u32[]{:S(2)}) copy-start(f32[3,32,16]{1,2,0:T(8,128)S(1)} %get-tuple-element.49) | copy-start | bytes 18436
  662.7 104.8 %copy-start.8 = (f32[16,512]{1,0:T(8,128)}, f32[16,512]{1,0:T(8,128)S(1)}, u32[]{:S(2)}) copy-start(f32[16,512]{1,0:T(8,128)S(1)} %get-tuple-element.46) | copy-start | bytes 98308
  662.7 104.8 %copy-start.9 = (f32[16,512]{1,0:T(8,128)}, f32[16,512]{1,0:T(8,128)S(1)}, u32[]{:S(2)}) copy-start(f32[16,512]{1,0:T(8,128)S(1)} %get-tuple-element.47) | copy-start | bytes 98308
  670.9 5.7 copy-start
Sparse Core Ops, SparseCore 0:
  394.8 132.8 reduce-scatter.6
  530.0 131.2 reduce-scatter.4
where the time goes:
time: 777 us; the launch traced here: 776 us
  blocking collectives  337 us (43%)
  waiting for transfers between devices  248 us (32%)
  matrix products  82.9 us (11%)
  local copies, waits for them, and re-layouts  45.2 us (6%)
  other arithmetic  33 us (4%)
  between operations  18.3 us (2%)
  starting transfers between devices  11.7 us (2%)
    all_gather x1, blocking collectives, shards(): lax.all_gather(adapters.astype(jnp.bfloat16), ('dp', 'member'), axis=2, t...  217 us
    reduce_scatter x1, waiting for transfers between devices, shards(): lax.psum_scatter(grad_matrix, ('dp', 'member'), scatter_dimension=0, tile...  133 us
    unnamed x3, waiting for transfers between devices  115 us
    psum x1, blocking collectives, shards(): update_sums = lax.psum(update_sq, ('dp', 'member'))  39.8 us
    all_gather x1, blocking collectives, shards(): lax.all_gather(matrix.astype(jnp.bfloat16), ('dp', 'member'), axis=0, til...  38.1 us
    dot_general x1, matrix products, shards(): jnp.dot(flat_mixed, matrix_low, preferred_element_type=jnp.float32)  36 us
    unnamed x1, blocking collectives  23.1 us
    dot_general x1, matrix products, shards(): lax.dot_general(grad_inner, matrix_low, (((1,), (1,)), ((), ())), preferr...  18.4 us
  transfers between devices with their start and end apart: 4, of which 2 were waited for; matrix products, arithmetic and copies ran while one was open for 5% of the time, Pallas kernels for 0%

commit v1 on v0

v1 whole, which is shorter than its diff:
```python
import functools
import jax
import jax.numpy as jnp
from jax import lax
from jax.experimental import pallas as pl
from jax.experimental.pallas import tpu as pltpu
from jax.sharding import PartitionSpec as P

LANES = 128
F32, BF16 = jnp.float32, jnp.bfloat16


def grad_kernel(
    count_ref, x_ref, cot_ref, packed_ref,
    grads_ref, heads_grad_ref, pred_ref, back_ref,
    rows_ref, cols_ref, heads_ref, weight_ref, xq_ref, q_ref, z0_ref, z1_ref, gp0_ref, gp1_ref, post_ref, pred_acc, sums_ref, gr_ref, sems,
):
    R, D = x_ref.shape
    K = heads_grad_ref.shape[0]
    z_refs, gp_refs = (z0_ref, z1_ref), (gp0_ref, gp1_ref)

    weight_ref[...] = packed_ref[:, :D].astype(F32)
    cols = packed_ref[:, D:D + LANES].astype(F32)
    cols_ref[...] = cols
    rows_ref[...] = cols.T
    L = packed_ref.shape[1] - D - LANES
    per_head = D // L
    for c in range(0, L, LANES):
        gr_ref[:K * per_head, :] = packed_ref[:K * per_head, D + LANES + c:D + 2 * LANES + c].astype(F32)
        for k in range(per_head):
            heads_ref[:, k * L + c:k * L + c + LANES] = gr_ref[pl.ds(k, K, stride=per_head), :]
    lane_rows = lax.broadcasted_iota(jnp.int32, (1, R), 1)
    q_row = jnp.where(lane_rows < count_ref[0], cot_ref[...], 0.0) * (1.0 / K)
    q_wide = jnp.broadcast_to(q_row, (LANES, R)).T
    q_ref[...] = q_wide
    half_q = 0.5 * q_row
    q_hi = half_q.astype(BF16)
    q_lo = (half_q - q_hi.astype(F32)).astype(BF16)
    xq_ref[:D, :] = (x_ref[...].astype(F32).T * half_q).astype(BF16)
    sub = lax.broadcasted_iota(jnp.int32, (16, R), 0)
    extra = jnp.where(sub == 0, q_hi.astype(F32), jnp.where(sub == 1, q_lo.astype(F32), 0.0))
    xq_ref[D:, :] = extra.astype(BF16)
    pred_acc[...] = jnp.zeros_like(pred_acc)
    gr_ref[...] = jnp.zeros_like(gr_ref)
    sums_ref[...] = jnp.zeros_like(sums_ref)
    grads_ref[...] = jnp.zeros_like(grads_ref)

    def forward(i, z_ref):
        r = rows_ref[pl.ds(i, 1), :].astype(BF16)
        step = 128
        for c in range(0, R, step):
            u = x_ref[c:c + step, :] * r
            z_ref[c:c + step, :] = jnp.dot(u, packed_ref[:, :D], preferred_element_type=F32)

    def middle(i, z_ref, gp_ref):
        s = 0.5 * rows_ref[pl.ds(K + i, 1), :]
        b = 0.5 * rows_ref[pl.ds(2 * K + i, 1), :]
        hb = heads_ref[pl.ds(i, 1), :]
        total = None
        step = 16
        for c in range(0, R, step):
            y = z_ref[c:c + step, :] * s + b
            t = jnp.tanh(y)
            a = 1.0 + t
            h = y * a
            d = a + h * (1.0 - t)
            gp_ref[c:c + step, :] = (hb * d).astype(BF16)
            hh = h * hb
            pred_acc[c:c + step, :] += sum(hh[:, l:l + LANES] for l in range(0, D, LANES))
            q = q_ref[c:c + step, :]
            qh = jnp.concatenate([h[:, l:l + LANES] * q for l in range(0, D, LANES)], axis=1)
            part = sum(qh[k:k + 8] for k in range(0, step, 8))
            total = part if total is None else total + part
        heads_grad_ref[pl.ds(i, 1), :] = jnp.sum(total, axis=0, keepdims=True)

    def after(i, gp_ref):
        s = rows_ref[pl.ds(K + i, 1), :]
        post_ref[...] = jnp.dot(xq_ref[...], gp_ref[...], preferred_element_type=F32)
        sums_ref[pl.ds(2 * K + i, 1), :] = post_ref[D:D + 1, :] + post_ref[D + 1:D + 2, :]
        total = None
        step = 16
        lane = lax.broadcasted_iota(jnp.int32, (step, LANES), 1)
        for c in range(0, D, step):
            g = post_ref[c:c + step, :]
            r = jnp.sum(jnp.where(lane == i, cols_ref[c:c + step, :], 0.0), axis=1, keepdims=True)
            t = g * weight_ref[c:c + step, :]
            rt = t * r
            part = sum(rt[k:k + 8] for k in range(0, step, 8))
            total = part if total is None else total + part
            st = t * s
            fold = sum(st[:, l:l + LANES] for l in range(0, D, LANES))
            gr_ref[c:c + step, :] += jnp.where(lane == i, jnp.sum(fold, axis=1, keepdims=True), 0.0)
            grads_ref[c:c + step, :D] += (g * s) * r
        sums_ref[pl.ds(K + i, 1), :] = jnp.sum(total, axis=0, keepdims=True)

    def send(i, which):
        return pltpu.make_async_copy(gp_refs[which], back_ref.at[i], sems.at[which])

    forward(0, z_refs[0])
    forward(1, z_refs[1])
    middle(0, z_refs[0], gp_refs[0])
    send(0, 0).start()
    forward(2, z_refs[0])
    middle(1, z_refs[1], gp_refs[1])
    after(0, gp_refs[0])
    send(1, 1).start()

    def pair(p, carry):
        i = 2 * p
        send(i - 2, 0).wait()
        forward(i + 1, z_refs[1])
        middle(i, z_refs[0], gp_refs[0])
        after(i - 1, gp_refs[1])
        send(i, 0).start()
        send(i - 1, 1).wait()
        forward(jnp.minimum(i + 2, K - 1), z_refs[0])
        middle(i + 1, z_refs[1], gp_refs[1])
        after(i, gp_refs[0])
        send(i + 1, 1).start()
        return carry

    lax.fori_loop(1, K // 2, pair, 0)
    after(K - 1, gp_refs[1])
    send(K - 2, 0).wait()
    send(K - 1, 1).wait()

    pred = jnp.sum(pred_acc[...].T, axis=0, keepdims=True)
    pred_ref[...] = jnp.where(lane_rows < count_ref[0], pred, 0.0) * (1.0 / K)
    grads_ref[:, D:] = sums_ref[...].T + gr_ref[...]


def grad_call(count, x, cot, packed, K):
    R, D = x.shape
    vm = pl.BlockSpec(memory_space=pltpu.VMEM)
    return pl.pallas_call(
        grad_kernel,
        out_shape=(
            jax.ShapeDtypeStruct((D, D + LANES), F32),
            jax.ShapeDtypeStruct((K, D), F32),
            jax.ShapeDtypeStruct((1, R), F32),
            jax.ShapeDtypeStruct((K, R, D), BF16),
        ),
        in_specs=[pl.BlockSpec(memory_space=pltpu.SMEM), vm, vm, vm],
        out_specs=(vm, vm, vm, pl.BlockSpec(memory_space=pl.ANY)),
        scratch_shapes=[
            pltpu.VMEM((LANES, D), F32), pltpu.VMEM((D, LANES), F32), pltpu.VMEM((K, D), F32), pltpu.VMEM((D, D), F32),
            pltpu.VMEM((D + 16, R), BF16), pltpu.VMEM((R, LANES), F32),
            pltpu.VMEM((R, D), F32), pltpu.VMEM((R, D), F32), pltpu.VMEM((R, D), BF16), pltpu.VMEM((R, D), BF16),
            pltpu.VMEM((D + 16, D), F32), pltpu.VMEM((R, LANES), F32), pltpu.VMEM((LANES, D), F32), pltpu.VMEM((D, LANES), F32),
            pltpu.SemaphoreType.DMA((2,)),
        ],
        compiler_params=pltpu.CompilerParams(vmem_limit_bytes=48 * 1024 * 1024),
        name="member_grads",
    )(count, x, cot, packed)


def back_kernel(G, count_ref, cot_ref, packed_ref, gp_ref, out_ref, rows_ref, cols_ref, wt_ref, ws_ref, acc_ref):
    n, R, D = gp_ref.shape
    step = pl.program_id(0)
    K = pl.num_programs(0) * n

    @pl.when(step == 0)
    def _():
        cols = packed_ref[:, D:D + LANES].astype(F32)
        cols_ref[...] = cols
        rows_ref[...] = cols.T
        wt_ref[...] = packed_ref[:, :D].astype(F32).T
        acc_ref[...] = jnp.zeros_like(acc_ref)

    lane = lax.broadcasted_iota(jnp.int32, (16, LANES), 1)
    for k in range(n):
        i = step * n + k
        r = rows_ref[pl.ds(i, 1), :]
        for c in range(0, D, 16):
            s = jnp.sum(jnp.where(lane == i + G, cols_ref[c:c + 16, :], 0.0), axis=1, keepdims=True)
            ws_ref[k * D + c:k * D + c + 16, :] = (wt_ref[c:c + 16, :] * s * r).astype(BF16)
    left = jnp.concatenate([gp_ref[k] for k in range(n)], axis=1)
    acc_ref[...] += jnp.dot(left, ws_ref[...], preferred_element_type=F32)

    @pl.when(step == pl.num_programs(0) - 1)
    def _():
        lane_rows = lax.broadcasted_iota(jnp.int32, (1, R), 1)
        q_row = jnp.where(lane_rows < count_ref[0], cot_ref[...], 0.0) * (0.5 / G)
        q_wide = jnp.broadcast_to(q_row, (LANES, R)).T
        for l in range(0, D, LANES):
            out_ref[:, l:l + LANES] = acc_ref[:, l:l + LANES] * q_wide


def back_call(count, cot, packed, back, n=4):
    K, R, D = back.shape
    vm = pl.BlockSpec(memory_space=pltpu.VMEM)
    return pl.pallas_call(
        functools.partial(back_kernel, K),
        grid=(K // n,),
        out_shape=jax.ShapeDtypeStruct((R, D), F32),
        in_specs=[pl.BlockSpec(memory_space=pltpu.SMEM), vm, vm, pl.BlockSpec((n, R, D), lambda i: (i, 0, 0))],
        out_specs=pl.BlockSpec((R, D), lambda i: (0, 0)),
        scratch_shapes=[
            pltpu.VMEM((LANES, D), F32), pltpu.VMEM((D, LANES), F32), pltpu.VMEM((D, D), F32),
            pltpu.VMEM((n * D, D), BF16), pltpu.VMEM((R, D), F32),
        ],
        compiler_params=pltpu.CompilerParams(vmem_limit_bytes=48 * 1024 * 1024),
        name="input_grads",
    )(count, cot, packed, back)


STEP = 10
beta_one = 0.5
beta_two = 0.5
epsilon = 1e-06
weight_decay = 0.01
learn_rate = 0.25
AXES = ("dp", "member")


def direction(weight, first_old, second_old, gradient):
    first_new = beta_one * first_old + (1.0 - beta_one) * gradient
    second_new = beta_two * second_old + (1.0 - beta_two) * gradient * gradient
    fix_one = 1.0 - beta_one**STEP
    fix_two = 1.0 - beta_two**STEP
    update = (
        first_new / fix_one / (jnp.sqrt(second_new / fix_two) + epsilon) + weight_decay * weight
    )
    return (first_new, second_new, update)


def bit_groups(n_dp, n_member):
    def split(low, count):
        bits = count.bit_length() - 1
        groups = []
        while bits > 0:
            take = 2 if bits >= 2 else 1
            bits -= take
            groups.append((low << bits, 1 << take))
        return groups

    return split(n_member, n_dp), split(2, n_member // 2) + [(1, 2)]


def swap(value, total, mask):
    return lax.ppermute(value, AXES, [(i, i ^ mask) for i in range(total)])


def gather_groups(value, groups, total, index):
    for axis, (low, size) in enumerate(groups):
        place = (index // low) % size
        held = [value] + [swap(value, total, low * m) for m in range(1, size)]
        value = jnp.stack([lax.select_n(place ^ p, *held) for p in range(size)], axis=axis)
    return value


def shards(n_dp, n_member, objects, counts, cotangent, matrix, matrix_first, matrix_second,
           adapters, adapter_first, adapter_second, head_weights, head_first, head_second):
    R, D = objects.shape
    K = adapters.shape[1]
    own, own_heads = matrix.shape[0], head_weights.shape[0]
    total = n_dp * n_member
    index = lax.axis_index("dp") * n_member + lax.axis_index("member")
    dp_groups, member_groups = bit_groups(n_dp, n_member)
    groups = dp_groups + member_groups

    columns = adapters.reshape(3 * K, own).T
    packed = jnp.concatenate(
        [matrix, columns, jnp.zeros((own, LANES - 3 * K), F32), head_weights.reshape(own, -1)], axis=1
    ).astype(BF16)
    full = gather_groups(packed, groups, total, index).reshape(D, -1)
    cot = cotangent.reshape(1, R)
    grads, head_grads, preds, back = grad_call(counts, objects, cot, full, K)
    input_grad = back_call(counts, cot, full, back)
    predictions = preds.reshape(R)

    grads = grads.reshape([n_dp] + [size for _, size in member_groups] + [own, D + LANES])
    head_grads = head_grads.reshape([size for _, size in member_groups] + [own_heads, D])
    head_grads = jnp.pad(head_grads, [(0, 0)] * len(member_groups) + [(0, 0), (0, LANES)])
    wide = jnp.concatenate(
        [grads.reshape((n_dp,) + grads.shape[1:]).transpose(list(range(1, 1 + len(member_groups))) + [0] + list(range(1 + len(member_groups), grads.ndim))).reshape(
            [size for _, size in member_groups] + [n_dp * own, D + LANES]), head_grads], axis=len(member_groups))
    for axis in reversed(range(len(member_groups))):
        low, size = member_groups[axis]
        place = (index // low) % size
        part = [lax.dynamic_index_in_dim(wide, place ^ m, axis, keepdims=False) for m in range(size)]
        wide = part[0]
        for m in range(1, size):
            wide = wide + swap(part[m].astype(BF16), total, low * m).astype(F32)
    mine = wide[: n_dp * own].reshape([size for _, size in dp_groups] + [own, D + LANES])
    heads = wide[n_dp * own:]
    for axis in reversed(range(len(dp_groups))):
        low, size = dp_groups[axis]
        place = (index // low) % size
        part = [lax.dynamic_index_in_dim(mine, place ^ m, axis, keepdims=False) for m in range(size)]
        mine = part[0]
        lead = part[0].shape[:-2]
        own_sum = heads
        for m in range(1, size):
            both = jnp.concatenate([part[m].reshape(-1, D + LANES), own_sum], axis=0)
            came = swap(both.astype(BF16), total, low * m).astype(F32)
            mine = mine + came[:-own_heads].reshape(lead + (own, D + LANES))
            heads = heads + came[-own_heads:]
    grad_matrix = mine[:, :D]
    grad_adapt = mine[:, D:D + 3 * K].T.reshape(3, K, own)
    head_grad = heads[:, :D]

    m_first, m_second, m_update = direction(matrix, matrix_first, matrix_second, grad_matrix)
    a_first, a_second, a_update = direction(adapters, adapter_first, adapter_second, grad_adapt)
    h_first, h_second, h_update = direction(head_weights, head_first, head_second, head_grad)

    def squares(m, a, h):
        return [jnp.sum(m * m)] + [jnp.sum(a[j] * a[j]) for j in range(3)] + [jnp.sum(h * h) / n_dp]

    sums = jnp.stack(squares(matrix, adapters, head_weights) + squares(m_update, a_update, h_update))
    for low, size in reversed(groups):
        came = [swap(sums, total, low * m) for m in range(1, size)]
        for c in came:
            sums = sums + c
    norms = jnp.sqrt(sums)
    weight_norm, update_norm = norms[:5], norms[5:]
    trust_ratio = weight_norm / update_norm
    new_matrix = matrix - learn_rate * trust_ratio[0] * m_update
    new_adapters = adapters - learn_rate * trust_ratio[1:4][:, None, None] * a_update
    new_heads = head_weights - learn_rate * trust_ratio[4] * h_update
    norm_pairs = jnp.stack([weight_norm, update_norm], axis=1)
    return (predictions, input_grad, new_matrix, m_first, m_second, new_adapters, a_first, a_second,
            new_heads, h_first, h_second, norm_pairs)


def solution(mesh):
    n_dp, n_member = mesh.shape["dp"], mesh.shape["member"]
    rows, cols = P(AXES, None), P(None, None, AXES)
    heads = P("member", None)
    return jax.shard_map(
        functools.partial(shards, n_dp, n_member),
        mesh=mesh,
        in_specs=(rows, P(AXES), P(AXES), rows, rows, rows, cols, cols, cols, heads, heads, heads),
        out_specs=(P(AXES), rows, rows, rows, rows, cols, cols, cols, heads, heads, heads, P()),
        check_vma=False,
    )
```

time: 777 us -> 130 us (0.17)
  blocking collectives: 337 us -> 0 us
  waiting for transfers between devices: 248 us -> 20.6 us
  matrix products: 82.9 us -> 0 us
  Pallas kernels: 0 us -> 60.2 us
  local copies, waits for them, and re-layouts: 45.2 us -> 8.48 us
  other arithmetic: 33 us -> 10.4 us
  between operations: 18.3 us -> 4.25 us
  starting transfers between devices: 11.7 us -> 25.5 us
    all_gather x3 -> x0, blocking collectives: 266 us -> none  [the longest x1 217 us: shards(): lax.all_gather(adapters.astype(jnp.bfloat16), ('dp', 'member'), axis=2, t...]
    reduce_scatter x1 -> x0, waiting for transfers between devices: 133 us -> none  [shards(): lax.psum_scatter(grad_matrix, ('dp', 'member'), scatter_dimension=0, tile...]
    unnamed x3 -> x0, waiting for transfers between devices: 115 us -> none
    dot_general x5 -> x0, matrix products: 82.9 us -> none  [the longest x1 36 us: shards(): jnp.dot(flat_mixed, matrix_low, preferred_element_type=jnp.float32)]
    pallas_call x0 -> x2, Pallas kernels: none -> 60.2 us  [the longest x1 45.4 us: grad_call(): pl.pallas_call(grad_kernel, out_shape=(jax.ShapeDtypeStruct((D, D + LANES...]
    psum x2 -> x0, blocking collectives: 48.3 us -> none  [the longest x1 39.8 us: shards(): update_sums = lax.psum(update_sq, ('dp', 'member'))]
    ppermute x0 -> x21, starting transfers between devices: none -> 25.5 us  [swap(): return lax.ppermute(value, AXES, [(i, i ^ mask) for i in range(total)])]
    all_to_all x2 -> x0, local copies, waits for them, and re-layouts: 24.3 us -> none  [the longest x1 16.2 us: shards(): lax.all_to_all(back_rows, 'member', split_axis=0, concat_axis=1, tiled=True)]
  transfers between devices with their start and end apart: 4 -> 21, of which waited for: 2 -> 16; matrix products, arithmetic and copies ran while one was open for 5% -> 1% of each run, Pallas kernels for 0% -> 11%
where the time goes in v1:
time: 130 us; the launch traced here: 129 us
  Pallas kernels  60.2 us (46%)
  starting transfers between devices  25.5 us (20%)
  waiting for transfers between devices  20.6 us (16%)
  other arithmetic  10.4 us (8%)
  local copies, waits for them, and re-layouts  8.48 us (7%)
  between operations  4.25 us (3%)
    pallas_call x1, Pallas kernels, grad_call(): pl.pallas_call(grad_kernel, out_shape=(jax.ShapeDtypeStruct((D, D + LANES...  45.4 us
    ppermute x21, starting transfers between devices, swap(): return lax.ppermute(value, AXES, [(i, i ^ mask) for i in range(total)])  25.5 us
    ppermute x21, waiting for transfers between devices, swap(): return lax.ppermute(value, AXES, [(i, i ^ mask) for i in range(total)])  20.6 us
    pallas_call x1, Pallas kernels, back_call(): pl.pallas_call(functools.partial(back_kernel, K), grid=(K // n,), out_sha...  14.8 us
    another operation x1, local copies, waits for them, and re-layouts, shards(): jnp.stack(squares(matrix, adapters, head_weights) + squares(m_update, a_u...  5.23 us
  transfers between devices with their start and end apart: 21, of which 16 were waited for; matrix products, arithmetic and copies ran while one was open for 1% of the time, Pallas kernels for 11%

profile of v1, /device:TPU:0, one launch (start us, length us, event | category | flops | bytes accessed | tf_op | source)
XLA Modules:
  0.0 129.4 jit_solution(8923254753345213530)
XLA Ops:
  3.1 4.1 %collective-permute-start.1 = (bf16[16,768]{1,0:T(8,128)(2,1)S(1)}, bf16[16,768]{1,0:T(8,128)(2,1)S(1)}, u32[]{:S(2)}, u32[]{:S(2)}) collective-permute-start(bf16[16,768]{1,0:T(8,128)(2,1)S(1)} %pad_maximum_fusion.6), channel_id=1, source_target_pairs={{0,16},{1,17},{2,18},{3,19},{4,20},{5,21},{6,22},{7,23},{8,24},{9,... | collective-permute-start | bytes 73736 | tf_op jit(solution)/shard_map/ppermute | solution.py:241
  7.2 1.3 %collective-permute-start.2 = (bf16[16,768]{1,0:T(8,128)(2,1)S(1)}, bf16[16,768]{1,0:T(8,128)(2,1)S(1)}, u32[]{:S(2)}, u32[]{:S(2)}) collective-permute-start(bf16[16,768]{1,0:T(8,128)(2,1)S(1)} %pad_maximum_fusion.6), channel_id=1, source_target_pairs={{0,24},{1,25},{2,26},{3,27},{4,28},{5,29},{6,30},{7,31},{8,16},{9,... | collective-permute-start | bytes 73736 | tf_op jit(solution)/shard_map/ppermute | solution.py:241
  9.0 3.8 %collective-permute-done.2 = bf16[16,768]{1,0:T(8,128)(2,1)S(1)} collective-permute-done((bf16[16,768]{1,0:T(8,128)(2,1)S(1)}, bf16[16,768]{1,0:T(8,128)(2,1)S(1)}, u32[]{:S(2)}, u32[]{:S(2)}) %collective-permute-start.2) | collective-permute-done | bytes 24608 | tf_op jit(solution)/shard_map/ppermute | solution.py:241
  12.8 1.6 %collective-permute-start.4 = (bf16[4,16,768]{2,1,0:T(8,128)(2,1)S(1)}, bf16[4,16,768]{2,1,0:T(8,128)(2,1)S(1)}, u32[]{:S(2)}, u32[]{:S(2)}) collective-permute-start(bf16[4,16,768]{2,1,0:T(8,128)(2,1)S(1)} %pad_maximum_fusion.2), channel_id=1, source_target_pairs={{0,4},{1,5},{2,6},{3,7},{4,0},{5,1},{6,2},{7,3},{8,12},{9,13},{10,... | collective-permute-start | bytes 294920 | tf_op jit(solution)/shard_map/ppermute | solution.py:241
  14.4 1.4 %collective-permute-start.5 = (bf16[4,16,768]{2,1,0:T(8,128)(2,1)S(1)}, bf16[4,16,768]{2,1,0:T(8,128)(2,1)S(1)}, u32[]{:S(2)}, u32[]{:S(2)}) collective-permute-start(bf16[4,16,768]{2,1,0:T(8,128)(2,1)S(1)} %pad_maximum_fusion.2), channel_id=1, source_target_pairs={{0,6},{1,7},{2,4},{3,5},{4,2},{5,3},{6,0},{7,1},{8,14},{9,15},{10,... | collective-permute-start | bytes 294920 | tf_op jit(solution)/shard_map/ppermute | solution.py:241
  16.4 1.8 %collective-permute-done.4 = bf16[4,16,768]{2,1,0:T(8,128)(2,1)S(1)} collective-permute-done((bf16[4,16,768]{2,1,0:T(8,128)(2,1)S(1)}, bf16[4,16,768]{2,1,0:T(8,128)(2,1)S(1)}, u32[]{:S(2)}, u32[]{:S(2)}) %collective-permute-start.4) | collective-permute-done | bytes 98336 | tf_op jit(solution)/shard_map/ppermute | solution.py:241
  18.1 1.8 %collective-permute-done.5 = bf16[4,16,768]{2,1,0:T(8,128)(2,1)S(1)} collective-permute-done((bf16[4,16,768]{2,1,0:T(8,128)(2,1)S(1)}, bf16[4,16,768]{2,1,0:T(8,128)(2,1)S(1)}, u32[]{:S(2)}, u32[]{:S(2)}) %collective-permute-start.5) | collective-permute-done | bytes 98336 | tf_op jit(solution)/shard_map/ppermute | solution.py:241
  23.5 45.4 %member_grads.1 = (f32[512,640]{1,0:T(8,128)S(1)}, f32[32,512]{1,0:T(8,128)S(1)}, f32[1,512]{1,0:T(1,128)}, bf16[32,512,512]{2,1,0:T(8,128)(2,1)}) custom-call(s32[1]{0:T(128)S(6)} %copy.52.count_ref, bf16[512,512]{1,0:T(8,128)(2,1)S(1)} %copy-done, f32[1,512]{1,0:T(1,128)S(1)} %bitcast.78, bf16[512,768]{1,0:T(8,128)(2,1)S(1)} %bitcast.75), custom_call_target="tpu_custom_call" | custom-call | tf_op jit(solution)/shard_map/member_grads/pallas_call | solution.py:135
  69.2 1.1 copy-done.2
  70.7 1.5 %collective-permute-done.7 = bf16[4,68,640]{2,1,0:T(8,128)(2,1)S(1)} collective-permute-done((bf16[4,68,640]{2,1,0:T(8,128)(2,1)S(1)}, bf16[4,68,640]{2,1,0:T(8,128)(2,1)S(1)}, u32[]{:S(2)}, u32[]{:S(2)}) %collective-permute-start.7) | collective-permute-done | bytes 348192 | tf_op jit(solution)/shard_map/ppermute | solution.py:241
  72.2 1.2 bitcast_add_fusion
  73.4 2.1 %collective-permute-start.10 = (bf16[68,640]{1,0:T(8,128)(2,1)S(1)}, bf16[68,640]{1,0:T(8,128)(2,1)S(1)}, u32[]{:S(2)}, u32[]{:S(2)}) collective-permute-start(bf16[68,640]{1,0:T(8,128)(2,1)S(1)} %get-tuple-element.52), channel_id=1, source_target_pairs={{0,6},{1,7},{2,4},{3,5},{4,2},{5,3},{6,0},{7,1},{8,14},{9,15},{10,... | collective-permute-start | bytes 261128 | tf_op jit(solution)/shard_map/ppermute | solution.py:241
  76.9 2.3 %collective-permute-done.10 = bf16[68,640]{1,0:T(8,128)(2,1)S(1)} collective-permute-done((bf16[68,640]{1,0:T(8,128)(2,1)S(1)}, bf16[68,640]{1,0:T(8,128)(2,1)S(1)}, u32[]{:S(2)}, u32[]{:S(2)}) %collective-permute-start.10) | collective-permute-done | bytes 87072 | tf_op jit(solution)/shard_map/ppermute | solution.py:241
  79.2 1.9 %collective-permute-done.9 = bf16[68,640]{1,0:T(8,128)(2,1)S(1)} collective-permute-done((bf16[68,640]{1,0:T(8,128)(2,1)S(1)}, bf16[68,640]{1,0:T(8,128)(2,1)S(1)}, u32[]{:S(2)}, u32[]{:S(2)}) %collective-permute-start.9) | collective-permute-done | bytes 87072 | tf_op jit(solution)/shard_map/ppermute | solution.py:241
  81.3 2.1 %collective-permute-start.13 = (bf16[20,640]{1,0:T(8,128)(2,1)S(1)}, bf16[20,640]{1,0:T(8,128)(2,1)S(1)}, u32[]{:S(2)}, u32[]{:S(2)}) collective-permute-start(bf16[20,640]{1,0:T(8,128)(2,1)S(1)} %get-tuple-element.68), channel_id=1, source_target_pairs={{0,24},{1,25},{2,26},{3,27},{4,28},{5,29},{6,30},{7,31},{8,16},{9,... | collective-permute-start | bytes 76808 | tf_op jit(solution)/shard_map/ppermute | solution.py:241
  83.4 2.4 %collective-permute-start.11 = (bf16[20,640]{1,0:T(8,128)(2,1)S(1)}, bf16[20,640]{1,0:T(8,128)(2,1)S(1)}, u32[]{:S(2)}, u32[]{:S(2)}) collective-permute-start(bf16[20,640]{1,0:T(8,128)(2,1)S(1)} %get-tuple-element.66), channel_id=1, source_target_pairs={{0,8},{1,9},{2,10},{3,11},{4,12},{5,13},{6,14},{7,15},{8,0},{9,1},... | collective-permute-start | bytes 76808 | tf_op jit(solution)/shard_map/ppermute | solution.py:241
  86.5 14.8 %input_grads.1 = f32[512,512]{1,0:T(8,128)} custom-call(s32[1]{0:T(128)S(6)} %copy.52.count_ref, f32[1,512]{1,0:T(1,128)S(1)} %bitcast.79, bf16[512,768]{1,0:T(8,128)(2,1)S(1)} %bitcast.76, bf16[32,512,512]{2,1,0:T(8,128)(2,1)} %get-tuple-element.17.gp_ref), custom_call_target="tpu_custom_call" | custom-call | tf_op jit(solution)/shard_map/input_grads/pallas_call | solution.py:192
  102.8 1.2 multiply_reduce_fusion.2
  106.0 5.2 %stack.104 = f32[10]{0:T(128)S(1)} concatenate(f32[1]{0:T(128)} %bitcast.14, f32[1]{0:T(128)} %bitcast.15, f32[1]{0:T(128)} %bitcast.16, f32[1]{0:T(128)} %bitcast.17, f32[1]{0:T(128)} %bitcast.18, f32[1]{0:T(128)} %bitcast.33, f32[1]{0:T(128)} %bitcast.35, f32[1]{0:T(128)} %bitcast.36, f32[1]{0:T(128)} %bitcast.37, f32[1]{0:T(128)} %bitcast.38), dimensions={0} | concatenate | bytes 80 | tf_op jit(solution)/shard_map/stack | solution.py:310
  111.3 1.1 collective-permute-done.14
  112.4 1.6 %collective-permute-start.17 = (f32[10]{0:T(128)S(1)}, f32[10]{0:T(128)S(1)}, u32[]{:S(2)}, u32[]{:S(2)}) collective-permute-start(f32[10]{0:T(128)S(1)} %add.189), channel_id=1, source_target_pairs={{0,6},{1,7},{2,4},{3,5},{4,2},{5,3},{6,0},{7,1},{8,14},{9,15},{10,... | collective-permute-start | bytes 128 | tf_op jit(solution)/shard_map/ppermute | solution.py:241
  118.4 2.0 %collective-permute-start.20 = (f32[10]{0:T(128)S(1)}, f32[10]{0:T(128)S(1)}, u32[]{:S(2)}, u32[]{:S(2)}) collective-permute-start(f32[10]{0:T(128)S(1)} %add_add_fusion), channel_id=1, source_target_pairs={{0,24},{1,25},{2,26},{3,27},{4,28},{5,29},{6,30},{7,31},{8,16},{9,... | collective-permute-start | bytes 128 | tf_op jit(solution)/shard_map/ppermute | solution.py:241
  120.4 2.4 %collective-permute-start.18 = (f32[10]{0:T(128)S(1)}, f32[10]{0:T(128)S(1)}, u32[]{:S(2)}, u32[]{:S(2)}) collective-permute-start(f32[10]{0:T(128)S(1)} %add_add_fusion), channel_id=1, source_target_pairs={{0,8},{1,9},{2,10},{3,11},{4,12},{5,13},{6,14},{7,15},{8,0},{9,1},... | collective-permute-start | bytes 128 | tf_op jit(solution)/shard_map/ppermute | solution.py:241
  123.8 1.1 collective-permute-done.19
  (102 shorter events, 20.0 us)
Async XLA Ops:
  3.1 5.9 %collective-permute-start.1 = (bf16[16,768]{1,0:T(8,128)(2,1)S(1)}, bf16[16,768]{1,0:T(8,128)(2,1)S(1)}, u32[]{:S(2)}, u32[]{:S(2)}) collective-permute-start(bf16[16,768]{1,0:T(8,128)(2,1)S(1)} %pad_maximum_fusion.6), channel_id=1, source_target_pairs={{0,16},{1,17},{2,18},{3,19},{4,20},{5,21},{6,22},{7,23},{8,24},{9,... | collective-permute-start | bytes 73736 | tf_op jit(solution)/shard_map/ppermute | solution.py:241
  7.2 5.6 %collective-permute-start.2 = (bf16[16,768]{1,0:T(8,128)(2,1)S(1)}, bf16[16,768]{1,0:T(8,128)(2,1)S(1)}, u32[]{:S(2)}, u32[]{:S(2)}) collective-permute-start(bf16[16,768]{1,0:T(8,128)(2,1)S(1)} %pad_maximum_fusion.6), channel_id=1, source_target_pairs={{0,24},{1,25},{2,26},{3,27},{4,28},{5,29},{6,30},{7,31},{8,16},{9,... | collective-permute-start | bytes 73736 | tf_op jit(solution)/shard_map/ppermute | solution.py:241
  8.5 4.3 %collective-permute-start = (bf16[16,768]{1,0:T(8,128)(2,1)S(1)}, bf16[16,768]{1,0:T(8,128)(2,1)S(1)}, u32[]{:S(2)}, u32[]{:S(2)}) collective-permute-start(bf16[16,768]{1,0:T(8,128)(2,1)S(1)} %pad_maximum_fusion.6), channel_id=1, source_target_pairs={{0,8},{1,9},{2,10},{3,11},{4,12},{5,13},{6,14},{7,15},{8,0},{9,1},... | collective-permute-start | bytes 73736 | tf_op jit(solution)/shard_map/ppermute | solution.py:241
  12.8 5.3 %collective-permute-start.4 = (bf16[4,16,768]{2,1,0:T(8,128)(2,1)S(1)}, bf16[4,16,768]{2,1,0:T(8,128)(2,1)S(1)}, u32[]{:S(2)}, u32[]{:S(2)}) collective-permute-start(bf16[4,16,768]{2,1,0:T(8,128)(2,1)S(1)} %pad_maximum_fusion.2), channel_id=1, source_target_pairs={{0,4},{1,5},{2,6},{3,7},{4,0},{5,1},{6,2},{7,3},{8,12},{9,13},{10,... | collective-permute-start | bytes 294920 | tf_op jit(solution)/shard_map/ppermute | solution.py:241
  14.4 5.5 %collective-permute-start.5 = (bf16[4,16,768]{2,1,0:T(8,128)(2,1)S(1)}, bf16[4,16,768]{2,1,0:T(8,128)(2,1)S(1)}, u32[]{:S(2)}, u32[]{:S(2)}) collective-permute-start(bf16[4,16,768]{2,1,0:T(8,128)(2,1)S(1)} %pad_maximum_fusion.2), channel_id=1, source_target_pairs={{0,6},{1,7},{2,4},{3,5},{4,2},{5,3},{6,0},{7,1},{8,14},{9,15},{10,... | collective-permute-start | bytes 294920 | tf_op jit(solution)/shard_map/ppermute | solution.py:241
  15.9 4.6 %collective-permute-start.3 = (bf16[4,16,768]{2,1,0:T(8,128)(2,1)S(1)}, bf16[4,16,768]{2,1,0:T(8,128)(2,1)S(1)}, u32[]{:S(2)}, u32[]{:S(2)}) collective-permute-start(bf16[4,16,768]{2,1,0:T(8,128)(2,1)S(1)} %pad_maximum_fusion.2), channel_id=1, source_target_pairs={{0,2},{1,3},{2,0},{3,1},{4,6},{5,7},{6,4},{7,5},{8,10},{9,11},{10,... | collective-permute-start | bytes 294920 | tf_op jit(solution)/shard_map/ppermute | solution.py:241
  20.6 1.8 %collective-permute-start.6 = (bf16[4,4,16,768]{3,2,0,1:T(8,128)(2,1)S(1)}, bf16[4,4,16,768]{3,2,0,1:T(8,128)(2,1)S(1)}, u32[]{:S(2)}, u32[]{:S(2)}) collective-permute-start(bf16[4,4,16,768]{3,2,0,1:T(8,128)(2,1)S(1)} %pad_maximum_fusion.1), channel_id=1, source_target_pairs={{0,1},{1,0},{2,3},{3,2},{4,5},{5,4},{6,7},{7,6},{8,9},{9,8},{10,11... | collective-permute-start | bytes 1179656 | tf_op jit(solution)/shard_map/ppermute | solution.py:241
  70.4 1.8 %collective-permute-start.7 = (bf16[4,68,640]{2,1,0:T(8,128)(2,1)S(1)}, bf16[4,68,640]{2,1,0:T(8,128)(2,1)S(1)}, u32[]{:S(2)}, u32[]{:S(2)}) collective-permute-start(bf16[4,68,640]{2,1,0:T(8,128)(2,1)S(1)} %fusion), channel_id=1, source_target_pairs={{0,1},{1,0},{2,3},{3,2},{4,5},{5,4},{6,7},{7,6},{8,9},{9,8},{10,11... | collective-permute-start | bytes 1044488 | tf_op jit(solution)/shard_map/ppermute | solution.py:241
  73.4 5.9 %collective-permute-start.10 = (bf16[68,640]{1,0:T(8,128)(2,1)S(1)}, bf16[68,640]{1,0:T(8,128)(2,1)S(1)}, u32[]{:S(2)}, u32[]{:S(2)}) collective-permute-start(bf16[68,640]{1,0:T(8,128)(2,1)S(1)} %get-tuple-element.52), channel_id=1, source_target_pairs={{0,6},{1,7},{2,4},{3,5},{4,2},{5,3},{6,0},{7,1},{8,14},{9,15},{10,... | collective-permute-start | bytes 261128 | tf_op jit(solution)/shard_map/ppermute | solution.py:241
  75.4 5.7 %collective-permute-start.9 = (bf16[68,640]{1,0:T(8,128)(2,1)S(1)}, bf16[68,640]{1,0:T(8,128)(2,1)S(1)}, u32[]{:S(2)}, u32[]{:S(2)}) collective-permute-start(bf16[68,640]{1,0:T(8,128)(2,1)S(1)} %get-tuple-element.53), channel_id=1, source_target_pairs={{0,4},{1,5},{2,6},{3,7},{4,0},{5,1},{6,2},{7,3},{8,12},{9,13},{10,... | collective-permute-start | bytes 261128 | tf_op jit(solution)/shard_map/ppermute | solution.py:241
  76.0 5.2 %collective-permute-start.8 = (bf16[68,640]{1,0:T(8,128)(2,1)S(1)}, bf16[68,640]{1,0:T(8,128)(2,1)S(1)}, u32[]{:S(2)}, u32[]{:S(2)}) collective-permute-start(bf16[68,640]{1,0:T(8,128)(2,1)S(1)} %get-tuple-element.51), channel_id=1, source_target_pairs={{0,2},{1,3},{2,0},{3,1},{4,6},{5,7},{6,4},{7,5},{8,10},{9,11},{10,... | collective-permute-start | bytes 261128 | tf_op jit(solution)/shard_map/ppermute | solution.py:241
  81.3 20.0 %collective-permute-start.13 = (bf16[20,640]{1,0:T(8,128)(2,1)S(1)}, bf16[20,640]{1,0:T(8,128)(2,1)S(1)}, u32[]{:S(2)}, u32[]{:S(2)}) collective-permute-start(bf16[20,640]{1,0:T(8,128)(2,1)S(1)} %get-tuple-element.68), channel_id=1, source_target_pairs={{0,24},{1,25},{2,26},{3,27},{4,28},{5,29},{6,30},{7,31},{8,16},{9,... | collective-permute-start | bytes 76808 | tf_op jit(solution)/shard_map/ppermute | solution.py:241
  83.4 17.9 %collective-permute-start.12 = (bf16[20,640]{1,0:T(8,128)(2,1)S(1)}, bf16[20,640]{1,0:T(8,128)(2,1)S(1)}, u32[]{:S(2)}, u32[]{:S(2)}) collective-permute-start(bf16[20,640]{1,0:T(8,128)(2,1)S(1)} %get-tuple-element.67), channel_id=1, source_target_pairs={{0,16},{1,17},{2,18},{3,19},{4,20},{5,21},{6,22},{7,23},{8,24},{9,... | collective-permute-start | bytes 76808 | tf_op jit(solution)/shard_map/ppermute | solution.py:241
  83.4 17.9 %collective-permute-start.11 = (bf16[20,640]{1,0:T(8,128)(2,1)S(1)}, bf16[20,640]{1,0:T(8,128)(2,1)S(1)}, u32[]{:S(2)}, u32[]{:S(2)}) collective-permute-start(bf16[20,640]{1,0:T(8,128)(2,1)S(1)} %get-tuple-element.66), channel_id=1, source_target_pairs={{0,8},{1,9},{2,10},{3,11},{4,12},{5,13},{6,14},{7,15},{8,0},{9,1},... | collective-permute-start | bytes 76808 | tf_op jit(solution)/shard_map/ppermute | solution.py:241
  86.5 18.9 %copy-start.4 = (f32[16,512]{1,0:T(8,128)S(1)}, f32[16,512]{1,0:T(8,128)}, u32[]{:S(2)}) copy-start(f32[16,512]{1,0:T(8,128)} %param.15) | copy-start | bytes 98308
  106.0 23.4 %copy-start.5 = (f32[16,512]{1,0:T(8,128)}, f32[16,512]{1,0:T(8,128)S(1)}, u32[]{:S(2)}) copy-start(f32[16,512]{1,0:T(8,128)S(1)} %get-tuple-element.47) | copy-start | bytes 98308
  106.0 23.4 %copy-start.6 = (f32[16,512]{1,0:T(8,128)}, f32[16,512]{1,0:T(8,128)S(1)}, u32[]{:S(2)}) copy-start(f32[16,512]{1,0:T(8,128)S(1)} %get-tuple-element.48) | copy-start | bytes 98308
  111.3 1.2 collective-permute-start.14
  112.4 4.4 %collective-permute-start.17 = (f32[10]{0:T(128)S(1)}, f32[10]{0:T(128)S(1)}, u32[]{:S(2)}, u32[]{:S(2)}) collective-permute-start(f32[10]{0:T(128)S(1)} %add.189), channel_id=1, source_target_pairs={{0,6},{1,7},{2,4},{3,5},{4,2},{5,3},{6,0},{7,1},{8,14},{9,15},{10,... | collective-permute-start | bytes 128 | tf_op jit(solution)/shard_map/ppermute | solution.py:241
  114.1 3.5 %collective-permute-start.16 = (f32[10]{0:T(128)S(1)}, f32[10]{0:T(128)S(1)}, u32[]{:S(2)}, u32[]{:S(2)}) collective-permute-start(f32[10]{0:T(128)S(1)} %add.189), channel_id=1, source_target_pairs={{0,4},{1,5},{2,6},{3,7},{4,0},{5,1},{6,2},{7,3},{8,12},{9,13},{10,... | collective-permute-start | bytes 128 | tf_op jit(solution)/shard_map/ppermute | solution.py:241
  114.9 3.5 %collective-permute-start.15 = (f32[10]{0:T(128)S(1)}, f32[10]{0:T(128)S(1)}, u32[]{:S(2)}, u32[]{:S(2)}) collective-permute-start(f32[10]{0:T(128)S(1)} %add.189), channel_id=1, source_target_pairs={{0,2},{1,3},{2,0},{3,1},{4,6},{5,7},{6,4},{7,5},{8,10},{9,11},{10,... | collective-permute-start | bytes 128 | tf_op jit(solution)/shard_map/ppermute | solution.py:241
  118.4 5.3 %collective-permute-start.20 = (f32[10]{0:T(128)S(1)}, f32[10]{0:T(128)S(1)}, u32[]{:S(2)}, u32[]{:S(2)}) collective-permute-start(f32[10]{0:T(128)S(1)} %add_add_fusion), channel_id=1, source_target_pairs={{0,24},{1,25},{2,26},{3,27},{4,28},{5,29},{6,30},{7,31},{8,16},{9,... | collective-permute-start | bytes 128 | tf_op jit(solution)/shard_map/ppermute | solution.py:241
  120.4 4.4 %collective-permute-start.19 = (f32[10]{0:T(128)S(1)}, f32[10]{0:T(128)S(1)}, u32[]{:S(2)}, u32[]{:S(2)}) collective-permute-start(f32[10]{0:T(128)S(1)} %add_add_fusion), channel_id=1, source_target_pairs={{0,16},{1,17},{2,18},{3,19},{4,20},{5,21},{6,22},{7,23},{8,24},{9,... | collective-permute-start | bytes 128 | tf_op jit(solution)/shard_map/ppermute | solution.py:241
  120.4 4.4 %collective-permute-start.18 = (f32[10]{0:T(128)S(1)}, f32[10]{0:T(128)S(1)}, u32[]{:S(2)}, u32[]{:S(2)}) collective-permute-start(f32[10]{0:T(128)S(1)} %add_add_fusion), channel_id=1, source_target_pairs={{0,8},{1,9},{2,10},{3,11},{4,12},{5,13},{6,14},{7,15},{8,0},{9,1},... | collective-permute-start | bytes 128 | tf_op jit(solution)/shard_map/ppermute | solution.py:241
  (11 other events, 135.0 us)

commit v2 on v1

v2 whole, which is shorter than its diff:
```python
import functools

import jax
import jax.numpy as jnp
from jax import lax
from jax.experimental import pallas as pl
from jax.experimental.pallas import tpu as pltpu
from jax.sharding import PartitionSpec as P

LANES = 128
F32, BF16 = jnp.float32, jnp.bfloat16
STEP = 10
beta_one = 0.5
beta_two = 0.5
epsilon = 1e-06
weight_decay = 0.01
learn_rate = 0.25
AXES = ("dp", "member")
VMEM = pl.BlockSpec(memory_space=pltpu.VMEM)
SMEM = pl.BlockSpec(memory_space=pltpu.SMEM)
LIMIT = 48 * 1024 * 1024


def shape(dims, dtype=F32):
    return jax.ShapeDtypeStruct(dims, dtype)


def this_core():
    return lax.rem(lax.axis_index("member"), 2)


def pack_kernel(count_ref, matrix_ref, adapters_ref, heads_ref, cot_ref, packed_ref, q_ref):
    own, D = matrix_ref.shape
    K = adapters_ref.shape[2]
    packed_ref[:, :D] = matrix_ref[...].astype(BF16)
    parts = [adapters_ref[k] for k in range(3)] + [jnp.zeros((own, LANES - 3 * K), F32)]
    packed_ref[:, D:D + LANES] = jnp.concatenate(parts, axis=1).astype(BF16)
    L = packed_ref.shape[1] - D - LANES
    rows = []
    for t in range(own):
        h, c = divmod(t * L, D)
        rows.append(heads_ref[h:h + 1, c:c + L])
    packed_ref[:, D + LANES:] = jnp.concatenate(rows, axis=0).astype(BF16)
    lane = lax.broadcasted_iota(jnp.int32, cot_ref.shape, 1)
    q_ref[...] = jnp.where(lane < count_ref[0], cot_ref[...], 0.0) * (1.0 / K)


def pack_call(counts, matrix, adapters_t, heads, cot):
    own, D = matrix.shape
    L = heads.shape[0] * D // own
    return pl.pallas_call(
        pack_kernel,
        out_shape=(shape((own, D + LANES + L), BF16), shape(cot.shape)),
        in_specs=[SMEM, VMEM, VMEM, VMEM, VMEM],
        out_specs=(VMEM, VMEM),
        name="pack_weights",
    )(counts, matrix, adapters_t, heads, cot)


def grad_kernel(
    x0_ref, x1_ref, q0_ref, q1_ref, packed_ref,
    keep_ref, sent_ref, heads_grad_ref, pred_ref, back_ref,
    rows_ref, cols_ref, heads_ref, weight_ref, x_ref, xq_ref, q_ref, z0_ref, z1_ref, gp0_ref, gp1_ref,
    post_ref, pred_acc, sums_ref, gr_ref, grads_ref, *, own,
):
    half, D = x0_ref.shape
    R = 2 * half
    K = heads_grad_ref.shape[0]
    members = K // 2
    n = back_ref.shape[0]
    step_id, steps = pl.program_id(0), pl.num_programs(0)
    core = this_core()
    base = core * members
    z_refs, gp_refs = (z0_ref, z1_ref), (gp0_ref, gp1_ref)

    def set_up():
        weight_ref[...] = packed_ref[:, :D].astype(F32)
        cols = packed_ref[:, D:D + LANES].astype(F32)
        cols_ref[...] = cols
        rows_ref[...] = cols.T
        L = packed_ref.shape[1] - D - LANES
        per_head = D // L
        for c in range(0, L, LANES):
            gr_ref[:K * per_head, :] = packed_ref[:K * per_head, D + LANES + c:D + 2 * LANES + c].astype(F32)
            for k in range(per_head):
                heads_ref[:, k * L + c:k * L + c + LANES] = gr_ref[pl.ds(k, K, stride=per_head), :]
        x_ref[:half, :] = x0_ref[...]
        x_ref[half:, :] = x1_ref[...]
        for side, (x_side, q_side) in enumerate(((x0_ref, q0_ref), (x1_ref, q1_ref))):
            at = slice(side * half, (side + 1) * half)
            q_row = q_side[...]
            q_ref[at, :] = jnp.broadcast_to(q_row, (LANES, half)).T
            half_q = 0.5 * q_row
            q_hi = half_q.astype(BF16)
            q_lo = (half_q - q_hi.astype(F32)).astype(BF16)
            xq_ref[:D, at] = (x_side[...].astype(F32).T * half_q).astype(BF16)
            sub = lax.broadcasted_iota(jnp.int32, (16, half), 0)
            extra = jnp.where(sub == 0, q_hi.astype(F32), jnp.where(sub == 1, q_lo.astype(F32), 0.0))
            xq_ref[D:, at] = extra.astype(BF16)
        for ref in (pred_acc, gr_ref, sums_ref, grads_ref, gp1_ref, heads_grad_ref):
            ref[...] = jnp.zeros_like(ref)

    def forward(i, z_ref):
        r = rows_ref[pl.ds(base + i, 1), :].astype(BF16)
        z_ref[...] = jnp.dot(x_ref[...] * r, packed_ref[:, :D], preferred_element_type=F32)

    def middle(i, k, z_ref, gp_ref):
        s = 0.5 * rows_ref[pl.ds(K + base + i, 1), :]
        b = 0.5 * rows_ref[pl.ds(2 * K + base + i, 1), :]
        hb = heads_ref[pl.ds(base + i, 1), :]
        total = None
        step = 16
        for c in range(0, R, step):
            y = z_ref[c:c + step, :] * s + b
            t = jnp.tanh(y)
            a = 1.0 + t
            h = y * a
            d = a + h * (1.0 - t)
            gp = (hb * d).astype(BF16)
            gp_ref[c:c + step, :] = gp
            back_ref[k, c:c + step, :] = gp
            hh = h * hb
            pred_acc[c:c + step, :] += sum(hh[:, l:l + LANES] for l in range(0, D, LANES))
            q = q_ref[c:c + step, :]
            qh = jnp.concatenate([h[:, l:l + LANES] * q for l in range(0, D, LANES)], axis=1)
            part = sum(qh[j:j + 8] for j in range(0, step, 8))
            total = part if total is None else total + part
        heads_grad_ref[pl.ds(base + i, 1), :] = jnp.sum(total, axis=0, keepdims=True)

    def after(i, gp_ref):
        s = rows_ref[pl.ds(K + base + i, 1), :]
        post_ref[...] = jnp.dot(xq_ref[...], gp_ref[...], preferred_element_type=F32)
        sums_ref[pl.ds(2 * K + base + i, 1), :] = post_ref[D:D + 1, :] + post_ref[D + 1:D + 2, :]
        total = None
        step = 16
        lane = lax.broadcasted_iota(jnp.int32, (step, LANES), 1)
        for c in range(0, D, step):
            g = post_ref[c:c + step, :]
            r = jnp.sum(jnp.where(lane == base + i, cols_ref[c:c + step, :], 0.0), axis=1, keepdims=True)
            t = g * weight_ref[c:c + step, :]
            rt = t * r
            part = sum(rt[j:j + 8] for j in range(0, step, 8))
            total = part if total is None else total + part
            st = t * s
            fold = sum(st[:, l:l + LANES] for l in range(0, D, LANES))
            gr_ref[c:c + step, :] += jnp.where(lane == base + i, jnp.sum(fold, axis=1, keepdims=True), 0.0)
            grads_ref[c:c + step, :D] += (g * s) * r
        sums_ref[pl.ds(K + base + i, 1), :] = jnp.sum(total, axis=0, keepdims=True)

    @pl.when(step_id == 0)
    def _():
        set_up()
        forward(0, z_refs[0])
        middle(0, 0, z_refs[0], gp_refs[0])
        forward(1, z_refs[1])

    @pl.when(step_id > 0)
    def _():
        i = step_id * n
        middle(i, 0, z_refs[0], gp_refs[0])
        after(i - 1, gp_refs[1])
        forward(i + 1, z_refs[1])

    for k in range(1, n):
        i, now, other = step_id * n + k, k % 2, (k + 1) % 2
        middle(i, k, z_refs[now], gp_refs[now])
        after(i - 1, gp_refs[other])
        forward(jnp.minimum(i + 1, members - 1), z_refs[other])

    @pl.when(step_id == steps - 1)
    def _():
        after(members - 1, gp_refs[1])
        for side in range(2):
            at = slice(side * half, (side + 1) * half)
            pred_ref[side:side + 1, :] = jnp.sum(pred_acc[at, :].T, axis=0, keepdims=True)
        grads_ref[:, D:] = sums_ref[...].T + gr_ref[...]
        for j in range(D // (2 * own)):
            low = grads_ref[2 * j * own:(2 * j + 1) * own, :]
            high = grads_ref[(2 * j + 1) * own:(2 * j + 2) * own, :]
            keep_ref[j * own:(j + 1) * own, :] = jnp.where(core == 0, low, high)
            sent_ref[j * own:(j + 1) * own, :] = jnp.where(core == 0, high, low).astype(BF16)


def grad_call(x0, x1, q0, q1, packed, K, own, n=2):
    half, D = x0.shape
    R = 2 * half
    members = K // 2
    flops = 4 * members * R * D * D
    return pl.pallas_call(
        functools.partial(grad_kernel, own=own),
        grid=(members // n,),
        out_shape=(
            shape((D // 2, D + LANES)), shape((D // 2, D + LANES), BF16), shape((K, D)), shape((2, half)),
            shape((members, R, D), BF16),
        ),
        in_specs=[VMEM] * 5,
        out_specs=(VMEM, VMEM, VMEM, VMEM, pl.BlockSpec((n, R, D), lambda i: (i, 0, 0))),
        scratch_shapes=[
            pltpu.VMEM((LANES, D), F32), pltpu.VMEM((D, LANES), F32), pltpu.VMEM((K, D), F32), pltpu.VMEM((D, D), F32),
            pltpu.VMEM((R, D), BF16), pltpu.VMEM((D + 16, R), BF16), pltpu.VMEM((R, LANES), F32),
            pltpu.VMEM((R, D), F32), pltpu.VMEM((R, D), F32), pltpu.VMEM((R, D), BF16), pltpu.VMEM((R, D), BF16),
            pltpu.VMEM((D + 16, D), F32), pltpu.VMEM((R, LANES), F32), pltpu.VMEM((LANES, D), F32),
            pltpu.VMEM((D, LANES), F32), pltpu.VMEM((D, D + LANES), F32),
        ],
        compiler_params=pltpu.CompilerParams(vmem_limit_bytes=LIMIT),
        cost_estimate=pl.CostEstimate(flops=2 * flops, bytes_accessed=members * R * D * 2, transcendentals=members * R * D),
        name="member_grads",
    )(x0, x1, q0, q1, packed)


def back_kernel(q_ref, packed_ref, gp_ref, *refs, members, other):
    if other:
        out_ref, rows_ref, cols_ref, wt_ref, ws_ref, acc_ref = refs
    else:
        came_ref, pred_ref, pred_came_ref, out_ref, pred_out_ref, rows_ref, cols_ref, wt_ref, ws_ref, acc_ref = refs
    n, R, D = gp_ref.shape
    step = pl.program_id(0)
    K = 2 * members
    base = this_core() * members

    @pl.when(step == 0)
    def _():
        cols = packed_ref[:, D:D + LANES].astype(F32)
        cols_ref[...] = cols
        rows_ref[...] = cols.T
        wt_ref[...] = packed_ref[:, :D].astype(F32).T
        acc_ref[...] = jnp.zeros_like(acc_ref)

    lane = lax.broadcasted_iota(jnp.int32, (16, LANES), 1)
    for k in range(n):
        i = base + step * n + k
        r = rows_ref[pl.ds(i, 1), :]
        for c in range(0, D, 16):
            s = jnp.sum(jnp.where(lane == i + K, cols_ref[c:c + 16, :], 0.0), axis=1, keepdims=True)
            ws_ref[k * D + c:k * D + c + 16, :] = (wt_ref[c:c + 16, :] * s * r).astype(BF16)
    left = jnp.concatenate([gp_ref[k] for k in range(n)], axis=1)
    acc_ref[...] += jnp.dot(left, ws_ref[...], preferred_element_type=F32)

    @pl.when(step == pl.num_programs(0) - 1)
    def _():
        q_wide = jnp.broadcast_to(0.5 * q_ref[...], (LANES, R)).T
        for l in range(0, D, LANES):
            value = acc_ref[:, l:l + LANES] * q_wide
            out_ref[:, l:l + LANES] = value if other else value + came_ref[:, l:l + LANES]
        if not other:
            pred_out_ref[...] = (pred_ref[0:1, :] + pred_came_ref[...]) * (1.0 / K)


def back_call(q, packed, back, came=None, n=4):
    members, R2, D = back.shape
    R = R2 // 2
    other = came is None
    where = 1 if other else 0
    more = [] if other else list(came)
    return pl.pallas_call(
        functools.partial(back_kernel, members=members, other=other),
        grid=(members // n,),
        out_shape=shape((R, D)) if other else (shape((R, D)), shape((1, R))),
        in_specs=[VMEM, VMEM, pl.BlockSpec((n, R, D), lambda i: (i, where, 0))] + [VMEM] * len(more),
        out_specs=VMEM if other else (VMEM, VMEM),
        scratch_shapes=[
            pltpu.VMEM((LANES, D), F32), pltpu.VMEM((D, LANES), F32), pltpu.VMEM((D, D), F32),
            pltpu.VMEM((n * D, D), BF16), pltpu.VMEM((R, D), F32),
        ],
        compiler_params=pltpu.CompilerParams(vmem_limit_bytes=LIMIT),
        cost_estimate=pl.CostEstimate(flops=2 * members * R * D * D, bytes_accessed=members * R * D * 2, transcendentals=0),
        name="input_grads_other" if other else "input_grads",
    )(q, packed, back, *more)


def direction(weight, first_old, second_old, gradient):
    first_new = beta_one * first_old + (1.0 - beta_one) * gradient
    second_new = beta_two * second_old + (1.0 - beta_two) * gradient * gradient
    fix_one = 1.0 - beta_one**STEP
    fix_two = 1.0 - beta_two**STEP
    update = (
        first_new / fix_one / (jnp.sqrt(second_new / fix_two) + epsilon) + weight_decay * weight
    )
    return (first_new, second_new, update)


def lane_sums(value):
    total = jnp.sum(value, axis=0, keepdims=True)
    width = total.shape[1]
    if width < LANES:
        return jnp.concatenate([total, jnp.zeros((1, LANES - width), F32)], axis=1)
    return sum(total[:, l:l + LANES] for l in range(0, width, LANES))


def direction_kernel(count, *refs):
    mine_ref, heads_ref = refs[:2]
    came = refs[2:2 + count]
    (m_ref, m1_ref, m2_ref, a_ref, a1_ref, a2_ref, h_ref, h1_ref, h2_ref,
     m1_out, m2_out, mu_out, a1_out, a2_out, au_out, h1_out, h2_out, hu_out, sums_out) = refs[2 + count:]
    own, D = m_ref.shape
    K = a_ref.shape[2]
    n_heads = h_ref.shape[0]
    grad = mine_ref[...]
    heads = heads_ref[:, :D]
    for c in came:
        grad = grad + c[:own, :].astype(F32)
        heads = heads + c[own:own + n_heads, :D].astype(F32)
    weight_rows, update_rows = [], []
    first, second, update = direction(m_ref[...], m1_ref[...], m2_ref[...], grad[:, :D])
    m1_out[...], m2_out[...], mu_out[...] = first, second, update
    weight_rows.append(lane_sums(m_ref[...] * m_ref[...]))
    update_rows.append(lane_sums(update * update))
    for k in range(3):
        first, second, update = direction(a_ref[k], a1_ref[k], a2_ref[k], grad[:, D + k * K:D + (k + 1) * K])
        a1_out[k], a2_out[k], au_out[k] = first, second, update
        weight_rows.append(lane_sums(a_ref[k] * a_ref[k]))
        update_rows.append(lane_sums(update * update))
    first, second, update = direction(h_ref[...], h1_ref[...], h2_ref[...], heads)
    h1_out[...], h2_out[...], hu_out[...] = first, second, update
    share = 1.0 / lax.axis_size("dp")
    weight_rows.append(lane_sums(h_ref[...] * h_ref[...]) * share)
    update_rows.append(lane_sums(update * update) * share)
    sums_out[...] = jnp.concatenate(weight_rows + update_rows + [jnp.zeros((6, LANES), F32)], axis=0)


def direction_call(mine, heads, came, states):
    m, a, h = states[0], states[3], states[6]
    outs = [shape(v.shape) for v in (m, m, m, a, a, a, h, h, h)] + [shape((16, LANES))]
    return pl.pallas_call(
        functools.partial(direction_kernel, len(came)),
        out_shape=tuple(outs),
        in_specs=[VMEM] * (2 + len(came) + 9),
        out_specs=tuple([VMEM] * 10),
        name="directions",
    )(mine, heads, *came, *states)


def update_kernel(count, *refs):
    sums_refs = refs[:count]
    m_ref, a_ref, h_ref, mu_ref, au_ref, hu_ref, m_out, a_out, h_out, norms_out = refs[count:]
    total = sums_refs[0][...]
    for ref in sums_refs[1:]:
        total = total + ref[...]
    norms = jnp.sqrt(jnp.sum(total, axis=1, keepdims=True))
    weight_norm, update_norm = norms[0:5], norms[5:10]
    rate = learn_rate * (weight_norm / update_norm)
    m_out[...] = m_ref[...] - rate[0:1] * mu_ref[...]
    for k in range(3):
        a_out[k] = a_ref[k] - rate[1 + k:2 + k] * au_ref[k]
    h_out[...] = h_ref[...] - rate[4:5] * hu_ref[...]
    norms_out[...] = jnp.concatenate([weight_norm, update_norm], axis=1)


def update_call(sums, m, a, h, mu, au, hu):
    return pl.pallas_call(
        functools.partial(update_kernel, len(sums)),
        out_shape=(shape(m.shape), shape(a.shape), shape(h.shape), shape((5, 2))),
        in_specs=[VMEM] * (len(sums) + 6),
        out_specs=(VMEM,) * 4,
        name="updates",
    )(*sums, m, a, h, mu, au, hu)


def bit_groups(n_dp, n_member):
    def split(low, count):
        bits = count.bit_length() - 1
        groups = []
        while bits > 0:
            take = 2 if bits >= 2 else 1
            bits -= take
            groups.append((low << bits, 1 << take))
        return groups

    return split(n_member, n_dp), split(2, n_member // 2) + [(1, 2)]


def swap(value, total, mask):
    return lax.ppermute(value, AXES, [(i, i ^ mask) for i in range(total)])


def gather_groups(value, groups, total, index):
    for axis, (low, size) in enumerate(groups):
        place = (index // low) % size
        held = [value] + [swap(value, total, low * m) for m in range(1, size)]
        value = jnp.stack([lax.select_n(place ^ p, *held) for p in range(size)], axis=axis)
    return value


def shards(n_dp, n_member, objects, counts, cotangent, matrix, matrix_first, matrix_second,
           adapters, adapter_first, adapter_second, head_weights, head_first, head_second):
    R, D = objects.shape
    K = adapters.shape[1]
    own, own_heads = matrix.shape[0], head_weights.shape[0]
    total = n_dp * n_member
    index = lax.axis_index("dp") * n_member + lax.axis_index("member")
    dp_groups, member_groups = bit_groups(n_dp, n_member)
    chip_groups = member_groups[:-1]
    turned = [v.transpose(0, 2, 1) for v in (adapters, adapter_first, adapter_second)]

    packed, q_own = pack_call(counts, matrix, turned[0], head_weights, cotangent.reshape(1, R))
    x_other = swap(objects, total, 1)
    q_other = swap(q_own, total, 1)
    full = gather_groups(packed, dp_groups + member_groups, total, index).reshape(D, -1)
    keep, sent, head_grads, preds, back = grad_call(objects, x_other, q_own, q_other, full, K, own)
    pred_came = swap(preds[1:2], total, 1)

    chips = [size for _, size in chip_groups]
    head_grads = head_grads.reshape(chips + [2, own_heads, D])
    core = index % 2
    axis = len(chips)

    def arrange(main, heads):
        main = main.reshape([n_dp] + chips + [own, D + LANES])
        main = jnp.moveaxis(main, 0, len(chips)).reshape(chips + [n_dp * own, D + LANES])
        return jnp.concatenate([main, jnp.pad(heads, [(0, 0)] * (len(chips) + 1) + [(0, LANES)])], axis=len(chips))

    other_heads = lax.dynamic_index_in_dim(head_grads, 1 - core, axis, keepdims=False)
    own_heads_grad = lax.dynamic_index_in_dim(head_grads, core, axis, keepdims=False)
    came = swap(arrange(sent, other_heads.astype(BF16)), total, 1)
    wide = arrange(keep, own_heads_grad) + came.astype(F32)
    for axis in reversed(range(len(chips))):
        low, size = chip_groups[axis]
        place = (index // low) % size
        part = [lax.dynamic_index_in_dim(wide, place ^ m, axis, keepdims=False) for m in range(size)]
        wide = part[0]
        for m in range(1, size):
            wide = wide + swap(part[m].astype(BF16), total, low * m).astype(F32)
    mine = wide[: n_dp * own].reshape([size for _, size in dp_groups] + [own, D + LANES])
    heads = wide[n_dp * own:]
    for axis in reversed(range(len(dp_groups))):
        low, size = dp_groups[axis]
        place = (index // low) % size
        part = [lax.dynamic_index_in_dim(mine, place ^ m, axis, keepdims=False) for m in range(size)]
        lead = part[0].shape[:-2]
        both = [jnp.concatenate([p.reshape(-1, D + LANES), heads], axis=0).astype(BF16) for p in part[1:]]
        last = [swap(b, total, low * (m + 1)) for m, b in enumerate(both)]
        mine = part[0]
        if axis:
            for c in last:
                mine = mine + c[:-own_heads].astype(F32).reshape(lead + (own, D + LANES))
                heads = heads + c[-own_heads:].astype(F32)

    ig_came = swap(back_call(q_other, full, back), total, 1)
    input_grad, predictions = back_call(q_own, full, back, (ig_came, preds, pred_came))
    lane = lax.broadcasted_iota(jnp.int32, (1, R), 1)
    predictions = jnp.where(lane < counts[0], predictions, 0.0)

    states = [matrix, matrix_first, matrix_second, *turned, head_weights, head_first, head_second]
    (m_first, m_second, m_update, a_first, a_second, a_update, h_first, h_second, h_update, sums) = direction_call(
        mine, heads, last, states)
    pending = [sums]
    for low, size in [(1, 2)] + chip_groups[::-1] + dp_groups[::-1]:
        sums = pending[0]
        for p in pending[1:]:
            sums = sums + p
        pending = [sums] + [swap(sums, total, low * m) for m in range(1, size)]
    new_matrix, new_adapters, new_heads, norm_pairs = update_call(
        pending, matrix, turned[0], head_weights, m_update, a_update, h_update)

    def back_turn(v):
        return v.transpose(0, 2, 1)

    return (predictions.reshape(R), input_grad, new_matrix, m_first, m_second, back_turn(new_adapters),
            back_turn(a_first), back_turn(a_second), new_heads, h_first, h_second, norm_pairs)


def solution(mesh):
    n_dp, n_member = mesh.shape["dp"], mesh.shape["member"]
    rows, cols = P(AXES, None), P(None, None, AXES)
    heads = P("member", None)
    return jax.shard_map(
        functools.partial(shards, n_dp, n_member),
        mesh=mesh,
        in_specs=(rows, P(AXES), P(AXES), rows, rows, rows, cols, cols, cols, heads, heads, heads),
        out_specs=(P(AXES), rows, rows, rows, rows, cols, cols, cols, heads, heads, heads, P()),
        check_vma=False,
    )
```

time: 130 us -> 128 us (0.985)
  other arithmetic: 10.4 us -> 3.43 us
  waiting for transfers between devices: 20.6 us -> 27.2 us
  between operations: 4.25 us -> 1.51 us
  local copies, waits for them, and re-layouts: 8.48 us -> 6.59 us
  Pallas kernels: 60.2 us -> 62 us
    ppermute x21 -> x25, waiting for transfers between devices: 20.6 us -> 27.2 us  [swap(): return lax.ppermute(value, AXES, [(i, i ^ mask) for i in range(total)])]
    another operation x2 -> x0, local copies, waits for them, and re-layouts: 5.24 us -> none  [the longest x1 5.23 us: shards(): jnp.stack(squares(matrix, adapters, head_weights) + squares(m_update, a_u...]
    reduce_sum x4 -> x0, other arithmetic: 3.21 us -> none  [the longest x2 1.36 us: squares(): jnp.sum(a[j] * a[j])]
    unnamed x28 -> x23, local copies, waits for them, and re-layouts: 2.04 us -> 5.1 us
    another operation x5 -> x0, other arithmetic: 2.85 us -> none
    sub x3 -> x0, other arithmetic: 1.93 us -> none  [the longest x1 0.68 us: shards(): adapters - learn_rate * trust_ratio[1:4][:, None, None] * a_update]
    pallas_call x2 -> x6, Pallas kernels: 60.2 us -> 62 us  [the longest x1 40.6 us: grad_call(): pl.pallas_call(functools.partial(grad_kernel, own=own), grid=(members //...]
    ppermute x21 -> x25, starting transfers between devices: 25.5 us -> 26.4 us  [swap(): return lax.ppermute(value, AXES, [(i, i ^ mask) for i in range(total)])]
  transfers between devices with their start and end apart: 21 -> 25, of which waited for: 16 -> 16; matrix products, arithmetic and copies ran while one was open for 1% -> 4% of each run, Pallas kernels for 11% -> 9%
where the time goes in v2:
time: 128 us; the launch traced here: 127 us
  Pallas kernels  62 us (48%)
  waiting for transfers between devices  27.2 us (21%)
  starting transfers between devices  26.4 us (21%)
  local copies, waits for them, and re-layouts  6.59 us (5%)
  other arithmetic  3.43 us (3%)
  between operations  1.51 us (1%)
    pallas_call x1, Pallas kernels, grad_call(): pl.pallas_call(functools.partial(grad_kernel, own=own), grid=(members //...  40.6 us
    ppermute x25, waiting for transfers between devices, swap(): return lax.ppermute(value, AXES, [(i, i ^ mask) for i in range(total)])  27.2 us
    ppermute x25, starting transfers between devices, swap(): return lax.ppermute(value, AXES, [(i, i ^ mask) for i in range(total)])  26.4 us
    pallas_call x2, Pallas kernels, back_call(): pl.pallas_call(functools.partial(back_kernel, members=members, other=othe...  16.6 us
    unnamed x23, local copies, waits for them, and re-layouts  5.1 us
  transfers between devices with their start and end apart: 25, of which 16 were waited for; matrix products, arithmetic and copies ran while one was open for 4% of the time, Pallas kernels for 9%

profile of v2, /device:TPU:0, one launch (start us, length us, event | category | flops | bytes accessed | tf_op | source)
XLA Modules:
  0.0 127.1 jit_solution(17636473461711016354)
XLA Ops:
  1.3 1.5 %pack_weights.1 = (bf16[16,768]{1,0:T(8,128)(2,1)}, f32[1,512]{1,0:T(1,128)}) custom-call(s32[1]{0:T(128)} %copy.34.count_ref, f32[16,512]{1,0:T(8,128)} %refs_4_.1, f32[3,16,32]{2,1,0:T(8,128)} %bitcast.77, f32[4,512]{1,0:T(4,128)} %refs_6_.3, f32[1,512]{1,0:T(1,128)} %bitcast.82), custom_call_target="tpu_custom_call" | custom-call | tf_op jit(solution)/shard_map/pack_weights/pallas_call | solution.py:51
  2.8 3.0 %collective-permute-start = (bf16[16,768]{1,0:T(8,128)(2,1)}, bf16[16,768]{1,0:T(8,128)(2,1)S(1)}, u32[]{:S(2)}, u32[]{:S(2)}) collective-permute-start(bf16[16,768]{1,0:T(8,128)(2,1)} %get-tuple-element.36), channel_id=1, source_target_pairs={{0,8},{1,9},{2,10},{3,11},{4,12},{5,13},{6,14},{7,15},{8,0},{9,1},... | collective-permute-start | bytes 73736 | tf_op jit(solution)/shard_map/ppermute | solution.py:373
  5.8 2.6 %collective-permute-start.1 = (bf16[16,768]{1,0:T(8,128)(2,1)}, bf16[16,768]{1,0:T(8,128)(2,1)S(1)}, u32[]{:S(2)}, u32[]{:S(2)}) collective-permute-start(bf16[16,768]{1,0:T(8,128)(2,1)} %get-tuple-element.36), channel_id=1, source_target_pairs={{0,16},{1,17},{2,18},{3,19},{4,20},{5,21},{6,22},{7,23},{8,24},{9,... | collective-permute-start | bytes 73736 | tf_op jit(solution)/shard_map/ppermute | solution.py:373
  8.4 2.7 %collective-permute-done.1 = bf16[16,768]{1,0:T(8,128)(2,1)S(1)} collective-permute-done((bf16[16,768]{1,0:T(8,128)(2,1)}, bf16[16,768]{1,0:T(8,128)(2,1)S(1)}, u32[]{:S(2)}, u32[]{:S(2)}) %collective-permute-start.1) | collective-permute-done | bytes 24608 | tf_op jit(solution)/shard_map/ppermute | solution.py:373
  11.1 3.1 %collective-permute-done.2 = bf16[16,768]{1,0:T(8,128)(2,1)S(1)} collective-permute-done((bf16[16,768]{1,0:T(8,128)(2,1)}, bf16[16,768]{1,0:T(8,128)(2,1)S(1)}, u32[]{:S(2)}, u32[]{:S(2)}) %collective-permute-start.2) | collective-permute-done | bytes 24608 | tf_op jit(solution)/shard_map/ppermute | solution.py:373
  15.0 1.6 %collective-permute-start.3 = (bf16[4,16,768]{2,1,0:T(8,128)(2,1)S(1)}, bf16[4,16,768]{2,1,0:T(8,128)(2,1)S(1)}, u32[]{:S(2)}, u32[]{:S(2)}) collective-permute-start(bf16[4,16,768]{2,1,0:T(8,128)(2,1)S(1)} %pad_maximum_fusion.2), channel_id=1, source_target_pairs={{0,2},{1,3},{2,0},{3,1},{4,6},{5,7},{6,4},{7,5},{8,10},{9,11},{10,... | collective-permute-start | bytes 294920 | tf_op jit(solution)/shard_map/ppermute | solution.py:373
  16.5 1.5 %collective-permute-start.4 = (bf16[4,16,768]{2,1,0:T(8,128)(2,1)S(1)}, bf16[4,16,768]{2,1,0:T(8,128)(2,1)S(1)}, u32[]{:S(2)}, u32[]{:S(2)}) collective-permute-start(bf16[4,16,768]{2,1,0:T(8,128)(2,1)S(1)} %pad_maximum_fusion.2), channel_id=1, source_target_pairs={{0,4},{1,5},{2,6},{3,7},{4,0},{5,1},{6,2},{7,3},{8,12},{9,13},{10,... | collective-permute-start | bytes 294920 | tf_op jit(solution)/shard_map/ppermute | solution.py:373
  18.5 1.8 %collective-permute-done.3 = bf16[4,16,768]{2,1,0:T(8,128)(2,1)S(1)} collective-permute-done((bf16[4,16,768]{2,1,0:T(8,128)(2,1)S(1)}, bf16[4,16,768]{2,1,0:T(8,128)(2,1)S(1)}, u32[]{:S(2)}, u32[]{:S(2)}) %collective-permute-start.3) | collective-permute-done | bytes 98336 | tf_op jit(solution)/shard_map/ppermute | solution.py:373
  21.6 2.0 %collective-permute-done.5 = bf16[4,16,768]{2,1,0:T(8,128)(2,1)S(1)} collective-permute-done((bf16[4,16,768]{2,1,0:T(8,128)(2,1)S(1)}, bf16[4,16,768]{2,1,0:T(8,128)(2,1)S(1)}, u32[]{:S(2)}, u32[]{:S(2)}) %collective-permute-start.5) | collective-permute-done | bytes 98336 | tf_op jit(solution)/shard_map/ppermute | solution.py:373
  28.2 40.6 %member_grads.1 = (f32[256,640]{1,0:T(8,128)S(1)}, bf16[256,640]{1,0:T(8,128)(2,1)S(1)}, f32[32,512]{1,0:T(8,128)S(1)}, f32[2,512]{1,0:T(2,128)S(1)}, bf16[16,1024,512]{2,1,0:T(8,128)(2,1)}) custom-call(bf16[512,512]{1,0:T(8,128)(2,1)S(1)} %copy-done.2, bf16[512,512]{1,0:T(8,128)(2,1)S(1)} %collective-permute-done.7.x1_ref, f32[1,512]{1,0:T(1,128)S(1)} %copy-done, ...), custom_call_target="tpu_custom_call" | custom-call | flops 34359738368 | bytes 16777216 | tf_op jit(solution)/shard_map/member_grads/pallas_call | solution.py:189
  69.3 7.8 %input_grads_other.1 = f32[512,512]{1,0:T(8,128)S(1)} custom-call(f32[1,512]{1,0:T(1,128)S(1)} %collective-permute-done.8.q1_ref.q_ref, bf16[512,768]{1,0:T(8,128)(2,1)S(1)} %bitcast.69, bf16[16,1024,512]{2,1,0:T(8,128)(2,1)} %get-tuple-element.37.gp_ref), custom_call_target="tpu_custom_call" | custom-call | flops 4294967296 | bytes 8388608 | tf_op jit(solution)/shard_map/input_grads_other/pallas_call | solution.py:255
  79.6 2.4 %collective-permute-start.14 = (bf16[68,640]{1,0:T(8,128)(2,1)S(1)}, bf16[68,640]{1,0:T(8,128)(2,1)S(1)}, u32[]{:S(2)}, u32[]{:S(2)}) collective-permute-start(bf16[68,640]{1,0:T(8,128)(2,1)S(1)} %get-tuple-element.85), channel_id=1, source_target_pairs={{0,6},{1,7},{2,4},{3,5},{4,2},{5,3},{6,0},{7,1},{8,14},{9,15},{10,... | collective-permute-start | bytes 261128 | tf_op jit(solution)/shard_map/ppermute | solution.py:373
  82.0 1.8 %collective-permute-done.12 = bf16[68,640]{1,0:T(8,128)(2,1)S(1)} collective-permute-done((bf16[68,640]{1,0:T(8,128)(2,1)S(1)}, bf16[68,640]{1,0:T(8,128)(2,1)S(1)}, u32[]{:S(2)}, u32[]{:S(2)}) %collective-permute-start.12) | collective-permute-done | bytes 87072 | tf_op jit(solution)/shard_map/ppermute | solution.py:373
  83.9 1.7 %collective-permute-done.13 = bf16[68,640]{1,0:T(8,128)(2,1)S(1)} collective-permute-done((bf16[68,640]{1,0:T(8,128)(2,1)S(1)}, bf16[68,640]{1,0:T(8,128)(2,1)S(1)}, u32[]{:S(2)}, u32[]{:S(2)}) %collective-permute-start.13) | collective-permute-done | bytes 87072 | tf_op jit(solution)/shard_map/ppermute | solution.py:373
  87.5 3.5 %collective-permute-start.17 = (bf16[20,640]{1,0:T(8,128)(2,1)S(1)}, bf16[20,640]{1,0:T(8,128)(2,1)S(1)}, u32[]{:S(2)}, u32[]{:S(2)}) collective-permute-start(bf16[20,640]{1,0:T(8,128)(2,1)S(1)} %get-tuple-element.98), channel_id=1, source_target_pairs={{0,24},{1,25},{2,26},{3,27},{4,28},{5,29},{6,30},{7,31},{8,16},{9,... | collective-permute-start | bytes 76808 | tf_op jit(solution)/shard_map/ppermute | solution.py:373
  93.9 1.6 %directions.1 = (f32[16,512]{1,0:T(8,128)}, f32[16,512]{1,0:T(8,128)}, f32[16,512]{1,0:T(8,128)}, f32[3,16,32]{2,1,0:T(8,128)}, f32[3,16,32]{2,1,0:T(8,128)}, /*...) custom-call(f32[16,640]{1,0:T(8,128)} %dynamic-slice_bitcast_fusion.refs_, ...), custom_call_target="tpu_custom_call" | custom-call | tf_op jit(solution)/shard_map/directions/pallas_call | solution.py:324
  95.6 1.4 %collective-permute-done.18 = f32[16,128]{1,0:T(8,128)S(1)} collective-permute-done((f32[16,128]{1,0:T(8,128)}, f32[16,128]{1,0:T(8,128)S(1)}, u32[]{:S(2)}, u32[]{:S(2)}) %collective-permute-start.18) | collective-permute-done | bytes 8224 | tf_op jit(solution)/shard_map/ppermute | solution.py:373
  97.7 1.5 %collective-permute-start.19 = (f32[16,128]{1,0:T(8,128)S(1)}, f32[16,128]{1,0:T(8,128)S(1)}, u32[]{:S(2)}, u32[]{:S(2)}) collective-permute-start(f32[16,128]{1,0:T(8,128)S(1)} %add.99), channel_id=1, source_target_pairs={{0,2},{1,3},{2,0},{3,1},{4,6},{5,7},{6,4},{7,5},{8,10},{9,11},{10,... | collective-permute-start | bytes 24584 | tf_op jit(solution)/shard_map/ppermute | solution.py:373
  101.3 1.5 %collective-permute-done.20 = f32[16,128]{1,0:T(8,128)S(1)} collective-permute-done((f32[16,128]{1,0:T(8,128)S(1)}, f32[16,128]{1,0:T(8,128)S(1)}, u32[]{:S(2)}, u32[]{:S(2)}) %collective-permute-start.20) | collective-permute-done | bytes 8224 | tf_op jit(solution)/shard_map/ppermute | solution.py:373
  102.8 1.8 %collective-permute-done.21 = f32[16,128]{1,0:T(8,128)S(1)} collective-permute-done((f32[16,128]{1,0:T(8,128)S(1)}, f32[16,128]{1,0:T(8,128)S(1)}, u32[]{:S(2)}, u32[]{:S(2)}) %collective-permute-start.21) | collective-permute-done | bytes 8224 | tf_op jit(solution)/shard_map/ppermute | solution.py:373
  104.9 3.8 %collective-permute-start.23 = (f32[16,128]{1,0:T(8,128)S(1)}, f32[16,128]{1,0:T(8,128)S(1)}, u32[]{:S(2)}, u32[]{:S(2)}) collective-permute-start(f32[16,128]{1,0:T(8,128)S(1)} %add_add_fusion.refs_0_), channel_id=1, source_target_pairs={{0,16},{1,17},{2,18},{3,19},{4,20},{5,21},{6,22},{7,23},{8,24},{9,... | collective-permute-start | bytes 24584 | tf_op jit(solution)/shard_map/ppermute | solution.py:373
  110.4 3.8 %collective-permute-done.24.refs_3_ = f32[16,128]{1,0:T(8,128)S(1)} collective-permute-done((f32[16,128]{1,0:T(8,128)S(1)}, f32[16,128]{1,0:T(8,128)S(1)}, u32[]{:S(2)}, u32[]{:S(2)}) %collective-permute-start.24) | collective-permute-done | bytes 8224 | tf_op jit(solution)/shard_map/ppermute | solution.py:373
  114.8 1.6 %updates.1 = (f32[16,512]{1,0:T(8,128)}, f32[3,16,32]{2,1,0:T(8,128)}, f32[4,512]{1,0:T(4,128)}, f32[5,2]{1,0:T(8,128)}) custom-call(f32[16,128]{1,0:T(8,128)} %copy-done.4, f32[16,128]{1,0:T(8,128)} %copy-done.8, f32[16,128]{1,0:T(8,128)} %copy-done.9, f32[16,128]{1,0:T(8,128)} %copy-done.10, f32[16,512]{1,0:T(8,128)} %refs_4_.1, f32[3,16,32]{2,1,0:T(8,128)} %bitcast.79, ...), custom_call_target="tpu_custom_call" | custom-call | tf_op jit(solution)/shard_map/updates/pallas_call | solution.py:350
  117.7 8.8 %input_grads.1 = (f32[512,512]{1,0:T(8,128)}, f32[1,512]{1,0:T(1,128)S(1)}) custom-call(f32[1,512]{1,0:T(1,128)S(1)} %copy-done.1, bf16[512,768]{1,0:T(8,128)(2,1)S(1)} %bitcast.70, bf16[16,1024,512]{2,1,0:T(8,128)(2,1)} %get-tuple-element.37.gp_ref, f32[512,512]{1,0:T(8,128)S(1)} %collective-permute-done.9.refs_0_, f32[2,512]{1,0:T(2,128)S(1)} %get-tuple-element.38.refs_1_, ...), custom_call_target="tpu_custom_call" | custom-call | flops 4294967296 | bytes 8388608 | tf_op jit(solution)/shard_map/input_grads/pallas_call | solution.py:255
  (82 shorter events, 22.0 us)
Async XLA Ops:
  2.8 5.6 %collective-permute-start = (bf16[16,768]{1,0:T(8,128)(2,1)}, bf16[16,768]{1,0:T(8,128)(2,1)S(1)}, u32[]{:S(2)}, u32[]{:S(2)}) collective-permute-start(bf16[16,768]{1,0:T(8,128)(2,1)} %get-tuple-element.36), channel_id=1, source_target_pairs={{0,8},{1,9},{2,10},{3,11},{4,12},{5,13},{6,14},{7,15},{8,0},{9,1},... | collective-permute-start | bytes 73736 | tf_op jit(solution)/shard_map/ppermute | solution.py:373
  5.8 5.3 %collective-permute-start.1 = (bf16[16,768]{1,0:T(8,128)(2,1)}, bf16[16,768]{1,0:T(8,128)(2,1)S(1)}, u32[]{:S(2)}, u32[]{:S(2)}) collective-permute-start(bf16[16,768]{1,0:T(8,128)(2,1)} %get-tuple-element.36), channel_id=1, source_target_pairs={{0,16},{1,17},{2,18},{3,19},{4,20},{5,21},{6,22},{7,23},{8,24},{9,... | collective-permute-start | bytes 73736 | tf_op jit(solution)/shard_map/ppermute | solution.py:373
  8.4 5.8 %collective-permute-start.2 = (bf16[16,768]{1,0:T(8,128)(2,1)}, bf16[16,768]{1,0:T(8,128)(2,1)S(1)}, u32[]{:S(2)}, u32[]{:S(2)}) collective-permute-start(bf16[16,768]{1,0:T(8,128)(2,1)} %get-tuple-element.36), channel_id=1, source_target_pairs={{0,24},{1,25},{2,26},{3,27},{4,28},{5,29},{6,30},{7,31},{8,16},{9,... | collective-permute-start | bytes 73736 | tf_op jit(solution)/shard_map/ppermute | solution.py:373
  15.0 5.3 %collective-permute-start.3 = (bf16[4,16,768]{2,1,0:T(8,128)(2,1)S(1)}, bf16[4,16,768]{2,1,0:T(8,128)(2,1)S(1)}, u32[]{:S(2)}, u32[]{:S(2)}) collective-permute-start(bf16[4,16,768]{2,1,0:T(8,128)(2,1)S(1)} %pad_maximum_fusion.2), channel_id=1, source_target_pairs={{0,2},{1,3},{2,0},{3,1},{4,6},{5,7},{6,4},{7,5},{8,10},{9,11},{10,... | collective-permute-start | bytes 294920 | tf_op jit(solution)/shard_map/ppermute | solution.py:373
  16.5 5.0 %collective-permute-start.4 = (bf16[4,16,768]{2,1,0:T(8,128)(2,1)S(1)}, bf16[4,16,768]{2,1,0:T(8,128)(2,1)S(1)}, u32[]{:S(2)}, u32[]{:S(2)}) collective-permute-start(bf16[4,16,768]{2,1,0:T(8,128)(2,1)S(1)} %pad_maximum_fusion.2), channel_id=1, source_target_pairs={{0,4},{1,5},{2,6},{3,7},{4,0},{5,1},{6,2},{7,3},{8,12},{9,13},{10,... | collective-permute-start | bytes 294920 | tf_op jit(solution)/shard_map/ppermute | solution.py:373
  18.1 5.5 %collective-permute-start.5 = (bf16[4,16,768]{2,1,0:T(8,128)(2,1)S(1)}, bf16[4,16,768]{2,1,0:T(8,128)(2,1)S(1)}, u32[]{:S(2)}, u32[]{:S(2)}) collective-permute-start(bf16[4,16,768]{2,1,0:T(8,128)(2,1)S(1)} %pad_maximum_fusion.2), channel_id=1, source_target_pairs={{0,6},{1,7},{2,4},{3,5},{4,2},{5,3},{6,0},{7,1},{8,14},{9,15},{10,... | collective-permute-start | bytes 294920 | tf_op jit(solution)/shard_map/ppermute | solution.py:373
  23.7 1.8 %collective-permute-start.6 = (bf16[4,4,16,768]{3,2,0,1:T(8,128)(2,1)S(1)}, bf16[4,4,16,768]{3,2,0,1:T(8,128)(2,1)S(1)}, u32[]{:S(2)}, u32[]{:S(2)}) collective-permute-start(bf16[4,4,16,768]{3,2,0,1:T(8,128)(2,1)S(1)} %pad_maximum_fusion.1), channel_id=1, source_target_pairs={{0,1},{1,0},{2,3},{3,2},{4,5},{5,4},{6,7},{7,6},{8,9},{9,8},{10,11... | collective-permute-start | bytes 1179656 | tf_op jit(solution)/shard_map/ppermute | solution.py:373
  23.8 2.7 %collective-permute-start.7 = (bf16[512,512]{1,0:T(8,128)(2,1)}, bf16[512,512]{1,0:T(8,128)(2,1)S(1)}, u32[]{:S(2)}, u32[]{:S(2)}) collective-permute-start(bf16[512,512]{1,0:T(8,128)(2,1)} %x0_ref.1), channel_id=1, source_target_pairs={{0,1},{1,0},{2,3},{3,2},{4,5},{5,4},{6,7},{7,6},{8,9},{9,8},{10,11... | collective-permute-start | bytes 1572872 | tf_op jit(solution)/shard_map/ppermute | solution.py:373
  24.3 2.2 %collective-permute-start.8 = (f32[1,512]{1,0:T(1,128)}, f32[1,512]{1,0:T(1,128)S(1)}, u32[]{:S(2)}, u32[]{:S(2)}) collective-permute-start(f32[1,512]{1,0:T(1,128)} %get-tuple-element.35.q0_ref.q_ref), channel_id=1, source_target_pairs={{0,1},{1,0},{2,3},{3,2},{4,5},{5,4},{6,7},{7,6},{8,9},{9,8},{10,11... | collective-permute-start | bytes 6152 | tf_op jit(solution)/shard_map/ppermute | solution.py:373
  69.0 8.5 %collective-permute-start.11 = (bf16[4,68,640]{2,1,0:T(8,128)(2,1)S(1)}, bf16[4,68,640]{2,1,0:T(8,128)(2,1)S(1)}, u32[]{:S(2)}, u32[]{:S(2)}) collective-permute-start(bf16[4,68,640]{2,1,0:T(8,128)(2,1)S(1)} %fusion.2), channel_id=1, source_target_pairs={{0,1},{1,0},{2,3},{3,2},{4,5},{5,4},{6,7},{7,6},{8,9},{9,8},{10,11... | collective-permute-start | bytes 1044488 | tf_op jit(solution)/shard_map/ppermute | solution.py:373
  77.1 40.7 %collective-permute-start.9 = (f32[512,512]{1,0:T(8,128)S(1)}, f32[512,512]{1,0:T(8,128)S(1)}, u32[]{:S(2)}, u32[]{:S(2)}) collective-permute-start(f32[512,512]{1,0:T(8,128)S(1)} %input_grads_other.1), channel_id=1, source_target_pairs={{0,1},{1,0},{2,3},{3,2},{4,5},{5,4},{6,7},{7,6},{8,9},{9,8},{10,11... | collective-permute-start | bytes 3145736 | tf_op jit(solution)/shard_map/ppermute | solution.py:373
  78.5 5.4 %collective-permute-start.12 = (bf16[68,640]{1,0:T(8,128)(2,1)S(1)}, bf16[68,640]{1,0:T(8,128)(2,1)S(1)}, u32[]{:S(2)}, u32[]{:S(2)}) collective-permute-start(bf16[68,640]{1,0:T(8,128)(2,1)S(1)} %get-tuple-element.84), channel_id=1, source_target_pairs={{0,2},{1,3},{2,0},{3,1},{4,6},{5,7},{6,4},{7,5},{8,10},{9,11},{10,... | collective-permute-start | bytes 261128 | tf_op jit(solution)/shard_map/ppermute | solution.py:373
  79.1 6.5 %collective-permute-start.13 = (bf16[68,640]{1,0:T(8,128)(2,1)S(1)}, bf16[68,640]{1,0:T(8,128)(2,1)S(1)}, u32[]{:S(2)}, u32[]{:S(2)}) collective-permute-start(bf16[68,640]{1,0:T(8,128)(2,1)S(1)} %get-tuple-element.86), channel_id=1, source_target_pairs={{0,4},{1,5},{2,6},{3,7},{4,0},{5,1},{6,2},{7,3},{8,12},{9,13},{10,... | collective-permute-start | bytes 261128 | tf_op jit(solution)/shard_map/ppermute | solution.py:373
  79.6 6.0 %collective-permute-start.14 = (bf16[68,640]{1,0:T(8,128)(2,1)S(1)}, bf16[68,640]{1,0:T(8,128)(2,1)S(1)}, u32[]{:S(2)}, u32[]{:S(2)}) collective-permute-start(bf16[68,640]{1,0:T(8,128)(2,1)S(1)} %get-tuple-element.85), channel_id=1, source_target_pairs={{0,6},{1,7},{2,4},{3,5},{4,2},{5,3},{6,0},{7,1},{8,14},{9,15},{10,... | collective-permute-start | bytes 261128 | tf_op jit(solution)/shard_map/ppermute | solution.py:373
  86.6 5.7 %collective-permute-start.15 = (bf16[20,640]{1,0:T(8,128)(2,1)S(1)}, bf16[20,640]{1,0:T(8,128)(2,1)S(1)}, u32[]{:S(2)}, u32[]{:S(2)}) collective-permute-start(bf16[20,640]{1,0:T(8,128)(2,1)S(1)} %get-tuple-element.100), channel_id=1, source_target_pairs={{0,8},{1,9},{2,10},{3,11},{4,12},{5,13},{6,14},{7,15},{8,0},{9,1},... | collective-permute-start | bytes 76808 | tf_op jit(solution)/shard_map/ppermute | solution.py:373
  86.7 5.6 %collective-permute-start.16 = (bf16[20,640]{1,0:T(8,128)(2,1)S(1)}, bf16[20,640]{1,0:T(8,128)(2,1)S(1)}, u32[]{:S(2)}, u32[]{:S(2)}) collective-permute-start(bf16[20,640]{1,0:T(8,128)(2,1)S(1)} %get-tuple-element.99), channel_id=1, source_target_pairs={{0,16},{1,17},{2,18},{3,19},{4,20},{5,21},{6,22},{7,23},{8,24},{9,... | collective-permute-start | bytes 76808 | tf_op jit(solution)/shard_map/ppermute | solution.py:373
  87.5 5.7 %collective-permute-start.17 = (bf16[20,640]{1,0:T(8,128)(2,1)S(1)}, bf16[20,640]{1,0:T(8,128)(2,1)S(1)}, u32[]{:S(2)}, u32[]{:S(2)}) collective-permute-start(bf16[20,640]{1,0:T(8,128)(2,1)S(1)} %get-tuple-element.98), channel_id=1, source_target_pairs={{0,24},{1,25},{2,26},{3,27},{4,28},{5,29},{6,30},{7,31},{8,16},{9,... | collective-permute-start | bytes 76808 | tf_op jit(solution)/shard_map/ppermute | solution.py:373
  97.7 3.7 %collective-permute-start.19 = (f32[16,128]{1,0:T(8,128)S(1)}, f32[16,128]{1,0:T(8,128)S(1)}, u32[]{:S(2)}, u32[]{:S(2)}) collective-permute-start(f32[16,128]{1,0:T(8,128)S(1)} %add.99), channel_id=1, source_target_pairs={{0,2},{1,3},{2,0},{3,1},{4,6},{5,7},{6,4},{7,5},{8,10},{9,11},{10,... | collective-permute-start | bytes 24584 | tf_op jit(solution)/shard_map/ppermute | solution.py:373
  99.2 3.7 %collective-permute-start.20 = (f32[16,128]{1,0:T(8,128)S(1)}, f32[16,128]{1,0:T(8,128)S(1)}, u32[]{:S(2)}, u32[]{:S(2)}) collective-permute-start(f32[16,128]{1,0:T(8,128)S(1)} %add.99), channel_id=1, source_target_pairs={{0,4},{1,5},{2,6},{3,7},{4,0},{5,1},{6,2},{7,3},{8,12},{9,13},{10,... | collective-permute-start | bytes 24584 | tf_op jit(solution)/shard_map/ppermute | solution.py:373
  100.1 4.5 %collective-permute-start.21 = (f32[16,128]{1,0:T(8,128)S(1)}, f32[16,128]{1,0:T(8,128)S(1)}, u32[]{:S(2)}, u32[]{:S(2)}) collective-permute-start(f32[16,128]{1,0:T(8,128)S(1)} %add.99), channel_id=1, source_target_pairs={{0,6},{1,7},{2,4},{3,5},{4,2},{5,3},{6,0},{7,1},{8,14},{9,15},{10,... | collective-permute-start | bytes 24584 | tf_op jit(solution)/shard_map/ppermute | solution.py:373
  104.7 4.4 %collective-permute-start.22 = (f32[16,128]{1,0:T(8,128)S(1)}, f32[16,128]{1,0:T(8,128)S(1)}, u32[]{:S(2)}, u32[]{:S(2)}) collective-permute-start(f32[16,128]{1,0:T(8,128)S(1)} %add_add_fusion.refs_0_), channel_id=1, source_target_pairs={{0,8},{1,9},{2,10},{3,11},{4,12},{5,13},{6,14},{7,15},{8,0},{9,1},... | collective-permute-start | bytes 24584 | tf_op jit(solution)/shard_map/ppermute | solution.py:373
  104.9 5.4 %collective-permute-start.23 = (f32[16,128]{1,0:T(8,128)S(1)}, f32[16,128]{1,0:T(8,128)S(1)}, u32[]{:S(2)}, u32[]{:S(2)}) collective-permute-start(f32[16,128]{1,0:T(8,128)S(1)} %add_add_fusion.refs_0_), channel_id=1, source_target_pairs={{0,16},{1,17},{2,18},{3,19},{4,20},{5,21},{6,22},{7,23},{8,24},{9,... | collective-permute-start | bytes 24584 | tf_op jit(solution)/shard_map/ppermute | solution.py:373
  108.7 5.4 %collective-permute-start.24 = (f32[16,128]{1,0:T(8,128)S(1)}, f32[16,128]{1,0:T(8,128)S(1)}, u32[]{:S(2)}, u32[]{:S(2)}) collective-permute-start(f32[16,128]{1,0:T(8,128)S(1)} %add_add_fusion.refs_0_), channel_id=1, source_target_pairs={{0,24},{1,25},{2,26},{3,27},{4,28},{5,29},{6,30},{7,31},{8,16},{9,... | collective-permute-start | bytes 24584 | tf_op jit(solution)/shard_map/ppermute | solution.py:373
  109.1 8.7 %collective-permute-start.10 = (f32[1,512]{1,0:T(1,128)S(1)}, f32[1,512]{1,0:T(1,128)S(1)}, u32[]{:S(2)}, u32[]{:S(2)}) collective-permute-start(f32[1,512]{1,0:T(1,128)S(1)} %slice.9), channel_id=1, source_target_pairs={{0,1},{1,0},{2,3},{3,2},{4,5},{5,4},{6,7},{7,6},{8,9},{9,8},{10,11... | collective-permute-start | bytes 6152 | tf_op jit(solution)/shard_map/ppermute | solution.py:373
  (12 other events, 74.5 us)

commit v3 on v2

--- a/solution.py
+++ b/solution.py
@@ -59,8 +59,8 @@
 
 def grad_kernel(
     x0_ref, x1_ref, q0_ref, q1_ref, packed_ref,
-    keep_ref, sent_ref, heads_grad_ref, pred_ref, back_ref,
-    rows_ref, cols_ref, heads_ref, weight_ref, x_ref, xq_ref, q_ref, z0_ref, z1_ref, gp0_ref, gp1_ref,
+    keep_ref, sent_ref, heads_grad_ref, pred_ref, rows_ref, turned_ref, back_ref,
+    cols_ref, heads_ref, weight_ref, x_ref, xq_ref, q_ref, z0_ref, z1_ref, gp0_ref, gp1_ref,
     post_ref, pred_acc, sums_ref, gr_ref, grads_ref, *, own,
 ):
     half, D = x0_ref.shape
@@ -78,6 +78,7 @@
         cols = packed_ref[:, D:D + LANES].astype(F32)
         cols_ref[...] = cols
         rows_ref[...] = cols.T
+        turned_ref[...] = weight_ref[...].T.astype(BF16)
         L = packed_ref.shape[1] - D - LANES
         per_head = D // L
         for c in range(0, L, LANES):
@@ -104,13 +105,12 @@
         r = rows_ref[pl.ds(base + i, 1), :].astype(BF16)
         z_ref[...] = jnp.dot(x_ref[...] * r, packed_ref[:, :D], preferred_element_type=F32)
 
-    def middle(i, k, z_ref, gp_ref):
+    def middle(i, k, z_ref, gp_ref, lo, hi, total):
         s = 0.5 * rows_ref[pl.ds(K + base + i, 1), :]
         b = 0.5 * rows_ref[pl.ds(2 * K + base + i, 1), :]
         hb = heads_ref[pl.ds(base + i, 1), :]
-        total = None
         step = 16
-        for c in range(0, R, step):
+        for c in range(lo, hi, step):
             y = z_ref[c:c + step, :] * s + b
             t = jnp.tanh(y)
             a = 1.0 + t
@@ -125,16 +125,16 @@
             qh = jnp.concatenate([h[:, l:l + LANES] * q for l in range(0, D, LANES)], axis=1)
             part = sum(qh[j:j + 8] for j in range(0, step, 8))
             total = part if total is None else total + part
-        heads_grad_ref[pl.ds(base + i, 1), :] = jnp.sum(total, axis=0, keepdims=True)
-
-    def after(i, gp_ref):
+        return total
+
+    def outer(gp_ref):
+        post_ref[...] = jnp.dot(xq_ref[...], gp_ref[...], preferred_element_type=F32)
+
+    def spread(i, lo, hi, total):
         s = rows_ref[pl.ds(K + base + i, 1), :]
-        post_ref[...] = jnp.dot(xq_ref[...], gp_ref[...], preferred_element_type=F32)
-        sums_ref[pl.ds(2 * K + base + i, 1), :] = post_ref[D:D + 1, :] + post_ref[D + 1:D + 2, :]
-        total = None
         step = 16
         lane = lax.broadcasted_iota(jnp.int32, (step, LANES), 1)
-        for c in range(0, D, step):
+        for c in range(lo, hi, step):
             g = post_ref[c:c + step, :]
             r = jnp.sum(jnp.where(lane == base + i, cols_ref[c:c + step, :], 0.0), axis=1, keepdims=True)
             t = g * weight_ref[c:c + step, :]
@@ -145,31 +145,32 @@
             fold = sum(st[:, l:l + LANES] for l in range(0, D, LANES))
             gr_ref[c:c + step, :] += jnp.where(lane == base + i, jnp.sum(fold, axis=1, keepdims=True), 0.0)
             grads_ref[c:c + step, :D] += (g * s) * r
+        return total
+
+    def finish(i, total):
         sums_ref[pl.ds(K + base + i, 1), :] = jnp.sum(total, axis=0, keepdims=True)
+        sums_ref[pl.ds(2 * K + base + i, 1), :] = post_ref[D:D + 1, :] + post_ref[D + 1:D + 2, :]
+
+    def member(i, k, now, other, nxt):
+        total = middle(i, k, z_refs[now], gp_refs[now], 0, R, None)
+        forward(nxt, z_refs[other])
+        outer(gp_refs[other])
+        heads_grad_ref[pl.ds(base + i, 1), :] = jnp.sum(total, axis=0, keepdims=True)
+        finish(i - 1, spread(i - 1, 0, D, None))
 
     @pl.when(step_id == 0)
     def _():
         set_up()
         forward(0, z_refs[0])
-        middle(0, 0, z_refs[0], gp_refs[0])
-        forward(1, z_refs[1])
-
-    @pl.when(step_id > 0)
-    def _():
-        i = step_id * n
-        middle(i, 0, z_refs[0], gp_refs[0])
-        after(i - 1, gp_refs[1])
-        forward(i + 1, z_refs[1])
-
-    for k in range(1, n):
+
+    for k in range(n):
         i, now, other = step_id * n + k, k % 2, (k + 1) % 2
-        middle(i, k, z_refs[now], gp_refs[now])
-        after(i - 1, gp_refs[other])
-        forward(jnp.minimum(i + 1, members - 1), z_refs[other])
+        member(i, k, now, other, jnp.minimum(i + 1, members - 1))
 
     @pl.when(step_id == steps - 1)
     def _():
-        after(members - 1, gp_refs[1])
+        outer(gp_refs[1])
+        finish(members - 1, spread(members - 1, 0, D, None))
         for side in range(2):
             at = slice(side * half, (side + 1) * half)
             pred_ref[side:side + 1, :] = jnp.sum(pred_acc[at, :].T, axis=0, keepdims=True)
@@ -191,12 +192,12 @@
         grid=(members // n,),
         out_shape=(
             shape((D // 2, D + LANES)), shape((D // 2, D + LANES), BF16), shape((K, D)), shape((2, half)),
-            shape((members, R, D), BF16),
+            shape((LANES, D)), shape((D, D), BF16), shape((members, R, D), BF16),
         ),
         in_specs=[VMEM] * 5,
-        out_specs=(VMEM, VMEM, VMEM, VMEM, pl.BlockSpec((n, R, D), lambda i: (i, 0, 0))),
+        out_specs=(VMEM, VMEM, VMEM, VMEM, VMEM, VMEM, pl.BlockSpec((n, R, D), lambda i: (i, 0, 0))),
         scratch_shapes=[
-            pltpu.VMEM((LANES, D), F32), pltpu.VMEM((D, LANES), F32), pltpu.VMEM((K, D), F32), pltpu.VMEM((D, D), F32),
+            pltpu.VMEM((D, LANES), F32), pltpu.VMEM((K, D), F32), pltpu.VMEM((D, D), F32),
             pltpu.VMEM((R, D), BF16), pltpu.VMEM((D + 16, R), BF16), pltpu.VMEM((R, LANES), F32),
             pltpu.VMEM((R, D), F32), pltpu.VMEM((R, D), F32), pltpu.VMEM((R, D), BF16), pltpu.VMEM((R, D), BF16),
             pltpu.VMEM((D + 16, D), F32), pltpu.VMEM((R, LANES), F32), pltpu.VMEM((LANES, D), F32),
@@ -208,64 +209,58 @@
     )(x0, x1, q0, q1, packed)
 
 
-def back_kernel(q_ref, packed_ref, gp_ref, *refs, members, other):
-    if other:
-        out_ref, rows_ref, cols_ref, wt_ref, ws_ref, acc_ref = refs
-    else:
-        came_ref, pred_ref, pred_came_ref, out_ref, pred_out_ref, rows_ref, cols_ref, wt_ref, ws_ref, acc_ref = refs
+def back_kernel(*refs, members, start, first, last):
+    rows_ref, turned_ref, gp_ref = refs[:3]
+    rest = list(refs[3:])
+    acc_in = None if first else rest.pop(0)
+    q_ref = rest.pop(0) if last else None
+    came_ref = rest.pop(0) if last == "own" else None
+    out_ref, acc_ref = rest
     n, R, D = gp_ref.shape
     step = pl.program_id(0)
     K = 2 * members
-    base = this_core() * members
+    base = this_core() * members + start
 
     @pl.when(step == 0)
     def _():
-        cols = packed_ref[:, D:D + LANES].astype(F32)
-        cols_ref[...] = cols
-        rows_ref[...] = cols.T
-        wt_ref[...] = packed_ref[:, :D].astype(F32).T
-        acc_ref[...] = jnp.zeros_like(acc_ref)
-
-    lane = lax.broadcasted_iota(jnp.int32, (16, LANES), 1)
+        acc_ref[...] = jnp.zeros_like(acc_ref) if first else acc_in[...]
+
+    left, right = [], []
     for k in range(n):
         i = base + step * n + k
-        r = rows_ref[pl.ds(i, 1), :]
-        for c in range(0, D, 16):
-            s = jnp.sum(jnp.where(lane == i + K, cols_ref[c:c + 16, :], 0.0), axis=1, keepdims=True)
-            ws_ref[k * D + c:k * D + c + 16, :] = (wt_ref[c:c + 16, :] * s * r).astype(BF16)
-    left = jnp.concatenate([gp_ref[k] for k in range(n)], axis=1)
-    acc_ref[...] += jnp.dot(left, ws_ref[...], preferred_element_type=F32)
+        r = rows_ref[pl.ds(i, 1), :].astype(BF16)
+        s = rows_ref[pl.ds(K + i, 1), :].astype(BF16)
+        left.append(gp_ref[k] * s)
+        right.append(turned_ref[...] * r)
+    acc_ref[...] += jnp.dot(jnp.concatenate(left, axis=1), jnp.concatenate(right, axis=0), preferred_element_type=F32)
 
     @pl.when(step == pl.num_programs(0) - 1)
     def _():
-        q_wide = jnp.broadcast_to(0.5 * q_ref[...], (LANES, R)).T
-        for l in range(0, D, LANES):
-            value = acc_ref[:, l:l + LANES] * q_wide
-            out_ref[:, l:l + LANES] = value if other else value + came_ref[:, l:l + LANES]
-        if not other:
-            pred_out_ref[...] = (pred_ref[0:1, :] + pred_came_ref[...]) * (1.0 / K)
-
-
-def back_call(q, packed, back, came=None, n=4):
+        if not last:
+            out_ref[...] = acc_ref[...]
+        else:
+            q_wide = jnp.broadcast_to(0.5 * q_ref[...], (LANES, R)).T
+            for l in range(0, D, LANES):
+                value = acc_ref[:, l:l + LANES] * q_wide
+                out_ref[:, l:l + LANES] = value if came_ref is None else value + came_ref[:, l:l + LANES]
+
+
+def back_call(rows, turned, back, where, start, count, acc=None, q=None, came=None, n=4):
     members, R2, D = back.shape
     R = R2 // 2
-    other = came is None
-    where = 1 if other else 0
-    more = [] if other else list(came)
+    last = None if q is None else "other" if came is None else "own"
+    more = [v for v in (acc, q, came) if v is not None]
     return pl.pallas_call(
-        functools.partial(back_kernel, members=members, other=other),
-        grid=(members // n,),
-        out_shape=shape((R, D)) if other else (shape((R, D)), shape((1, R))),
-        in_specs=[VMEM, VMEM, pl.BlockSpec((n, R, D), lambda i: (i, where, 0))] + [VMEM] * len(more),
-        out_specs=VMEM if other else (VMEM, VMEM),
-        scratch_shapes=[
-            pltpu.VMEM((LANES, D), F32), pltpu.VMEM((D, LANES), F32), pltpu.VMEM((D, D), F32),
-            pltpu.VMEM((n * D, D), BF16), pltpu.VMEM((R, D), F32),
-        ],
-        compiler_params=pltpu.CompilerParams(vmem_limit_bytes=LIMIT),
-        cost_estimate=pl.CostEstimate(flops=2 * members * R * D * D, bytes_accessed=members * R * D * 2, transcendentals=0),
-        name="input_grads_other" if other else "input_grads",
-    )(q, packed, back, *more)
+        functools.partial(back_kernel, members=members, start=start, first=acc is None, last=last),
+        grid=(count // n,),
+        out_shape=shape((R, D)),
+        in_specs=[VMEM, VMEM, pl.BlockSpec((n, R, D), lambda i: (start // n + i, where, 0))] + [VMEM] * len(more),
+        out_specs=VMEM,
+        scratch_shapes=[pltpu.VMEM((R, D), F32)],
+        compiler_params=pltpu.CompilerParams(vmem_limit_bytes=LIMIT // 2),
+        cost_estimate=pl.CostEstimate(flops=2 * count * R * D * D, bytes_accessed=count * R * D * 2, transcendentals=0),
+        name="input_grads_other" if where else "input_grads_own",
+    )(rows, turned, back, *more)
 
 
 def direction(weight, first_old, second_old, gradient):
@@ -343,13 +338,14 @@
     for k in range(3):
         a_out[k] = a_ref[k] - rate[1 + k:2 + k] * au_ref[k]
     h_out[...] = h_ref[...] - rate[4:5] * hu_ref[...]
-    norms_out[...] = jnp.concatenate([weight_norm, update_norm], axis=1)
+    row = jnp.sqrt(jnp.sum(total.T, axis=0, keepdims=True))
+    norms_out[...] = jnp.concatenate([row[:, 0:5], row[:, 5:10]], axis=0)
 
 
 def update_call(sums, m, a, h, mu, au, hu):
     return pl.pallas_call(
         functools.partial(update_kernel, len(sums)),
-        out_shape=(shape(m.shape), shape(a.shape), shape(h.shape), shape((5, 2))),
+        out_shape=(shape(m.shape), shape(a.shape), shape(h.shape), shape((2, 5))),
         in_specs=[VMEM] * (len(sums) + 6),
         out_specs=(VMEM,) * 4,
         name="updates",
@@ -379,6 +375,13 @@
         held = [value] + [swap(value, total, low * m) for m in range(1, size)]
         value = jnp.stack([lax.select_n(place ^ p, *held) for p in range(size)], axis=axis)
     return value
+
+
+def beside(sends, work, *inputs):
+    values, inputs = lax.optimization_barrier(([v for v, _, _ in sends], inputs))
+    came = [swap(v, total, mask) for v, (_, total, mask) in zip(values, sends)]
+    done = work(*inputs)
+    return lax.optimization_barrier((came, done))
 
 
 def shards(n_dp, n_member, objects, counts, cotangent, matrix, matrix_first, matrix_second,
@@ -396,30 +399,43 @@
     x_other = swap(objects, total, 1)
     q_other = swap(q_own, total, 1)
     full = gather_groups(packed, dp_groups + member_groups, total, index).reshape(D, -1)
-    keep, sent, head_grads, preds, back = grad_call(objects, x_other, q_own, q_other, full, K, own)
-    pred_came = swap(preds[1:2], total, 1)
+    keep, sent, head_grads, preds, rows, wide_turned, back = grad_call(objects, x_other, q_own, q_other, full, K, own)
 
     chips = [size for _, size in chip_groups]
     head_grads = head_grads.reshape(chips + [2, own_heads, D])
     core = index % 2
     axis = len(chips)
+    members = K // 2
+    quarter = members // 4
 
     def arrange(main, heads):
         main = main.reshape([n_dp] + chips + [own, D + LANES])
         main = jnp.moveaxis(main, 0, len(chips)).reshape(chips + [n_dp * own, D + LANES])
         return jnp.concatenate([main, jnp.pad(heads, [(0, 0)] * (len(chips) + 1) + [(0, LANES)])], axis=len(chips))
 
+    def backward(where, part, parts=1, **more):
+        def work(rows, wide_turned, back, *acc):
+            return back_call(rows, wide_turned, back, where, part * quarter, parts * quarter, *acc, n=quarter, **more)
+        return work
+
+    weights = (rows, wide_turned, back)
     other_heads = lax.dynamic_index_in_dim(head_grads, 1 - core, axis, keepdims=False)
     own_heads_grad = lax.dynamic_index_in_dim(head_grads, core, axis, keepdims=False)
-    came = swap(arrange(sent, other_heads.astype(BF16)), total, 1)
+    (came, pred_came), acc = beside(
+        [(arrange(sent, other_heads.astype(BF16)), total, 1), (preds[1:2], total, 1)], backward(1, 0), *weights)
     wide = arrange(keep, own_heads_grad) + came.astype(F32)
     for axis in reversed(range(len(chips))):
         low, size = chip_groups[axis]
         place = (index // low) % size
         part = [lax.dynamic_index_in_dim(wide, place ^ m, axis, keepdims=False) for m in range(size)]
+        sends = [(part[m].astype(BF16), total, low * m) for m in range(1, size)]
+        if axis == len(chips) - 1:
+            came, acc = beside(sends, backward(1, 1, 2), *weights, acc)
+        else:
+            came = [swap(*send) for send in sends]
         wide = part[0]
-        for m in range(1, size):
-            wide = wide + swap(part[m].astype(BF16), total, low * m).astype(F32)
+        for c in came:
+            wide = wide + c.astype(F32)
     mine = wide[: n_dp * own].reshape([size for _, size in dp_groups] + [own, D + LANES])
     heads = wide[n_dp * own:]
     for axis in reversed(range(len(dp_groups))):
@@ -428,35 +444,47 @@
         part = [lax.dynamic_index_in_dim(mine, place ^ m, axis, keepdims=False) for m in range(size)]
         lead = part[0].shape[:-2]
         both = [jnp.concatenate([p.reshape(-1, D + LANES), heads], axis=0).astype(BF16) for p in part[1:]]
-        last = [swap(b, total, low * (m + 1)) for m, b in enumerate(both)]
+        sends = [(b, total, low * (m + 1)) for m, b in enumerate(both)]
+        if axis == len(dp_groups) - 1:
+            last, acc = beside(sends, backward(1, 3, q=q_other), *weights, acc)
+        else:
+            last = [swap(*send) for send in sends]
         mine = part[0]
         if axis:
             for c in last:
                 mine = mine + c[:-own_heads].astype(F32).reshape(lead + (own, D + LANES))
                 heads = heads + c[-own_heads:].astype(F32)
-
-    ig_came = swap(back_call(q_other, full, back), total, 1)
-    input_grad, predictions = back_call(q_own, full, back, (ig_came, preds, pred_came))
-    lane = lax.broadcasted_iota(jnp.int32, (1, R), 1)
-    predictions = jnp.where(lane < counts[0], predictions, 0.0)
+    ig_came = swap(acc, total, 1)
 
     states = [matrix, matrix_first, matrix_second, *turned, head_weights, head_first, head_second]
     (m_first, m_second, m_update, a_first, a_second, a_update, h_first, h_second, h_update, sums) = direction_call(
         mine, heads, last, states)
-    pending = [sums]
-    for low, size in [(1, 2)] + chip_groups[::-1] + dp_groups[::-1]:
+
+    rounds = [(1, 2)] + chip_groups[::-1] + dp_groups[::-1]
+    plan = {0: backward(0, 0), 1: backward(0, 1, 2), len(rounds) - 1: backward(0, 3, q=q_own, came=ig_came)}
+    pending, acc = [sums], ()
+    for step, (low, size) in enumerate(rounds):
         sums = pending[0]
         for p in pending[1:]:
             sums = sums + p
-        pending = [sums] + [swap(sums, total, low * m) for m in range(1, size)]
+        sends = [(sums, total, low * m) for m in range(1, size)]
+        if step in plan:
+            came, acc = beside(sends, plan[step], *weights, *acc)
+            acc = (acc,)
+        else:
+            came = [swap(*send) for send in sends]
+        pending = [sums] + list(came)
+    input_grad = acc[0]
     new_matrix, new_adapters, new_heads, norm_pairs = update_call(
         pending, matrix, turned[0], head_weights, m_update, a_update, h_update)
+    lane = lax.broadcasted_iota(jnp.int32, (1, R), 1)
+    predictions = jnp.where(lane < counts[0], preds[0:1] + pred_came, 0.0) * (1.0 / K)
 
     def back_turn(v):
         return v.transpose(0, 2, 1)
 
     return (predictions.reshape(R), input_grad, new_matrix, m_first, m_second, back_turn(new_adapters),
-            back_turn(a_first), back_turn(a_second), new_heads, h_first, h_second, norm_pairs)
+            back_turn(a_first), back_turn(a_second), new_heads, h_first, h_second, norm_pairs.T)
 
 
 def solution(mesh):

time: 128 us -> 115 us (0.90)
  Pallas kernels: 62 us -> 51.5 us
  waiting for transfers between devices: 27.2 us -> 17.4 us
  local copies, waits for them, and re-layouts: 6.59 us -> 15.4 us
  other arithmetic: 3.43 us -> 1.82 us
    ppermute x25, waiting for transfers between devices: 27.2 us -> 17.4 us  [swap(): return lax.ppermute(value, AXES, [(i, i ^ mask) for i in range(total)])]
    unnamed x23 -> x42, local copies, waits for them, and re-layouts: 5.1 us -> 13.9 us
    pallas_call x1, Pallas kernels: 40.6 us -> 34.7 us  [grad_call(): pl.pallas_call(functools.partial(grad_kernel, own=own), grid=(members //...]
    pallas_call x2 -> x6, Pallas kernels: 16.6 us -> 12 us  [back_call(): pl.pallas_call(functools.partial(back_kernel, members=members, start=star...]
  transfers between devices with their start and end apart: 25 -> 25, of which waited for: 16 -> 11; matrix products, arithmetic and copies ran while one was open for 4% -> 2% of each run, Pallas kernels for 9% -> 12%
where the time goes in v3:
time: 115 us
  Pallas kernels  51.5 us (45%)
  starting transfers between devices  26.9 us (23%)
  waiting for transfers between devices  17.4 us (15%)
  local copies, waits for them, and re-layouts  15.4 us (13%)
  other arithmetic  1.82 us (2%)
  between operations  1.7 us (1%)
    pallas_call x1, Pallas kernels, grad_call(): pl.pallas_call(functools.partial(grad_kernel, own=own), grid=(members //...  34.7 us
    ppermute x25, starting transfers between devices, swap(): return lax.ppermute(value, AXES, [(i, i ^ mask) for i in range(total)])  26.9 us
    ppermute x25, waiting for transfers between devices, swap(): return lax.ppermute(value, AXES, [(i, i ^ mask) for i in range(total)])  17.4 us
    unnamed x42, local copies, waits for them, and re-layouts  13.9 us
    pallas_call x6, Pallas kernels, back_call(): pl.pallas_call(functools.partial(back_kernel, members=members, start=star...  12 us
  transfers between devices with their start and end apart: 25, of which 11 were waited for; matrix products, arithmetic and copies ran while one was open for 2% of the time, Pallas kernels for 12%

profile of v3, /device:TPU:0, one launch (start us, length us, event | category | flops | bytes accessed | tf_op | source)
XLA Modules:
  0.0 114.8 jit_solution(7008083424114690117)
XLA Ops:
  1.3 1.5 %pack_weights.1 = (bf16[16,768]{1,0:T(8,128)(2,1)}, f32[1,512]{1,0:T(1,128)}) custom-call(s32[1]{0:T(128)} %copy.32.count_ref, f32[16,512]{1,0:T(8,128)} %refs_4_.1, f32[3,16,32]{2,1,0:T(8,128)} %bitcast.80, f32[4,512]{1,0:T(4,128)} %refs_6_.3, f32[1,512]{1,0:T(1,128)} %bitcast.85), custom_call_target="tpu_custom_call" | custom-call | tf_op jit(solution)/shard_map/pack_weights/pallas_call | solution.py:51
  2.8 3.0 %collective-permute-start.2 = (bf16[16,768]{1,0:T(8,128)(2,1)}, bf16[16,768]{1,0:T(8,128)(2,1)S(1)}, u32[]{:S(2)}, u32[]{:S(2)}) collective-permute-start(bf16[16,768]{1,0:T(8,128)(2,1)} %get-tuple-element.94), channel_id=1, source_target_pairs={{0,8},{1,9},{2,10},{3,11},{4,12},{5,13},{6,14},{7,15},{8,0},{9,1},... | collective-permute-start | bytes 73736 | tf_op jit(solution)/shard_map/ppermute | solution.py:369
  5.8 2.6 %collective-permute-start.3 = (bf16[16,768]{1,0:T(8,128)(2,1)}, bf16[16,768]{1,0:T(8,128)(2,1)S(1)}, u32[]{:S(2)}, u32[]{:S(2)}) collective-permute-start(bf16[16,768]{1,0:T(8,128)(2,1)} %get-tuple-element.94), channel_id=1, source_target_pairs={{0,16},{1,17},{2,18},{3,19},{4,20},{5,21},{6,22},{7,23},{8,24},{9,... | collective-permute-start | bytes 73736 | tf_op jit(solution)/shard_map/ppermute | solution.py:369
  8.4 2.7 %collective-permute-done.3 = bf16[16,768]{1,0:T(8,128)(2,1)S(1)} collective-permute-done((bf16[16,768]{1,0:T(8,128)(2,1)}, bf16[16,768]{1,0:T(8,128)(2,1)S(1)}, u32[]{:S(2)}, u32[]{:S(2)}) %collective-permute-start.3) | collective-permute-done | bytes 24608 | tf_op jit(solution)/shard_map/ppermute | solution.py:369
  11.1 3.1 %collective-permute-done.4 = bf16[16,768]{1,0:T(8,128)(2,1)S(1)} collective-permute-done((bf16[16,768]{1,0:T(8,128)(2,1)}, bf16[16,768]{1,0:T(8,128)(2,1)S(1)}, u32[]{:S(2)}, u32[]{:S(2)}) %collective-permute-start.4) | collective-permute-done | bytes 24608 | tf_op jit(solution)/shard_map/ppermute | solution.py:369
  15.0 1.6 %collective-permute-start.5 = (bf16[4,16,768]{2,1,0:T(8,128)(2,1)S(1)}, bf16[4,16,768]{2,1,0:T(8,128)(2,1)S(1)}, u32[]{:S(2)}, u32[]{:S(2)}) collective-permute-start(bf16[4,16,768]{2,1,0:T(8,128)(2,1)S(1)} %pad_maximum_fusion.2), channel_id=1, source_target_pairs={{0,2},{1,3},{2,0},{3,1},{4,6},{5,7},{6,4},{7,5},{8,10},{9,11},{10,... | collective-permute-start | bytes 294920 | tf_op jit(solution)/shard_map/ppermute | solution.py:369
  16.5 1.5 %collective-permute-start.6 = (bf16[4,16,768]{2,1,0:T(8,128)(2,1)S(1)}, bf16[4,16,768]{2,1,0:T(8,128)(2,1)S(1)}, u32[]{:S(2)}, u32[]{:S(2)}) collective-permute-start(bf16[4,16,768]{2,1,0:T(8,128)(2,1)S(1)} %pad_maximum_fusion.2), channel_id=1, source_target_pairs={{0,4},{1,5},{2,6},{3,7},{4,0},{5,1},{6,2},{7,3},{8,12},{9,13},{10,... | collective-permute-start | bytes 294920 | tf_op jit(solution)/shard_map/ppermute | solution.py:369
  18.5 1.8 %collective-permute-done.5 = bf16[4,16,768]{2,1,0:T(8,128)(2,1)S(1)} collective-permute-done((bf16[4,16,768]{2,1,0:T(8,128)(2,1)S(1)}, bf16[4,16,768]{2,1,0:T(8,128)(2,1)S(1)}, u32[]{:S(2)}, u32[]{:S(2)}) %collective-permute-start.5) | collective-permute-done | bytes 98336 | tf_op jit(solution)/shard_map/ppermute | solution.py:369
  20.3 1.3 %collective-permute-done.6 = bf16[4,16,768]{2,1,0:T(8,128)(2,1)S(1)} collective-permute-done((bf16[4,16,768]{2,1,0:T(8,128)(2,1)S(1)}, bf16[4,16,768]{2,1,0:T(8,128)(2,1)S(1)}, u32[]{:S(2)}, u32[]{:S(2)}) %collective-permute-start.6) | collective-permute-done | bytes 98336 | tf_op jit(solution)/shard_map/ppermute | solution.py:369
  21.6 2.0 %collective-permute-done.7 = bf16[4,16,768]{2,1,0:T(8,128)(2,1)S(1)} collective-permute-done((bf16[4,16,768]{2,1,0:T(8,128)(2,1)S(1)}, bf16[4,16,768]{2,1,0:T(8,128)(2,1)S(1)}, u32[]{:S(2)}, u32[]{:S(2)}) %collective-permute-start.7) | collective-permute-done | bytes 98336 | tf_op jit(solution)/shard_map/ppermute | solution.py:369
  28.2 34.7 %member_grads.1 = (f32[256,640]{1,0:T(8,128)S(1)}, bf16[256,640]{1,0:T(8,128)(2,1)S(1)}, f32[32,512]{1,0:T(8,128)S(1)}, f32[2,512]{1,0:T(2,128)S(1)}, f32[128,51...) custom-call(bf16[512,512]{1,0:T(8,128)(2,1)S(1)} %copy-done.4, ...), custom_call_target="tpu_custom_call" | custom-call | flops 34359738368 | bytes 16777216 | tf_op jit(solution)/shard_map/member_grads/pallas_call | solution.py:190
  63.6 5.8 %copy-done = bf16[16,1024,512]{2,1,0:T(8,128)(2,1)S(1)} copy-done((bf16[16,1024,512]{2,1,0:T(8,128)(2,1)S(1)}, bf16[16,1024,512]{2,1,0:T(8,128)(2,1)}, u32[]{:S(2)}) %copy-start) | copy-done | bytes 16777240
  72.0 2.4 %collective-permute-start.13 = (bf16[68,640]{1,0:T(8,128)(2,1)S(1)}, bf16[68,640]{1,0:T(8,128)(2,1)S(1)}, u32[]{:S(2)}, u32[]{:S(2)}) collective-permute-start(bf16[68,640]{1,0:T(8,128)(2,1)S(1)} %get-tuple-element.112), channel_id=1, source_target_pairs={{0,6},{1,7},{2,4},{3,5},{4,2},{5,3},{6,0},{7,1},{8,14},{9,15},{10,... | collective-permute-start | bytes 261128 | tf_op jit(solution)/shard_map/ppermute | solution.py:369
  74.4 3.0 %input_grads_other.4.refs_3_ = f32[512,512]{1,0:T(8,128)S(1)} custom-call(f32[128,512]{1,0:T(8,128)S(1)} %get-tuple-element.152.refs_0_, bf16[512,512]{1,0:T(8,128)(2,1)S(1)} %get-tuple-element.153.refs_1_, bf16[16,1024,512]{2,1,0:T(8,128)(2,1)S(1)} %copy-done, f32[512,512]{1,0:T(8,128)S(1)} %input_grads_other.3.refs_3_), custom_call_target="tpu_custom_call" | custom-call | flops 2147483648 | bytes 4194304 | tf_op jit(solution)/shard_map/input_grads_other/pallas_call | solution.py:253
  79.0 3.6 %collective-permute-start.16 = (bf16[20,640]{1,0:T(8,128)(2,1)S(1)}, bf16[20,640]{1,0:T(8,128)(2,1)S(1)}, u32[]{:S(2)}, u32[]{:S(2)}) collective-permute-start(bf16[20,640]{1,0:T(8,128)(2,1)S(1)} %get-tuple-element.123), channel_id=1, source_target_pairs={{0,24},{1,25},{2,26},{3,27},{4,28},{5,29},{6,30},{7,31},{8,16},{9,... | collective-permute-start | bytes 76808 | tf_op jit(solution)/shard_map/ppermute | solution.py:369
  82.6 1.3 %input_grads_other.5 = f32[512,512]{1,0:T(8,128)S(1)} custom-call(f32[128,512]{1,0:T(8,128)S(1)} %get-tuple-element.152.refs_0_, bf16[512,512]{1,0:T(8,128)(2,1)S(1)} %get-tuple-element.153.refs_1_, bf16[16,1024,512]{2,1,0:T(8,128)(2,1)S(1)} %bitcast.70, f32[512,512]{1,0:T(8,128)S(1)} %input_grads_other.4.refs_3_, ...), custom_call_target="tpu_custom_call" | custom-call | flops 1073741824 | bytes 2097152 | tf_op jit(solution)/shard_map/input_grads_other/pallas_call | solution.py:253
  86.6 1.7 %directions.1 = (f32[16,512]{1,0:T(8,128)}, f32[16,512]{1,0:T(8,128)}, f32[16,512]{1,0:T(8,128)}, f32[3,16,32]{2,1,0:T(8,128)}, f32[3,16,32]{2,1,0:T(8,128)}, /*...) custom-call(f32[16,640]{1,0:T(8,128)} %dynamic-slice_bitcast_fusion.refs_, ...), custom_call_target="tpu_custom_call" | custom-call | tf_op jit(solution)/shard_map/directions/pallas_call | solution.py:319
  88.9 5.8 %copy-done.1 = bf16[16,1024,512]{2,1,0:T(8,128)(2,1)S(1)} copy-done((bf16[16,1024,512]{2,1,0:T(8,128)(2,1)S(1)}, bf16[16,1024,512]{2,1,0:T(8,128)(2,1)}, u32[]{:S(2)}) %copy-start.1) | copy-done | bytes 16777240
  96.0 1.5 %collective-permute-start.18 = (f32[16,128]{1,0:T(8,128)S(1)}, f32[16,128]{1,0:T(8,128)S(1)}, u32[]{:S(2)}, u32[]{:S(2)}) collective-permute-start(f32[16,128]{1,0:T(8,128)S(1)} %add.103), channel_id=1, source_target_pairs={{0,2},{1,3},{2,0},{3,1},{4,6},{5,7},{6,4},{7,5},{8,10},{9,11},{10,... | collective-permute-start | bytes 24584 | tf_op jit(solution)/shard_map/ppermute | solution.py:369
  99.5 3.0 %input_grads_own.4.refs_3_ = f32[512,512]{1,0:T(8,128)S(1)} custom-call(f32[128,512]{1,0:T(8,128)S(1)} %get-tuple-element.152.refs_0_, bf16[512,512]{1,0:T(8,128)(2,1)S(1)} %get-tuple-element.153.refs_1_, bf16[16,1024,512]{2,1,0:T(8,128)(2,1)S(1)} %copy-done.1, f32[512,512]{1,0:T(8,128)S(1)} %input_grads_own.3.refs_3_), custom_call_target="tpu_custom_call" | custom-call | flops 2147483648 | bytes 4194304 | tf_op jit(solution)/shard_map/input_grads_own/pallas_call | solution.py:253
  103.3 3.8 %collective-permute-start.22 = (f32[16,128]{1,0:T(8,128)S(1)}, f32[16,128]{1,0:T(8,128)S(1)}, u32[]{:S(2)}, u32[]{:S(2)}) collective-permute-start(f32[16,128]{1,0:T(8,128)S(1)} %add_add_fusion.refs_0_), channel_id=1, source_target_pairs={{0,16},{1,17},{2,18},{3,19},{4,20},{5,21},{6,22},{7,23},{8,24},{9,... | collective-permute-start | bytes 24584 | tf_op jit(solution)/shard_map/ppermute | solution.py:369
  107.5 2.3 %input_grads_own.5 = f32[512,512]{1,0:T(8,128)} custom-call(f32[128,512]{1,0:T(8,128)S(1)} %get-tuple-element.152.refs_0_, bf16[512,512]{1,0:T(8,128)(2,1)S(1)} %get-tuple-element.153.refs_1_, bf16[16,1024,512]{2,1,0:T(8,128)(2,1)S(1)} %bitcast.72, f32[512,512]{1,0:T(8,128)S(1)} %input_grads_own.4.refs_3_, f32[1,512]{1,0:T(1,128)S(1)} %copy-done.3, ...), custom_call_target="tpu_custom_call" | custom-call | flops 1073741824 | bytes 2097152 | tf_op jit(solution)/shard_map/input_grads_own/pallas_call | solution.py:253
  109.7 2.8 %collective-permute-done.23.refs_3_ = f32[16,128]{1,0:T(8,128)S(1)} collective-permute-done((f32[16,128]{1,0:T(8,128)S(1)}, f32[16,128]{1,0:T(8,128)S(1)}, u32[]{:S(2)}, u32[]{:S(2)}) %collective-permute-start.23) | collective-permute-done | bytes 8224 | tf_op jit(solution)/shard_map/ppermute | solution.py:369
  113.1 1.6 %updates.1 = (f32[16,512]{1,0:T(8,128)}, f32[3,16,32]{2,1,0:T(8,128)}, f32[4,512]{1,0:T(4,128)}, f32[2,5]{1,0:T(2,128)}) custom-call(f32[16,128]{1,0:T(8,128)} %copy-done.5, f32[16,128]{1,0:T(8,128)} %copy-done.9, f32[16,128]{1,0:T(8,128)} %copy-done.10, f32[16,128]{1,0:T(8,128)} %copy-done.11, f32[16,512]{1,0:T(8,128)} %refs_4_.1, f32[3,16,32]{2,1,0:T(8,128)} %bitcast.82, ...), custom_call_target="tpu_custom_call" | custom-call | tf_op jit(solution)/shard_map/updates/pallas_call | solution.py:346
  (107 shorter events, 18.9 us)
Async XLA Ops:
  2.8 5.6 %collective-permute-start.2 = (bf16[16,768]{1,0:T(8,128)(2,1)}, bf16[16,768]{1,0:T(8,128)(2,1)S(1)}, u32[]{:S(2)}, u32[]{:S(2)}) collective-permute-start(bf16[16,768]{1,0:T(8,128)(2,1)} %get-tuple-element.94), channel_id=1, source_target_pairs={{0,8},{1,9},{2,10},{3,11},{4,12},{5,13},{6,14},{7,15},{8,0},{9,1},... | collective-permute-start | bytes 73736 | tf_op jit(solution)/shard_map/ppermute | solution.py:369
  5.8 5.3 %collective-permute-start.3 = (bf16[16,768]{1,0:T(8,128)(2,1)}, bf16[16,768]{1,0:T(8,128)(2,1)S(1)}, u32[]{:S(2)}, u32[]{:S(2)}) collective-permute-start(bf16[16,768]{1,0:T(8,128)(2,1)} %get-tuple-element.94), channel_id=1, source_target_pairs={{0,16},{1,17},{2,18},{3,19},{4,20},{5,21},{6,22},{7,23},{8,24},{9,... | collective-permute-start | bytes 73736 | tf_op jit(solution)/shard_map/ppermute | solution.py:369
  8.4 5.8 %collective-permute-start.4 = (bf16[16,768]{1,0:T(8,128)(2,1)}, bf16[16,768]{1,0:T(8,128)(2,1)S(1)}, u32[]{:S(2)}, u32[]{:S(2)}) collective-permute-start(bf16[16,768]{1,0:T(8,128)(2,1)} %get-tuple-element.94), channel_id=1, source_target_pairs={{0,24},{1,25},{2,26},{3,27},{4,28},{5,29},{6,30},{7,31},{8,16},{9,... | collective-permute-start | bytes 73736 | tf_op jit(solution)/shard_map/ppermute | solution.py:369
  15.0 5.3 %collective-permute-start.5 = (bf16[4,16,768]{2,1,0:T(8,128)(2,1)S(1)}, bf16[4,16,768]{2,1,0:T(8,128)(2,1)S(1)}, u32[]{:S(2)}, u32[]{:S(2)}) collective-permute-start(bf16[4,16,768]{2,1,0:T(8,128)(2,1)S(1)} %pad_maximum_fusion.2), channel_id=1, source_target_pairs={{0,2},{1,3},{2,0},{3,1},{4,6},{5,7},{6,4},{7,5},{8,10},{9,11},{10,... | collective-permute-start | bytes 294920 | tf_op jit(solution)/shard_map/ppermute | solution.py:369
  16.5 5.0 %collective-permute-start.6 = (bf16[4,16,768]{2,1,0:T(8,128)(2,1)S(1)}, bf16[4,16,768]{2,1,0:T(8,128)(2,1)S(1)}, u32[]{:S(2)}, u32[]{:S(2)}) collective-permute-start(bf16[4,16,768]{2,1,0:T(8,128)(2,1)S(1)} %pad_maximum_fusion.2), channel_id=1, source_target_pairs={{0,4},{1,5},{2,6},{3,7},{4,0},{5,1},{6,2},{7,3},{8,12},{9,13},{10,... | collective-permute-start | bytes 294920 | tf_op jit(solution)/shard_map/ppermute | solution.py:369
  18.1 5.5 %collective-permute-start.7 = (bf16[4,16,768]{2,1,0:T(8,128)(2,1)S(1)}, bf16[4,16,768]{2,1,0:T(8,128)(2,1)S(1)}, u32[]{:S(2)}, u32[]{:S(2)}) collective-permute-start(bf16[4,16,768]{2,1,0:T(8,128)(2,1)S(1)} %pad_maximum_fusion.2), channel_id=1, source_target_pairs={{0,6},{1,7},{2,4},{3,5},{4,2},{5,3},{6,0},{7,1},{8,14},{9,15},{10,... | collective-permute-start | bytes 294920 | tf_op jit(solution)/shard_map/ppermute | solution.py:369
  23.8 2.7 %collective-permute-start = (bf16[512,512]{1,0:T(8,128)(2,1)}, bf16[512,512]{1,0:T(8,128)(2,1)S(1)}, u32[]{:S(2)}, u32[]{:S(2)}) collective-permute-start(bf16[512,512]{1,0:T(8,128)(2,1)} %x0_ref.1), channel_id=1, source_target_pairs={{0,1},{1,0},{2,3},{3,2},{4,5},{5,4},{6,7},{7,6},{8,9},{9,8},{10,11... | collective-permute-start | bytes 1572872 | tf_op jit(solution)/shard_map/ppermute | solution.py:369
  24.3 2.2 %collective-permute-start.1 = (f32[1,512]{1,0:T(1,128)}, f32[1,512]{1,0:T(1,128)S(1)}, u32[]{:S(2)}, u32[]{:S(2)}) collective-permute-start(f32[1,512]{1,0:T(1,128)} %get-tuple-element.93.q0_ref.refs_4_), channel_id=1, source_target_pairs={{0,1},{1,0},{2,3},{3,2},{4,5},{5,4},{6,7},{7,6},{8,9},{9,8},{10,11... | collective-permute-start | bytes 6152 | tf_op jit(solution)/shard_map/ppermute | solution.py:369
  63.0 7.7 %collective-permute-start.9 = (bf16[4,68,640]{2,1,0:T(8,128)(2,1)S(1)}, bf16[4,68,640]{2,1,0:T(8,128)(2,1)S(1)}, u32[]{:S(2)}, u32[]{:S(2)}) collective-permute-start(bf16[4,68,640]{2,1,0:T(8,128)(2,1)S(1)} %fusion.2), channel_id=1, source_target_pairs={{0,1},{1,0},{2,3},{3,2},{4,5},{5,4},{6,7},{7,6},{8,9},{9,8},{10,11... | collective-permute-start | bytes 1044488 | tf_op jit(solution)/shard_map/ppermute | solution.py:369
  63.2 7.5 %collective-permute-start.10 = (f32[1,512]{1,0:T(1,128)S(1)}, f32[1,512]{1,0:T(1,128)S(1)}, u32[]{:S(2)}, u32[]{:S(2)}) collective-permute-start(f32[1,512]{1,0:T(1,128)S(1)} %slice.13), channel_id=1, source_target_pairs={{0,1},{1,0},{2,3},{3,2},{4,5},{5,4},{6,7},{7,6},{8,9},{9,8},{10,11... | collective-permute-start | bytes 6152 | tf_op jit(solution)/shard_map/ppermute | solution.py:369
  70.9 6.5 %collective-permute-start.11 = (bf16[68,640]{1,0:T(8,128)(2,1)S(1)}, bf16[68,640]{1,0:T(8,128)(2,1)S(1)}, u32[]{:S(2)}, u32[]{:S(2)}) collective-permute-start(bf16[68,640]{1,0:T(8,128)(2,1)S(1)} %get-tuple-element.110), channel_id=1, source_target_pairs={{0,2},{1,3},{2,0},{3,1},{4,6},{5,7},{6,4},{7,5},{8,10},{9,11},{10,... | collective-permute-start | bytes 261128 | tf_op jit(solution)/shard_map/ppermute | solution.py:369
  71.5 6.5 %collective-permute-start.12 = (bf16[68,640]{1,0:T(8,128)(2,1)S(1)}, bf16[68,640]{1,0:T(8,128)(2,1)S(1)}, u32[]{:S(2)}, u32[]{:S(2)}) collective-permute-start(bf16[68,640]{1,0:T(8,128)(2,1)S(1)} %get-tuple-element.111), channel_id=1, source_target_pairs={{0,4},{1,5},{2,6},{3,7},{4,0},{5,1},{6,2},{7,3},{8,12},{9,13},{10,... | collective-permute-start | bytes 261128 | tf_op jit(solution)/shard_map/ppermute | solution.py:369
  72.0 6.0 %collective-permute-start.13 = (bf16[68,640]{1,0:T(8,128)(2,1)S(1)}, bf16[68,640]{1,0:T(8,128)(2,1)S(1)}, u32[]{:S(2)}, u32[]{:S(2)}) collective-permute-start(bf16[68,640]{1,0:T(8,128)(2,1)S(1)} %get-tuple-element.112), channel_id=1, source_target_pairs={{0,6},{1,7},{2,4},{3,5},{4,2},{5,3},{6,0},{7,1},{8,14},{9,15},{10,... | collective-permute-start | bytes 261128 | tf_op jit(solution)/shard_map/ppermute | solution.py:369
  78.1 5.8 %collective-permute-start.14 = (bf16[20,640]{1,0:T(8,128)(2,1)S(1)}, bf16[20,640]{1,0:T(8,128)(2,1)S(1)}, u32[]{:S(2)}, u32[]{:S(2)}) collective-permute-start(bf16[20,640]{1,0:T(8,128)(2,1)S(1)} %get-tuple-element.121), channel_id=1, source_target_pairs={{0,8},{1,9},{2,10},{3,11},{4,12},{5,13},{6,14},{7,15},{8,0},{9,1},... | collective-permute-start | bytes 76808 | tf_op jit(solution)/shard_map/ppermute | solution.py:369
  78.2 5.7 %collective-permute-start.15 = (bf16[20,640]{1,0:T(8,128)(2,1)S(1)}, bf16[20,640]{1,0:T(8,128)(2,1)S(1)}, u32[]{:S(2)}, u32[]{:S(2)}) collective-permute-start(bf16[20,640]{1,0:T(8,128)(2,1)S(1)} %get-tuple-element.122), channel_id=1, source_target_pairs={{0,16},{1,17},{2,18},{3,19},{4,20},{5,21},{6,22},{7,23},{8,24},{9,... | collective-permute-start | bytes 76808 | tf_op jit(solution)/shard_map/ppermute | solution.py:369
  79.0 5.8 %collective-permute-start.16 = (bf16[20,640]{1,0:T(8,128)(2,1)S(1)}, bf16[20,640]{1,0:T(8,128)(2,1)S(1)}, u32[]{:S(2)}, u32[]{:S(2)}) collective-permute-start(bf16[20,640]{1,0:T(8,128)(2,1)S(1)} %get-tuple-element.123), channel_id=1, source_target_pairs={{0,24},{1,25},{2,26},{3,27},{4,28},{5,29},{6,30},{7,31},{8,16},{9,... | collective-permute-start | bytes 76808 | tf_op jit(solution)/shard_map/ppermute | solution.py:369
  84.8 22.6 %collective-permute-start.24 = (f32[512,512]{1,0:T(8,128)S(1)}, f32[512,512]{1,0:T(8,128)S(1)}, u32[]{:S(2)}, u32[]{:S(2)}) collective-permute-start(f32[512,512]{1,0:T(8,128)S(1)} %input_grads_other.5), channel_id=1, source_target_pairs={{0,1},{1,0},{2,3},{3,2},{4,5},{5,4},{6,7},{7,6},{8,9},{9,8},{10,11... | collective-permute-start | bytes 3145736 | tf_op jit(solution)/shard_map/ppermute | solution.py:369
  88.3 7.6 %collective-permute-start.17 = (f32[16,128]{1,0:T(8,128)}, f32[16,128]{1,0:T(8,128)S(1)}, u32[]{:S(2)}, u32[]{:S(2)}) collective-permute-start(f32[16,128]{1,0:T(8,128)} %get-tuple-element.132), channel_id=1, source_target_pairs={{0,1},{1,0},{2,3},{3,2},{4,5},{5,4},{6,7},{7,6},{8,9},{9,8},{10,11... | collective-permute-start | bytes 24584 | tf_op jit(solution)/shard_map/ppermute | solution.py:369
  96.0 6.5 %collective-permute-start.18 = (f32[16,128]{1,0:T(8,128)S(1)}, f32[16,128]{1,0:T(8,128)S(1)}, u32[]{:S(2)}, u32[]{:S(2)}) collective-permute-start(f32[16,128]{1,0:T(8,128)S(1)} %add.103), channel_id=1, source_target_pairs={{0,2},{1,3},{2,0},{3,1},{4,6},{5,7},{6,4},{7,5},{8,10},{9,11},{10,... | collective-permute-start | bytes 24584 | tf_op jit(solution)/shard_map/ppermute | solution.py:369
  97.5 5.0 %collective-permute-start.19 = (f32[16,128]{1,0:T(8,128)S(1)}, f32[16,128]{1,0:T(8,128)S(1)}, u32[]{:S(2)}, u32[]{:S(2)}) collective-permute-start(f32[16,128]{1,0:T(8,128)S(1)} %add.103), channel_id=1, source_target_pairs={{0,4},{1,5},{2,6},{3,7},{4,0},{5,1},{6,2},{7,3},{8,12},{9,13},{10,... | collective-permute-start | bytes 24584 | tf_op jit(solution)/shard_map/ppermute | solution.py:369
  98.5 4.5 %collective-permute-start.20 = (f32[16,128]{1,0:T(8,128)S(1)}, f32[16,128]{1,0:T(8,128)S(1)}, u32[]{:S(2)}, u32[]{:S(2)}) collective-permute-start(f32[16,128]{1,0:T(8,128)S(1)} %add.103), channel_id=1, source_target_pairs={{0,6},{1,7},{2,4},{3,5},{4,2},{5,3},{6,0},{7,1},{8,14},{9,15},{10,... | collective-permute-start | bytes 24584 | tf_op jit(solution)/shard_map/ppermute | solution.py:369
  103.0 6.7 %collective-permute-start.21 = (f32[16,128]{1,0:T(8,128)S(1)}, f32[16,128]{1,0:T(8,128)S(1)}, u32[]{:S(2)}, u32[]{:S(2)}) collective-permute-start(f32[16,128]{1,0:T(8,128)S(1)} %add_add_fusion.refs_0_), channel_id=1, source_target_pairs={{0,8},{1,9},{2,10},{3,11},{4,12},{5,13},{6,14},{7,15},{8,0},{9,1},... | collective-permute-start | bytes 24584 | tf_op jit(solution)/shard_map/ppermute | solution.py:369
  103.3 6.4 %collective-permute-start.22 = (f32[16,128]{1,0:T(8,128)S(1)}, f32[16,128]{1,0:T(8,128)S(1)}, u32[]{:S(2)}, u32[]{:S(2)}) collective-permute-start(f32[16,128]{1,0:T(8,128)S(1)} %add_add_fusion.refs_0_), channel_id=1, source_target_pairs={{0,16},{1,17},{2,18},{3,19},{4,20},{5,21},{6,22},{7,23},{8,24},{9,... | collective-permute-start | bytes 24584 | tf_op jit(solution)/shard_map/ppermute | solution.py:369
  107.1 5.4 %collective-permute-start.23 = (f32[16,128]{1,0:T(8,128)S(1)}, f32[16,128]{1,0:T(8,128)S(1)}, u32[]{:S(2)}, u32[]{:S(2)}) collective-permute-start(f32[16,128]{1,0:T(8,128)S(1)} %add_add_fusion.refs_0_), channel_id=1, source_target_pairs={{0,24},{1,25},{2,26},{3,27},{4,28},{5,29},{6,30},{7,31},{8,16},{9,... | collective-permute-start | bytes 24584 | tf_op jit(solution)/shard_map/ppermute | solution.py:369
  (22 other events, 150.6 us)

commit v4 on v3

--- a/solution.py
+++ b/solution.py
@@ -78,7 +78,7 @@
         cols = packed_ref[:, D:D + LANES].astype(F32)
         cols_ref[...] = cols
         rows_ref[...] = cols.T
-        turned_ref[...] = weight_ref[...].T.astype(BF16)
+        turned_ref[...] = packed_ref[:, :D].T
         L = packed_ref.shape[1] - D - LANES
         per_head = D // L
         for c in range(0, L, LANES):
@@ -94,7 +94,7 @@
             half_q = 0.5 * q_row
             q_hi = half_q.astype(BF16)
             q_lo = (half_q - q_hi.astype(F32)).astype(BF16)
-            xq_ref[:D, at] = (x_side[...].astype(F32).T * half_q).astype(BF16)
+            xq_ref[:D, at] = (x_side[...].T.astype(F32) * half_q).astype(BF16)
             sub = lax.broadcasted_iota(jnp.int32, (16, half), 0)
             extra = jnp.where(sub == 0, q_hi.astype(F32), jnp.where(sub == 1, q_lo.astype(F32), 0.0))
             xq_ref[D:, at] = extra.astype(BF16)
@@ -257,7 +257,7 @@
         in_specs=[VMEM, VMEM, pl.BlockSpec((n, R, D), lambda i: (start // n + i, where, 0))] + [VMEM] * len(more),
         out_specs=VMEM,
         scratch_shapes=[pltpu.VMEM((R, D), F32)],
-        compiler_params=pltpu.CompilerParams(vmem_limit_bytes=LIMIT // 2),
+        compiler_params=pltpu.CompilerParams(vmem_limit_bytes=LIMIT),
         cost_estimate=pl.CostEstimate(flops=2 * count * R * D * D, bytes_accessed=count * R * D * 2, transcendentals=0),
         name="input_grads_other" if where else "input_grads_own",
     )(rows, turned, back, *more)
@@ -282,16 +282,20 @@
     return sum(total[:, l:l + LANES] for l in range(0, width, LANES))
 
 
-def direction_kernel(count, *refs):
-    mine_ref, heads_ref = refs[:2]
-    came = refs[2:2 + count]
+def direction_kernel(low, size, *refs):
+    wide_ref = refs[0]
+    count = size - 1
+    came = refs[1:1 + count]
     (m_ref, m1_ref, m2_ref, a_ref, a1_ref, a2_ref, h_ref, h1_ref, h2_ref,
-     m1_out, m2_out, mu_out, a1_out, a2_out, au_out, h1_out, h2_out, hu_out, sums_out) = refs[2 + count:]
+     m1_out, m2_out, mu_out, a1_out, a2_out, au_out, h1_out, h2_out, hu_out, sums_out) = refs[1 + count:]
     own, D = m_ref.shape
     K = a_ref.shape[2]
     n_heads = h_ref.shape[0]
-    grad = mine_ref[...]
-    heads = heads_ref[:, :D]
+    place = lax.rem(lax.axis_index("dp") // low, size)
+    grad = wide_ref[:own, :]
+    for v in range(1, size):
+        grad = jnp.where(place == v, wide_ref[v * own:(v + 1) * own, :], grad)
+    heads = wide_ref[size * own:size * own + n_heads, :D]
     for c in came:
         grad = grad + c[:own, :].astype(F32)
         heads = heads + c[own:own + n_heads, :D].astype(F32)
@@ -313,16 +317,16 @@
     sums_out[...] = jnp.concatenate(weight_rows + update_rows + [jnp.zeros((6, LANES), F32)], axis=0)
 
 
-def direction_call(mine, heads, came, states):
+def direction_call(wide, came, low, states):
     m, a, h = states[0], states[3], states[6]
     outs = [shape(v.shape) for v in (m, m, m, a, a, a, h, h, h)] + [shape((16, LANES))]
     return pl.pallas_call(
-        functools.partial(direction_kernel, len(came)),
+        functools.partial(direction_kernel, low, len(came) + 1),
         out_shape=tuple(outs),
-        in_specs=[VMEM] * (2 + len(came) + 9),
+        in_specs=[VMEM] * (1 + len(came) + 9),
         out_specs=tuple([VMEM] * 10),
         name="directions",
-    )(mine, heads, *came, *states)
+    )(wide, *came, *states)
 
 
 def update_kernel(count, *refs):
@@ -369,12 +373,16 @@
     return lax.ppermute(value, AXES, [(i, i ^ mask) for i in range(total)])
 
 
-def gather_groups(value, groups, total, index):
+def gather_groups(value, groups, total, index, *also):
+    brought = ()
     for axis, (low, size) in enumerate(groups):
         place = (index // low) % size
         held = [value] + [swap(value, total, low * m) for m in range(1, size)]
+        if axis == 0:
+            brought = tuple(swap(v, total, mask) for v, mask in also)
+            held, brought = lax.optimization_barrier((held, brought))
         value = jnp.stack([lax.select_n(place ^ p, *held) for p in range(size)], axis=axis)
-    return value
+    return value, brought
 
 
 def beside(sends, work, *inputs):
@@ -396,9 +404,9 @@
     turned = [v.transpose(0, 2, 1) for v in (adapters, adapter_first, adapter_second)]
 
     packed, q_own = pack_call(counts, matrix, turned[0], head_weights, cotangent.reshape(1, R))
-    x_other = swap(objects, total, 1)
-    q_other = swap(q_own, total, 1)
-    full = gather_groups(packed, dp_groups + member_groups, total, index).reshape(D, -1)
+    full, (x_other, q_other) = gather_groups(
+        packed, dp_groups + member_groups, total, index, (objects, 1), (q_own, 1))
+    full = full.reshape(D, -1)
     keep, sent, head_grads, preds, rows, wide_turned, back = grad_call(objects, x_other, q_own, q_other, full, K, own)
 
     chips = [size for _, size in chip_groups]
@@ -436,29 +444,31 @@
         wide = part[0]
         for c in came:
             wide = wide + c.astype(F32)
-    mine = wide[: n_dp * own].reshape([size for _, size in dp_groups] + [own, D + LANES])
-    heads = wide[n_dp * own:]
     for axis in reversed(range(len(dp_groups))):
         low, size = dp_groups[axis]
         place = (index // low) % size
-        part = [lax.dynamic_index_in_dim(mine, place ^ m, axis, keepdims=False) for m in range(size)]
-        lead = part[0].shape[:-2]
-        both = [jnp.concatenate([p.reshape(-1, D + LANES), heads], axis=0).astype(BF16) for p in part[1:]]
-        sends = [(b, total, low * (m + 1)) for m, b in enumerate(both)]
+        outer_count = (wide.shape[0] - own_heads) // (own * size)
+        main = wide[:-own_heads].reshape(outer_count, size * own, D + LANES)
+        heads = wide[-own_heads:]
+
+        def chunk(v):
+            at = lax.dynamic_slice_in_dim(main, v * own, own, 1)
+            return jnp.concatenate([at.reshape(-1, D + LANES), heads], axis=0)
+
+        sends = [(chunk(place ^ m).astype(BF16), total, low * m) for m in range(1, size)]
         if axis == len(dp_groups) - 1:
             last, acc = beside(sends, backward(1, 3, q=q_other), *weights, acc)
         else:
             last = [swap(*send) for send in sends]
-        mine = part[0]
         if axis:
+            wide = chunk(place)
             for c in last:
-                mine = mine + c[:-own_heads].astype(F32).reshape(lead + (own, D + LANES))
-                heads = heads + c[-own_heads:].astype(F32)
+                wide = wide + c.astype(F32)
     ig_came = swap(acc, total, 1)
 
     states = [matrix, matrix_first, matrix_second, *turned, head_weights, head_first, head_second]
     (m_first, m_second, m_update, a_first, a_second, a_update, h_first, h_second, h_update, sums) = direction_call(
-        mine, heads, last, states)
+        wide, last, dp_groups[0][0] // n_member, states)
 
     rounds = [(1, 2)] + chip_groups[::-1] + dp_groups[::-1]
     plan = {0: backward(0, 0), 1: backward(0, 1, 2), len(rounds) - 1: backward(0, 3, q=q_own, came=ig_came)}

time: 115 us -> 107 us (0.930)
  local copies, waits for them, and re-layouts: 15.4 us -> 2.63 us
  Pallas kernels: 51.5 us -> 60.6 us
  waiting for transfers between devices: 17.4 us -> 13.1 us
    unnamed x42 -> x24, local copies, waits for them, and re-layouts: 13.9 us -> 2.35 us
    pallas_call x6, Pallas kernels: 12 us -> 20.9 us  [back_call(): pl.pallas_call(functools.partial(back_kernel, members=members, start=star...]
    ppermute x25, waiting for transfers between devices: 17.4 us -> 13.1 us  [swap(): return lax.ppermute(value, AXES, [(i, i ^ mask) for i in range(total)])]
  transfers between devices with their start and end apart: 25 -> 25, of which waited for: 11 -> 8; matrix products, arithmetic and copies ran while one was open for 2% -> 1% of each run, Pallas kernels for 12% -> 23%
where the time goes in v4:
time: 107 us; the launch traced here: 106 us
  Pallas kernels  60.6 us (57%)
  starting transfers between devices  26.5 us (25%)
  waiting for transfers between devices  13.1 us (12%)
  local copies, waits for them, and re-layouts  2.63 us (2%)
  other arithmetic  1.82 us (2%)
  between operations  1.73 us (2%)
    pallas_call x1, Pallas kernels, grad_call(): pl.pallas_call(functools.partial(grad_kernel, own=own), grid=(members //...  34.8 us
    ppermute x25, starting transfers between devices, swap(): return lax.ppermute(value, AXES, [(i, i ^ mask) for i in range(total)])  26.5 us
    pallas_call x6, Pallas kernels, back_call(): pl.pallas_call(functools.partial(back_kernel, members=members, start=star...  20.9 us
    ppermute x25, waiting for transfers between devices, swap(): return lax.ppermute(value, AXES, [(i, i ^ mask) for i in range(total)])  13.1 us
    unnamed x24, local copies, waits for them, and re-layouts  2.35 us
  transfers between devices with their start and end apart: 25, of which 8 were waited for; matrix products, arithmetic and copies ran while one was open for 1% of the time, Pallas kernels for 23%

profile of v4, /device:TPU:0, one launch (start us, length us, event | category | flops | bytes accessed | tf_op | source)
XLA Modules:
  0.0 106.4 jit_solution(17495632880054297077)
XLA Ops:
  1.8 1.5 %pack_weights.1 = (bf16[16,768]{1,0:T(8,128)(2,1)}, f32[1,512]{1,0:T(1,128)}) custom-call(s32[1]{0:T(128)} %copy.32.count_ref, f32[16,512]{1,0:T(8,128)} %refs_4_.3, f32[3,16,32]{2,1,0:T(8,128)} %bitcast.65, f32[4,512]{1,0:T(4,128)} %refs_6_.3, f32[1,512]{1,0:T(1,128)} %bitcast.70), custom_call_target="tpu_custom_call" | custom-call | tf_op jit(solution)/shard_map/pack_weights/pallas_call | solution.py:51
  3.3 2.6 %collective-permute-start = (bf16[16,768]{1,0:T(8,128)(2,1)}, bf16[16,768]{1,0:T(8,128)(2,1)S(1)}, u32[]{:S(2)}, u32[]{:S(2)}) collective-permute-start(bf16[16,768]{1,0:T(8,128)(2,1)} %get-tuple-element.103), channel_id=1, source_target_pairs={{0,8},{1,9},{2,10},{3,11},{4,12},{5,13},{6,14},{7,15},{8,0},{9,1},... | collective-permute-start | bytes 73736 | tf_op jit(solution)/shard_map/ppermute | solution.py:373
  5.9 2.6 %collective-permute-start.1 = (bf16[16,768]{1,0:T(8,128)(2,1)}, bf16[16,768]{1,0:T(8,128)(2,1)S(1)}, u32[]{:S(2)}, u32[]{:S(2)}) collective-permute-start(bf16[16,768]{1,0:T(8,128)(2,1)} %get-tuple-element.103), channel_id=1, source_target_pairs={{0,16},{1,17},{2,18},{3,19},{4,20},{5,21},{6,22},{7,23},{8,24},{9,... | collective-permute-start | bytes 73736 | tf_op jit(solution)/shard_map/ppermute | solution.py:373
  8.5 1.4 %collective-permute-done.4.q1_ref.refs_4_ = f32[1,512]{1,0:T(1,128)S(1)} collective-permute-done((f32[1,512]{1,0:T(1,128)}, f32[1,512]{1,0:T(1,128)S(1)}, u32[]{:S(2)}, u32[]{:S(2)}) %collective-permute-start.4) | collective-permute-done | bytes 2080 | tf_op jit(solution)/shard_map/ppermute | solution.py:373
  10.9 3.4 %collective-permute-done.2 = bf16[16,768]{1,0:T(8,128)(2,1)S(1)} collective-permute-done((bf16[16,768]{1,0:T(8,128)(2,1)}, bf16[16,768]{1,0:T(8,128)(2,1)S(1)}, u32[]{:S(2)}, u32[]{:S(2)}) %collective-permute-start.2) | collective-permute-done | bytes 24608 | tf_op jit(solution)/shard_map/ppermute | solution.py:373
  15.1 1.6 %collective-permute-start.5 = (bf16[4,16,768]{2,1,0:T(8,128)(2,1)S(1)}, bf16[4,16,768]{2,1,0:T(8,128)(2,1)S(1)}, u32[]{:S(2)}, u32[]{:S(2)}) collective-permute-start(bf16[4,16,768]{2,1,0:T(8,128)(2,1)S(1)} %pad_maximum_fusion.2), channel_id=1, source_target_pairs={{0,2},{1,3},{2,0},{3,1},{4,6},{5,7},{6,4},{7,5},{8,10},{9,11},{10,... | collective-permute-start | bytes 294920 | tf_op jit(solution)/shard_map/ppermute | solution.py:373
  16.6 1.5 %collective-permute-start.6 = (bf16[4,16,768]{2,1,0:T(8,128)(2,1)S(1)}, bf16[4,16,768]{2,1,0:T(8,128)(2,1)S(1)}, u32[]{:S(2)}, u32[]{:S(2)}) collective-permute-start(bf16[4,16,768]{2,1,0:T(8,128)(2,1)S(1)} %pad_maximum_fusion.2), channel_id=1, source_target_pairs={{0,4},{1,5},{2,6},{3,7},{4,0},{5,1},{6,2},{7,3},{8,12},{9,13},{10,... | collective-permute-start | bytes 294920 | tf_op jit(solution)/shard_map/ppermute | solution.py:373
  18.6 2.0 %collective-permute-done.5 = bf16[4,16,768]{2,1,0:T(8,128)(2,1)S(1)} collective-permute-done((bf16[4,16,768]{2,1,0:T(8,128)(2,1)S(1)}, bf16[4,16,768]{2,1,0:T(8,128)(2,1)S(1)}, u32[]{:S(2)}, u32[]{:S(2)}) %collective-permute-start.5) | collective-permute-done | bytes 98336 | tf_op jit(solution)/shard_map/ppermute | solution.py:373
  20.6 1.6 %collective-permute-done.6 = bf16[4,16,768]{2,1,0:T(8,128)(2,1)S(1)} collective-permute-done((bf16[4,16,768]{2,1,0:T(8,128)(2,1)S(1)}, bf16[4,16,768]{2,1,0:T(8,128)(2,1)S(1)}, u32[]{:S(2)}, u32[]{:S(2)}) %collective-permute-start.6) | collective-permute-done | bytes 98336 | tf_op jit(solution)/shard_map/ppermute | solution.py:373
  22.1 1.5 %collective-permute-done.7 = bf16[4,16,768]{2,1,0:T(8,128)(2,1)S(1)} collective-permute-done((bf16[4,16,768]{2,1,0:T(8,128)(2,1)S(1)}, bf16[4,16,768]{2,1,0:T(8,128)(2,1)S(1)}, u32[]{:S(2)}, u32[]{:S(2)}) %collective-permute-start.7) | collective-permute-done | bytes 98336 | tf_op jit(solution)/shard_map/ppermute | solution.py:373
  23.9 1.7 %collective-permute-done.8 = bf16[4,4,16,768]{3,2,0,1:T(8,128)(2,1)S(1)} collective-permute-done((bf16[4,4,16,768]{3,2,0,1:T(8,128)(2,1)S(1)}, bf16[4,4,16,768]{3,2,0,1:T(8,128)(2,1)S(1)}, u32[]{:S(2)}, u32[]{:S(2)}) %collective-permute-start.8) | collective-permute-done | bytes 393248 | tf_op jit(solution)/shard_map/ppermute | solution.py:373
  27.6 34.8 %member_grads.1 = (f32[256,640]{1,0:T(8,128)S(1)}, bf16[256,640]{1,0:T(8,128)(2,1)S(1)}, f32[32,512]{1,0:T(8,128)S(1)}, f32[2,512]{1,0:T(2,128)S(1)}, f32[128,51...) custom-call(bf16[512,512]{1,0:T(8,128)(2,1)S(1)} %copy-done.2, ...), custom_call_target="tpu_custom_call" | custom-call | flops 34359738368 | bytes 16777216 | tf_op jit(solution)/shard_map/member_grads/pallas_call | solution.py:190
  63.1 2.8 %input_grads_other.3.refs_3_ = f32[512,512]{1,0:T(8,128)S(1)} custom-call(f32[128,512]{1,0:T(8,128)S(1)} %get-tuple-element.164.refs_0_, bf16[512,512]{1,0:T(8,128)(2,1)S(1)} %get-tuple-element.165.refs_1_, bf16[16,1024,512]{2,1,0:T(8,128)(2,1)} %get-tuple-element.166.refs_2_), custom_call_target="tpu_custom_call" | custom-call | flops 1073741824 | bytes 2097152 | tf_op jit(solution)/shard_map/input_grads_other/pallas_call | solution.py:253
  67.2 2.4 %collective-permute-start.13 = (bf16[68,640]{1,0:T(8,128)(2,1)S(1)}, bf16[68,640]{1,0:T(8,128)(2,1)S(1)}, u32[]{:S(2)}, u32[]{:S(2)}) collective-permute-start(bf16[68,640]{1,0:T(8,128)(2,1)S(1)} %get-tuple-element.124), channel_id=1, source_target_pairs={{0,6},{1,7},{2,4},{3,5},{4,2},{5,3},{6,0},{7,1},{8,14},{9,15},{10,... | collective-permute-start | bytes 261128 | tf_op jit(solution)/shard_map/ppermute | solution.py:373
  69.7 4.3 %input_grads_other.4.refs_3_ = f32[512,512]{1,0:T(8,128)S(1)} custom-call(f32[128,512]{1,0:T(8,128)S(1)} %get-tuple-element.164.refs_0_, bf16[512,512]{1,0:T(8,128)(2,1)S(1)} %get-tuple-element.165.refs_1_, bf16[16,1024,512]{2,1,0:T(8,128)(2,1)} %get-tuple-element.166.refs_2_, f32[512,512]{1,0:T(8,128)S(1)} %input_grads_other.3.refs_3_), custom_call_target="tpu_custom_call" | custom-call | flops 2147483648 | bytes 4194304 | tf_op jit(solution)/shard_map/input_grads_other/pallas_call | solution.py:253
  75.1 3.5 %collective-permute-start.16 = (bf16[20,640]{1,0:T(8,128)(2,1)S(1)}, bf16[20,640]{1,0:T(8,128)(2,1)S(1)}, u32[]{:S(2)}, u32[]{:S(2)}) collective-permute-start(bf16[20,640]{1,0:T(8,128)(2,1)S(1)} %get-tuple-element.135), channel_id=1, source_target_pairs={{0,24},{1,25},{2,26},{3,27},{4,28},{5,29},{6,30},{7,31},{8,16},{9,... | collective-permute-start | bytes 76808 | tf_op jit(solution)/shard_map/ppermute | solution.py:373
  78.6 2.8 %input_grads_other.5 = f32[512,512]{1,0:T(8,128)S(1)} custom-call(f32[128,512]{1,0:T(8,128)S(1)} %get-tuple-element.164.refs_0_, bf16[512,512]{1,0:T(8,128)(2,1)S(1)} %get-tuple-element.165.refs_1_, bf16[16,1024,512]{2,1,0:T(8,128)(2,1)} %get-tuple-element.166.refs_2_, f32[512,512]{1,0:T(8,128)S(1)} %input_grads_other.4.refs_3_, ...), custom_call_target="tpu_custom_call" | custom-call | flops 1073741824 | bytes 2097152 | tf_op jit(solution)/shard_map/input_grads_other/pallas_call | solution.py:253
  82.2 1.8 %directions.1 = (f32[16,512]{1,0:T(8,128)}, f32[16,512]{1,0:T(8,128)}, f32[16,512]{1,0:T(8,128)}, f32[3,16,32]{2,1,0:T(8,128)}, f32[3,16,32]{2,1,0:T(8,128)}, /*...) custom-call(f32[68,640]{1,0:T(8,128)} %copy-done.3, ...), custom_call_target="tpu_custom_call" | custom-call | tf_op jit(solution)/shard_map/directions/pallas_call | solution.py:323
  84.6 2.8 %input_grads_own.3.refs_3_ = f32[512,512]{1,0:T(8,128)S(1)} custom-call(f32[128,512]{1,0:T(8,128)S(1)} %get-tuple-element.164.refs_0_, bf16[512,512]{1,0:T(8,128)(2,1)S(1)} %get-tuple-element.165.refs_1_, bf16[16,1024,512]{2,1,0:T(8,128)(2,1)} %get-tuple-element.166.refs_2_), custom_call_target="tpu_custom_call" | custom-call | flops 1073741824 | bytes 2097152 | tf_op jit(solution)/shard_map/input_grads_own/pallas_call | solution.py:253
  89.2 1.8 %collective-permute-start.20 = (f32[16,128]{1,0:T(8,128)S(1)}, f32[16,128]{1,0:T(8,128)S(1)}, u32[]{:S(2)}, u32[]{:S(2)}) collective-permute-start(f32[16,128]{1,0:T(8,128)S(1)} %add.98), channel_id=1, source_target_pairs={{0,6},{1,7},{2,4},{3,5},{4,2},{5,3},{6,0},{7,1},{8,14},{9,15},{10,... | collective-permute-start | bytes 24584 | tf_op jit(solution)/shard_map/ppermute | solution.py:373
  91.0 4.3 %input_grads_own.4.refs_3_ = f32[512,512]{1,0:T(8,128)S(1)} custom-call(f32[128,512]{1,0:T(8,128)S(1)} %get-tuple-element.164.refs_0_, bf16[512,512]{1,0:T(8,128)(2,1)S(1)} %get-tuple-element.165.refs_1_, bf16[16,1024,512]{2,1,0:T(8,128)(2,1)} %get-tuple-element.166.refs_2_, f32[512,512]{1,0:T(8,128)S(1)} %input_grads_own.3.refs_3_), custom_call_target="tpu_custom_call" | custom-call | flops 2147483648 | bytes 4194304 | tf_op jit(solution)/shard_map/input_grads_own/pallas_call | solution.py:253
  95.4 3.3 %collective-permute-start.22 = (f32[16,128]{1,0:T(8,128)S(1)}, f32[16,128]{1,0:T(8,128)S(1)}, u32[]{:S(2)}, u32[]{:S(2)}) collective-permute-start(f32[16,128]{1,0:T(8,128)S(1)} %add_add_fusion.refs_0_), channel_id=1, source_target_pairs={{0,16},{1,17},{2,18},{3,19},{4,20},{5,21},{6,22},{7,23},{8,24},{9,... | collective-permute-start | bytes 24584 | tf_op jit(solution)/shard_map/ppermute | solution.py:373
  99.8 3.8 %input_grads_own.5 = f32[512,512]{1,0:T(8,128)} custom-call(f32[128,512]{1,0:T(8,128)S(1)} %get-tuple-element.164.refs_0_, bf16[512,512]{1,0:T(8,128)(2,1)S(1)} %get-tuple-element.165.refs_1_, bf16[16,1024,512]{2,1,0:T(8,128)(2,1)} %get-tuple-element.166.refs_2_, f32[512,512]{1,0:T(8,128)S(1)} %input_grads_own.4.refs_3_, f32[1,512]{1,0:T(1,128)S(1)} %copy-done.1, ...), custom_call_target="tpu_custom_call" | custom-call | flops 1073741824 | bytes 2097152 | tf_op jit(solution)/shard_map/input_grads_own/pallas_call | solution.py:253
  104.7 1.6 %updates.1 = (f32[16,512]{1,0:T(8,128)}, f32[3,16,32]{2,1,0:T(8,128)}, f32[4,512]{1,0:T(4,128)}, f32[2,5]{1,0:T(2,128)}) custom-call(f32[16,128]{1,0:T(8,128)} %copy-done.4, f32[16,128]{1,0:T(8,128)} %copy-done.8, f32[16,128]{1,0:T(8,128)} %copy-done.9, f32[16,128]{1,0:T(8,128)} %copy-done.10, f32[16,512]{1,0:T(8,128)} %refs_4_.3, f32[3,16,32]{2,1,0:T(8,128)} %bitcast.67, ...), custom_call_target="tpu_custom_call" | custom-call | tf_op jit(solution)/shard_map/updates/pallas_call | solution.py:350
  (85 shorter events, 13.4 us)
Async XLA Ops:
  0.6 13.6 %collective-permute-start.3 = (bf16[512,512]{1,0:T(8,128)(2,1)}, bf16[512,512]{1,0:T(8,128)(2,1)S(1)}, u32[]{:S(2)}, u32[]{:S(2)}) collective-permute-start(bf16[512,512]{1,0:T(8,128)(2,1)} %x0_ref.1), channel_id=1, source_target_pairs={{0,1},{1,0},{2,3},{3,2},{4,5},{5,4},{6,7},{7,6},{8,9},{9,8},{10,11... | collective-permute-start | bytes 1572872 | tf_op jit(solution)/shard_map/ppermute | solution.py:373
  3.3 6.5 %collective-permute-start = (bf16[16,768]{1,0:T(8,128)(2,1)}, bf16[16,768]{1,0:T(8,128)(2,1)S(1)}, u32[]{:S(2)}, u32[]{:S(2)}) collective-permute-start(bf16[16,768]{1,0:T(8,128)(2,1)} %get-tuple-element.103), channel_id=1, source_target_pairs={{0,8},{1,9},{2,10},{3,11},{4,12},{5,13},{6,14},{7,15},{8,0},{9,1},... | collective-permute-start | bytes 73736 | tf_op jit(solution)/shard_map/ppermute | solution.py:373
  5.9 5.1 %collective-permute-start.1 = (bf16[16,768]{1,0:T(8,128)(2,1)}, bf16[16,768]{1,0:T(8,128)(2,1)S(1)}, u32[]{:S(2)}, u32[]{:S(2)}) collective-permute-start(bf16[16,768]{1,0:T(8,128)(2,1)} %get-tuple-element.103), channel_id=1, source_target_pairs={{0,16},{1,17},{2,18},{3,19},{4,20},{5,21},{6,22},{7,23},{8,24},{9,... | collective-permute-start | bytes 73736 | tf_op jit(solution)/shard_map/ppermute | solution.py:373
  8.5 5.8 %collective-permute-start.2 = (bf16[16,768]{1,0:T(8,128)(2,1)}, bf16[16,768]{1,0:T(8,128)(2,1)S(1)}, u32[]{:S(2)}, u32[]{:S(2)}) collective-permute-start(bf16[16,768]{1,0:T(8,128)(2,1)} %get-tuple-element.103), channel_id=1, source_target_pairs={{0,24},{1,25},{2,26},{3,27},{4,28},{5,29},{6,30},{7,31},{8,16},{9,... | collective-permute-start | bytes 73736 | tf_op jit(solution)/shard_map/ppermute | solution.py:373
  15.1 5.5 %collective-permute-start.5 = (bf16[4,16,768]{2,1,0:T(8,128)(2,1)S(1)}, bf16[4,16,768]{2,1,0:T(8,128)(2,1)S(1)}, u32[]{:S(2)}, u32[]{:S(2)}) collective-permute-start(bf16[4,16,768]{2,1,0:T(8,128)(2,1)S(1)} %pad_maximum_fusion.2), channel_id=1, source_target_pairs={{0,2},{1,3},{2,0},{3,1},{4,6},{5,7},{6,4},{7,5},{8,10},{9,11},{10,... | collective-permute-start | bytes 294920 | tf_op jit(solution)/shard_map/ppermute | solution.py:373
  16.6 5.5 %collective-permute-start.6 = (bf16[4,16,768]{2,1,0:T(8,128)(2,1)S(1)}, bf16[4,16,768]{2,1,0:T(8,128)(2,1)S(1)}, u32[]{:S(2)}, u32[]{:S(2)}) collective-permute-start(bf16[4,16,768]{2,1,0:T(8,128)(2,1)S(1)} %pad_maximum_fusion.2), channel_id=1, source_target_pairs={{0,4},{1,5},{2,6},{3,7},{4,0},{5,1},{6,2},{7,3},{8,12},{9,13},{10,... | collective-permute-start | bytes 294920 | tf_op jit(solution)/shard_map/ppermute | solution.py:373
  18.2 5.5 %collective-permute-start.7 = (bf16[4,16,768]{2,1,0:T(8,128)(2,1)S(1)}, bf16[4,16,768]{2,1,0:T(8,128)(2,1)S(1)}, u32[]{:S(2)}, u32[]{:S(2)}) collective-permute-start(bf16[4,16,768]{2,1,0:T(8,128)(2,1)S(1)} %pad_maximum_fusion.2), channel_id=1, source_target_pairs={{0,6},{1,7},{2,4},{3,5},{4,2},{5,3},{6,0},{7,1},{8,14},{9,15},{10,... | collective-permute-start | bytes 294920 | tf_op jit(solution)/shard_map/ppermute | solution.py:373
  23.8 1.8 %collective-permute-start.8 = (bf16[4,4,16,768]{3,2,0,1:T(8,128)(2,1)S(1)}, bf16[4,4,16,768]{3,2,0,1:T(8,128)(2,1)S(1)}, u32[]{:S(2)}, u32[]{:S(2)}) collective-permute-start(bf16[4,4,16,768]{3,2,0,1:T(8,128)(2,1)S(1)} %pad_maximum_fusion.1), channel_id=1, source_target_pairs={{0,1},{1,0},{2,3},{3,2},{4,5},{5,4},{6,7},{7,6},{8,9},{9,8},{10,11... | collective-permute-start | bytes 1179656 | tf_op jit(solution)/shard_map/ppermute | solution.py:373
  62.5 3.5 %collective-permute-start.9 = (bf16[4,68,640]{2,1,0:T(8,128)(2,1)S(1)}, bf16[4,68,640]{2,1,0:T(8,128)(2,1)S(1)}, u32[]{:S(2)}, u32[]{:S(2)}) collective-permute-start(bf16[4,68,640]{2,1,0:T(8,128)(2,1)S(1)} %fusion.2), channel_id=1, source_target_pairs={{0,1},{1,0},{2,3},{3,2},{4,5},{5,4},{6,7},{7,6},{8,9},{9,8},{10,11... | collective-permute-start | bytes 1044488 | tf_op jit(solution)/shard_map/ppermute | solution.py:373
  62.7 3.3 %collective-permute-start.10 = (f32[1,512]{1,0:T(1,128)S(1)}, f32[1,512]{1,0:T(1,128)S(1)}, u32[]{:S(2)}, u32[]{:S(2)}) collective-permute-start(f32[1,512]{1,0:T(1,128)S(1)} %slice.13), channel_id=1, source_target_pairs={{0,1},{1,0},{2,3},{3,2},{4,5},{5,4},{6,7},{7,6},{8,9},{9,8},{10,11... | collective-permute-start | bytes 6152 | tf_op jit(solution)/shard_map/ppermute | solution.py:373
  66.1 7.8 %collective-permute-start.11 = (bf16[68,640]{1,0:T(8,128)(2,1)S(1)}, bf16[68,640]{1,0:T(8,128)(2,1)S(1)}, u32[]{:S(2)}, u32[]{:S(2)}) collective-permute-start(bf16[68,640]{1,0:T(8,128)(2,1)S(1)} %get-tuple-element.122), channel_id=1, source_target_pairs={{0,2},{1,3},{2,0},{3,1},{4,6},{5,7},{6,4},{7,5},{8,10},{9,11},{10,... | collective-permute-start | bytes 261128 | tf_op jit(solution)/shard_map/ppermute | solution.py:373
  66.7 7.2 %collective-permute-start.12 = (bf16[68,640]{1,0:T(8,128)(2,1)S(1)}, bf16[68,640]{1,0:T(8,128)(2,1)S(1)}, u32[]{:S(2)}, u32[]{:S(2)}) collective-permute-start(bf16[68,640]{1,0:T(8,128)(2,1)S(1)} %get-tuple-element.123), channel_id=1, source_target_pairs={{0,4},{1,5},{2,6},{3,7},{4,0},{5,1},{6,2},{7,3},{8,12},{9,13},{10,... | collective-permute-start | bytes 261128 | tf_op jit(solution)/shard_map/ppermute | solution.py:373
  67.2 6.7 %collective-permute-start.13 = (bf16[68,640]{1,0:T(8,128)(2,1)S(1)}, bf16[68,640]{1,0:T(8,128)(2,1)S(1)}, u32[]{:S(2)}, u32[]{:S(2)}) collective-permute-start(bf16[68,640]{1,0:T(8,128)(2,1)S(1)} %get-tuple-element.124), channel_id=1, source_target_pairs={{0,6},{1,7},{2,4},{3,5},{4,2},{5,3},{6,0},{7,1},{8,14},{9,15},{10,... | collective-permute-start | bytes 261128 | tf_op jit(solution)/shard_map/ppermute | solution.py:373
  74.1 7.3 %collective-permute-start.14 = (bf16[20,640]{1,0:T(8,128)(2,1)S(1)}, bf16[20,640]{1,0:T(8,128)(2,1)S(1)}, u32[]{:S(2)}, u32[]{:S(2)}) collective-permute-start(bf16[20,640]{1,0:T(8,128)(2,1)S(1)} %get-tuple-element.133), channel_id=1, source_target_pairs={{0,8},{1,9},{2,10},{3,11},{4,12},{5,13},{6,14},{7,15},{8,0},{9,1},... | collective-permute-start | bytes 76808 | tf_op jit(solution)/shard_map/ppermute | solution.py:373
  74.2 7.3 %collective-permute-start.15 = (bf16[20,640]{1,0:T(8,128)(2,1)S(1)}, bf16[20,640]{1,0:T(8,128)(2,1)S(1)}, u32[]{:S(2)}, u32[]{:S(2)}) collective-permute-start(bf16[20,640]{1,0:T(8,128)(2,1)S(1)} %get-tuple-element.134), channel_id=1, source_target_pairs={{0,16},{1,17},{2,18},{3,19},{4,20},{5,21},{6,22},{7,23},{8,24},{9,... | collective-permute-start | bytes 76808 | tf_op jit(solution)/shard_map/ppermute | solution.py:373
  75.1 6.4 %collective-permute-start.16 = (bf16[20,640]{1,0:T(8,128)(2,1)S(1)}, bf16[20,640]{1,0:T(8,128)(2,1)S(1)}, u32[]{:S(2)}, u32[]{:S(2)}) collective-permute-start(bf16[20,640]{1,0:T(8,128)(2,1)S(1)} %get-tuple-element.135), channel_id=1, source_target_pairs={{0,24},{1,25},{2,26},{3,27},{4,28},{5,29},{6,30},{7,31},{8,16},{9,... | collective-permute-start | bytes 76808 | tf_op jit(solution)/shard_map/ppermute | solution.py:373
  81.5 18.3 %collective-permute-start.24 = (f32[512,512]{1,0:T(8,128)S(1)}, f32[512,512]{1,0:T(8,128)S(1)}, u32[]{:S(2)}, u32[]{:S(2)}) collective-permute-start(f32[512,512]{1,0:T(8,128)S(1)} %input_grads_other.5), channel_id=1, source_target_pairs={{0,1},{1,0},{2,3},{3,2},{4,5},{5,4},{6,7},{7,6},{8,9},{9,8},{10,11... | collective-permute-start | bytes 3145736 | tf_op jit(solution)/shard_map/ppermute | solution.py:373
  84.0 3.4 %collective-permute-start.17 = (f32[16,128]{1,0:T(8,128)}, f32[16,128]{1,0:T(8,128)S(1)}, u32[]{:S(2)}, u32[]{:S(2)}) collective-permute-start(f32[16,128]{1,0:T(8,128)} %get-tuple-element.144), channel_id=1, source_target_pairs={{0,1},{1,0},{2,3},{3,2},{4,5},{5,4},{6,7},{7,6},{8,9},{9,8},{10,11... | collective-permute-start | bytes 24584 | tf_op jit(solution)/shard_map/ppermute | solution.py:373
  87.4 7.8 %collective-permute-start.18 = (f32[16,128]{1,0:T(8,128)S(1)}, f32[16,128]{1,0:T(8,128)S(1)}, u32[]{:S(2)}, u32[]{:S(2)}) collective-permute-start(f32[16,128]{1,0:T(8,128)S(1)} %add.98), channel_id=1, source_target_pairs={{0,2},{1,3},{2,0},{3,1},{4,6},{5,7},{6,4},{7,5},{8,10},{9,11},{10,... | collective-permute-start | bytes 24584 | tf_op jit(solution)/shard_map/ppermute | solution.py:373
  88.3 7.0 %collective-permute-start.19 = (f32[16,128]{1,0:T(8,128)S(1)}, f32[16,128]{1,0:T(8,128)S(1)}, u32[]{:S(2)}, u32[]{:S(2)}) collective-permute-start(f32[16,128]{1,0:T(8,128)S(1)} %add.98), channel_id=1, source_target_pairs={{0,4},{1,5},{2,6},{3,7},{4,0},{5,1},{6,2},{7,3},{8,12},{9,13},{10,... | collective-permute-start | bytes 24584 | tf_op jit(solution)/shard_map/ppermute | solution.py:373
  89.2 6.1 %collective-permute-start.20 = (f32[16,128]{1,0:T(8,128)S(1)}, f32[16,128]{1,0:T(8,128)S(1)}, u32[]{:S(2)}, u32[]{:S(2)}) collective-permute-start(f32[16,128]{1,0:T(8,128)S(1)} %add.98), channel_id=1, source_target_pairs={{0,6},{1,7},{2,4},{3,5},{4,2},{5,3},{6,0},{7,1},{8,14},{9,15},{10,... | collective-permute-start | bytes 24584 | tf_op jit(solution)/shard_map/ppermute | solution.py:373
  95.3 8.3 %collective-permute-start.21 = (f32[16,128]{1,0:T(8,128)S(1)}, f32[16,128]{1,0:T(8,128)S(1)}, u32[]{:S(2)}, u32[]{:S(2)}) collective-permute-start(f32[16,128]{1,0:T(8,128)S(1)} %add_add_fusion.refs_0_), channel_id=1, source_target_pairs={{0,8},{1,9},{2,10},{3,11},{4,12},{5,13},{6,14},{7,15},{8,0},{9,1},... | collective-permute-start | bytes 24584 | tf_op jit(solution)/shard_map/ppermute | solution.py:373
  95.4 8.2 %collective-permute-start.22 = (f32[16,128]{1,0:T(8,128)S(1)}, f32[16,128]{1,0:T(8,128)S(1)}, u32[]{:S(2)}, u32[]{:S(2)}) collective-permute-start(f32[16,128]{1,0:T(8,128)S(1)} %add_add_fusion.refs_0_), channel_id=1, source_target_pairs={{0,16},{1,17},{2,18},{3,19},{4,20},{5,21},{6,22},{7,23},{8,24},{9,... | collective-permute-start | bytes 24584 | tf_op jit(solution)/shard_map/ppermute | solution.py:373
  98.7 5.4 %collective-permute-start.23 = (f32[16,128]{1,0:T(8,128)S(1)}, f32[16,128]{1,0:T(8,128)S(1)}, u32[]{:S(2)}, u32[]{:S(2)}) collective-permute-start(f32[16,128]{1,0:T(8,128)S(1)} %add_add_fusion.refs_0_), channel_id=1, source_target_pairs={{0,24},{1,25},{2,26},{3,27},{4,28},{5,29},{6,30},{7,31},{8,16},{9,... | collective-permute-start | bytes 24584 | tf_op jit(solution)/shard_map/ppermute | solution.py:373
  (13 other events, 43.2 us)

commit v5 on v4

--- a/solution.py
+++ b/solution.py
@@ -18,7 +18,7 @@
 AXES = ("dp", "member")
 VMEM = pl.BlockSpec(memory_space=pltpu.VMEM)
 SMEM = pl.BlockSpec(memory_space=pltpu.SMEM)
-LIMIT = 48 * 1024 * 1024
+LIMIT = 28 * 1024 * 1024
 
 
 def shape(dims, dtype=F32):
@@ -58,13 +58,13 @@
 
 
 def grad_kernel(
-    x0_ref, x1_ref, q0_ref, q1_ref, packed_ref,
+    x_ref, rows_q_ref, packed_ref,
     keep_ref, sent_ref, heads_grad_ref, pred_ref, rows_ref, turned_ref, back_ref,
-    cols_ref, heads_ref, weight_ref, x_ref, xq_ref, q_ref, z0_ref, z1_ref, gp0_ref, gp1_ref,
+    cols_ref, heads_ref, weight_ref, xq_ref, q_ref, z0_ref, z1_ref, gp0_ref, gp1_ref,
     post_ref, pred_acc, sums_ref, gr_ref, grads_ref, *, own,
 ):
-    half, D = x0_ref.shape
-    R = 2 * half
+    R, D = x_ref.shape
+    half = R // 2
     K = heads_grad_ref.shape[0]
     members = K // 2
     n = back_ref.shape[0]
@@ -85,21 +85,17 @@
             gr_ref[:K * per_head, :] = packed_ref[:K * per_head, D + LANES + c:D + 2 * LANES + c].astype(F32)
             for k in range(per_head):
                 heads_ref[:, k * L + c:k * L + c + LANES] = gr_ref[pl.ds(k, K, stride=per_head), :]
-        x_ref[:half, :] = x0_ref[...]
-        x_ref[half:, :] = x1_ref[...]
-        for side, (x_side, q_side) in enumerate(((x0_ref, q0_ref), (x1_ref, q1_ref))):
-            at = slice(side * half, (side + 1) * half)
-            q_row = q_side[...]
-            q_ref[at, :] = jnp.broadcast_to(q_row, (LANES, half)).T
-            half_q = 0.5 * q_row
-            q_hi = half_q.astype(BF16)
-            q_lo = (half_q - q_hi.astype(F32)).astype(BF16)
-            xq_ref[:D, at] = (x_side[...].T.astype(F32) * half_q).astype(BF16)
-            sub = lax.broadcasted_iota(jnp.int32, (16, half), 0)
-            extra = jnp.where(sub == 0, q_hi.astype(F32), jnp.where(sub == 1, q_lo.astype(F32), 0.0))
-            xq_ref[D:, at] = extra.astype(BF16)
         for ref in (pred_acc, gr_ref, sums_ref, grads_ref, gp1_ref, heads_grad_ref):
             ref[...] = jnp.zeros_like(ref)
+        q_row = rows_q_ref[...]
+        q_ref[...] = jnp.broadcast_to(q_row, (LANES, R)).T
+        half_q = 0.5 * q_row
+        q_hi = half_q.astype(BF16)
+        q_lo = (half_q - q_hi.astype(F32)).astype(BF16)
+        xq_ref[:D, :] = (x_ref[...].T.astype(F32) * half_q).astype(BF16)
+        sub = lax.broadcasted_iota(jnp.int32, (16, R), 0)
+        extra = jnp.where(sub == 0, q_hi.astype(F32), jnp.where(sub == 1, q_lo.astype(F32), 0.0))
+        xq_ref[D:, :] = extra.astype(BF16)
 
     def forward(i, z_ref):
         r = rows_ref[pl.ds(base + i, 1), :].astype(BF16)
@@ -182,9 +178,9 @@
             sent_ref[j * own:(j + 1) * own, :] = jnp.where(core == 0, high, low).astype(BF16)
 
 
-def grad_call(x0, x1, q0, q1, packed, K, own, n=2):
-    half, D = x0.shape
-    R = 2 * half
+def grad_call(x, q, packed, K, own, n=2):
+    R, D = x.shape
+    half = R // 2
     members = K // 2
     flops = 4 * members * R * D * D
     return pl.pallas_call(
@@ -194,11 +190,11 @@
             shape((D // 2, D + LANES)), shape((D // 2, D + LANES), BF16), shape((K, D)), shape((2, half)),
             shape((LANES, D)), shape((D, D), BF16), shape((members, R, D), BF16),
         ),
-        in_specs=[VMEM] * 5,
+        in_specs=[VMEM] * 3,
         out_specs=(VMEM, VMEM, VMEM, VMEM, VMEM, VMEM, pl.BlockSpec((n, R, D), lambda i: (i, 0, 0))),
         scratch_shapes=[
             pltpu.VMEM((D, LANES), F32), pltpu.VMEM((K, D), F32), pltpu.VMEM((D, D), F32),
-            pltpu.VMEM((R, D), BF16), pltpu.VMEM((D + 16, R), BF16), pltpu.VMEM((R, LANES), F32),
+            pltpu.VMEM((D + 16, R), BF16), pltpu.VMEM((R, LANES), F32),
             pltpu.VMEM((R, D), F32), pltpu.VMEM((R, D), F32), pltpu.VMEM((R, D), BF16), pltpu.VMEM((R, D), BF16),
             pltpu.VMEM((D + 16, D), F32), pltpu.VMEM((R, LANES), F32), pltpu.VMEM((LANES, D), F32),
             pltpu.VMEM((D, LANES), F32), pltpu.VMEM((D, D + LANES), F32),
@@ -206,7 +202,7 @@
         compiler_params=pltpu.CompilerParams(vmem_limit_bytes=LIMIT),
         cost_estimate=pl.CostEstimate(flops=2 * flops, bytes_accessed=members * R * D * 2, transcendentals=members * R * D),
         name="member_grads",
-    )(x0, x1, q0, q1, packed)
+    )(x, q, packed)
 
 
 def back_kernel(*refs, members, start, first, last):
@@ -214,8 +210,12 @@
     rest = list(refs[3:])
     acc_in = None if first else rest.pop(0)
     q_ref = rest.pop(0) if last else None
-    came_ref = rest.pop(0) if last == "own" else None
-    out_ref, acc_ref = rest
+    if last == "own":
+        came_ref, pred_ref, pred_came_ref, count_ref = [rest.pop(0) for _ in range(4)]
+        out_ref, pred_out_ref, acc_ref = rest
+    else:
+        came_ref = None
+        out_ref, acc_ref = rest
     n, R, D = gp_ref.shape
     step = pl.program_id(0)
     K = 2 * members
@@ -243,19 +243,26 @@
             for l in range(0, D, LANES):
                 value = acc_ref[:, l:l + LANES] * q_wide
                 out_ref[:, l:l + LANES] = value if came_ref is None else value + came_ref[:, l:l + LANES]
+        if last == "own":
+            lane = lax.broadcasted_iota(jnp.int32, (1, R), 1)
+            total = pred_ref[0:1, :] + pred_came_ref[...]
+            pred_out_ref[...] = jnp.where(lane < count_ref[0], total, 0.0) * (1.0 / K)
 
 
 def back_call(rows, turned, back, where, start, count, acc=None, q=None, came=None, n=4):
     members, R2, D = back.shape
     R = R2 // 2
     last = None if q is None else "other" if came is None else "own"
-    more = [v for v in (acc, q, came) if v is not None]
+    more = [v for v in (acc, q, *(came or ())) if v is not None]
+    specs = [VMEM] * len(more)
+    if last == "own":
+        specs[-1] = SMEM
     return pl.pallas_call(
         functools.partial(back_kernel, members=members, start=start, first=acc is None, last=last),
         grid=(count // n,),
-        out_shape=shape((R, D)),
-        in_specs=[VMEM, VMEM, pl.BlockSpec((n, R, D), lambda i: (start // n + i, where, 0))] + [VMEM] * len(more),
-        out_specs=VMEM,
+        out_shape=(shape((R, D)), shape((1, R))) if last == "own" else shape((R, D)),
+        in_specs=[VMEM, VMEM, pl.BlockSpec((n, R, D), lambda i: (start // n + i, where, 0))] + specs,
+        out_specs=(VMEM, VMEM) if last == "own" else VMEM,
         scratch_shapes=[pltpu.VMEM((R, D), F32)],
         compiler_params=pltpu.CompilerParams(vmem_limit_bytes=LIMIT),
         cost_estimate=pl.CostEstimate(flops=2 * count * R * D * D, bytes_accessed=count * R * D * 2, transcendentals=0),
@@ -373,16 +380,19 @@
     return lax.ppermute(value, AXES, [(i, i ^ mask) for i in range(total)])
 
 
-def gather_groups(value, groups, total, index, *also):
-    brought = ()
+def gather_groups(value, groups, total, index, objects, q):
+    rows = (objects, q)
     for axis, (low, size) in enumerate(groups):
         place = (index // low) % size
         held = [value] + [swap(value, total, low * m) for m in range(1, size)]
         if axis == 0:
-            brought = tuple(swap(v, total, mask) for v, mask in also)
-            held, brought = lax.optimization_barrier((held, brought))
+            rows = rows + tuple(swap(v, total, 1) for v in rows)
+            held, rows = lax.optimization_barrier((held, rows))
+        elif axis == 1:
+            rows = (jnp.concatenate([rows[0], rows[2]], axis=0), jnp.concatenate([rows[1], rows[3]], axis=1))
+            held, rows = lax.optimization_barrier((held, rows))
         value = jnp.stack([lax.select_n(place ^ p, *held) for p in range(size)], axis=axis)
-    return value, brought
+    return (value,) + rows
 
 
 def beside(sends, work, *inputs):
@@ -404,10 +414,10 @@
     turned = [v.transpose(0, 2, 1) for v in (adapters, adapter_first, adapter_second)]
 
     packed, q_own = pack_call(counts, matrix, turned[0], head_weights, cotangent.reshape(1, R))
-    full, (x_other, q_other) = gather_groups(
-        packed, dp_groups + member_groups, total, index, (objects, 1), (q_own, 1))
+    full, x_both, q_both = gather_groups(packed, dp_groups + member_groups, total, index, objects, q_own)
     full = full.reshape(D, -1)
-    keep, sent, head_grads, preds, rows, wide_turned, back = grad_call(objects, x_other, q_own, q_other, full, K, own)
+    q_other = q_both[:, R:]
+    keep, sent, head_grads, preds, rows, wide_turned, back = grad_call(x_both, q_both, full, K, own)
 
     chips = [size for _, size in chip_groups]
     head_grads = head_grads.reshape(chips + [2, own_heads, D])
@@ -423,7 +433,7 @@
 
     def backward(where, part, parts=1, **more):
         def work(rows, wide_turned, back, *acc):
-            return back_call(rows, wide_turned, back, where, part * quarter, parts * quarter, *acc, n=quarter, **more)
+            return back_call(rows, wide_turned, back, where, part * quarter, parts * quarter, *acc, n=1, **more)
         return work
 
     weights = (rows, wide_turned, back)
@@ -471,7 +481,7 @@
         wide, last, dp_groups[0][0] // n_member, states)
 
     rounds = [(1, 2)] + chip_groups[::-1] + dp_groups[::-1]
-    plan = {0: backward(0, 0), 1: backward(0, 1, 2), len(rounds) - 1: backward(0, 3, q=q_own, came=ig_came)}
+    plan = {0: backward(0, 0), 1: backward(0, 1, 2), len(rounds) - 1: backward(0, 3, q=q_own, came=(ig_came, preds, pred_came, counts))}
     pending, acc = [sums], ()
     for step, (low, size) in enumerate(rounds):
         sums = pending[0]
@@ -484,11 +494,9 @@
         else:
             came = [swap(*send) for send in sends]
         pending = [sums] + list(came)
-    input_grad = acc[0]
+    input_grad, predictions = acc[0]
     new_matrix, new_adapters, new_heads, norm_pairs = update_call(
         pending, matrix, turned[0], head_weights, m_update, a_update, h_update)
-    lane = lax.broadcasted_iota(jnp.int32, (1, R), 1)
-    predictions = jnp.where(lane < counts[0], preds[0:1] + pred_came, 0.0) * (1.0 / K)
 
     def back_turn(v):
         return v.transpose(0, 2, 1)

time: 107 us -> 120 us (1.12)
  local copies, waits for them, and re-layouts: 2.63 us -> 20.9 us
  Pallas kernels: 60.6 us -> 57.2 us
  waiting for transfers between devices: 13.1 us -> 11.5 us
    unnamed x24 -> x38, local copies, waits for them, and re-layouts: 2.35 us -> 20.6 us
    pallas_call x6, Pallas kernels: 20.9 us -> 19 us  [back_call(): pl.pallas_call(functools.partial(back_kernel, members=members, start=star...]
    ppermute x25, waiting for transfers between devices: 13.1 us -> 11.5 us  [swap(): return lax.ppermute(value, AXES, [(i, i ^ mask) for i in range(total)])]
    pallas_call x1, Pallas kernels: 34.8 us -> 33.3 us  [grad_call(): pl.pallas_call(functools.partial(grad_kernel, own=own), grid=(members //...]
  transfers between devices with their start and end apart: 25 -> 25, of which waited for: 8 -> 7; matrix products, arithmetic and copies ran while one was open for 1% -> 1% of each run, Pallas kernels for 23% -> 19%
where the time goes in v5:
time: 120 us
  Pallas kernels  57.2 us (48%)
  starting transfers between devices  26 us (22%)
  local copies, waits for them, and re-layouts  20.9 us (17%)
  waiting for transfers between devices  11.5 us (10%)
  other arithmetic  2.33 us (2%)
  between operations  1.79 us (1%)
    pallas_call x1, Pallas kernels, grad_call(): pl.pallas_call(functools.partial(grad_kernel, own=own), grid=(members //...  33.3 us
    ppermute x25, starting transfers between devices, swap(): return lax.ppermute(value, AXES, [(i, i ^ mask) for i in range(total)])  26 us
    unnamed x38, local copies, waits for them, and re-layouts  20.6 us
    pallas_call x6, Pallas kernels, back_call(): pl.pallas_call(functools.partial(back_kernel, members=members, start=star...  19 us
    ppermute x25, waiting for transfers between devices, swap(): return lax.ppermute(value, AXES, [(i, i ^ mask) for i in range(total)])  11.5 us
  transfers between devices with their start and end apart: 25, of which 7 were waited for; matrix products, arithmetic and copies ran while one was open for 1% of the time, Pallas kernels for 19%

profile of v5, /device:TPU:0, one launch (start us, length us, event | category | flops | bytes accessed | tf_op | source)
XLA Modules:
  0.0 119.7 jit_solution(9833311114270894583)
XLA Ops:
  1.8 1.5 %pack_weights.1 = (bf16[16,768]{1,0:T(8,128)(2,1)}, f32[1,512]{1,0:T(1,128)}) custom-call(s32[1]{0:T(128)S(6)} %copy.32.count_ref.refs_8_, f32[16,512]{1,0:T(8,128)} %refs_4_.3, f32[3,16,32]{2,1,0:T(8,128)} %bitcast.65, f32[4,512]{1,0:T(4,128)} %refs_6_.3, f32[1,512]{1,0:T(1,128)} %bitcast.70), custom_call_target="tpu_custom_call" | custom-call | tf_op jit(solution)/shard_map/pack_weights/pallas_call | solution.py:51
  3.3 2.6 %collective-permute-start = (bf16[16,768]{1,0:T(8,128)(2,1)}, bf16[16,768]{1,0:T(8,128)(2,1)S(1)}, u32[]{:S(2)}, u32[]{:S(2)}) collective-permute-start(bf16[16,768]{1,0:T(8,128)(2,1)} %get-tuple-element.112), channel_id=1, source_target_pairs={{0,8},{1,9},{2,10},{3,11},{4,12},{5,13},{6,14},{7,15},{8,0},{9,1},... | collective-permute-start | bytes 73736 | tf_op jit(solution)/shard_map/ppermute | solution.py:380
  5.9 2.6 %collective-permute-start.1 = (bf16[16,768]{1,0:T(8,128)(2,1)}, bf16[16,768]{1,0:T(8,128)(2,1)S(1)}, u32[]{:S(2)}, u32[]{:S(2)}) collective-permute-start(bf16[16,768]{1,0:T(8,128)(2,1)} %get-tuple-element.112), channel_id=1, source_target_pairs={{0,16},{1,17},{2,18},{3,19},{4,20},{5,21},{6,22},{7,23},{8,24},{9,... | collective-permute-start | bytes 73736 | tf_op jit(solution)/shard_map/ppermute | solution.py:380
  10.9 3.4 %collective-permute-done.2 = bf16[16,768]{1,0:T(8,128)(2,1)S(1)} collective-permute-done((bf16[16,768]{1,0:T(8,128)(2,1)}, bf16[16,768]{1,0:T(8,128)(2,1)S(1)}, u32[]{:S(2)}, u32[]{:S(2)}) %collective-permute-start.2) | collective-permute-done | bytes 24608 | tf_op jit(solution)/shard_map/ppermute | solution.py:380
  15.1 1.6 %collective-permute-start.5 = (bf16[4,16,768]{2,1,0:T(8,128)(2,1)S(1)}, bf16[4,16,768]{2,1,0:T(8,128)(2,1)S(1)}, u32[]{:S(2)}, u32[]{:S(2)}) collective-permute-start(bf16[4,16,768]{2,1,0:T(8,128)(2,1)S(1)} %pad_maximum_fusion.3), channel_id=1, source_target_pairs={{0,2},{1,3},{2,0},{3,1},{4,6},{5,7},{6,4},{7,5},{8,10},{9,11},{10,... | collective-permute-start | bytes 294920 | tf_op jit(solution)/shard_map/ppermute | solution.py:380
  16.6 1.5 %collective-permute-start.6 = (bf16[4,16,768]{2,1,0:T(8,128)(2,1)S(1)}, bf16[4,16,768]{2,1,0:T(8,128)(2,1)S(1)}, u32[]{:S(2)}, u32[]{:S(2)}) collective-permute-start(bf16[4,16,768]{2,1,0:T(8,128)(2,1)S(1)} %pad_maximum_fusion.3), channel_id=1, source_target_pairs={{0,4},{1,5},{2,6},{3,7},{4,0},{5,1},{6,2},{7,3},{8,12},{9,13},{10,... | collective-permute-start | bytes 294920 | tf_op jit(solution)/shard_map/ppermute | solution.py:380
  20.6 1.6 %collective-permute-done.6 = bf16[4,16,768]{2,1,0:T(8,128)(2,1)S(1)} collective-permute-done((bf16[4,16,768]{2,1,0:T(8,128)(2,1)S(1)}, bf16[4,16,768]{2,1,0:T(8,128)(2,1)S(1)}, u32[]{:S(2)}, u32[]{:S(2)}) %collective-permute-start.6) | collective-permute-done | bytes 98336 | tf_op jit(solution)/shard_map/ppermute | solution.py:380
  22.1 1.5 %collective-permute-done.7 = bf16[4,16,768]{2,1,0:T(8,128)(2,1)S(1)} collective-permute-done((bf16[4,16,768]{2,1,0:T(8,128)(2,1)S(1)}, bf16[4,16,768]{2,1,0:T(8,128)(2,1)S(1)}, u32[]{:S(2)}, u32[]{:S(2)}) %collective-permute-start.7) | collective-permute-done | bytes 98336 | tf_op jit(solution)/shard_map/ppermute | solution.py:380
  23.9 1.7 %collective-permute-done.8 = bf16[4,4,16,768]{3,2,0,1:T(8,128)(2,1)S(1)} collective-permute-done((bf16[4,4,16,768]{3,2,0,1:T(8,128)(2,1)S(1)}, bf16[4,4,16,768]{3,2,0,1:T(8,128)(2,1)S(1)}, u32[]{:S(2)}, u32[]{:S(2)}) %collective-permute-start.8) | collective-permute-done | bytes 393248 | tf_op jit(solution)/shard_map/ppermute | solution.py:380
  25.8 33.3 %member_grads.1 = (f32[256,640]{1,0:T(8,128)S(1)}, bf16[256,640]{1,0:T(8,128)(2,1)S(1)}, f32[32,512]{1,0:T(8,128)S(1)}, f32[2,512]{1,0:T(2,128)S(1)}, f32[128,51...) custom-call(bf16[1024,512]{1,0:T(8,128)(2,1)S(1)} %pad_maximum_fusion.x_ref, ...), custom_call_target="tpu_custom_call" | custom-call | flops 34359738368 | bytes 16777216 | tf_op jit(solution)/shard_map/member_grads/pallas_call | solution.py:186
  59.2 5.8 %copy-done = bf16[16,1024,512]{2,1,0:T(8,128)(2,1)} copy-done((bf16[16,1024,512]{2,1,0:T(8,128)(2,1)}, bf16[16,1024,512]{2,1,0:T(8,128)(2,1)S(1)}, u32[]{:S(2)}) %copy-start) | copy-done | bytes 16777240
  65.7 5.8 %copy-done.1 = bf16[16,1024,512]{2,1,0:T(8,128)(2,1)S(1)} copy-done((bf16[16,1024,512]{2,1,0:T(8,128)(2,1)S(1)}, bf16[16,1024,512]{2,1,0:T(8,128)(2,1)}, u32[]{:S(2)}) %copy-start.1) | copy-done | bytes 16777240
  71.4 2.0 %input_grads_other.3.refs_3_ = f32[512,512]{1,0:T(8,128)S(1)} custom-call(f32[128,512]{1,0:T(8,128)S(1)} %get-tuple-element.182.refs_0_, bf16[512,512]{1,0:T(8,128)(2,1)S(1)} %get-tuple-element.183.refs_1_, bf16[16,1024,512]{2,1,0:T(8,128)(2,1)S(1)} %copy-done.1), custom_call_target="tpu_custom_call" | custom-call | flops 1073741824 | bytes 2097152 | tf_op jit(solution)/shard_map/input_grads_other/pallas_call | solution.py:260
  74.8 2.4 %collective-permute-start.13 = (bf16[68,640]{1,0:T(8,128)(2,1)S(1)}, bf16[68,640]{1,0:T(8,128)(2,1)S(1)}, u32[]{:S(2)}, u32[]{:S(2)}) collective-permute-start(bf16[68,640]{1,0:T(8,128)(2,1)S(1)} %get-tuple-element.142), channel_id=1, source_target_pairs={{0,6},{1,7},{2,4},{3,5},{4,2},{5,3},{6,0},{7,1},{8,14},{9,15},{10,... | collective-permute-start | bytes 261128 | tf_op jit(solution)/shard_map/ppermute | solution.py:380
  77.2 3.8 %input_grads_other.4.refs_3_ = f32[512,512]{1,0:T(8,128)S(1)} custom-call(f32[128,512]{1,0:T(8,128)S(1)} %get-tuple-element.182.refs_0_, bf16[512,512]{1,0:T(8,128)(2,1)S(1)} %get-tuple-element.183.refs_1_, bf16[16,1024,512]{2,1,0:T(8,128)(2,1)S(1)} %copy-done.1, f32[512,512]{1,0:T(8,128)S(1)} %input_grads_other.3.refs_3_), custom_call_target="tpu_custom_call" | custom-call | flops 2147483648 | bytes 4194304 | tf_op jit(solution)/shard_map/input_grads_other/pallas_call | solution.py:260
  82.1 3.5 %collective-permute-start.16 = (bf16[20,640]{1,0:T(8,128)(2,1)S(1)}, bf16[20,640]{1,0:T(8,128)(2,1)S(1)}, u32[]{:S(2)}, u32[]{:S(2)}) collective-permute-start(bf16[20,640]{1,0:T(8,128)(2,1)S(1)} %get-tuple-element.153), channel_id=1, source_target_pairs={{0,24},{1,25},{2,26},{3,27},{4,28},{5,29},{6,30},{7,31},{8,16},{9,... | collective-permute-start | bytes 76808 | tf_op jit(solution)/shard_map/ppermute | solution.py:380
  85.7 3.1 %input_grads_other.5 = f32[512,512]{1,0:T(8,128)} custom-call(f32[128,512]{1,0:T(8,128)S(1)} %get-tuple-element.182.refs_0_, bf16[512,512]{1,0:T(8,128)(2,1)S(1)} %get-tuple-element.183.refs_1_, bf16[16,1024,512]{2,1,0:T(8,128)(2,1)S(1)} %copy-done.1, f32[512,512]{1,0:T(8,128)S(1)} %input_grads_other.4.refs_3_, f32[1,512]{1,0:T(1,128)S(1)} %slice.15.refs_4_), custom_call_target="tpu_custom_call" | custom-call | flops 1073741824 | bytes 2097152 | tf_op jit(solution)/shard_map/input_grads_other/pallas_call | solution.py:260
  89.4 1.8 %directions.1 = (f32[16,512]{1,0:T(8,128)}, f32[16,512]{1,0:T(8,128)}, f32[16,512]{1,0:T(8,128)}, f32[3,16,32]{2,1,0:T(8,128)}, f32[3,16,32]{2,1,0:T(8,128)}, /*...) custom-call(f32[68,640]{1,0:T(8,128)} %copy-done.6, ...), custom_call_target="tpu_custom_call" | custom-call | tf_op jit(solution)/shard_map/directions/pallas_call | solution.py:330
  91.2 5.8 %copy-done.2 = bf16[16,1024,512]{2,1,0:T(8,128)(2,1)S(1)} copy-done((bf16[16,1024,512]{2,1,0:T(8,128)(2,1)S(1)}, bf16[16,1024,512]{2,1,0:T(8,128)(2,1)}, u32[]{:S(2)}) %copy-start.2) | copy-done | bytes 16777240
  97.0 2.0 %input_grads_own.3.refs_3_ = f32[512,512]{1,0:T(8,128)S(1)} custom-call(f32[128,512]{1,0:T(8,128)S(1)} %get-tuple-element.182.refs_0_, bf16[512,512]{1,0:T(8,128)(2,1)S(1)} %get-tuple-element.183.refs_1_, bf16[16,1024,512]{2,1,0:T(8,128)(2,1)S(1)} %copy-done.2), custom_call_target="tpu_custom_call" | custom-call | flops 1073741824 | bytes 2097152 | tf_op jit(solution)/shard_map/input_grads_own/pallas_call | solution.py:260
  102.6 3.8 %input_grads_own.4.refs_3_ = f32[512,512]{1,0:T(8,128)S(1)} custom-call(f32[128,512]{1,0:T(8,128)S(1)} %get-tuple-element.182.refs_0_, bf16[512,512]{1,0:T(8,128)(2,1)S(1)} %get-tuple-element.183.refs_1_, bf16[16,1024,512]{2,1,0:T(8,128)(2,1)S(1)} %copy-done.2, f32[512,512]{1,0:T(8,128)S(1)} %input_grads_own.3.refs_3_), custom_call_target="tpu_custom_call" | custom-call | flops 2147483648 | bytes 4194304 | tf_op jit(solution)/shard_map/input_grads_own/pallas_call | solution.py:260
  107.5 3.1 %collective-permute-start.22 = (f32[16,128]{1,0:T(8,128)S(1)}, f32[16,128]{1,0:T(8,128)S(1)}, u32[]{:S(2)}, u32[]{:S(2)}) collective-permute-start(f32[16,128]{1,0:T(8,128)S(1)} %add_add_fusion.refs_0_), channel_id=1, source_target_pairs={{0,16},{1,17},{2,18},{3,19},{4,20},{5,21},{6,22},{7,23},{8,24},{9,... | collective-permute-start | bytes 24584 | tf_op jit(solution)/shard_map/ppermute | solution.py:380
  113.2 4.3 %input_grads_own.5 = (f32[512,512]{1,0:T(8,128)}, f32[1,512]{1,0:T(1,128)}) custom-call(f32[128,512]{1,0:T(8,128)S(1)} %get-tuple-element.182.refs_0_, bf16[512,512]{1,0:T(8,128)(2,1)S(1)} %get-tuple-element.183.refs_1_, bf16[16,1024,512]{2,1,0:T(8,128)(2,1)S(1)} %bitcast.59, f32[512,512]{1,0:T(8,128)S(1)} %copy-done.4, f32[1,512]{1,0:T(1,128)S(1)} %copy-done.5, ...), custom_call_target="tpu_custom_call" | custom-call | flops 1073741824 | bytes 2097152 | tf_op jit(solution)/shard_map/input_grads_own/pallas_call | solution.py:260
  118.1 1.6 %updates.1 = (f32[16,512]{1,0:T(8,128)}, f32[3,16,32]{2,1,0:T(8,128)}, f32[4,512]{1,0:T(4,128)}, f32[2,5]{1,0:T(2,128)}) custom-call(f32[16,128]{1,0:T(8,128)} %copy-done.7, f32[16,128]{1,0:T(8,128)} %copy-done.11, f32[16,128]{1,0:T(8,128)} %copy-done.12, f32[16,128]{1,0:T(8,128)} %copy-done.13, f32[16,512]{1,0:T(8,128)} %refs_4_.3, f32[3,16,32]{2,1,0:T(8,128)} %bitcast.67, ...), custom_call_target="tpu_custom_call" | custom-call | tf_op jit(solution)/shard_map/updates/pallas_call | solution.py:357
  (101 shorter events, 18.0 us)
Async XLA Ops:
  0.6 13.6 %collective-permute-start.3 = (bf16[512,512]{1,0:T(8,128)(2,1)}, bf16[512,512]{1,0:T(8,128)(2,1)S(1)}, u32[]{:S(2)}, u32[]{:S(2)}) collective-permute-start(bf16[512,512]{1,0:T(8,128)(2,1)} %param.12), channel_id=1, source_target_pairs={{0,1},{1,0},{2,3},{3,2},{4,5},{5,4},{6,7},{7,6},{8,9},{9,8},{10,11... | collective-permute-start | bytes 1572872 | tf_op jit(solution)/shard_map/ppermute | solution.py:380
  3.3 6.5 %collective-permute-start = (bf16[16,768]{1,0:T(8,128)(2,1)}, bf16[16,768]{1,0:T(8,128)(2,1)S(1)}, u32[]{:S(2)}, u32[]{:S(2)}) collective-permute-start(bf16[16,768]{1,0:T(8,128)(2,1)} %get-tuple-element.112), channel_id=1, source_target_pairs={{0,8},{1,9},{2,10},{3,11},{4,12},{5,13},{6,14},{7,15},{8,0},{9,1},... | collective-permute-start | bytes 73736 | tf_op jit(solution)/shard_map/ppermute | solution.py:380
  5.9 5.1 %collective-permute-start.1 = (bf16[16,768]{1,0:T(8,128)(2,1)}, bf16[16,768]{1,0:T(8,128)(2,1)S(1)}, u32[]{:S(2)}, u32[]{:S(2)}) collective-permute-start(bf16[16,768]{1,0:T(8,128)(2,1)} %get-tuple-element.112), channel_id=1, source_target_pairs={{0,16},{1,17},{2,18},{3,19},{4,20},{5,21},{6,22},{7,23},{8,24},{9,... | collective-permute-start | bytes 73736 | tf_op jit(solution)/shard_map/ppermute | solution.py:380
  8.5 5.8 %collective-permute-start.2 = (bf16[16,768]{1,0:T(8,128)(2,1)}, bf16[16,768]{1,0:T(8,128)(2,1)S(1)}, u32[]{:S(2)}, u32[]{:S(2)}) collective-permute-start(bf16[16,768]{1,0:T(8,128)(2,1)} %get-tuple-element.112), channel_id=1, source_target_pairs={{0,24},{1,25},{2,26},{3,27},{4,28},{5,29},{6,30},{7,31},{8,16},{9,... | collective-permute-start | bytes 73736 | tf_op jit(solution)/shard_map/ppermute | solution.py:380
  15.1 5.5 %collective-permute-start.5 = (bf16[4,16,768]{2,1,0:T(8,128)(2,1)S(1)}, bf16[4,16,768]{2,1,0:T(8,128)(2,1)S(1)}, u32[]{:S(2)}, u32[]{:S(2)}) collective-permute-start(bf16[4,16,768]{2,1,0:T(8,128)(2,1)S(1)} %pad_maximum_fusion.3), channel_id=1, source_target_pairs={{0,2},{1,3},{2,0},{3,1},{4,6},{5,7},{6,4},{7,5},{8,10},{9,11},{10,... | collective-permute-start | bytes 294920 | tf_op jit(solution)/shard_map/ppermute | solution.py:380
  16.6 5.5 %collective-permute-start.6 = (bf16[4,16,768]{2,1,0:T(8,128)(2,1)S(1)}, bf16[4,16,768]{2,1,0:T(8,128)(2,1)S(1)}, u32[]{:S(2)}, u32[]{:S(2)}) collective-permute-start(bf16[4,16,768]{2,1,0:T(8,128)(2,1)S(1)} %pad_maximum_fusion.3), channel_id=1, source_target_pairs={{0,4},{1,5},{2,6},{3,7},{4,0},{5,1},{6,2},{7,3},{8,12},{9,13},{10,... | collective-permute-start | bytes 294920 | tf_op jit(solution)/shard_map/ppermute | solution.py:380
  18.2 5.5 %collective-permute-start.7 = (bf16[4,16,768]{2,1,0:T(8,128)(2,1)S(1)}, bf16[4,16,768]{2,1,0:T(8,128)(2,1)S(1)}, u32[]{:S(2)}, u32[]{:S(2)}) collective-permute-start(bf16[4,16,768]{2,1,0:T(8,128)(2,1)S(1)} %pad_maximum_fusion.3), channel_id=1, source_target_pairs={{0,6},{1,7},{2,4},{3,5},{4,2},{5,3},{6,0},{7,1},{8,14},{9,15},{10,... | collective-permute-start | bytes 294920 | tf_op jit(solution)/shard_map/ppermute | solution.py:380
  23.8 1.8 %collective-permute-start.8 = (bf16[4,4,16,768]{3,2,0,1:T(8,128)(2,1)S(1)}, bf16[4,4,16,768]{3,2,0,1:T(8,128)(2,1)S(1)}, u32[]{:S(2)}, u32[]{:S(2)}) collective-permute-start(bf16[4,4,16,768]{3,2,0,1:T(8,128)(2,1)S(1)} %pad_maximum_fusion.2), channel_id=1, source_target_pairs={{0,1},{1,0},{2,3},{3,2},{4,5},{5,4},{6,7},{7,6},{8,9},{9,8},{10,11... | collective-permute-start | bytes 1179656 | tf_op jit(solution)/shard_map/ppermute | solution.py:380
  65.1 8.4 %collective-permute-start.9 = (bf16[4,68,640]{2,1,0:T(8,128)(2,1)S(1)}, bf16[4,68,640]{2,1,0:T(8,128)(2,1)S(1)}, u32[]{:S(2)}, u32[]{:S(2)}) collective-permute-start(bf16[4,68,640]{2,1,0:T(8,128)(2,1)S(1)} %fusion.2), channel_id=1, source_target_pairs={{0,1},{1,0},{2,3},{3,2},{4,5},{5,4},{6,7},{7,6},{8,9},{9,8},{10,11... | collective-permute-start | bytes 1044488 | tf_op jit(solution)/shard_map/ppermute | solution.py:380
  65.3 8.2 %collective-permute-start.10 = (f32[1,512]{1,0:T(1,128)S(1)}, f32[1,512]{1,0:T(1,128)S(1)}, u32[]{:S(2)}, u32[]{:S(2)}) collective-permute-start(f32[1,512]{1,0:T(1,128)S(1)} %slice.12), channel_id=1, source_target_pairs={{0,1},{1,0},{2,3},{3,2},{4,5},{5,4},{6,7},{7,6},{8,9},{9,8},{10,11... | collective-permute-start | bytes 6152 | tf_op jit(solution)/shard_map/ppermute | solution.py:380
  73.6 7.4 %collective-permute-start.11 = (bf16[68,640]{1,0:T(8,128)(2,1)S(1)}, bf16[68,640]{1,0:T(8,128)(2,1)S(1)}, u32[]{:S(2)}, u32[]{:S(2)}) collective-permute-start(bf16[68,640]{1,0:T(8,128)(2,1)S(1)} %get-tuple-element.140), channel_id=1, source_target_pairs={{0,2},{1,3},{2,0},{3,1},{4,6},{5,7},{6,4},{7,5},{8,10},{9,11},{10,... | collective-permute-start | bytes 261128 | tf_op jit(solution)/shard_map/ppermute | solution.py:380
  74.2 6.8 %collective-permute-start.12 = (bf16[68,640]{1,0:T(8,128)(2,1)S(1)}, bf16[68,640]{1,0:T(8,128)(2,1)S(1)}, u32[]{:S(2)}, u32[]{:S(2)}) collective-permute-start(bf16[68,640]{1,0:T(8,128)(2,1)S(1)} %get-tuple-element.141), channel_id=1, source_target_pairs={{0,4},{1,5},{2,6},{3,7},{4,0},{5,1},{6,2},{7,3},{8,12},{9,13},{10,... | collective-permute-start | bytes 261128 | tf_op jit(solution)/shard_map/ppermute | solution.py:380
  74.8 6.3 %collective-permute-start.13 = (bf16[68,640]{1,0:T(8,128)(2,1)S(1)}, bf16[68,640]{1,0:T(8,128)(2,1)S(1)}, u32[]{:S(2)}, u32[]{:S(2)}) collective-permute-start(bf16[68,640]{1,0:T(8,128)(2,1)S(1)} %get-tuple-element.142), channel_id=1, source_target_pairs={{0,6},{1,7},{2,4},{3,5},{4,2},{5,3},{6,0},{7,1},{8,14},{9,15},{10,... | collective-permute-start | bytes 261128 | tf_op jit(solution)/shard_map/ppermute | solution.py:380
  81.2 7.5 %collective-permute-start.14 = (bf16[20,640]{1,0:T(8,128)(2,1)S(1)}, bf16[20,640]{1,0:T(8,128)(2,1)S(1)}, u32[]{:S(2)}, u32[]{:S(2)}) collective-permute-start(bf16[20,640]{1,0:T(8,128)(2,1)S(1)} %get-tuple-element.151), channel_id=1, source_target_pairs={{0,8},{1,9},{2,10},{3,11},{4,12},{5,13},{6,14},{7,15},{8,0},{9,1},... | collective-permute-start | bytes 76808 | tf_op jit(solution)/shard_map/ppermute | solution.py:380
  81.3 7.5 %collective-permute-start.15 = (bf16[20,640]{1,0:T(8,128)(2,1)S(1)}, bf16[20,640]{1,0:T(8,128)(2,1)S(1)}, u32[]{:S(2)}, u32[]{:S(2)}) collective-permute-start(bf16[20,640]{1,0:T(8,128)(2,1)S(1)} %get-tuple-element.152), channel_id=1, source_target_pairs={{0,16},{1,17},{2,18},{3,19},{4,20},{5,21},{6,22},{7,23},{8,24},{9,... | collective-permute-start | bytes 76808 | tf_op jit(solution)/shard_map/ppermute | solution.py:380
  82.1 6.6 %collective-permute-start.16 = (bf16[20,640]{1,0:T(8,128)(2,1)S(1)}, bf16[20,640]{1,0:T(8,128)(2,1)S(1)}, u32[]{:S(2)}, u32[]{:S(2)}) collective-permute-start(bf16[20,640]{1,0:T(8,128)(2,1)S(1)} %get-tuple-element.153), channel_id=1, source_target_pairs={{0,24},{1,25},{2,26},{3,27},{4,28},{5,29},{6,30},{7,31},{8,16},{9,... | collective-permute-start | bytes 76808 | tf_op jit(solution)/shard_map/ppermute | solution.py:380
  88.8 23.1 %collective-permute-start.24 = (f32[512,512]{1,0:T(8,128)}, f32[512,512]{1,0:T(8,128)}, u32[]{:S(2)}, u32[]{:S(2)}) collective-permute-start(f32[512,512]{1,0:T(8,128)} %input_grads_other.5), channel_id=1, source_target_pairs={{0,1},{1,0},{2,3},{3,2},{4,5},{5,4},{6,7},{7,6},{8,9},{9,8},{10,11... | collective-permute-start | bytes 3145736 | tf_op jit(solution)/shard_map/ppermute | solution.py:380
  91.2 7.8 %collective-permute-start.17 = (f32[16,128]{1,0:T(8,128)}, f32[16,128]{1,0:T(8,128)S(1)}, u32[]{:S(2)}, u32[]{:S(2)}) collective-permute-start(f32[16,128]{1,0:T(8,128)} %get-tuple-element.162), channel_id=1, source_target_pairs={{0,1},{1,0},{2,3},{3,2},{4,5},{5,4},{6,7},{7,6},{8,9},{9,8},{10,11... | collective-permute-start | bytes 24584 | tf_op jit(solution)/shard_map/ppermute | solution.py:380
  99.1 8.4 %collective-permute-start.18 = (f32[16,128]{1,0:T(8,128)S(1)}, f32[16,128]{1,0:T(8,128)S(1)}, u32[]{:S(2)}, u32[]{:S(2)}) collective-permute-start(f32[16,128]{1,0:T(8,128)S(1)} %add.94), channel_id=1, source_target_pairs={{0,2},{1,3},{2,0},{3,1},{4,6},{5,7},{6,4},{7,5},{8,10},{9,11},{10,... | collective-permute-start | bytes 24584 | tf_op jit(solution)/shard_map/ppermute | solution.py:380
  100.3 7.1 %collective-permute-start.19 = (f32[16,128]{1,0:T(8,128)S(1)}, f32[16,128]{1,0:T(8,128)S(1)}, u32[]{:S(2)}, u32[]{:S(2)}) collective-permute-start(f32[16,128]{1,0:T(8,128)S(1)} %add.94), channel_id=1, source_target_pairs={{0,4},{1,5},{2,6},{3,7},{4,0},{5,1},{6,2},{7,3},{8,12},{9,13},{10,... | collective-permute-start | bytes 24584 | tf_op jit(solution)/shard_map/ppermute | solution.py:380
  101.3 6.2 %collective-permute-start.20 = (f32[16,128]{1,0:T(8,128)S(1)}, f32[16,128]{1,0:T(8,128)S(1)}, u32[]{:S(2)}, u32[]{:S(2)}) collective-permute-start(f32[16,128]{1,0:T(8,128)S(1)} %add.94), channel_id=1, source_target_pairs={{0,6},{1,7},{2,4},{3,5},{4,2},{5,3},{6,0},{7,1},{8,14},{9,15},{10,... | collective-permute-start | bytes 24584 | tf_op jit(solution)/shard_map/ppermute | solution.py:380
  107.5 10.0 %collective-permute-start.21 = (f32[16,128]{1,0:T(8,128)S(1)}, f32[16,128]{1,0:T(8,128)S(1)}, u32[]{:S(2)}, u32[]{:S(2)}) collective-permute-start(f32[16,128]{1,0:T(8,128)S(1)} %add_add_fusion.refs_0_), channel_id=1, source_target_pairs={{0,8},{1,9},{2,10},{3,11},{4,12},{5,13},{6,14},{7,15},{8,0},{9,1},... | collective-permute-start | bytes 24584 | tf_op jit(solution)/shard_map/ppermute | solution.py:380
  107.5 9.9 %collective-permute-start.22 = (f32[16,128]{1,0:T(8,128)S(1)}, f32[16,128]{1,0:T(8,128)S(1)}, u32[]{:S(2)}, u32[]{:S(2)}) collective-permute-start(f32[16,128]{1,0:T(8,128)S(1)} %add_add_fusion.refs_0_), channel_id=1, source_target_pairs={{0,16},{1,17},{2,18},{3,19},{4,20},{5,21},{6,22},{7,23},{8,24},{9,... | collective-permute-start | bytes 24584 | tf_op jit(solution)/shard_map/ppermute | solution.py:380
  110.7 6.8 %collective-permute-start.23 = (f32[16,128]{1,0:T(8,128)S(1)}, f32[16,128]{1,0:T(8,128)S(1)}, u32[]{:S(2)}, u32[]{:S(2)}) collective-permute-start(f32[16,128]{1,0:T(8,128)S(1)} %add_add_fusion.refs_0_), channel_id=1, source_target_pairs={{0,24},{1,25},{2,26},{3,27},{4,28},{5,29},{6,30},{7,31},{8,16},{9,... | collective-permute-start | bytes 24584 | tf_op jit(solution)/shard_map/ppermute | solution.py:380
  (20 other events, 116.3 us)

commit v6 on v5

--- a/solution.py
+++ b/solution.py
@@ -18,7 +18,7 @@
 AXES = ("dp", "member")
 VMEM = pl.BlockSpec(memory_space=pltpu.VMEM)
 SMEM = pl.BlockSpec(memory_space=pltpu.SMEM)
-LIMIT = 28 * 1024 * 1024
+LIMIT = 48 * 1024 * 1024
 
 
 def shape(dims, dtype=F32):
@@ -433,7 +433,7 @@
 
     def backward(where, part, parts=1, **more):
         def work(rows, wide_turned, back, *acc):
-            return back_call(rows, wide_turned, back, where, part * quarter, parts * quarter, *acc, n=1, **more)
+            return back_call(rows, wide_turned, back, where, part * quarter, parts * quarter, *acc, n=2, **more)
         return work
 
     weights = (rows, wide_turned, back)

time: 120 us -> 106 us (0.88)
  local copies, waits for them, and re-layouts: 20.9 us -> 1.41 us
  Pallas kernels: 57.2 us -> 61.7 us
    unnamed x38 -> x20, local copies, waits for them, and re-layouts: 20.6 us -> 1.14 us
    pallas_call x6, Pallas kernels: 19 us -> 22.2 us  [back_call(): pl.pallas_call(functools.partial(back_kernel, members=members, start=star...]
    pallas_call x1, Pallas kernels: 33.3 us -> 34.6 us  [grad_call(): pl.pallas_call(functools.partial(grad_kernel, own=own), grid=(members //...]
  transfers between devices with their start and end apart: 25 -> 25, of which waited for: 7 -> 8; matrix products, arithmetic and copies ran while one was open for 1% -> 1% of each run, Pallas kernels for 19% -> 24%
where the time goes in v6:
time: 106 us; the launch traced here: 105 us
  Pallas kernels  61.7 us (58%)
  starting transfers between devices  26 us (25%)
  waiting for transfers between devices  11.9 us (11%)
  other arithmetic  2.34 us (2%)
  between operations  1.75 us (2%)
  local copies, waits for them, and re-layouts  1.41 us (1%)
    pallas_call x1, Pallas kernels, grad_call(): pl.pallas_call(functools.partial(grad_kernel, own=own), grid=(members //...  34.6 us
    ppermute x25, starting transfers between devices, swap(): return lax.ppermute(value, AXES, [(i, i ^ mask) for i in range(total)])  26 us
    pallas_call x6, Pallas kernels, back_call(): pl.pallas_call(functools.partial(back_kernel, members=members, start=star...  22.2 us
    ppermute x25, waiting for transfers between devices, swap(): return lax.ppermute(value, AXES, [(i, i ^ mask) for i in range(total)])  11.9 us
  transfers between devices with their start and end apart: 25, of which 8 were waited for; matrix products, arithmetic and copies ran while one was open for 1% of the time, Pallas kernels for 24%

profile of v6, /device:TPU:0, one launch (start us, length us, event | category | flops | bytes accessed | tf_op | source)
XLA Modules:
  0.0 105.1 jit_solution(15380063196047449919)
XLA Ops:
  1.8 1.5 %pack_weights.1 = (bf16[16,768]{1,0:T(8,128)(2,1)}, f32[1,512]{1,0:T(1,128)}) custom-call(s32[1]{0:T(128)S(6)} %copy.32.count_ref.refs_8_, f32[16,512]{1,0:T(8,128)} %refs_4_.3, f32[3,16,32]{2,1,0:T(8,128)} %bitcast.63, f32[4,512]{1,0:T(4,128)} %refs_6_.3, f32[1,512]{1,0:T(1,128)} %bitcast.68), custom_call_target="tpu_custom_call" | custom-call | tf_op jit(solution)/shard_map/pack_weights/pallas_call | solution.py:51
  3.3 2.6 %collective-permute-start = (bf16[16,768]{1,0:T(8,128)(2,1)}, bf16[16,768]{1,0:T(8,128)(2,1)S(1)}, u32[]{:S(2)}, u32[]{:S(2)}) collective-permute-start(bf16[16,768]{1,0:T(8,128)(2,1)} %get-tuple-element.112), channel_id=1, source_target_pairs={{0,8},{1,9},{2,10},{3,11},{4,12},{5,13},{6,14},{7,15},{8,0},{9,1},... | collective-permute-start | bytes 73736 | tf_op jit(solution)/shard_map/ppermute | solution.py:380
  5.9 2.6 %collective-permute-start.1 = (bf16[16,768]{1,0:T(8,128)(2,1)}, bf16[16,768]{1,0:T(8,128)(2,1)S(1)}, u32[]{:S(2)}, u32[]{:S(2)}) collective-permute-start(bf16[16,768]{1,0:T(8,128)(2,1)} %get-tuple-element.112), channel_id=1, source_target_pairs={{0,16},{1,17},{2,18},{3,19},{4,20},{5,21},{6,22},{7,23},{8,24},{9,... | collective-permute-start | bytes 73736 | tf_op jit(solution)/shard_map/ppermute | solution.py:380
  8.5 1.4 %collective-permute-done.4 = f32[1,512]{1,0:T(1,128)S(1)} collective-permute-done((f32[1,512]{1,0:T(1,128)}, f32[1,512]{1,0:T(1,128)S(1)}, u32[]{:S(2)}, u32[]{:S(2)}) %collective-permute-start.4) | collective-permute-done | bytes 2080 | tf_op jit(solution)/shard_map/ppermute | solution.py:380
  10.9 3.4 %collective-permute-done.2 = bf16[16,768]{1,0:T(8,128)(2,1)S(1)} collective-permute-done((bf16[16,768]{1,0:T(8,128)(2,1)}, bf16[16,768]{1,0:T(8,128)(2,1)S(1)}, u32[]{:S(2)}, u32[]{:S(2)}) %collective-permute-start.2) | collective-permute-done | bytes 24608 | tf_op jit(solution)/shard_map/ppermute | solution.py:380
  15.1 1.6 %collective-permute-start.5 = (bf16[4,16,768]{2,1,0:T(8,128)(2,1)S(1)}, bf16[4,16,768]{2,1,0:T(8,128)(2,1)S(1)}, u32[]{:S(2)}, u32[]{:S(2)}) collective-permute-start(bf16[4,16,768]{2,1,0:T(8,128)(2,1)S(1)} %pad_maximum_fusion.3), channel_id=1, source_target_pairs={{0,2},{1,3},{2,0},{3,1},{4,6},{5,7},{6,4},{7,5},{8,10},{9,11},{10,... | collective-permute-start | bytes 294920 | tf_op jit(solution)/shard_map/ppermute | solution.py:380
  16.6 1.5 %collective-permute-start.6 = (bf16[4,16,768]{2,1,0:T(8,128)(2,1)S(1)}, bf16[4,16,768]{2,1,0:T(8,128)(2,1)S(1)}, u32[]{:S(2)}, u32[]{:S(2)}) collective-permute-start(bf16[4,16,768]{2,1,0:T(8,128)(2,1)S(1)} %pad_maximum_fusion.3), channel_id=1, source_target_pairs={{0,4},{1,5},{2,6},{3,7},{4,0},{5,1},{6,2},{7,3},{8,12},{9,13},{10,... | collective-permute-start | bytes 294920 | tf_op jit(solution)/shard_map/ppermute | solution.py:380
  18.6 1.1 %pad_maximum_fusion.x_ref = bf16[1024,512]{1,0:T(8,128)(2,1)S(1)} fusion(bf16[512,512]{1,0:T(8,128)(2,1)S(1)} %collective-permute-done.3, bf16[512,512]{1,0:T(8,128)(2,1)} %param.12), kind=kLoop, calls=%fused_computation | loop fusion | flops 2097152 | bytes 2097152 | tf_op jit(solution)/shard_map/concatenate | solution.py:392
  20.6 1.6 %collective-permute-done.6 = bf16[4,16,768]{2,1,0:T(8,128)(2,1)S(1)} collective-permute-done((bf16[4,16,768]{2,1,0:T(8,128)(2,1)S(1)}, bf16[4,16,768]{2,1,0:T(8,128)(2,1)S(1)}, u32[]{:S(2)}, u32[]{:S(2)}) %collective-permute-start.6) | collective-permute-done | bytes 98336 | tf_op jit(solution)/shard_map/ppermute | solution.py:380
  22.1 1.5 %collective-permute-done.7 = bf16[4,16,768]{2,1,0:T(8,128)(2,1)S(1)} collective-permute-done((bf16[4,16,768]{2,1,0:T(8,128)(2,1)S(1)}, bf16[4,16,768]{2,1,0:T(8,128)(2,1)S(1)}, u32[]{:S(2)}, u32[]{:S(2)}) %collective-permute-start.7) | collective-permute-done | bytes 98336 | tf_op jit(solution)/shard_map/ppermute | solution.py:380
  23.9 1.7 %collective-permute-done.8 = bf16[4,4,16,768]{3,2,0,1:T(8,128)(2,1)S(1)} collective-permute-done((bf16[4,4,16,768]{3,2,0,1:T(8,128)(2,1)S(1)}, bf16[4,4,16,768]{3,2,0,1:T(8,128)(2,1)S(1)}, u32[]{:S(2)}, u32[]{:S(2)}) %collective-permute-start.8) | collective-permute-done | bytes 393248 | tf_op jit(solution)/shard_map/ppermute | solution.py:380
  25.8 34.6 %member_grads.1 = (f32[256,640]{1,0:T(8,128)S(1)}, bf16[256,640]{1,0:T(8,128)(2,1)S(1)}, f32[32,512]{1,0:T(8,128)S(1)}, f32[2,512]{1,0:T(2,128)S(1)}, f32[128,51...) custom-call(bf16[1024,512]{1,0:T(8,128)(2,1)S(1)} %pad_maximum_fusion.x_ref, ...), custom_call_target="tpu_custom_call" | custom-call | flops 34359738368 | bytes 16777216 | tf_op jit(solution)/shard_map/member_grads/pallas_call | solution.py:186
  61.2 2.8 %input_grads_other.3.refs_3_ = f32[512,512]{1,0:T(8,128)S(1)} custom-call(f32[128,512]{1,0:T(8,128)S(1)} %get-tuple-element.182.refs_0_, bf16[512,512]{1,0:T(8,128)(2,1)S(1)} %get-tuple-element.183.refs_1_, bf16[16,1024,512]{2,1,0:T(8,128)(2,1)} %get-tuple-element.184.refs_2_), custom_call_target="tpu_custom_call" | custom-call | flops 1073741824 | bytes 2097152 | tf_op jit(solution)/shard_map/input_grads_other/pallas_call | solution.py:260
  65.3 2.4 %collective-permute-start.13 = (bf16[68,640]{1,0:T(8,128)(2,1)S(1)}, bf16[68,640]{1,0:T(8,128)(2,1)S(1)}, u32[]{:S(2)}, u32[]{:S(2)}) collective-permute-start(bf16[68,640]{1,0:T(8,128)(2,1)S(1)} %get-tuple-element.142), channel_id=1, source_target_pairs={{0,6},{1,7},{2,4},{3,5},{4,2},{5,3},{6,0},{7,1},{8,14},{9,15},{10,... | collective-permute-start | bytes 261128 | tf_op jit(solution)/shard_map/ppermute | solution.py:380
  67.8 4.9 %input_grads_other.4.refs_3_ = f32[512,512]{1,0:T(8,128)S(1)} custom-call(f32[128,512]{1,0:T(8,128)S(1)} %get-tuple-element.182.refs_0_, bf16[512,512]{1,0:T(8,128)(2,1)S(1)} %get-tuple-element.183.refs_1_, bf16[16,1024,512]{2,1,0:T(8,128)(2,1)} %get-tuple-element.184.refs_2_, f32[512,512]{1,0:T(8,128)S(1)} %input_grads_other.3.refs_3_), custom_call_target="tpu_custom_call" | custom-call | flops 2147483648 | bytes 4194304 | tf_op jit(solution)/shard_map/input_grads_other/pallas_call | solution.py:260
  73.8 3.5 %collective-permute-start.16 = (bf16[20,640]{1,0:T(8,128)(2,1)S(1)}, bf16[20,640]{1,0:T(8,128)(2,1)S(1)}, u32[]{:S(2)}, u32[]{:S(2)}) collective-permute-start(bf16[20,640]{1,0:T(8,128)(2,1)S(1)} %get-tuple-element.153), channel_id=1, source_target_pairs={{0,24},{1,25},{2,26},{3,27},{4,28},{5,29},{6,30},{7,31},{8,16},{9,... | collective-permute-start | bytes 76808 | tf_op jit(solution)/shard_map/ppermute | solution.py:380
  77.3 2.9 %input_grads_other.5 = f32[512,512]{1,0:T(8,128)S(1)} custom-call(f32[128,512]{1,0:T(8,128)S(1)} %get-tuple-element.182.refs_0_, bf16[512,512]{1,0:T(8,128)(2,1)S(1)} %get-tuple-element.183.refs_1_, bf16[16,1024,512]{2,1,0:T(8,128)(2,1)} %get-tuple-element.184.refs_2_, f32[512,512]{1,0:T(8,128)S(1)} %input_grads_other.4.refs_3_, f32[1,512]{1,0:T(1,128)S(1)} %slice.15.refs_4_), custom_call_target="tpu_custom_call" | custom-call | flops 1073741824 | bytes 2097152 | tf_op jit(solution)/shard_map/input_grads_other/pallas_call | solution.py:260
  80.9 1.8 %directions.1 = (f32[16,512]{1,0:T(8,128)}, f32[16,512]{1,0:T(8,128)}, f32[16,512]{1,0:T(8,128)}, f32[3,16,32]{2,1,0:T(8,128)}, f32[3,16,32]{2,1,0:T(8,128)}, /*...) custom-call(f32[68,640]{1,0:T(8,128)} %copy-done.1, ...), custom_call_target="tpu_custom_call" | custom-call | tf_op jit(solution)/shard_map/directions/pallas_call | solution.py:330
  82.7 2.8 %input_grads_own.3.refs_3_ = f32[512,512]{1,0:T(8,128)S(1)} custom-call(f32[128,512]{1,0:T(8,128)S(1)} %get-tuple-element.182.refs_0_, bf16[512,512]{1,0:T(8,128)(2,1)S(1)} %get-tuple-element.183.refs_1_, bf16[16,1024,512]{2,1,0:T(8,128)(2,1)} %get-tuple-element.184.refs_2_), custom_call_target="tpu_custom_call" | custom-call | flops 1073741824 | bytes 2097152 | tf_op jit(solution)/shard_map/input_grads_own/pallas_call | solution.py:260
  86.8 2.4 %collective-permute-start.20 = (f32[16,128]{1,0:T(8,128)S(1)}, f32[16,128]{1,0:T(8,128)S(1)}, u32[]{:S(2)}, u32[]{:S(2)}) collective-permute-start(f32[16,128]{1,0:T(8,128)S(1)} %add.94), channel_id=1, source_target_pairs={{0,6},{1,7},{2,4},{3,5},{4,2},{5,3},{6,0},{7,1},{8,14},{9,15},{10,... | collective-permute-start | bytes 24584 | tf_op jit(solution)/shard_map/ppermute | solution.py:380
  89.2 4.9 %input_grads_own.4.refs_3_ = f32[512,512]{1,0:T(8,128)S(1)} custom-call(f32[128,512]{1,0:T(8,128)S(1)} %get-tuple-element.182.refs_0_, bf16[512,512]{1,0:T(8,128)(2,1)S(1)} %get-tuple-element.183.refs_1_, bf16[16,1024,512]{2,1,0:T(8,128)(2,1)} %get-tuple-element.184.refs_2_, f32[512,512]{1,0:T(8,128)S(1)} %input_grads_own.3.refs_3_), custom_call_target="tpu_custom_call" | custom-call | flops 2147483648 | bytes 4194304 | tf_op jit(solution)/shard_map/input_grads_own/pallas_call | solution.py:260
  94.2 3.3 %collective-permute-start.22 = (f32[16,128]{1,0:T(8,128)S(1)}, f32[16,128]{1,0:T(8,128)S(1)}, u32[]{:S(2)}, u32[]{:S(2)}) collective-permute-start(f32[16,128]{1,0:T(8,128)S(1)} %add_add_fusion.refs_0_), channel_id=1, source_target_pairs={{0,16},{1,17},{2,18},{3,19},{4,20},{5,21},{6,22},{7,23},{8,24},{9,... | collective-permute-start | bytes 24584 | tf_op jit(solution)/shard_map/ppermute | solution.py:380
  98.6 3.9 %input_grads_own.5 = (f32[512,512]{1,0:T(8,128)}, f32[1,512]{1,0:T(1,128)}) custom-call(f32[128,512]{1,0:T(8,128)S(1)} %get-tuple-element.182.refs_0_, bf16[512,512]{1,0:T(8,128)(2,1)S(1)} %get-tuple-element.183.refs_1_, bf16[16,1024,512]{2,1,0:T(8,128)(2,1)} %get-tuple-element.184.refs_2_, f32[512,512]{1,0:T(8,128)S(1)} %input_grads_own.4.refs_3_, ...), custom_call_target="tpu_custom_call" | custom-call | flops 1073741824 | bytes 2097152 | tf_op jit(solution)/shard_map/input_grads_own/pallas_call | solution.py:260
  103.5 1.6 %updates.1 = (f32[16,512]{1,0:T(8,128)}, f32[3,16,32]{2,1,0:T(8,128)}, f32[4,512]{1,0:T(4,128)}, f32[2,5]{1,0:T(2,128)}) custom-call(f32[16,128]{1,0:T(8,128)} %copy-done.2, f32[16,128]{1,0:T(8,128)} %copy-done.6, f32[16,128]{1,0:T(8,128)} %copy-done.7, f32[16,128]{1,0:T(8,128)} %copy-done.8, f32[16,512]{1,0:T(8,128)} %refs_4_.3, f32[3,16,32]{2,1,0:T(8,128)} %bitcast.65, ...), custom_call_target="tpu_custom_call" | custom-call | tf_op jit(solution)/shard_map/updates/pallas_call | solution.py:357
  (82 shorter events, 11.2 us)
Async XLA Ops:
  0.6 13.6 %collective-permute-start.3 = (bf16[512,512]{1,0:T(8,128)(2,1)}, bf16[512,512]{1,0:T(8,128)(2,1)S(1)}, u32[]{:S(2)}, u32[]{:S(2)}) collective-permute-start(bf16[512,512]{1,0:T(8,128)(2,1)} %param.12), channel_id=1, source_target_pairs={{0,1},{1,0},{2,3},{3,2},{4,5},{5,4},{6,7},{7,6},{8,9},{9,8},{10,11... | collective-permute-start | bytes 1572872 | tf_op jit(solution)/shard_map/ppermute | solution.py:380
  3.3 6.5 %collective-permute-start = (bf16[16,768]{1,0:T(8,128)(2,1)}, bf16[16,768]{1,0:T(8,128)(2,1)S(1)}, u32[]{:S(2)}, u32[]{:S(2)}) collective-permute-start(bf16[16,768]{1,0:T(8,128)(2,1)} %get-tuple-element.112), channel_id=1, source_target_pairs={{0,8},{1,9},{2,10},{3,11},{4,12},{5,13},{6,14},{7,15},{8,0},{9,1},... | collective-permute-start | bytes 73736 | tf_op jit(solution)/shard_map/ppermute | solution.py:380
  5.9 5.1 %collective-permute-start.1 = (bf16[16,768]{1,0:T(8,128)(2,1)}, bf16[16,768]{1,0:T(8,128)(2,1)S(1)}, u32[]{:S(2)}, u32[]{:S(2)}) collective-permute-start(bf16[16,768]{1,0:T(8,128)(2,1)} %get-tuple-element.112), channel_id=1, source_target_pairs={{0,16},{1,17},{2,18},{3,19},{4,20},{5,21},{6,22},{7,23},{8,24},{9,... | collective-permute-start | bytes 73736 | tf_op jit(solution)/shard_map/ppermute | solution.py:380
  8.5 5.8 %collective-permute-start.2 = (bf16[16,768]{1,0:T(8,128)(2,1)}, bf16[16,768]{1,0:T(8,128)(2,1)S(1)}, u32[]{:S(2)}, u32[]{:S(2)}) collective-permute-start(bf16[16,768]{1,0:T(8,128)(2,1)} %get-tuple-element.112), channel_id=1, source_target_pairs={{0,24},{1,25},{2,26},{3,27},{4,28},{5,29},{6,30},{7,31},{8,16},{9,... | collective-permute-start | bytes 73736 | tf_op jit(solution)/shard_map/ppermute | solution.py:380
  15.1 5.5 %collective-permute-start.5 = (bf16[4,16,768]{2,1,0:T(8,128)(2,1)S(1)}, bf16[4,16,768]{2,1,0:T(8,128)(2,1)S(1)}, u32[]{:S(2)}, u32[]{:S(2)}) collective-permute-start(bf16[4,16,768]{2,1,0:T(8,128)(2,1)S(1)} %pad_maximum_fusion.3), channel_id=1, source_target_pairs={{0,2},{1,3},{2,0},{3,1},{4,6},{5,7},{6,4},{7,5},{8,10},{9,11},{10,... | collective-permute-start | bytes 294920 | tf_op jit(solution)/shard_map/ppermute | solution.py:380
  16.6 5.5 %collective-permute-start.6 = (bf16[4,16,768]{2,1,0:T(8,128)(2,1)S(1)}, bf16[4,16,768]{2,1,0:T(8,128)(2,1)S(1)}, u32[]{:S(2)}, u32[]{:S(2)}) collective-permute-start(bf16[4,16,768]{2,1,0:T(8,128)(2,1)S(1)} %pad_maximum_fusion.3), channel_id=1, source_target_pairs={{0,4},{1,5},{2,6},{3,7},{4,0},{5,1},{6,2},{7,3},{8,12},{9,13},{10,... | collective-permute-start | bytes 294920 | tf_op jit(solution)/shard_map/ppermute | solution.py:380
  18.2 5.5 %collective-permute-start.7 = (bf16[4,16,768]{2,1,0:T(8,128)(2,1)S(1)}, bf16[4,16,768]{2,1,0:T(8,128)(2,1)S(1)}, u32[]{:S(2)}, u32[]{:S(2)}) collective-permute-start(bf16[4,16,768]{2,1,0:T(8,128)(2,1)S(1)} %pad_maximum_fusion.3), channel_id=1, source_target_pairs={{0,6},{1,7},{2,4},{3,5},{4,2},{5,3},{6,0},{7,1},{8,14},{9,15},{10,... | collective-permute-start | bytes 294920 | tf_op jit(solution)/shard_map/ppermute | solution.py:380
  23.8 1.8 %collective-permute-start.8 = (bf16[4,4,16,768]{3,2,0,1:T(8,128)(2,1)S(1)}, bf16[4,4,16,768]{3,2,0,1:T(8,128)(2,1)S(1)}, u32[]{:S(2)}, u32[]{:S(2)}) collective-permute-start(bf16[4,4,16,768]{3,2,0,1:T(8,128)(2,1)S(1)} %pad_maximum_fusion.2), channel_id=1, source_target_pairs={{0,1},{1,0},{2,3},{3,2},{4,5},{5,4},{6,7},{7,6},{8,9},{9,8},{10,11... | collective-permute-start | bytes 1179656 | tf_op jit(solution)/shard_map/ppermute | solution.py:380
  60.6 3.5 %collective-permute-start.9 = (bf16[4,68,640]{2,1,0:T(8,128)(2,1)S(1)}, bf16[4,68,640]{2,1,0:T(8,128)(2,1)S(1)}, u32[]{:S(2)}, u32[]{:S(2)}) collective-permute-start(bf16[4,68,640]{2,1,0:T(8,128)(2,1)S(1)} %fusion.2), channel_id=1, source_target_pairs={{0,1},{1,0},{2,3},{3,2},{4,5},{5,4},{6,7},{7,6},{8,9},{9,8},{10,11... | collective-permute-start | bytes 1044488 | tf_op jit(solution)/shard_map/ppermute | solution.py:380
  60.8 3.3 %collective-permute-start.10 = (f32[1,512]{1,0:T(1,128)S(1)}, f32[1,512]{1,0:T(1,128)S(1)}, u32[]{:S(2)}, u32[]{:S(2)}) collective-permute-start(f32[1,512]{1,0:T(1,128)S(1)} %slice.12), channel_id=1, source_target_pairs={{0,1},{1,0},{2,3},{3,2},{4,5},{5,4},{6,7},{7,6},{8,9},{9,8},{10,11... | collective-permute-start | bytes 6152 | tf_op jit(solution)/shard_map/ppermute | solution.py:380
  64.2 8.4 %collective-permute-start.11 = (bf16[68,640]{1,0:T(8,128)(2,1)S(1)}, bf16[68,640]{1,0:T(8,128)(2,1)S(1)}, u32[]{:S(2)}, u32[]{:S(2)}) collective-permute-start(bf16[68,640]{1,0:T(8,128)(2,1)S(1)} %get-tuple-element.140), channel_id=1, source_target_pairs={{0,2},{1,3},{2,0},{3,1},{4,6},{5,7},{6,4},{7,5},{8,10},{9,11},{10,... | collective-permute-start | bytes 261128 | tf_op jit(solution)/shard_map/ppermute | solution.py:380
  64.9 7.8 %collective-permute-start.12 = (bf16[68,640]{1,0:T(8,128)(2,1)S(1)}, bf16[68,640]{1,0:T(8,128)(2,1)S(1)}, u32[]{:S(2)}, u32[]{:S(2)}) collective-permute-start(bf16[68,640]{1,0:T(8,128)(2,1)S(1)} %get-tuple-element.141), channel_id=1, source_target_pairs={{0,4},{1,5},{2,6},{3,7},{4,0},{5,1},{6,2},{7,3},{8,12},{9,13},{10,... | collective-permute-start | bytes 261128 | tf_op jit(solution)/shard_map/ppermute | solution.py:380
  65.3 7.3 %collective-permute-start.13 = (bf16[68,640]{1,0:T(8,128)(2,1)S(1)}, bf16[68,640]{1,0:T(8,128)(2,1)S(1)}, u32[]{:S(2)}, u32[]{:S(2)}) collective-permute-start(bf16[68,640]{1,0:T(8,128)(2,1)S(1)} %get-tuple-element.142), channel_id=1, source_target_pairs={{0,6},{1,7},{2,4},{3,5},{4,2},{5,3},{6,0},{7,1},{8,14},{9,15},{10,... | collective-permute-start | bytes 261128 | tf_op jit(solution)/shard_map/ppermute | solution.py:380
  72.8 7.4 %collective-permute-start.14 = (bf16[20,640]{1,0:T(8,128)(2,1)S(1)}, bf16[20,640]{1,0:T(8,128)(2,1)S(1)}, u32[]{:S(2)}, u32[]{:S(2)}) collective-permute-start(bf16[20,640]{1,0:T(8,128)(2,1)S(1)} %get-tuple-element.151), channel_id=1, source_target_pairs={{0,8},{1,9},{2,10},{3,11},{4,12},{5,13},{6,14},{7,15},{8,0},{9,1},... | collective-permute-start | bytes 76808 | tf_op jit(solution)/shard_map/ppermute | solution.py:380
  72.9 7.3 %collective-permute-start.15 = (bf16[20,640]{1,0:T(8,128)(2,1)S(1)}, bf16[20,640]{1,0:T(8,128)(2,1)S(1)}, u32[]{:S(2)}, u32[]{:S(2)}) collective-permute-start(bf16[20,640]{1,0:T(8,128)(2,1)S(1)} %get-tuple-element.152), channel_id=1, source_target_pairs={{0,16},{1,17},{2,18},{3,19},{4,20},{5,21},{6,22},{7,23},{8,24},{9,... | collective-permute-start | bytes 76808 | tf_op jit(solution)/shard_map/ppermute | solution.py:380
  73.8 6.5 %collective-permute-start.16 = (bf16[20,640]{1,0:T(8,128)(2,1)S(1)}, bf16[20,640]{1,0:T(8,128)(2,1)S(1)}, u32[]{:S(2)}, u32[]{:S(2)}) collective-permute-start(bf16[20,640]{1,0:T(8,128)(2,1)S(1)} %get-tuple-element.153), channel_id=1, source_target_pairs={{0,24},{1,25},{2,26},{3,27},{4,28},{5,29},{6,30},{7,31},{8,16},{9,... | collective-permute-start | bytes 76808 | tf_op jit(solution)/shard_map/ppermute | solution.py:380
  80.3 18.3 %collective-permute-start.24 = (f32[512,512]{1,0:T(8,128)S(1)}, f32[512,512]{1,0:T(8,128)S(1)}, u32[]{:S(2)}, u32[]{:S(2)}) collective-permute-start(f32[512,512]{1,0:T(8,128)S(1)} %input_grads_other.5), channel_id=1, source_target_pairs={{0,1},{1,0},{2,3},{3,2},{4,5},{5,4},{6,7},{7,6},{8,9},{9,8},{10,11... | collective-permute-start | bytes 3145736 | tf_op jit(solution)/shard_map/ppermute | solution.py:380
  82.7 2.9 %collective-permute-start.17 = (f32[16,128]{1,0:T(8,128)}, f32[16,128]{1,0:T(8,128)S(1)}, u32[]{:S(2)}, u32[]{:S(2)}) collective-permute-start(f32[16,128]{1,0:T(8,128)} %get-tuple-element.162), channel_id=1, source_target_pairs={{0,1},{1,0},{2,3},{3,2},{4,5},{5,4},{6,7},{7,6},{8,9},{9,8},{10,11... | collective-permute-start | bytes 24584 | tf_op jit(solution)/shard_map/ppermute | solution.py:380
  85.6 8.4 %collective-permute-start.18 = (f32[16,128]{1,0:T(8,128)S(1)}, f32[16,128]{1,0:T(8,128)S(1)}, u32[]{:S(2)}, u32[]{:S(2)}) collective-permute-start(f32[16,128]{1,0:T(8,128)S(1)} %add.94), channel_id=1, source_target_pairs={{0,2},{1,3},{2,0},{3,1},{4,6},{5,7},{6,4},{7,5},{8,10},{9,11},{10,... | collective-permute-start | bytes 24584 | tf_op jit(solution)/shard_map/ppermute | solution.py:380
  86.3 7.8 %collective-permute-start.19 = (f32[16,128]{1,0:T(8,128)S(1)}, f32[16,128]{1,0:T(8,128)S(1)}, u32[]{:S(2)}, u32[]{:S(2)}) collective-permute-start(f32[16,128]{1,0:T(8,128)S(1)} %add.94), channel_id=1, source_target_pairs={{0,4},{1,5},{2,6},{3,7},{4,0},{5,1},{6,2},{7,3},{8,12},{9,13},{10,... | collective-permute-start | bytes 24584 | tf_op jit(solution)/shard_map/ppermute | solution.py:380
  86.8 7.3 %collective-permute-start.20 = (f32[16,128]{1,0:T(8,128)S(1)}, f32[16,128]{1,0:T(8,128)S(1)}, u32[]{:S(2)}, u32[]{:S(2)}) collective-permute-start(f32[16,128]{1,0:T(8,128)S(1)} %add.94), channel_id=1, source_target_pairs={{0,6},{1,7},{2,4},{3,5},{4,2},{5,3},{6,0},{7,1},{8,14},{9,15},{10,... | collective-permute-start | bytes 24584 | tf_op jit(solution)/shard_map/ppermute | solution.py:380
  94.1 8.4 %collective-permute-start.21 = (f32[16,128]{1,0:T(8,128)S(1)}, f32[16,128]{1,0:T(8,128)S(1)}, u32[]{:S(2)}, u32[]{:S(2)}) collective-permute-start(f32[16,128]{1,0:T(8,128)S(1)} %add_add_fusion.refs_0_), channel_id=1, source_target_pairs={{0,8},{1,9},{2,10},{3,11},{4,12},{5,13},{6,14},{7,15},{8,0},{9,1},... | collective-permute-start | bytes 24584 | tf_op jit(solution)/shard_map/ppermute | solution.py:380
  94.2 8.3 %collective-permute-start.22 = (f32[16,128]{1,0:T(8,128)S(1)}, f32[16,128]{1,0:T(8,128)S(1)}, u32[]{:S(2)}, u32[]{:S(2)}) collective-permute-start(f32[16,128]{1,0:T(8,128)S(1)} %add_add_fusion.refs_0_), channel_id=1, source_target_pairs={{0,16},{1,17},{2,18},{3,19},{4,20},{5,21},{6,22},{7,23},{8,24},{9,... | collective-permute-start | bytes 24584 | tf_op jit(solution)/shard_map/ppermute | solution.py:380
  97.5 5.4 %collective-permute-start.23 = (f32[16,128]{1,0:T(8,128)S(1)}, f32[16,128]{1,0:T(8,128)S(1)}, u32[]{:S(2)}, u32[]{:S(2)}) collective-permute-start(f32[16,128]{1,0:T(8,128)S(1)} %add_add_fusion.refs_0_), channel_id=1, source_target_pairs={{0,24},{1,25},{2,26},{3,27},{4,28},{5,29},{6,30},{7,31},{8,16},{9,... | collective-permute-start | bytes 24584 | tf_op jit(solution)/shard_map/ppermute | solution.py:380
  (11 other events, 40.2 us)

commit v7 on v6

--- a/solution.py
+++ b/solution.py
@@ -18,6 +18,7 @@
 AXES = ("dp", "member")
 VMEM = pl.BlockSpec(memory_space=pltpu.VMEM)
 SMEM = pl.BlockSpec(memory_space=pltpu.SMEM)
+ANY = pl.BlockSpec(memory_space=pl.ANY)
 LIMIT = 48 * 1024 * 1024
 
 
@@ -205,51 +206,50 @@
     )(x, q, packed)
 
 
-def back_kernel(*refs, members, start, first, last):
-    rows_ref, turned_ref, gp_ref = refs[:3]
+def back_kernel(*refs, where, start, first, last):
+    rows_ref, turned_ref, gp_hbm = refs[:3]
     rest = list(refs[3:])
     acc_in = None if first else rest.pop(0)
     q_ref = rest.pop(0) if last else None
     if last == "own":
         came_ref, pred_ref, pred_came_ref, count_ref = [rest.pop(0) for _ in range(4)]
-        out_ref, pred_out_ref, acc_ref = rest
+        out_ref, pred_out_ref, gp_ref, sems = rest
     else:
         came_ref = None
-        out_ref, acc_ref = rest
+        out_ref, gp_ref, sems = rest
     n, R, D = gp_ref.shape
-    step = pl.program_id(0)
-    K = 2 * members
-    base = this_core() * members + start
-
-    @pl.when(step == 0)
-    def _():
-        acc_ref[...] = jnp.zeros_like(acc_ref) if first else acc_in[...]
-
-    left, right = [], []
-    for k in range(n):
-        i = base + step * n + k
-        r = rows_ref[pl.ds(i, 1), :].astype(BF16)
-        s = rows_ref[pl.ds(K + i, 1), :].astype(BF16)
-        left.append(gp_ref[k] * s)
-        right.append(turned_ref[...] * r)
-    acc_ref[...] += jnp.dot(jnp.concatenate(left, axis=1), jnp.concatenate(right, axis=0), preferred_element_type=F32)
-
-    @pl.when(step == pl.num_programs(0) - 1)
-    def _():
-        if not last:
-            out_ref[...] = acc_ref[...]
+    K = 2 * gp_hbm.shape[0]
+    base = this_core() * gp_hbm.shape[0] + start
+    copies = [
+        pltpu.make_async_copy(gp_hbm.at[start + k, pl.ds(where * R, R)], gp_ref.at[k], sems.at[k]) for k in range(n)]
+    for copy in copies:
+        copy.start()
+    if q_ref is not None:
+        q_wide = jnp.broadcast_to(0.5 * q_ref[...], (LANES, R)).T
+    if last == "own":
+        lane = lax.broadcasted_iota(jnp.int32, (1, R), 1)
+        total = pred_ref[0:1, :] + pred_came_ref[...]
+        pred_out_ref[...] = jnp.where(lane < count_ref[0], total, 0.0) * (1.0 / K)
+    for k in range(0, n, 2):
+        left, right = [], []
+        for j in (k, k + 1):
+            r = rows_ref[pl.ds(base + j, 1), :].astype(BF16)
+            s = rows_ref[pl.ds(K + base + j, 1), :].astype(BF16)
+            right.append(turned_ref[...] * r)
+            copies[j].wait()
+            left.append(gp_ref[j] * s)
+        value = jnp.dot(jnp.concatenate(left, axis=1), jnp.concatenate(right, axis=0), preferred_element_type=F32)
+        if k or not first:
+            value = value + (out_ref if k else acc_in)[...]
+        if last and k + 2 == n:
+            for l in range(0, D, LANES):
+                part = value[:, l:l + LANES] * q_wide
+                out_ref[:, l:l + LANES] = part if came_ref is None else part + came_ref[:, l:l + LANES]
         else:
-            q_wide = jnp.broadcast_to(0.5 * q_ref[...], (LANES, R)).T
-            for l in range(0, D, LANES):
-                value = acc_ref[:, l:l + LANES] * q_wide
-                out_ref[:, l:l + LANES] = value if came_ref is None else value + came_ref[:, l:l + LANES]
-        if last == "own":
-            lane = lax.broadcasted_iota(jnp.int32, (1, R), 1)
-            total = pred_ref[0:1, :] + pred_came_ref[...]
-            pred_out_ref[...] = jnp.where(lane < count_ref[0], total, 0.0) * (1.0 / K)
-
-
-def back_call(rows, turned, back, where, start, count, acc=None, q=None, came=None, n=4):
+            out_ref[...] = value
+
+
+def back_call(rows, turned, back, where, start, count, acc=None, q=None, came=None):
     members, R2, D = back.shape
     R = R2 // 2
     last = None if q is None else "other" if came is None else "own"
@@ -258,12 +258,11 @@
     if last == "own":
         specs[-1] = SMEM
     return pl.pallas_call(
-        functools.partial(back_kernel, members=members, start=start, first=acc is None, last=last),
-        grid=(count // n,),
+        functools.partial(back_kernel, where=where, start=start, first=acc is None, last=last),
         out_shape=(shape((R, D)), shape((1, R))) if last == "own" else shape((R, D)),
-        in_specs=[VMEM, VMEM, pl.BlockSpec((n, R, D), lambda i: (start // n + i, where, 0))] + specs,
+        in_specs=[VMEM, VMEM, ANY] + specs,
         out_specs=(VMEM, VMEM) if last == "own" else VMEM,
-        scratch_shapes=[pltpu.VMEM((R, D), F32)],
+        scratch_shapes=[pltpu.VMEM((count, R, D), BF16), pltpu.SemaphoreType.DMA((count,))],
         compiler_params=pltpu.CompilerParams(vmem_limit_bytes=LIMIT),
         cost_estimate=pl.CostEstimate(flops=2 * count * R * D * D, bytes_accessed=count * R * D * 2, transcendentals=0),
         name="input_grads_other" if where else "input_grads_own",
@@ -433,7 +432,7 @@
 
     def backward(where, part, parts=1, **more):
         def work(rows, wide_turned, back, *acc):
-            return back_call(rows, wide_turned, back, where, part * quarter, parts * quarter, *acc, n=2, **more)
+            return back_call(rows, wide_turned, back, where, part * quarter, parts * quarter, *acc, **more)
         return work
 
     weights = (rows, wide_turned, back)
@@ -481,7 +480,7 @@
         wide, last, dp_groups[0][0] // n_member, states)
 
     rounds = [(1, 2)] + chip_groups[::-1] + dp_groups[::-1]
-    plan = {0: backward(0, 0), 1: backward(0, 1, 2), len(rounds) - 1: backward(0, 3, q=q_own, came=(ig_came, preds, pred_came, counts))}
+    plan = {1: backward(0, 0, 2), len(rounds) - 1: backward(0, 2, 2, q=q_own, came=(ig_came, preds, pred_came, counts))}
     pending, acc = [sums], ()
     for step, (low, size) in enumerate(rounds):
         sums = pending[0]

time: 106 us -> 103 us (0.972)
  Pallas kernels: 61.7 us -> 57.7 us
    pallas_call x6 -> x5, Pallas kernels: 22.2 us -> 18.2 us  [back_call(): pl.pallas_call(functools.partial(back_kernel, where=where, start=start, f...]
  transfers between devices with their start and end apart: 25 -> 25, of which waited for: 8 -> 8; matrix products, arithmetic and copies ran while one was open for 1% -> 2% of each run, Pallas kernels for 24% -> 21%
where the time goes in v7:
time: 103 us
  Pallas kernels  57.7 us (56%)
  starting transfers between devices  26 us (25%)
  waiting for transfers between devices  12.8 us (12%)
  other arithmetic  3.04 us (3%)
  between operations  1.76 us (2%)
  local copies, waits for them, and re-layouts  1.41 us (1%)
    pallas_call x1, Pallas kernels, grad_call(): pl.pallas_call(functools.partial(grad_kernel, own=own), grid=(members //...  34.6 us
    ppermute x25, starting transfers between devices, swap(): return lax.ppermute(value, AXES, [(i, i ^ mask) for i in range(total)])  26 us
    pallas_call x5, Pallas kernels, back_call(): pl.pallas_call(functools.partial(back_kernel, where=where, start=start, f...  18.2 us
    ppermute x25, waiting for transfers between devices, swap(): return lax.ppermute(value, AXES, [(i, i ^ mask) for i in range(total)])  12.8 us
  transfers between devices with their start and end apart: 25, of which 8 were waited for; matrix products, arithmetic and copies ran while one was open for 2% of the time, Pallas kernels for 21%

profile of v7, /device:TPU:0, one launch (start us, length us, event | category | flops | bytes accessed | tf_op | source)
XLA Modules:
  0.0 102.7 jit_solution(2904000384517404111)
XLA Ops:
  1.8 1.5 %pack_weights.1 = (bf16[16,768]{1,0:T(8,128)(2,1)}, f32[1,512]{1,0:T(1,128)}) custom-call(s32[1]{0:T(128)S(6)} %copy.32.count_ref.refs_8_, f32[16,512]{1,0:T(8,128)} %refs_4_.3, f32[3,16,32]{2,1,0:T(8,128)} %bitcast.63, f32[4,512]{1,0:T(4,128)} %refs_6_.3, f32[1,512]{1,0:T(1,128)} %bitcast.68), custom_call_target="tpu_custom_call" | custom-call | tf_op jit(solution)/shard_map/pack_weights/pallas_call | solution.py:52
  3.3 2.6 %collective-permute-start = (bf16[16,768]{1,0:T(8,128)(2,1)}, bf16[16,768]{1,0:T(8,128)(2,1)S(1)}, u32[]{:S(2)}, u32[]{:S(2)}) collective-permute-start(bf16[16,768]{1,0:T(8,128)(2,1)} %get-tuple-element.105), channel_id=1, source_target_pairs={{0,8},{1,9},{2,10},{3,11},{4,12},{5,13},{6,14},{7,15},{8,0},{9,1},... | collective-permute-start | bytes 73736 | tf_op jit(solution)/shard_map/ppermute | solution.py:379
  5.9 2.6 %collective-permute-start.1 = (bf16[16,768]{1,0:T(8,128)(2,1)}, bf16[16,768]{1,0:T(8,128)(2,1)S(1)}, u32[]{:S(2)}, u32[]{:S(2)}) collective-permute-start(bf16[16,768]{1,0:T(8,128)(2,1)} %get-tuple-element.105), channel_id=1, source_target_pairs={{0,16},{1,17},{2,18},{3,19},{4,20},{5,21},{6,22},{7,23},{8,24},{9,... | collective-permute-start | bytes 73736 | tf_op jit(solution)/shard_map/ppermute | solution.py:379
  8.5 1.4 %collective-permute-done.4 = f32[1,512]{1,0:T(1,128)S(1)} collective-permute-done((f32[1,512]{1,0:T(1,128)}, f32[1,512]{1,0:T(1,128)S(1)}, u32[]{:S(2)}, u32[]{:S(2)}) %collective-permute-start.4) | collective-permute-done | bytes 2080 | tf_op jit(solution)/shard_map/ppermute | solution.py:379
  10.9 3.4 %collective-permute-done.2 = bf16[16,768]{1,0:T(8,128)(2,1)S(1)} collective-permute-done((bf16[16,768]{1,0:T(8,128)(2,1)}, bf16[16,768]{1,0:T(8,128)(2,1)S(1)}, u32[]{:S(2)}, u32[]{:S(2)}) %collective-permute-start.2) | collective-permute-done | bytes 24608 | tf_op jit(solution)/shard_map/ppermute | solution.py:379
  15.1 1.6 %collective-permute-start.5 = (bf16[4,16,768]{2,1,0:T(8,128)(2,1)S(1)}, bf16[4,16,768]{2,1,0:T(8,128)(2,1)S(1)}, u32[]{:S(2)}, u32[]{:S(2)}) collective-permute-start(bf16[4,16,768]{2,1,0:T(8,128)(2,1)S(1)} %pad_maximum_fusion.3), channel_id=1, source_target_pairs={{0,2},{1,3},{2,0},{3,1},{4,6},{5,7},{6,4},{7,5},{8,10},{9,11},{10,... | collective-permute-start | bytes 294920 | tf_op jit(solution)/shard_map/ppermute | solution.py:379
  16.6 1.5 %collective-permute-start.6 = (bf16[4,16,768]{2,1,0:T(8,128)(2,1)S(1)}, bf16[4,16,768]{2,1,0:T(8,128)(2,1)S(1)}, u32[]{:S(2)}, u32[]{:S(2)}) collective-permute-start(bf16[4,16,768]{2,1,0:T(8,128)(2,1)S(1)} %pad_maximum_fusion.3), channel_id=1, source_target_pairs={{0,4},{1,5},{2,6},{3,7},{4,0},{5,1},{6,2},{7,3},{8,12},{9,13},{10,... | collective-permute-start | bytes 294920 | tf_op jit(solution)/shard_map/ppermute | solution.py:379
  18.6 1.1 %pad_maximum_fusion.x_ref = bf16[1024,512]{1,0:T(8,128)(2,1)S(1)} fusion(bf16[512,512]{1,0:T(8,128)(2,1)S(1)} %collective-permute-done.3, bf16[512,512]{1,0:T(8,128)(2,1)} %param.12), kind=kLoop, calls=%fused_computation | loop fusion | flops 2097152 | bytes 2097152 | tf_op jit(solution)/shard_map/concatenate | solution.py:391
  20.6 1.6 %collective-permute-done.6 = bf16[4,16,768]{2,1,0:T(8,128)(2,1)S(1)} collective-permute-done((bf16[4,16,768]{2,1,0:T(8,128)(2,1)S(1)}, bf16[4,16,768]{2,1,0:T(8,128)(2,1)S(1)}, u32[]{:S(2)}, u32[]{:S(2)}) %collective-permute-start.6) | collective-permute-done | bytes 98336 | tf_op jit(solution)/shard_map/ppermute | solution.py:379
  22.1 1.5 %collective-permute-done.7 = bf16[4,16,768]{2,1,0:T(8,128)(2,1)S(1)} collective-permute-done((bf16[4,16,768]{2,1,0:T(8,128)(2,1)S(1)}, bf16[4,16,768]{2,1,0:T(8,128)(2,1)S(1)}, u32[]{:S(2)}, u32[]{:S(2)}) %collective-permute-start.7) | collective-permute-done | bytes 98336 | tf_op jit(solution)/shard_map/ppermute | solution.py:379
  23.9 1.7 %collective-permute-done.8 = bf16[4,4,16,768]{3,2,0,1:T(8,128)(2,1)S(1)} collective-permute-done((bf16[4,4,16,768]{3,2,0,1:T(8,128)(2,1)S(1)}, bf16[4,4,16,768]{3,2,0,1:T(8,128)(2,1)S(1)}, u32[]{:S(2)}, u32[]{:S(2)}) %collective-permute-start.8) | collective-permute-done | bytes 393248 | tf_op jit(solution)/shard_map/ppermute | solution.py:379
  25.8 34.6 %member_grads.1 = (f32[256,640]{1,0:T(8,128)S(1)}, bf16[256,640]{1,0:T(8,128)(2,1)S(1)}, f32[32,512]{1,0:T(8,128)S(1)}, f32[2,512]{1,0:T(2,128)S(1)}, f32[128,51...) custom-call(bf16[1024,512]{1,0:T(8,128)(2,1)S(1)} %pad_maximum_fusion.x_ref, ...), custom_call_target="tpu_custom_call" | custom-call | flops 34359738368 | bytes 16777216 | tf_op jit(solution)/shard_map/member_grads/pallas_call | solution.py:187
  61.2 2.6 %input_grads_other.3.refs_3_ = f32[512,512]{1,0:T(8,128)S(1)} custom-call(f32[128,512]{1,0:T(8,128)S(1)} %get-tuple-element.168.refs_0_, bf16[512,512]{1,0:T(8,128)(2,1)S(1)} %get-tuple-element.169.refs_1_, bf16[16,1024,512]{2,1,0:T(8,128)(2,1)} %get-tuple-element.170.refs_2_), custom_call_target="tpu_custom_call" | custom-call | flops 1073741824 | bytes 2097152 | tf_op jit(solution)/shard_map/input_grads_other/pallas_call | solution.py:260
  65.1 2.4 %collective-permute-start.13 = (bf16[68,640]{1,0:T(8,128)(2,1)S(1)}, bf16[68,640]{1,0:T(8,128)(2,1)S(1)}, u32[]{:S(2)}, u32[]{:S(2)}) collective-permute-start(bf16[68,640]{1,0:T(8,128)(2,1)S(1)} %get-tuple-element.135), channel_id=1, source_target_pairs={{0,6},{1,7},{2,4},{3,5},{4,2},{5,3},{6,0},{7,1},{8,14},{9,15},{10,... | collective-permute-start | bytes 261128 | tf_op jit(solution)/shard_map/ppermute | solution.py:379
  67.6 4.0 %input_grads_other.4.refs_3_ = f32[512,512]{1,0:T(8,128)S(1)} custom-call(f32[128,512]{1,0:T(8,128)S(1)} %get-tuple-element.168.refs_0_, bf16[512,512]{1,0:T(8,128)(2,1)S(1)} %get-tuple-element.169.refs_1_, bf16[16,1024,512]{2,1,0:T(8,128)(2,1)} %get-tuple-element.170.refs_2_, f32[512,512]{1,0:T(8,128)S(1)} %input_grads_other.3.refs_3_), custom_call_target="tpu_custom_call" | custom-call | flops 2147483648 | bytes 4194304 | tf_op jit(solution)/shard_map/input_grads_other/pallas_call | solution.py:260
  72.7 3.5 %collective-permute-start.16 = (bf16[20,640]{1,0:T(8,128)(2,1)S(1)}, bf16[20,640]{1,0:T(8,128)(2,1)S(1)}, u32[]{:S(2)}, u32[]{:S(2)}) collective-permute-start(bf16[20,640]{1,0:T(8,128)(2,1)S(1)} %get-tuple-element.146), channel_id=1, source_target_pairs={{0,24},{1,25},{2,26},{3,27},{4,28},{5,29},{6,30},{7,31},{8,16},{9,... | collective-permute-start | bytes 76808 | tf_op jit(solution)/shard_map/ppermute | solution.py:379
  76.2 2.7 %input_grads_other.5 = f32[512,512]{1,0:T(8,128)S(1)} custom-call(f32[128,512]{1,0:T(8,128)S(1)} %get-tuple-element.168.refs_0_, bf16[512,512]{1,0:T(8,128)(2,1)S(1)} %get-tuple-element.169.refs_1_, bf16[16,1024,512]{2,1,0:T(8,128)(2,1)} %get-tuple-element.170.refs_2_, f32[512,512]{1,0:T(8,128)S(1)} %input_grads_other.4.refs_3_, f32[1,512]{1,0:T(1,128)S(1)} %slice.15.refs_4_), custom_call_target="tpu_custom_call" | custom-call | flops 1073741824 | bytes 2097152 | tf_op jit(solution)/shard_map/input_grads_other/pallas_call | solution.py:260
  79.5 1.8 %directions.1 = (f32[16,512]{1,0:T(8,128)}, f32[16,512]{1,0:T(8,128)}, f32[16,512]{1,0:T(8,128)}, f32[3,16,32]{2,1,0:T(8,128)}, f32[3,16,32]{2,1,0:T(8,128)}, /*...) custom-call(f32[68,640]{1,0:T(8,128)} %copy-done.1, ...), custom_call_target="tpu_custom_call" | custom-call | tf_op jit(solution)/shard_map/directions/pallas_call | solution.py:329
  81.4 1.4 %collective-permute-done.17 = f32[16,128]{1,0:T(8,128)S(1)} collective-permute-done((f32[16,128]{1,0:T(8,128)}, f32[16,128]{1,0:T(8,128)S(1)}, u32[]{:S(2)}, u32[]{:S(2)}) %collective-permute-start.17) | collective-permute-done | bytes 8224 | tf_op jit(solution)/shard_map/ppermute | solution.py:379
  85.4 1.5 %collective-permute-start.20 = (f32[16,128]{1,0:T(8,128)S(1)}, f32[16,128]{1,0:T(8,128)S(1)}, u32[]{:S(2)}, u32[]{:S(2)}) collective-permute-start(f32[16,128]{1,0:T(8,128)S(1)} %add.94), channel_id=1, source_target_pairs={{0,6},{1,7},{2,4},{3,5},{4,2},{5,3},{6,0},{7,1},{8,14},{9,15},{10,... | collective-permute-start | bytes 24584 | tf_op jit(solution)/shard_map/ppermute | solution.py:379
  86.9 4.0 %input_grads_own.2.refs_3_ = f32[512,512]{1,0:T(8,128)S(1)} custom-call(f32[128,512]{1,0:T(8,128)S(1)} %get-tuple-element.168.refs_0_, bf16[512,512]{1,0:T(8,128)(2,1)S(1)} %get-tuple-element.169.refs_1_, bf16[16,1024,512]{2,1,0:T(8,128)(2,1)} %get-tuple-element.170.refs_2_), custom_call_target="tpu_custom_call" | custom-call | flops 2147483648 | bytes 4194304 | tf_op jit(solution)/shard_map/input_grads_own/pallas_call | solution.py:260
  91.0 3.5 %collective-permute-start.22 = (f32[16,128]{1,0:T(8,128)S(1)}, f32[16,128]{1,0:T(8,128)S(1)}, u32[]{:S(2)}, u32[]{:S(2)}) collective-permute-start(f32[16,128]{1,0:T(8,128)S(1)} %add_add_fusion.refs_0_), channel_id=1, source_target_pairs={{0,16},{1,17},{2,18},{3,19},{4,20},{5,21},{6,22},{7,23},{8,24},{9,... | collective-permute-start | bytes 24584 | tf_op jit(solution)/shard_map/ppermute | solution.py:379
  95.4 5.0 %input_grads_own.3 = (f32[512,512]{1,0:T(8,128)}, f32[1,512]{1,0:T(1,128)}) custom-call(f32[128,512]{1,0:T(8,128)S(1)} %get-tuple-element.168.refs_0_, bf16[512,512]{1,0:T(8,128)(2,1)S(1)} %get-tuple-element.169.refs_1_, bf16[16,1024,512]{2,1,0:T(8,128)(2,1)} %get-tuple-element.170.refs_2_, f32[512,512]{1,0:T(8,128)S(1)} %input_grads_own.2.refs_3_, ...), custom_call_target="tpu_custom_call" | custom-call | flops 2147483648 | bytes 4194304 | tf_op jit(solution)/shard_map/input_grads_own/pallas_call | solution.py:260
  101.1 1.6 %updates.1 = (f32[16,512]{1,0:T(8,128)}, f32[3,16,32]{2,1,0:T(8,128)}, f32[4,512]{1,0:T(4,128)}, f32[2,5]{1,0:T(2,128)}) custom-call(f32[16,128]{1,0:T(8,128)} %copy-done.2, f32[16,128]{1,0:T(8,128)} %copy-done.6, f32[16,128]{1,0:T(8,128)} %copy-done.7, f32[16,128]{1,0:T(8,128)} %copy-done.8, f32[16,512]{1,0:T(8,128)} %refs_4_.3, f32[3,16,32]{2,1,0:T(8,128)} %bitcast.65, ...), custom_call_target="tpu_custom_call" | custom-call | tf_op jit(solution)/shard_map/updates/pallas_call | solution.py:356
  (79 shorter events, 12.1 us)
Async XLA Ops:
  0.6 13.6 %collective-permute-start.3 = (bf16[512,512]{1,0:T(8,128)(2,1)}, bf16[512,512]{1,0:T(8,128)(2,1)S(1)}, u32[]{:S(2)}, u32[]{:S(2)}) collective-permute-start(bf16[512,512]{1,0:T(8,128)(2,1)} %param.12), channel_id=1, source_target_pairs={{0,1},{1,0},{2,3},{3,2},{4,5},{5,4},{6,7},{7,6},{8,9},{9,8},{10,11... | collective-permute-start | bytes 1572872 | tf_op jit(solution)/shard_map/ppermute | solution.py:379
  3.3 6.5 %collective-permute-start = (bf16[16,768]{1,0:T(8,128)(2,1)}, bf16[16,768]{1,0:T(8,128)(2,1)S(1)}, u32[]{:S(2)}, u32[]{:S(2)}) collective-permute-start(bf16[16,768]{1,0:T(8,128)(2,1)} %get-tuple-element.105), channel_id=1, source_target_pairs={{0,8},{1,9},{2,10},{3,11},{4,12},{5,13},{6,14},{7,15},{8,0},{9,1},... | collective-permute-start | bytes 73736 | tf_op jit(solution)/shard_map/ppermute | solution.py:379
  5.9 5.1 %collective-permute-start.1 = (bf16[16,768]{1,0:T(8,128)(2,1)}, bf16[16,768]{1,0:T(8,128)(2,1)S(1)}, u32[]{:S(2)}, u32[]{:S(2)}) collective-permute-start(bf16[16,768]{1,0:T(8,128)(2,1)} %get-tuple-element.105), channel_id=1, source_target_pairs={{0,16},{1,17},{2,18},{3,19},{4,20},{5,21},{6,22},{7,23},{8,24},{9,... | collective-permute-start | bytes 73736 | tf_op jit(solution)/shard_map/ppermute | solution.py:379
  8.5 5.8 %collective-permute-start.2 = (bf16[16,768]{1,0:T(8,128)(2,1)}, bf16[16,768]{1,0:T(8,128)(2,1)S(1)}, u32[]{:S(2)}, u32[]{:S(2)}) collective-permute-start(bf16[16,768]{1,0:T(8,128)(2,1)} %get-tuple-element.105), channel_id=1, source_target_pairs={{0,24},{1,25},{2,26},{3,27},{4,28},{5,29},{6,30},{7,31},{8,16},{9,... | collective-permute-start | bytes 73736 | tf_op jit(solution)/shard_map/ppermute | solution.py:379
  15.1 5.5 %collective-permute-start.5 = (bf16[4,16,768]{2,1,0:T(8,128)(2,1)S(1)}, bf16[4,16,768]{2,1,0:T(8,128)(2,1)S(1)}, u32[]{:S(2)}, u32[]{:S(2)}) collective-permute-start(bf16[4,16,768]{2,1,0:T(8,128)(2,1)S(1)} %pad_maximum_fusion.3), channel_id=1, source_target_pairs={{0,2},{1,3},{2,0},{3,1},{4,6},{5,7},{6,4},{7,5},{8,10},{9,11},{10,... | collective-permute-start | bytes 294920 | tf_op jit(solution)/shard_map/ppermute | solution.py:379
  16.6 5.5 %collective-permute-start.6 = (bf16[4,16,768]{2,1,0:T(8,128)(2,1)S(1)}, bf16[4,16,768]{2,1,0:T(8,128)(2,1)S(1)}, u32[]{:S(2)}, u32[]{:S(2)}) collective-permute-start(bf16[4,16,768]{2,1,0:T(8,128)(2,1)S(1)} %pad_maximum_fusion.3), channel_id=1, source_target_pairs={{0,4},{1,5},{2,6},{3,7},{4,0},{5,1},{6,2},{7,3},{8,12},{9,13},{10,... | collective-permute-start | bytes 294920 | tf_op jit(solution)/shard_map/ppermute | solution.py:379
  18.2 5.5 %collective-permute-start.7 = (bf16[4,16,768]{2,1,0:T(8,128)(2,1)S(1)}, bf16[4,16,768]{2,1,0:T(8,128)(2,1)S(1)}, u32[]{:S(2)}, u32[]{:S(2)}) collective-permute-start(bf16[4,16,768]{2,1,0:T(8,128)(2,1)S(1)} %pad_maximum_fusion.3), channel_id=1, source_target_pairs={{0,6},{1,7},{2,4},{3,5},{4,2},{5,3},{6,0},{7,1},{8,14},{9,15},{10,... | collective-permute-start | bytes 294920 | tf_op jit(solution)/shard_map/ppermute | solution.py:379
  23.8 1.8 %collective-permute-start.8 = (bf16[4,4,16,768]{3,2,0,1:T(8,128)(2,1)S(1)}, bf16[4,4,16,768]{3,2,0,1:T(8,128)(2,1)S(1)}, u32[]{:S(2)}, u32[]{:S(2)}) collective-permute-start(bf16[4,4,16,768]{3,2,0,1:T(8,128)(2,1)S(1)} %pad_maximum_fusion.2), channel_id=1, source_target_pairs={{0,1},{1,0},{2,3},{3,2},{4,5},{5,4},{6,7},{7,6},{8,9},{9,8},{10,11... | collective-permute-start | bytes 1179656 | tf_op jit(solution)/shard_map/ppermute | solution.py:379
  60.6 3.3 %collective-permute-start.9 = (bf16[4,68,640]{2,1,0:T(8,128)(2,1)S(1)}, bf16[4,68,640]{2,1,0:T(8,128)(2,1)S(1)}, u32[]{:S(2)}, u32[]{:S(2)}) collective-permute-start(bf16[4,68,640]{2,1,0:T(8,128)(2,1)S(1)} %fusion.2), channel_id=1, source_target_pairs={{0,1},{1,0},{2,3},{3,2},{4,5},{5,4},{6,7},{7,6},{8,9},{9,8},{10,11... | collective-permute-start | bytes 1044488 | tf_op jit(solution)/shard_map/ppermute | solution.py:379
  60.8 3.0 %collective-permute-start.10 = (f32[1,512]{1,0:T(1,128)S(1)}, f32[1,512]{1,0:T(1,128)S(1)}, u32[]{:S(2)}, u32[]{:S(2)}) collective-permute-start(f32[1,512]{1,0:T(1,128)S(1)} %slice.12), channel_id=1, source_target_pairs={{0,1},{1,0},{2,3},{3,2},{4,5},{5,4},{6,7},{7,6},{8,9},{9,8},{10,11... | collective-permute-start | bytes 6152 | tf_op jit(solution)/shard_map/ppermute | solution.py:379
  64.0 7.6 %collective-permute-start.11 = (bf16[68,640]{1,0:T(8,128)(2,1)S(1)}, bf16[68,640]{1,0:T(8,128)(2,1)S(1)}, u32[]{:S(2)}, u32[]{:S(2)}) collective-permute-start(bf16[68,640]{1,0:T(8,128)(2,1)S(1)} %get-tuple-element.133), channel_id=1, source_target_pairs={{0,2},{1,3},{2,0},{3,1},{4,6},{5,7},{6,4},{7,5},{8,10},{9,11},{10,... | collective-permute-start | bytes 261128 | tf_op jit(solution)/shard_map/ppermute | solution.py:379
  64.6 7.0 %collective-permute-start.12 = (bf16[68,640]{1,0:T(8,128)(2,1)S(1)}, bf16[68,640]{1,0:T(8,128)(2,1)S(1)}, u32[]{:S(2)}, u32[]{:S(2)}) collective-permute-start(bf16[68,640]{1,0:T(8,128)(2,1)S(1)} %get-tuple-element.134), channel_id=1, source_target_pairs={{0,4},{1,5},{2,6},{3,7},{4,0},{5,1},{6,2},{7,3},{8,12},{9,13},{10,... | collective-permute-start | bytes 261128 | tf_op jit(solution)/shard_map/ppermute | solution.py:379
  65.1 6.5 %collective-permute-start.13 = (bf16[68,640]{1,0:T(8,128)(2,1)S(1)}, bf16[68,640]{1,0:T(8,128)(2,1)S(1)}, u32[]{:S(2)}, u32[]{:S(2)}) collective-permute-start(bf16[68,640]{1,0:T(8,128)(2,1)S(1)} %get-tuple-element.135), channel_id=1, source_target_pairs={{0,6},{1,7},{2,4},{3,5},{4,2},{5,3},{6,0},{7,1},{8,14},{9,15},{10,... | collective-permute-start | bytes 261128 | tf_op jit(solution)/shard_map/ppermute | solution.py:379
  71.7 7.1 %collective-permute-start.14 = (bf16[20,640]{1,0:T(8,128)(2,1)S(1)}, bf16[20,640]{1,0:T(8,128)(2,1)S(1)}, u32[]{:S(2)}, u32[]{:S(2)}) collective-permute-start(bf16[20,640]{1,0:T(8,128)(2,1)S(1)} %get-tuple-element.144), channel_id=1, source_target_pairs={{0,8},{1,9},{2,10},{3,11},{4,12},{5,13},{6,14},{7,15},{8,0},{9,1},... | collective-permute-start | bytes 76808 | tf_op jit(solution)/shard_map/ppermute | solution.py:379
  71.8 7.1 %collective-permute-start.15 = (bf16[20,640]{1,0:T(8,128)(2,1)S(1)}, bf16[20,640]{1,0:T(8,128)(2,1)S(1)}, u32[]{:S(2)}, u32[]{:S(2)}) collective-permute-start(bf16[20,640]{1,0:T(8,128)(2,1)S(1)} %get-tuple-element.145), channel_id=1, source_target_pairs={{0,16},{1,17},{2,18},{3,19},{4,20},{5,21},{6,22},{7,23},{8,24},{9,... | collective-permute-start | bytes 76808 | tf_op jit(solution)/shard_map/ppermute | solution.py:379
  72.7 6.2 %collective-permute-start.16 = (bf16[20,640]{1,0:T(8,128)(2,1)S(1)}, bf16[20,640]{1,0:T(8,128)(2,1)S(1)}, u32[]{:S(2)}, u32[]{:S(2)}) collective-permute-start(bf16[20,640]{1,0:T(8,128)(2,1)S(1)} %get-tuple-element.146), channel_id=1, source_target_pairs={{0,24},{1,25},{2,26},{3,27},{4,28},{5,29},{6,30},{7,31},{8,16},{9,... | collective-permute-start | bytes 76808 | tf_op jit(solution)/shard_map/ppermute | solution.py:379
  78.9 16.5 %collective-permute-start.24 = (f32[512,512]{1,0:T(8,128)S(1)}, f32[512,512]{1,0:T(8,128)S(1)}, u32[]{:S(2)}, u32[]{:S(2)}) collective-permute-start(f32[512,512]{1,0:T(8,128)S(1)} %input_grads_other.5), channel_id=1, source_target_pairs={{0,1},{1,0},{2,3},{3,2},{4,5},{5,4},{6,7},{7,6},{8,9},{9,8},{10,11... | collective-permute-start | bytes 3145736 | tf_op jit(solution)/shard_map/ppermute | solution.py:379
  81.3 1.4 %collective-permute-start.17 = (f32[16,128]{1,0:T(8,128)}, f32[16,128]{1,0:T(8,128)S(1)}, u32[]{:S(2)}, u32[]{:S(2)}) collective-permute-start(f32[16,128]{1,0:T(8,128)} %get-tuple-element.154), channel_id=1, source_target_pairs={{0,1},{1,0},{2,3},{3,2},{4,5},{5,4},{6,7},{7,6},{8,9},{9,8},{10,11... | collective-permute-start | bytes 24584 | tf_op jit(solution)/shard_map/ppermute | solution.py:379
  83.4 7.5 %collective-permute-start.18 = (f32[16,128]{1,0:T(8,128)S(1)}, f32[16,128]{1,0:T(8,128)S(1)}, u32[]{:S(2)}, u32[]{:S(2)}) collective-permute-start(f32[16,128]{1,0:T(8,128)S(1)} %add.94), channel_id=1, source_target_pairs={{0,2},{1,3},{2,0},{3,1},{4,6},{5,7},{6,4},{7,5},{8,10},{9,11},{10,... | collective-permute-start | bytes 24584 | tf_op jit(solution)/shard_map/ppermute | solution.py:379
  84.5 6.4 %collective-permute-start.19 = (f32[16,128]{1,0:T(8,128)S(1)}, f32[16,128]{1,0:T(8,128)S(1)}, u32[]{:S(2)}, u32[]{:S(2)}) collective-permute-start(f32[16,128]{1,0:T(8,128)S(1)} %add.94), channel_id=1, source_target_pairs={{0,4},{1,5},{2,6},{3,7},{4,0},{5,1},{6,2},{7,3},{8,12},{9,13},{10,... | collective-permute-start | bytes 24584 | tf_op jit(solution)/shard_map/ppermute | solution.py:379
  85.4 5.5 %collective-permute-start.20 = (f32[16,128]{1,0:T(8,128)S(1)}, f32[16,128]{1,0:T(8,128)S(1)}, u32[]{:S(2)}, u32[]{:S(2)}) collective-permute-start(f32[16,128]{1,0:T(8,128)S(1)} %add.94), channel_id=1, source_target_pairs={{0,6},{1,7},{2,4},{3,5},{4,2},{5,3},{6,0},{7,1},{8,14},{9,15},{10,... | collective-permute-start | bytes 24584 | tf_op jit(solution)/shard_map/ppermute | solution.py:379
  91.0 9.5 %collective-permute-start.21 = (f32[16,128]{1,0:T(8,128)S(1)}, f32[16,128]{1,0:T(8,128)S(1)}, u32[]{:S(2)}, u32[]{:S(2)}) collective-permute-start(f32[16,128]{1,0:T(8,128)S(1)} %add_add_fusion.refs_0_), channel_id=1, source_target_pairs={{0,8},{1,9},{2,10},{3,11},{4,12},{5,13},{6,14},{7,15},{8,0},{9,1},... | collective-permute-start | bytes 24584 | tf_op jit(solution)/shard_map/ppermute | solution.py:379
  91.0 9.4 %collective-permute-start.22 = (f32[16,128]{1,0:T(8,128)S(1)}, f32[16,128]{1,0:T(8,128)S(1)}, u32[]{:S(2)}, u32[]{:S(2)}) collective-permute-start(f32[16,128]{1,0:T(8,128)S(1)} %add_add_fusion.refs_0_), channel_id=1, source_target_pairs={{0,16},{1,17},{2,18},{3,19},{4,20},{5,21},{6,22},{7,23},{8,24},{9,... | collective-permute-start | bytes 24584 | tf_op jit(solution)/shard_map/ppermute | solution.py:379
  94.6 5.9 %collective-permute-start.23 = (f32[16,128]{1,0:T(8,128)S(1)}, f32[16,128]{1,0:T(8,128)S(1)}, u32[]{:S(2)}, u32[]{:S(2)}) collective-permute-start(f32[16,128]{1,0:T(8,128)S(1)} %add_add_fusion.refs_0_), channel_id=1, source_target_pairs={{0,24},{1,25},{2,26},{3,27},{4,28},{5,29},{6,30},{7,31},{8,16},{9,... | collective-permute-start | bytes 24584 | tf_op jit(solution)/shard_map/ppermute | solution.py:379
  (10 other events, 38.1 us)

commit v8 on v7

--- a/solution.py
+++ b/solution.py
@@ -60,7 +60,7 @@
 
 def grad_kernel(
     x_ref, rows_q_ref, packed_ref,
-    keep_ref, sent_ref, heads_grad_ref, pred_ref, rows_ref, turned_ref, back_ref,
+    keep_ref, sent_ref, heads_grad_ref, pred_ref, rows_ref, turned_ref, back0_ref, back1_ref,
     cols_ref, heads_ref, weight_ref, xq_ref, q_ref, z0_ref, z1_ref, gp0_ref, gp1_ref,
     post_ref, pred_acc, sums_ref, gr_ref, grads_ref, *, own,
 ):
@@ -68,7 +68,7 @@
     half = R // 2
     K = heads_grad_ref.shape[0]
     members = K // 2
-    n = back_ref.shape[0]
+    n = back0_ref.shape[0]
     step_id, steps = pl.program_id(0), pl.num_programs(0)
     core = this_core()
     base = core * members
@@ -115,7 +115,8 @@
             d = a + h * (1.0 - t)
             gp = (hb * d).astype(BF16)
             gp_ref[c:c + step, :] = gp
-            back_ref[k, c:c + step, :] = gp
+            back_ref, at = (back0_ref, c) if c < half else (back1_ref, c - half)
+            back_ref[k, at:at + step, :] = gp
             hh = h * hb
             pred_acc[c:c + step, :] += sum(hh[:, l:l + LANES] for l in range(0, D, LANES))
             q = q_ref[c:c + step, :]
@@ -189,10 +190,10 @@
         grid=(members // n,),
         out_shape=(
             shape((D // 2, D + LANES)), shape((D // 2, D + LANES), BF16), shape((K, D)), shape((2, half)),
-            shape((LANES, D)), shape((D, D), BF16), shape((members, R, D), BF16),
+            shape((LANES, D)), shape((D, D), BF16), shape((members, half, D), BF16), shape((members, half, D), BF16),
         ),
         in_specs=[VMEM] * 3,
-        out_specs=(VMEM, VMEM, VMEM, VMEM, VMEM, VMEM, pl.BlockSpec((n, R, D), lambda i: (i, 0, 0))),
+        out_specs=(VMEM,) * 6 + (pl.BlockSpec((n, half, D), lambda i: (i, 0, 0)),) * 2,
         scratch_shapes=[
             pltpu.VMEM((D, LANES), F32), pltpu.VMEM((K, D), F32), pltpu.VMEM((D, D), F32),
             pltpu.VMEM((D + 16, R), BF16), pltpu.VMEM((R, LANES), F32),
@@ -206,7 +207,7 @@
     )(x, q, packed)
 
 
-def back_kernel(*refs, where, start, first, last):
+def back_kernel(*refs, start, first, last):
     rows_ref, turned_ref, gp_hbm = refs[:3]
     rest = list(refs[3:])
     acc_in = None if first else rest.pop(0)
@@ -221,7 +222,7 @@
     K = 2 * gp_hbm.shape[0]
     base = this_core() * gp_hbm.shape[0] + start
     copies = [
-        pltpu.make_async_copy(gp_hbm.at[start + k, pl.ds(where * R, R)], gp_ref.at[k], sems.at[k]) for k in range(n)]
+        pltpu.make_async_copy(gp_hbm.at[start + k], gp_ref.at[k], sems.at[k]) for k in range(n)]
     for copy in copies:
         copy.start()
     if q_ref is not None:
@@ -249,23 +250,22 @@
             out_ref[...] = value
 
 
-def back_call(rows, turned, back, where, start, count, acc=None, q=None, came=None):
-    members, R2, D = back.shape
-    R = R2 // 2
+def back_call(rows, turned, back, start, count, acc=None, q=None, came=None):
+    members, R, D = back.shape
     last = None if q is None else "other" if came is None else "own"
     more = [v for v in (acc, q, *(came or ())) if v is not None]
     specs = [VMEM] * len(more)
     if last == "own":
         specs[-1] = SMEM
     return pl.pallas_call(
-        functools.partial(back_kernel, where=where, start=start, first=acc is None, last=last),
+        functools.partial(back_kernel, start=start, first=acc is None, last=last),
         out_shape=(shape((R, D)), shape((1, R))) if last == "own" else shape((R, D)),
         in_specs=[VMEM, VMEM, ANY] + specs,
         out_specs=(VMEM, VMEM) if last == "own" else VMEM,
         scratch_shapes=[pltpu.VMEM((count, R, D), BF16), pltpu.SemaphoreType.DMA((count,))],
         compiler_params=pltpu.CompilerParams(vmem_limit_bytes=LIMIT),
         cost_estimate=pl.CostEstimate(flops=2 * count * R * D * D, bytes_accessed=count * R * D * 2, transcendentals=0),
-        name="input_grads_other" if where else "input_grads_own",
+        name="input_grads",
     )(rows, turned, back, *more)
 
 
@@ -380,10 +380,11 @@
 
 
 def gather_groups(value, groups, total, index, objects, q):
+    value, objects, q = lax.optimization_barrier((value, objects, q))
     rows = (objects, q)
     for axis, (low, size) in enumerate(groups):
         place = (index // low) % size
-        held = [value] + [swap(value, total, low * m) for m in range(1, size)]
+        held = [value] + [swap(value, total, low * m) for m in reversed(range(1, size))][::-1]
         if axis == 0:
             rows = rows + tuple(swap(v, total, 1) for v in rows)
             held, rows = lax.optimization_barrier((held, rows))
@@ -396,7 +397,7 @@
 
 def beside(sends, work, *inputs):
     values, inputs = lax.optimization_barrier(([v for v, _, _ in sends], inputs))
-    came = [swap(v, total, mask) for v, (_, total, mask) in zip(values, sends)]
+    came = [swap(v, total, mask) for v, (_, total, mask) in reversed(list(zip(values, sends)))][::-1]
     done = work(*inputs)
     return lax.optimization_barrier((came, done))
 
@@ -416,7 +417,7 @@
     full, x_both, q_both = gather_groups(packed, dp_groups + member_groups, total, index, objects, q_own)
     full = full.reshape(D, -1)
     q_other = q_both[:, R:]
-    keep, sent, head_grads, preds, rows, wide_turned, back = grad_call(x_both, q_both, full, K, own)
+    keep, sent, head_grads, preds, rows, wide_turned, back_own, back_other = grad_call(x_both, q_both, full, K, own)
 
     chips = [size for _, size in chip_groups]
     head_grads = head_grads.reshape(chips + [2, own_heads, D])
@@ -430,16 +431,16 @@
         main = jnp.moveaxis(main, 0, len(chips)).reshape(chips + [n_dp * own, D + LANES])
         return jnp.concatenate([main, jnp.pad(heads, [(0, 0)] * (len(chips) + 1) + [(0, LANES)])], axis=len(chips))
 
-    def backward(where, part, parts=1, **more):
+    def backward(part, parts=1, **more):
         def work(rows, wide_turned, back, *acc):
-            return back_call(rows, wide_turned, back, where, part * quarter, parts * quarter, *acc, **more)
+            return back_call(rows, wide_turned, back, part * quarter, parts * quarter, *acc, **more)
         return work
 
-    weights = (rows, wide_turned, back)
+    weights = (rows, wide_turned, back_other)
     other_heads = lax.dynamic_index_in_dim(head_grads, 1 - core, axis, keepdims=False)
     own_heads_grad = lax.dynamic_index_in_dim(head_grads, core, axis, keepdims=False)
     (came, pred_came), acc = beside(
-        [(arrange(sent, other_heads.astype(BF16)), total, 1), (preds[1:2], total, 1)], backward(1, 0), *weights)
+        [(arrange(sent, other_heads.astype(BF16)), total, 1), (preds[1:2], total, 1)], backward(0), *weights)
     wide = arrange(keep, own_heads_grad) + came.astype(F32)
     for axis in reversed(range(len(chips))):
         low, size = chip_groups[axis]
@@ -447,7 +448,7 @@
         part = [lax.dynamic_index_in_dim(wide, place ^ m, axis, keepdims=False) for m in range(size)]
         sends = [(part[m].astype(BF16), total, low * m) for m in range(1, size)]
         if axis == len(chips) - 1:
-            came, acc = beside(sends, backward(1, 1, 2), *weights, acc)
+            came, acc = beside(sends, backward(1, 2), *weights, acc)
         else:
             came = [swap(*send) for send in sends]
         wide = part[0]
@@ -466,7 +467,7 @@
 
         sends = [(chunk(place ^ m).astype(BF16), total, low * m) for m in range(1, size)]
         if axis == len(dp_groups) - 1:
-            last, acc = beside(sends, backward(1, 3, q=q_other), *weights, acc)
+            last, acc = beside(sends, backward(3, q=q_other), *weights, acc)
         else:
             last = [swap(*send) for send in sends]
         if axis:
@@ -480,7 +481,7 @@
         wide, last, dp_groups[0][0] // n_member, states)
 
     rounds = [(1, 2)] + chip_groups[::-1] + dp_groups[::-1]
-    plan = {1: backward(0, 0, 2), len(rounds) - 1: backward(0, 2, 2, q=q_own, came=(ig_came, preds, pred_came, counts))}
+    plan = {1: backward(0, 2), len(rounds) - 1: backward(2, 2, q=q_own, came=(ig_came, preds, pred_came, counts))}
     pending, acc = [sums], ()
     for step, (low, size) in enumerate(rounds):
         sums = pending[0]
@@ -488,7 +489,7 @@
             sums = sums + p
         sends = [(sums, total, low * m) for m in range(1, size)]
         if step in plan:
-            came, acc = beside(sends, plan[step], *weights, *acc)
+            came, acc = beside(sends, plan[step], rows, wide_turned, back_own, *acc)
             acc = (acc,)
         else:
             came = [swap(*send) for send in sends]

time: 103 us -> 102 us (level)
  waiting for transfers between devices: 12.8 us -> 11.2 us
    ppermute x25, waiting for transfers between devices: 12.8 us -> 11.2 us  [swap(): return lax.ppermute(value, AXES, [(i, i ^ mask) for i in range(total)])]
  transfers between devices with their start and end apart: 25 -> 25, of which waited for: 8 -> 9; matrix products, arithmetic and copies ran while one was open for 2% -> 2% of each run, Pallas kernels for 21% -> 20%
where the time goes in v8:
time: 102 us; the launch traced here: 101 us
  Pallas kernels  57.7 us (57%)
  starting transfers between devices  26 us (25%)
  waiting for transfers between devices  11.2 us (11%)
  other arithmetic  3.03 us (3%)
  between operations  1.71 us (2%)
  local copies, waits for them, and re-layouts  1.48 us (1%)
    pallas_call x1, Pallas kernels, grad_call(): pl.pallas_call(functools.partial(grad_kernel, own=own), grid=(members //...  34.7 us
    ppermute x25, starting transfers between devices, swap(): return lax.ppermute(value, AXES, [(i, i ^ mask) for i in range(total)])  26 us
    pallas_call x5, Pallas kernels, back_call(): pl.pallas_call(functools.partial(back_kernel, start=start, first=acc is N...  18.2 us
    ppermute x25, waiting for transfers between devices, swap(): return lax.ppermute(value, AXES, [(i, i ^ mask) for i in range(total)])  11.2 us
  transfers between devices with their start and end apart: 25, of which 9 were waited for; matrix products, arithmetic and copies ran while one was open for 2% of the time, Pallas kernels for 20%

profile of v8, /device:TPU:0, one launch (start us, length us, event | category | flops | bytes accessed | tf_op | source)
XLA Modules:
  0.0 101.2 jit_solution(5220083125097208614)
XLA Ops:
  1.3 1.5 %pack_weights.1 = (bf16[16,768]{1,0:T(8,128)(2,1)}, f32[1,512]{1,0:T(1,128)}) custom-call(s32[1]{0:T(128)S(6)} %copy.32.count_ref.refs_8_, f32[16,512]{1,0:T(8,128)} %refs_4_.3, f32[3,16,32]{2,1,0:T(8,128)} %bitcast.63, f32[4,512]{1,0:T(4,128)} %refs_6_.3, f32[1,512]{1,0:T(1,128)} %bitcast.68), custom_call_target="tpu_custom_call" | custom-call | tf_op jit(solution)/shard_map/pack_weights/pallas_call | solution.py:52
  3.2 4.7 %collective-permute-start.2 = (bf16[16,768]{1,0:T(8,128)(2,1)}, bf16[16,768]{1,0:T(8,128)(2,1)S(1)}, u32[]{:S(2)}, u32[]{:S(2)}) collective-permute-start(bf16[16,768]{1,0:T(8,128)(2,1)} %get-tuple-element.112), channel_id=1, source_target_pairs={{0,24},{1,25},{2,26},{3,27},{4,28},{5,29},{6,30},{7,31},{8,16},{9,... | collective-permute-start | bytes 73736 | tf_op jit(solution)/shard_map/ppermute | solution.py:379
  8.5 1.4 %collective-permute-done.4 = f32[1,512]{1,0:T(1,128)S(1)} collective-permute-done((f32[1,512]{1,0:T(1,128)}, f32[1,512]{1,0:T(1,128)S(1)}, u32[]{:S(2)}, u32[]{:S(2)}) %collective-permute-start.4) | collective-permute-done | bytes 2080 | tf_op jit(solution)/shard_map/ppermute | solution.py:379
  9.9 2.9 %collective-permute-done.1 = bf16[16,768]{1,0:T(8,128)(2,1)S(1)} collective-permute-done((bf16[16,768]{1,0:T(8,128)(2,1)}, bf16[16,768]{1,0:T(8,128)(2,1)S(1)}, u32[]{:S(2)}, u32[]{:S(2)}) %collective-permute-start.1) | collective-permute-done | bytes 24608 | tf_op jit(solution)/shard_map/ppermute | solution.py:379
  13.6 2.5 %collective-permute-start.7 = (bf16[4,16,768]{2,1,0:T(8,128)(2,1)S(1)}, bf16[4,16,768]{2,1,0:T(8,128)(2,1)S(1)}, u32[]{:S(2)}, u32[]{:S(2)}) collective-permute-start(bf16[4,16,768]{2,1,0:T(8,128)(2,1)S(1)} %pad_maximum_fusion.3), channel_id=1, source_target_pairs={{0,6},{1,7},{2,4},{3,5},{4,2},{5,3},{6,0},{7,1},{8,14},{9,15},{10,... | collective-permute-start | bytes 294920 | tf_op jit(solution)/shard_map/ppermute | solution.py:379
  18.3 1.3 %collective-permute-done.7 = bf16[4,16,768]{2,1,0:T(8,128)(2,1)S(1)} collective-permute-done((bf16[4,16,768]{2,1,0:T(8,128)(2,1)S(1)}, bf16[4,16,768]{2,1,0:T(8,128)(2,1)S(1)}, u32[]{:S(2)}, u32[]{:S(2)}) %collective-permute-start.7) | collective-permute-done | bytes 98336 | tf_op jit(solution)/shard_map/ppermute | solution.py:379
  21.5 1.7 %collective-permute-done.8 = bf16[4,4,16,768]{3,2,0,1:T(8,128)(2,1)S(1)} collective-permute-done((bf16[4,4,16,768]{3,2,0,1:T(8,128)(2,1)S(1)}, bf16[4,4,16,768]{3,2,0,1:T(8,128)(2,1)S(1)}, u32[]{:S(2)}, u32[]{:S(2)}) %collective-permute-start.8) | collective-permute-done | bytes 393248 | tf_op jit(solution)/shard_map/ppermute | solution.py:379
  23.4 34.7 %member_grads.1 = (f32[256,640]{1,0:T(8,128)S(1)}, bf16[256,640]{1,0:T(8,128)(2,1)S(1)}, f32[32,512]{1,0:T(8,128)S(1)}, f32[2,512]{1,0:T(2,128)S(1)}, f32[128,51...) custom-call(bf16[1024,512]{1,0:T(8,128)(2,1)S(1)} %pad_maximum_fusio, ...), custom_call_target="tpu_custom_call" | custom-call | flops 34359738368 | bytes 16777216 | tf_op jit(solution)/shard_map/member_grads/pallas_call | solution.py:188
  58.8 2.6 %input_grads.5.refs_3_ = f32[512,512]{1,0:T(8,128)S(1)} custom-call(f32[128,512]{1,0:T(8,128)S(1)} %get-tuple-element.176.refs_0_, bf16[512,512]{1,0:T(8,128)(2,1)S(1)} %get-tuple-element.177.refs_1_, bf16[16,512,512]{2,1,0:T(8,128)(2,1)} %get-tuple-element.156.refs_2_), custom_call_target="tpu_custom_call" | custom-call | flops 1073741824 | bytes 2097152 | tf_op jit(solution)/shard_map/input_grads/pallas_call | solution.py:260
  62.6 1.2 %collective-permute-start.12 = (bf16[68,640]{1,0:T(8,128)(2,1)S(1)}, bf16[68,640]{1,0:T(8,128)(2,1)S(1)}, u32[]{:S(2)}, u32[]{:S(2)}) collective-permute-start(bf16[68,640]{1,0:T(8,128)(2,1)S(1)} %get-tuple-element.141), channel_id=1, source_target_pairs={{0,4},{1,5},{2,6},{3,7},{4,0},{5,1},{6,2},{7,3},{8,12},{9,13},{10,... | collective-permute-start | bytes 261128 | tf_op jit(solution)/shard_map/ppermute | solution.py:379
  63.7 1.4 %collective-permute-start.13 = (bf16[68,640]{1,0:T(8,128)(2,1)S(1)}, bf16[68,640]{1,0:T(8,128)(2,1)S(1)}, u32[]{:S(2)}, u32[]{:S(2)}) collective-permute-start(bf16[68,640]{1,0:T(8,128)(2,1)S(1)} %get-tuple-element.142), channel_id=1, source_target_pairs={{0,6},{1,7},{2,4},{3,5},{4,2},{5,3},{6,0},{7,1},{8,14},{9,15},{10,... | collective-permute-start | bytes 261128 | tf_op jit(solution)/shard_map/ppermute | solution.py:379
  65.1 4.0 %input_grads.6.refs_3_ = f32[512,512]{1,0:T(8,128)S(1)} custom-call(f32[128,512]{1,0:T(8,128)S(1)} %get-tuple-element.176.refs_0_, bf16[512,512]{1,0:T(8,128)(2,1)S(1)} %get-tuple-element.177.refs_1_, bf16[16,512,512]{2,1,0:T(8,128)(2,1)} %get-tuple-element.156.refs_2_, f32[512,512]{1,0:T(8,128)S(1)} %input_grads.5.refs_3_), custom_call_target="tpu_custom_call" | custom-call | flops 2147483648 | bytes 4194304 | tf_op jit(solution)/shard_map/input_grads/pallas_call | solution.py:260
  69.7 2.0 %collective-permute-start.15 = (bf16[20,640]{1,0:T(8,128)(2,1)S(1)}, bf16[20,640]{1,0:T(8,128)(2,1)S(1)}, u32[]{:S(2)}, u32[]{:S(2)}) collective-permute-start(bf16[20,640]{1,0:T(8,128)(2,1)S(1)} %get-tuple-element.152), channel_id=1, source_target_pairs={{0,16},{1,17},{2,18},{3,19},{4,20},{5,21},{6,22},{7,23},{8,24},{9,... | collective-permute-start | bytes 76808 | tf_op jit(solution)/shard_map/ppermute | solution.py:379
  71.7 2.2 %collective-permute-start.16 = (bf16[20,640]{1,0:T(8,128)(2,1)S(1)}, bf16[20,640]{1,0:T(8,128)(2,1)S(1)}, u32[]{:S(2)}, u32[]{:S(2)}) collective-permute-start(bf16[20,640]{1,0:T(8,128)(2,1)S(1)} %get-tuple-element.153), channel_id=1, source_target_pairs={{0,24},{1,25},{2,26},{3,27},{4,28},{5,29},{6,30},{7,31},{8,16},{9,... | collective-permute-start | bytes 76808 | tf_op jit(solution)/shard_map/ppermute | solution.py:379
  73.9 2.7 %input_grads.7 = f32[512,512]{1,0:T(8,128)S(1)} custom-call(f32[128,512]{1,0:T(8,128)S(1)} %get-tuple-element.176.refs_0_, bf16[512,512]{1,0:T(8,128)(2,1)S(1)} %get-tuple-element.177.refs_1_, bf16[16,512,512]{2,1,0:T(8,128)(2,1)} %get-tuple-element.156.refs_2_, f32[512,512]{1,0:T(8,128)S(1)} %input_grads.6.refs_3_, f32[1,512]{1,0:T(1,128)S(1)} %slice.15.refs_4_), custom_call_target="tpu_custom_call" | custom-call | flops 1073741824 | bytes 2097152 | tf_op jit(solution)/shard_map/input_grads/pallas_call | solution.py:260
  78.0 1.8 %directions.1 = (f32[16,512]{1,0:T(8,128)}, f32[16,512]{1,0:T(8,128)}, f32[16,512]{1,0:T(8,128)}, f32[3,16,32]{2,1,0:T(8,128)}, f32[3,16,32]{2,1,0:T(8,128)}, /*...) custom-call(f32[68,640]{1,0:T(8,128)} %copy-done.1, ...), custom_call_target="tpu_custom_call" | custom-call | tf_op jit(solution)/shard_map/directions/pallas_call | solution.py:329
  79.9 1.4 %collective-permute-done.17 = f32[16,128]{1,0:T(8,128)S(1)} collective-permute-done((f32[16,128]{1,0:T(8,128)}, f32[16,128]{1,0:T(8,128)S(1)}, u32[]{:S(2)}, u32[]{:S(2)}) %collective-permute-start.17) | collective-permute-done | bytes 8224 | tf_op jit(solution)/shard_map/ppermute | solution.py:379
  81.9 1.2 %collective-permute-start.18 = (f32[16,128]{1,0:T(8,128)S(1)}, f32[16,128]{1,0:T(8,128)S(1)}, u32[]{:S(2)}, u32[]{:S(2)}) collective-permute-start(f32[16,128]{1,0:T(8,128)S(1)} %add.94), channel_id=1, source_target_pairs={{0,2},{1,3},{2,0},{3,1},{4,6},{5,7},{6,4},{7,5},{8,10},{9,11},{10,... | collective-permute-start | bytes 24584 | tf_op jit(solution)/shard_map/ppermute | solution.py:379
  84.3 1.2 %collective-permute-start.20 = (f32[16,128]{1,0:T(8,128)S(1)}, f32[16,128]{1,0:T(8,128)S(1)}, u32[]{:S(2)}, u32[]{:S(2)}) collective-permute-start(f32[16,128]{1,0:T(8,128)S(1)} %add.94), channel_id=1, source_target_pairs={{0,6},{1,7},{2,4},{3,5},{4,2},{5,3},{6,0},{7,1},{8,14},{9,15},{10,... | collective-permute-start | bytes 24584 | tf_op jit(solution)/shard_map/ppermute | solution.py:379
  85.4 4.0 %input_grads.8.refs_3_ = f32[512,512]{1,0:T(8,128)S(1)} custom-call(f32[128,512]{1,0:T(8,128)S(1)} %get-tuple-element.176.refs_0_, bf16[512,512]{1,0:T(8,128)(2,1)S(1)} %get-tuple-element.177.refs_1_, bf16[16,512,512]{2,1,0:T(8,128)(2,1)} %get-tuple-element.178.refs_2_), custom_call_target="tpu_custom_call" | custom-call | flops 2147483648 | bytes 4194304 | tf_op jit(solution)/shard_map/input_grads/pallas_call | solution.py:260
  89.6 2.7 %collective-permute-start.22 = (f32[16,128]{1,0:T(8,128)S(1)}, f32[16,128]{1,0:T(8,128)S(1)}, u32[]{:S(2)}, u32[]{:S(2)}) collective-permute-start(f32[16,128]{1,0:T(8,128)S(1)} %add_add_fusion.refs_0_), channel_id=1, source_target_pairs={{0,16},{1,17},{2,18},{3,19},{4,20},{5,21},{6,22},{7,23},{8,24},{9,... | collective-permute-start | bytes 24584 | tf_op jit(solution)/shard_map/ppermute | solution.py:379
  92.3 1.6 %collective-permute-start.23 = (f32[16,128]{1,0:T(8,128)S(1)}, f32[16,128]{1,0:T(8,128)S(1)}, u32[]{:S(2)}, u32[]{:S(2)}) collective-permute-start(f32[16,128]{1,0:T(8,128)S(1)} %add_add_fusion.refs_0_), channel_id=1, source_target_pairs={{0,24},{1,25},{2,26},{3,27},{4,28},{5,29},{6,30},{7,31},{8,16},{9,... | collective-permute-start | bytes 24584 | tf_op jit(solution)/shard_map/ppermute | solution.py:379
  93.9 5.0 %input_grads.9 = (f32[512,512]{1,0:T(8,128)}, f32[1,512]{1,0:T(1,128)}) custom-call(f32[128,512]{1,0:T(8,128)S(1)} %get-tuple-element.176.refs_0_, bf16[512,512]{1,0:T(8,128)(2,1)S(1)} %get-tuple-element.177.refs_1_, bf16[16,512,512]{2,1,0:T(8,128)(2,1)} %get-tuple-element.178.refs_2_, f32[512,512]{1,0:T(8,128)S(1)} %input_grads.8.refs_3_, ...), custom_call_target="tpu_custom_call" | custom-call | flops 2147483648 | bytes 4194304 | tf_op jit(solution)/shard_map/input_grads/pallas_call | solution.py:260
  99.6 1.6 %updates.1 = (f32[16,512]{1,0:T(8,128)}, f32[3,16,32]{2,1,0:T(8,128)}, f32[4,512]{1,0:T(4,128)}, f32[2,5]{1,0:T(2,128)}) custom-call(f32[16,128]{1,0:T(8,128)} %copy-done.2, f32[16,128]{1,0:T(8,128)} %copy-done.6, f32[16,128]{1,0:T(8,128)} %copy-done.7, f32[16,128]{1,0:T(8,128)} %copy-done.8, f32[16,512]{1,0:T(8,128)} %refs_4_.3, f32[3,16,32]{2,1,0:T(8,128)} %bitcast.65, ...), custom_call_target="tpu_custom_call" | custom-call | tf_op jit(solution)/shard_map/updates/pallas_call | solution.py:356
  (79 shorter events, 12.3 us)
Async XLA Ops:
  2.8 10.1 %collective-permute-start.3 = (bf16[512,512]{1,0:T(8,128)(2,1)}, bf16[512,512]{1,0:T(8,128)(2,1)S(1)}, u32[]{:S(2)}, u32[]{:S(2)}) collective-permute-start(bf16[512,512]{1,0:T(8,128)(2,1)} %param.12), channel_id=1, source_target_pairs={{0,1},{1,0},{2,3},{3,2},{4,5},{5,4},{6,7},{7,6},{8,9},{9,8},{10,11... | collective-permute-start | bytes 1572872 | tf_op jit(solution)/shard_map/ppermute | solution.py:379
  3.2 6.7 %collective-permute-start.2 = (bf16[16,768]{1,0:T(8,128)(2,1)}, bf16[16,768]{1,0:T(8,128)(2,1)S(1)}, u32[]{:S(2)}, u32[]{:S(2)}) collective-permute-start(bf16[16,768]{1,0:T(8,128)(2,1)} %get-tuple-element.112), channel_id=1, source_target_pairs={{0,24},{1,25},{2,26},{3,27},{4,28},{5,29},{6,30},{7,31},{8,16},{9,... | collective-permute-start | bytes 73736 | tf_op jit(solution)/shard_map/ppermute | solution.py:379
  7.9 4.9 %collective-permute-start.1 = (bf16[16,768]{1,0:T(8,128)(2,1)}, bf16[16,768]{1,0:T(8,128)(2,1)S(1)}, u32[]{:S(2)}, u32[]{:S(2)}) collective-permute-start(bf16[16,768]{1,0:T(8,128)(2,1)} %get-tuple-element.112), channel_id=1, source_target_pairs={{0,16},{1,17},{2,18},{3,19},{4,20},{5,21},{6,22},{7,23},{8,24},{9,... | collective-permute-start | bytes 73736 | tf_op jit(solution)/shard_map/ppermute | solution.py:379
  7.9 4.9 %collective-permute-start = (bf16[16,768]{1,0:T(8,128)(2,1)}, bf16[16,768]{1,0:T(8,128)(2,1)S(1)}, u32[]{:S(2)}, u32[]{:S(2)}) collective-permute-start(bf16[16,768]{1,0:T(8,128)(2,1)} %get-tuple-element.112), channel_id=1, source_target_pairs={{0,8},{1,9},{2,10},{3,11},{4,12},{5,13},{6,14},{7,15},{8,0},{9,1},... | collective-permute-start | bytes 73736 | tf_op jit(solution)/shard_map/ppermute | solution.py:379
  13.6 6.0 %collective-permute-start.7 = (bf16[4,16,768]{2,1,0:T(8,128)(2,1)S(1)}, bf16[4,16,768]{2,1,0:T(8,128)(2,1)S(1)}, u32[]{:S(2)}, u32[]{:S(2)}) collective-permute-start(bf16[4,16,768]{2,1,0:T(8,128)(2,1)S(1)} %pad_maximum_fusion.3), channel_id=1, source_target_pairs={{0,6},{1,7},{2,4},{3,5},{4,2},{5,3},{6,0},{7,1},{8,14},{9,15},{10,... | collective-permute-start | bytes 294920 | tf_op jit(solution)/shard_map/ppermute | solution.py:379
  16.1 4.7 %collective-permute-start.6 = (bf16[4,16,768]{2,1,0:T(8,128)(2,1)S(1)}, bf16[4,16,768]{2,1,0:T(8,128)(2,1)S(1)}, u32[]{:S(2)}, u32[]{:S(2)}) collective-permute-start(bf16[4,16,768]{2,1,0:T(8,128)(2,1)S(1)} %pad_maximum_fusion.3), channel_id=1, source_target_pairs={{0,4},{1,5},{2,6},{3,7},{4,0},{5,1},{6,2},{7,3},{8,12},{9,13},{10,... | collective-permute-start | bytes 294920 | tf_op jit(solution)/shard_map/ppermute | solution.py:379
  16.6 4.6 %collective-permute-start.5 = (bf16[4,16,768]{2,1,0:T(8,128)(2,1)S(1)}, bf16[4,16,768]{2,1,0:T(8,128)(2,1)S(1)}, u32[]{:S(2)}, u32[]{:S(2)}) collective-permute-start(bf16[4,16,768]{2,1,0:T(8,128)(2,1)S(1)} %pad_maximum_fusion.3), channel_id=1, source_target_pairs={{0,2},{1,3},{2,0},{3,1},{4,6},{5,7},{6,4},{7,5},{8,10},{9,11},{10,... | collective-permute-start | bytes 294920 | tf_op jit(solution)/shard_map/ppermute | solution.py:379
  21.4 1.8 %collective-permute-start.8 = (bf16[4,4,16,768]{3,2,0,1:T(8,128)(2,1)S(1)}, bf16[4,4,16,768]{3,2,0,1:T(8,128)(2,1)S(1)}, u32[]{:S(2)}, u32[]{:S(2)}) collective-permute-start(bf16[4,4,16,768]{3,2,0,1:T(8,128)(2,1)S(1)} %pad_maximum_fusion.2), channel_id=1, source_target_pairs={{0,1},{1,0},{2,3},{3,2},{4,5},{5,4},{6,7},{7,6},{8,9},{9,8},{10,11... | collective-permute-start | bytes 1179656 | tf_op jit(solution)/shard_map/ppermute | solution.py:379
  58.2 3.3 %collective-permute-start.9 = (bf16[4,68,640]{2,1,0:T(8,128)(2,1)S(1)}, bf16[4,68,640]{2,1,0:T(8,128)(2,1)S(1)}, u32[]{:S(2)}, u32[]{:S(2)}) collective-permute-start(bf16[4,68,640]{2,1,0:T(8,128)(2,1)S(1)} %fusion.2), channel_id=1, source_target_pairs={{0,1},{1,0},{2,3},{3,2},{4,5},{5,4},{6,7},{7,6},{8,9},{9,8},{10,11... | collective-permute-start | bytes 1044488 | tf_op jit(solution)/shard_map/ppermute | solution.py:379
  58.4 3.0 %collective-permute-start.10 = (f32[1,512]{1,0:T(1,128)S(1)}, f32[1,512]{1,0:T(1,128)S(1)}, u32[]{:S(2)}, u32[]{:S(2)}) collective-permute-start(f32[1,512]{1,0:T(1,128)S(1)} %slice.12), channel_id=1, source_target_pairs={{0,1},{1,0},{2,3},{3,2},{4,5},{5,4},{6,7},{7,6},{8,9},{9,8},{10,11... | collective-permute-start | bytes 6152 | tf_op jit(solution)/shard_map/ppermute | solution.py:379
  61.6 7.6 %collective-permute-start.11 = (bf16[68,640]{1,0:T(8,128)(2,1)S(1)}, bf16[68,640]{1,0:T(8,128)(2,1)S(1)}, u32[]{:S(2)}, u32[]{:S(2)}) collective-permute-start(bf16[68,640]{1,0:T(8,128)(2,1)S(1)} %get-tuple-element.140), channel_id=1, source_target_pairs={{0,2},{1,3},{2,0},{3,1},{4,6},{5,7},{6,4},{7,5},{8,10},{9,11},{10,... | collective-permute-start | bytes 261128 | tf_op jit(solution)/shard_map/ppermute | solution.py:379
  62.6 6.6 %collective-permute-start.12 = (bf16[68,640]{1,0:T(8,128)(2,1)S(1)}, bf16[68,640]{1,0:T(8,128)(2,1)S(1)}, u32[]{:S(2)}, u32[]{:S(2)}) collective-permute-start(bf16[68,640]{1,0:T(8,128)(2,1)S(1)} %get-tuple-element.141), channel_id=1, source_target_pairs={{0,4},{1,5},{2,6},{3,7},{4,0},{5,1},{6,2},{7,3},{8,12},{9,13},{10,... | collective-permute-start | bytes 261128 | tf_op jit(solution)/shard_map/ppermute | solution.py:379
  63.7 5.6 %collective-permute-start.13 = (bf16[68,640]{1,0:T(8,128)(2,1)S(1)}, bf16[68,640]{1,0:T(8,128)(2,1)S(1)}, u32[]{:S(2)}, u32[]{:S(2)}) collective-permute-start(bf16[68,640]{1,0:T(8,128)(2,1)S(1)} %get-tuple-element.142), channel_id=1, source_target_pairs={{0,6},{1,7},{2,4},{3,5},{4,2},{5,3},{6,0},{7,1},{8,14},{9,15},{10,... | collective-permute-start | bytes 261128 | tf_op jit(solution)/shard_map/ppermute | solution.py:379
  69.4 7.1 %collective-permute-start.14 = (bf16[20,640]{1,0:T(8,128)(2,1)S(1)}, bf16[20,640]{1,0:T(8,128)(2,1)S(1)}, u32[]{:S(2)}, u32[]{:S(2)}) collective-permute-start(bf16[20,640]{1,0:T(8,128)(2,1)S(1)} %get-tuple-element.151), channel_id=1, source_target_pairs={{0,8},{1,9},{2,10},{3,11},{4,12},{5,13},{6,14},{7,15},{8,0},{9,1},... | collective-permute-start | bytes 76808 | tf_op jit(solution)/shard_map/ppermute | solution.py:379
  69.7 6.9 %collective-permute-start.15 = (bf16[20,640]{1,0:T(8,128)(2,1)S(1)}, bf16[20,640]{1,0:T(8,128)(2,1)S(1)}, u32[]{:S(2)}, u32[]{:S(2)}) collective-permute-start(bf16[20,640]{1,0:T(8,128)(2,1)S(1)} %get-tuple-element.152), channel_id=1, source_target_pairs={{0,16},{1,17},{2,18},{3,19},{4,20},{5,21},{6,22},{7,23},{8,24},{9,... | collective-permute-start | bytes 76808 | tf_op jit(solution)/shard_map/ppermute | solution.py:379
  71.7 5.7 %collective-permute-start.16 = (bf16[20,640]{1,0:T(8,128)(2,1)S(1)}, bf16[20,640]{1,0:T(8,128)(2,1)S(1)}, u32[]{:S(2)}, u32[]{:S(2)}) collective-permute-start(bf16[20,640]{1,0:T(8,128)(2,1)S(1)} %get-tuple-element.153), channel_id=1, source_target_pairs={{0,24},{1,25},{2,26},{3,27},{4,28},{5,29},{6,30},{7,31},{8,16},{9,... | collective-permute-start | bytes 76808 | tf_op jit(solution)/shard_map/ppermute | solution.py:379
  77.4 16.5 %collective-permute-start.24 = (f32[512,512]{1,0:T(8,128)S(1)}, f32[512,512]{1,0:T(8,128)S(1)}, u32[]{:S(2)}, u32[]{:S(2)}) collective-permute-start(f32[512,512]{1,0:T(8,128)S(1)} %input_grads.7), channel_id=1, source_target_pairs={{0,1},{1,0},{2,3},{3,2},{4,5},{5,4},{6,7},{7,6},{8,9},{9,8},{10,11... | collective-permute-start | bytes 3145736 | tf_op jit(solution)/shard_map/ppermute | solution.py:379
  79.8 1.4 %collective-permute-start.17 = (f32[16,128]{1,0:T(8,128)}, f32[16,128]{1,0:T(8,128)S(1)}, u32[]{:S(2)}, u32[]{:S(2)}) collective-permute-start(f32[16,128]{1,0:T(8,128)} %get-tuple-element.161), channel_id=1, source_target_pairs={{0,1},{1,0},{2,3},{3,2},{4,5},{5,4},{6,7},{7,6},{8,9},{9,8},{10,11... | collective-permute-start | bytes 24584 | tf_op jit(solution)/shard_map/ppermute | solution.py:379
  81.9 7.5 %collective-permute-start.18 = (f32[16,128]{1,0:T(8,128)S(1)}, f32[16,128]{1,0:T(8,128)S(1)}, u32[]{:S(2)}, u32[]{:S(2)}) collective-permute-start(f32[16,128]{1,0:T(8,128)S(1)} %add.94), channel_id=1, source_target_pairs={{0,2},{1,3},{2,0},{3,1},{4,6},{5,7},{6,4},{7,5},{8,10},{9,11},{10,... | collective-permute-start | bytes 24584 | tf_op jit(solution)/shard_map/ppermute | solution.py:379
  83.2 6.2 %collective-permute-start.19 = (f32[16,128]{1,0:T(8,128)S(1)}, f32[16,128]{1,0:T(8,128)S(1)}, u32[]{:S(2)}, u32[]{:S(2)}) collective-permute-start(f32[16,128]{1,0:T(8,128)S(1)} %add.94), channel_id=1, source_target_pairs={{0,4},{1,5},{2,6},{3,7},{4,0},{5,1},{6,2},{7,3},{8,12},{9,13},{10,... | collective-permute-start | bytes 24584 | tf_op jit(solution)/shard_map/ppermute | solution.py:379
  84.3 5.2 %collective-permute-start.20 = (f32[16,128]{1,0:T(8,128)S(1)}, f32[16,128]{1,0:T(8,128)S(1)}, u32[]{:S(2)}, u32[]{:S(2)}) collective-permute-start(f32[16,128]{1,0:T(8,128)S(1)} %add.94), channel_id=1, source_target_pairs={{0,6},{1,7},{2,4},{3,5},{4,2},{5,3},{6,0},{7,1},{8,14},{9,15},{10,... | collective-permute-start | bytes 24584 | tf_op jit(solution)/shard_map/ppermute | solution.py:379
  89.4 9.5 %collective-permute-start.21 = (f32[16,128]{1,0:T(8,128)S(1)}, f32[16,128]{1,0:T(8,128)S(1)}, u32[]{:S(2)}, u32[]{:S(2)}) collective-permute-start(f32[16,128]{1,0:T(8,128)S(1)} %add_add_fusion.refs_0_), channel_id=1, source_target_pairs={{0,8},{1,9},{2,10},{3,11},{4,12},{5,13},{6,14},{7,15},{8,0},{9,1},... | collective-permute-start | bytes 24584 | tf_op jit(solution)/shard_map/ppermute | solution.py:379
  89.6 9.4 %collective-permute-start.22 = (f32[16,128]{1,0:T(8,128)S(1)}, f32[16,128]{1,0:T(8,128)S(1)}, u32[]{:S(2)}, u32[]{:S(2)}) collective-permute-start(f32[16,128]{1,0:T(8,128)S(1)} %add_add_fusion.refs_0_), channel_id=1, source_target_pairs={{0,16},{1,17},{2,18},{3,19},{4,20},{5,21},{6,22},{7,23},{8,24},{9,... | collective-permute-start | bytes 24584 | tf_op jit(solution)/shard_map/ppermute | solution.py:379
  92.3 6.7 %collective-permute-start.23 = (f32[16,128]{1,0:T(8,128)S(1)}, f32[16,128]{1,0:T(8,128)S(1)}, u32[]{:S(2)}, u32[]{:S(2)}) collective-permute-start(f32[16,128]{1,0:T(8,128)S(1)} %add_add_fusion.refs_0_), channel_id=1, source_target_pairs={{0,24},{1,25},{2,26},{3,27},{4,28},{5,29},{6,30},{7,31},{8,16},{9,... | collective-permute-start | bytes 24584 | tf_op jit(solution)/shard_map/ppermute | solution.py:379
  (10 other events, 37.6 us)

commit v9 on v8

--- a/solution.py
+++ b/solution.py
@@ -20,6 +20,7 @@
 SMEM = pl.BlockSpec(memory_space=pltpu.SMEM)
 ANY = pl.BlockSpec(memory_space=pl.ANY)
 LIMIT = 48 * 1024 * 1024
+SMALL = pltpu.CompilerParams(vmem_limit_bytes=8 * 1024 * 1024)
 
 
 def shape(dims, dtype=F32):
@@ -54,6 +55,7 @@
         out_shape=(shape((own, D + LANES + L), BF16), shape(cot.shape)),
         in_specs=[SMEM, VMEM, VMEM, VMEM, VMEM],
         out_specs=(VMEM, VMEM),
+        compiler_params=SMALL,
         name="pack_weights",
     )(counts, matrix, adapters_t, heads, cot)
 
@@ -331,6 +333,7 @@
         out_shape=tuple(outs),
         in_specs=[VMEM] * (1 + len(came) + 9),
         out_specs=tuple([VMEM] * 10),
+        compiler_params=SMALL,
         name="directions",
     )(wide, *came, *states)
 
@@ -358,6 +361,7 @@
         out_shape=(shape(m.shape), shape(a.shape), shape(h.shape), shape((2, 5))),
         in_specs=[VMEM] * (len(sums) + 6),
         out_specs=(VMEM,) * 4,
+        compiler_params=SMALL,
         name="updates",
     )(*sums, m, a, h, mu, au, hu)
 
@@ -424,23 +428,22 @@
     core = index % 2
     axis = len(chips)
     members = K // 2
-    quarter = members // 4
 
     def arrange(main, heads):
         main = main.reshape([n_dp] + chips + [own, D + LANES])
         main = jnp.moveaxis(main, 0, len(chips)).reshape(chips + [n_dp * own, D + LANES])
         return jnp.concatenate([main, jnp.pad(heads, [(0, 0)] * (len(chips) + 1) + [(0, LANES)])], axis=len(chips))
 
-    def backward(part, parts=1, **more):
+    def backward(start, count, **more):
         def work(rows, wide_turned, back, *acc):
-            return back_call(rows, wide_turned, back, part * quarter, parts * quarter, *acc, **more)
+            return back_call(rows, wide_turned, back, start, count, *acc, **more)
         return work
 
     weights = (rows, wide_turned, back_other)
     other_heads = lax.dynamic_index_in_dim(head_grads, 1 - core, axis, keepdims=False)
     own_heads_grad = lax.dynamic_index_in_dim(head_grads, core, axis, keepdims=False)
     (came, pred_came), acc = beside(
-        [(arrange(sent, other_heads.astype(BF16)), total, 1), (preds[1:2], total, 1)], backward(0), *weights)
+        [(arrange(sent, other_heads.astype(BF16)), total, 1), (preds[1:2], total, 1)], backward(0, 2), *weights)
     wide = arrange(keep, own_heads_grad) + came.astype(F32)
     for axis in reversed(range(len(chips))):
         low, size = chip_groups[axis]
@@ -448,7 +451,7 @@
         part = [lax.dynamic_index_in_dim(wide, place ^ m, axis, keepdims=False) for m in range(size)]
         sends = [(part[m].astype(BF16), total, low * m) for m in range(1, size)]
         if axis == len(chips) - 1:
-            came, acc = beside(sends, backward(1, 2), *weights, acc)
+            came, acc = beside(sends, backward(2, 8), *weights, acc)
         else:
             came = [swap(*send) for send in sends]
         wide = part[0]
@@ -467,7 +470,7 @@
 
         sends = [(chunk(place ^ m).astype(BF16), total, low * m) for m in range(1, size)]
         if axis == len(dp_groups) - 1:
-            last, acc = beside(sends, backward(3, q=q_other), *weights, acc)
+            last, acc = beside(sends, backward(10, 6, q=q_other), *weights, acc)
         else:
             last = [swap(*send) for send in sends]
         if axis:
@@ -481,7 +484,7 @@
         wide, last, dp_groups[0][0] // n_member, states)
 
     rounds = [(1, 2)] + chip_groups[::-1] + dp_groups[::-1]
-    plan = {1: backward(0, 2), len(rounds) - 1: backward(2, 2, q=q_own, came=(ig_came, preds, pred_came, counts))}
+    plan = {1: backward(0, 8), len(rounds) - 1: backward(8, 8, q=q_own, came=(ig_came, preds, pred_came, counts))}
     pending, acc = [sums], ()
     for step, (low, size) in enumerate(rounds):
         sums = pending[0]

time: 102 us -> 98.2 us (0.963)
  Pallas kernels: 57.7 us -> 54.5 us
  local copies, waits for them, and re-layouts: 1.48 us -> 3.2 us
  other arithmetic: 3.03 us -> 1.58 us
    unnamed x18 -> x26, local copies, waits for them, and re-layouts: 1.2 us -> 2.92 us
    pallas_call x1, Pallas kernels: 1.47 us -> 0.08 us  [pack_call(): pl.pallas_call(pack_kernel, out_shape=(shape((own, D + LANES + L), BF16),...]
    pallas_call x1, Pallas kernels: 1.78 us -> 0.73 us  [direction_call(): pl.pallas_call(functools.partial(direction_kernel, low, len(came) + 1), o...]
  transfers between devices with their start and end apart: 25 -> 25, of which waited for: 9 -> 9; matrix products, arithmetic and copies ran while one was open for 2% -> 1% of each run, Pallas kernels for 20% -> 19%
where the time goes in v9:
time: 98.2 us; the launch traced here: 97.8 us
  Pallas kernels  54.5 us (55%)
  starting transfers between devices  26.4 us (27%)
  waiting for transfers between devices  10.4 us (11%)
  local copies, waits for them, and re-layouts  3.2 us (3%)
  between operations  1.75 us (2%)
  other arithmetic  1.58 us (2%)
    pallas_call x1, Pallas kernels, grad_call(): pl.pallas_call(functools.partial(grad_kernel, own=own), grid=(members //...  34.6 us
    ppermute x25, starting transfers between devices, swap(): return lax.ppermute(value, AXES, [(i, i ^ mask) for i in range(total)])  26.4 us
    pallas_call x5, Pallas kernels, back_call(): pl.pallas_call(functools.partial(back_kernel, start=start, first=acc is N...  18.2 us
    ppermute x25, waiting for transfers between devices, swap(): return lax.ppermute(value, AXES, [(i, i ^ mask) for i in range(total)])  10.4 us
    unnamed x26, local copies, waits for them, and re-layouts  2.92 us
  transfers between devices with their start and end apart: 25, of which 9 were waited for; matrix products, arithmetic and copies ran while one was open for 1% of the time, Pallas kernels for 19%

profile of v9, /device:TPU:0, one launch (start us, length us, event | category | flops | bytes accessed | tf_op | source)
XLA Modules:
  0.0 97.8 jit_solution(11148239537539664453)
XLA Ops:
  4.7 4.7 %collective-permute-start.2 = (bf16[16,768]{1,0:T(8,128)(2,1)S(1)}, bf16[16,768]{1,0:T(8,128)(2,1)S(1)}, u32[]{:S(2)}, u32[]{:S(2)}) collective-permute-start(bf16[16,768]{1,0:T(8,128)(2,1)S(1)} %get-tuple-element.112), channel_id=1, source_target_pairs={{0,24},{1,25},{2,26},{3,27},{4,28},{5,29},{6,30},{7,31},{8,16},{9,... | collective-permute-start | bytes 73736 | tf_op jit(solution)/shard_map/ppermute | solution.py:383
  10.0 1.2 %collective-permute-done.4 = f32[1,512]{1,0:T(1,128)S(1)} collective-permute-done((f32[1,512]{1,0:T(1,128)S(1)}, f32[1,512]{1,0:T(1,128)S(1)}, u32[]{:S(2)}, u32[]{:S(2)}) %collective-permute-start.4) | collective-permute-done | bytes 2080 | tf_op jit(solution)/shard_map/ppermute | solution.py:383
  11.2 2.9 %collective-permute-done.1 = bf16[16,768]{1,0:T(8,128)(2,1)S(1)} collective-permute-done((bf16[16,768]{1,0:T(8,128)(2,1)S(1)}, bf16[16,768]{1,0:T(8,128)(2,1)S(1)}, u32[]{:S(2)}, u32[]{:S(2)}) %collective-permute-start.1) | collective-permute-done | bytes 24608 | tf_op jit(solution)/shard_map/ppermute | solution.py:383
  14.2 2.5 %collective-permute-start.7 = (bf16[4,16,768]{2,1,0:T(8,128)(2,1)S(1)}, bf16[4,16,768]{2,1,0:T(8,128)(2,1)S(1)}, u32[]{:S(2)}, u32[]{:S(2)}) collective-permute-start(bf16[4,16,768]{2,1,0:T(8,128)(2,1)S(1)} %pad_maximum_fusion.3), channel_id=1, source_target_pairs={{0,6},{1,7},{2,4},{3,5},{4,2},{5,3},{6,0},{7,1},{8,14},{9,15},{10,... | collective-permute-start | bytes 294920 | tf_op jit(solution)/shard_map/ppermute | solution.py:383
  17.7 1.1 %pad_maximum_fusion.x_ref = bf16[1024,512]{1,0:T(8,128)(2,1)S(1)} fusion(bf16[512,512]{1,0:T(8,128)(2,1)S(1)} %collective-permute-done.3, bf16[512,512]{1,0:T(8,128)(2,1)} %param.12), kind=kLoop, calls=%fused_computation | loop fusion | flops 2097152 | bytes 2097152 | tf_op jit(solution)/shard_map/concatenate | solution.py:396
  18.8 1.3 %collective-permute-done.7 = bf16[4,16,768]{2,1,0:T(8,128)(2,1)S(1)} collective-permute-done((bf16[4,16,768]{2,1,0:T(8,128)(2,1)S(1)}, bf16[4,16,768]{2,1,0:T(8,128)(2,1)S(1)}, u32[]{:S(2)}, u32[]{:S(2)}) %collective-permute-start.7) | collective-permute-done | bytes 98336 | tf_op jit(solution)/shard_map/ppermute | solution.py:383
  20.2 1.1 %collective-permute-done.6 = bf16[4,16,768]{2,1,0:T(8,128)(2,1)S(1)} collective-permute-done((bf16[4,16,768]{2,1,0:T(8,128)(2,1)S(1)}, bf16[4,16,768]{2,1,0:T(8,128)(2,1)S(1)}, u32[]{:S(2)}, u32[]{:S(2)}) %collective-permute-start.6) | collective-permute-done | bytes 98336 | tf_op jit(solution)/shard_map/ppermute | solution.py:383
  22.0 1.7 %collective-permute-done.8 = bf16[4,4,16,768]{3,2,0,1:T(8,128)(2,1)S(1)} collective-permute-done((bf16[4,4,16,768]{3,2,0,1:T(8,128)(2,1)S(1)}, bf16[4,4,16,768]{3,2,0,1:T(8,128)(2,1)S(1)}, u32[]{:S(2)}, u32[]{:S(2)}) %collective-permute-start.8) | collective-permute-done | bytes 393248 | tf_op jit(solution)/shard_map/ppermute | solution.py:383
  24.0 34.6 %member_grads.1 = (f32[256,640]{1,0:T(8,128)S(1)}, bf16[256,640]{1,0:T(8,128)(2,1)S(1)}, f32[32,512]{1,0:T(8,128)S(1)}, f32[2,512]{1,0:T(2,128)S(1)}, f32[128,51...) custom-call(bf16[1024,512]{1,0:T(8,128)(2,1)S(1)} %pad_maximum_fusio, ...), custom_call_target="tpu_custom_call" | custom-call | flops 34359738368 | bytes 16777216 | tf_op jit(solution)/shard_map/member_grads/pallas_call | solution.py:190
  59.3 1.9 %input_grads.5.refs_3_ = f32[512,512]{1,0:T(8,128)S(1)} custom-call(f32[128,512]{1,0:T(8,128)S(1)} %get-tuple-element.176.refs_0_, bf16[512,512]{1,0:T(8,128)(2,1)S(1)} %get-tuple-element.177.refs_1_, bf16[16,512,512]{2,1,0:T(8,128)(2,1)} %get-tuple-element.156.refs_2_), custom_call_target="tpu_custom_call" | custom-call | flops 536870912 | bytes 1048576 | tf_op jit(solution)/shard_map/input_grads/pallas_call | solution.py:262
  62.4 1.1 %collective-permute-start.12 = (bf16[68,640]{1,0:T(8,128)(2,1)S(1)}, bf16[68,640]{1,0:T(8,128)(2,1)S(1)}, u32[]{:S(2)}, u32[]{:S(2)}) collective-permute-start(bf16[68,640]{1,0:T(8,128)(2,1)S(1)} %get-tuple-element.141), channel_id=1, source_target_pairs={{0,4},{1,5},{2,6},{3,7},{4,0},{5,1},{6,2},{7,3},{8,12},{9,13},{10,... | collective-permute-start | bytes 261128 | tf_op jit(solution)/shard_map/ppermute | solution.py:383
  63.6 1.4 %collective-permute-start.13 = (bf16[68,640]{1,0:T(8,128)(2,1)S(1)}, bf16[68,640]{1,0:T(8,128)(2,1)S(1)}, u32[]{:S(2)}, u32[]{:S(2)}) collective-permute-start(bf16[68,640]{1,0:T(8,128)(2,1)S(1)} %get-tuple-element.142), channel_id=1, source_target_pairs={{0,6},{1,7},{2,4},{3,5},{4,2},{5,3},{6,0},{7,1},{8,14},{9,15},{10,... | collective-permute-start | bytes 261128 | tf_op jit(solution)/shard_map/ppermute | solution.py:383
  65.0 4.0 %input_grads.6.refs_3_ = f32[512,512]{1,0:T(8,128)S(1)} custom-call(f32[128,512]{1,0:T(8,128)S(1)} %get-tuple-element.176.refs_0_, bf16[512,512]{1,0:T(8,128)(2,1)S(1)} %get-tuple-element.177.refs_1_, bf16[16,512,512]{2,1,0:T(8,128)(2,1)} %get-tuple-element.156.refs_2_, f32[512,512]{1,0:T(8,128)S(1)} %input_grads.5.refs_3_), custom_call_target="tpu_custom_call" | custom-call | flops 2147483648 | bytes 4194304 | tf_op jit(solution)/shard_map/input_grads/pallas_call | solution.py:262
  69.6 2.0 %collective-permute-start.15 = (bf16[20,640]{1,0:T(8,128)(2,1)S(1)}, bf16[20,640]{1,0:T(8,128)(2,1)S(1)}, u32[]{:S(2)}, u32[]{:S(2)}) collective-permute-start(bf16[20,640]{1,0:T(8,128)(2,1)S(1)} %get-tuple-element.152), channel_id=1, source_target_pairs={{0,16},{1,17},{2,18},{3,19},{4,20},{5,21},{6,22},{7,23},{8,24},{9,... | collective-permute-start | bytes 76808 | tf_op jit(solution)/shard_map/ppermute | solution.py:383
  71.7 2.2 %collective-permute-start.16 = (bf16[20,640]{1,0:T(8,128)(2,1)S(1)}, bf16[20,640]{1,0:T(8,128)(2,1)S(1)}, u32[]{:S(2)}, u32[]{:S(2)}) collective-permute-start(bf16[20,640]{1,0:T(8,128)(2,1)S(1)} %get-tuple-element.153), channel_id=1, source_target_pairs={{0,24},{1,25},{2,26},{3,27},{4,28},{5,29},{6,30},{7,31},{8,16},{9,... | collective-permute-start | bytes 76808 | tf_op jit(solution)/shard_map/ppermute | solution.py:383
  73.8 3.3 %input_grads.7 = f32[512,512]{1,0:T(8,128)S(1)} custom-call(f32[128,512]{1,0:T(8,128)S(1)} %get-tuple-element.176.refs_0_, bf16[512,512]{1,0:T(8,128)(2,1)S(1)} %get-tuple-element.177.refs_1_, bf16[16,512,512]{2,1,0:T(8,128)(2,1)} %get-tuple-element.156.refs_2_, f32[512,512]{1,0:T(8,128)S(1)} %input_grads.6.refs_3_, f32[1,512]{1,0:T(1,128)S(1)} %slice.15.refs_4_), custom_call_target="tpu_custom_call" | custom-call | flops 1610612736 | bytes 3145728 | tf_op jit(solution)/shard_map/input_grads/pallas_call | solution.py:262
  78.7 1.4 %collective-permute-done.17 = f32[16,128]{1,0:T(8,128)S(1)} collective-permute-done((f32[16,128]{1,0:T(8,128)S(1)}, f32[16,128]{1,0:T(8,128)S(1)}, u32[]{:S(2)}, u32[]{:S(2)}) %collective-permute-start.17) | collective-permute-done | bytes 8224 | tf_op jit(solution)/shard_map/ppermute | solution.py:383
  80.0 1.3 %collective-permute-start.18 = (f32[16,128]{1,0:T(8,128)S(1)}, f32[16,128]{1,0:T(8,128)S(1)}, u32[]{:S(2)}, u32[]{:S(2)}) collective-permute-start(f32[16,128]{1,0:T(8,128)S(1)} %add.94), channel_id=1, source_target_pairs={{0,2},{1,3},{2,0},{3,1},{4,6},{5,7},{6,4},{7,5},{8,10},{9,11},{10,... | collective-permute-start | bytes 24584 | tf_op jit(solution)/shard_map/ppermute | solution.py:383
  81.3 1.1 %collective-permute-start.19 = (f32[16,128]{1,0:T(8,128)S(1)}, f32[16,128]{1,0:T(8,128)S(1)}, u32[]{:S(2)}, u32[]{:S(2)}) collective-permute-start(f32[16,128]{1,0:T(8,128)S(1)} %add.94), channel_id=1, source_target_pairs={{0,4},{1,5},{2,6},{3,7},{4,0},{5,1},{6,2},{7,3},{8,12},{9,13},{10,... | collective-permute-start | bytes 24584 | tf_op jit(solution)/shard_map/ppermute | solution.py:383
  82.4 1.1 %collective-permute-start.20 = (f32[16,128]{1,0:T(8,128)S(1)}, f32[16,128]{1,0:T(8,128)S(1)}, u32[]{:S(2)}, u32[]{:S(2)}) collective-permute-start(f32[16,128]{1,0:T(8,128)S(1)} %add.94), channel_id=1, source_target_pairs={{0,6},{1,7},{2,4},{3,5},{4,2},{5,3},{6,0},{7,1},{8,14},{9,15},{10,... | collective-permute-start | bytes 24584 | tf_op jit(solution)/shard_map/ppermute | solution.py:383
  83.5 4.0 %input_grads.8.refs_3_ = f32[512,512]{1,0:T(8,128)S(1)} custom-call(f32[128,512]{1,0:T(8,128)S(1)} %get-tuple-element.176.refs_0_, bf16[512,512]{1,0:T(8,128)(2,1)S(1)} %get-tuple-element.177.refs_1_, bf16[16,512,512]{2,1,0:T(8,128)(2,1)} %get-tuple-element.178.refs_2_), custom_call_target="tpu_custom_call" | custom-call | flops 2147483648 | bytes 4194304 | tf_op jit(solution)/shard_map/input_grads/pallas_call | solution.py:262
  87.7 2.7 %collective-permute-start.22 = (f32[16,128]{1,0:T(8,128)S(1)}, f32[16,128]{1,0:T(8,128)S(1)}, u32[]{:S(2)}, u32[]{:S(2)}) collective-permute-start(f32[16,128]{1,0:T(8,128)S(1)} %add_add_fusion.refs_0_), channel_id=1, source_target_pairs={{0,16},{1,17},{2,18},{3,19},{4,20},{5,21},{6,22},{7,23},{8,24},{9,... | collective-permute-start | bytes 24584 | tf_op jit(solution)/shard_map/ppermute | solution.py:383
  90.4 1.6 %collective-permute-start.23 = (f32[16,128]{1,0:T(8,128)S(1)}, f32[16,128]{1,0:T(8,128)S(1)}, u32[]{:S(2)}, u32[]{:S(2)}) collective-permute-start(f32[16,128]{1,0:T(8,128)S(1)} %add_add_fusion.refs_0_), channel_id=1, source_target_pairs={{0,24},{1,25},{2,26},{3,27},{4,28},{5,29},{6,30},{7,31},{8,16},{9,... | collective-permute-start | bytes 24584 | tf_op jit(solution)/shard_map/ppermute | solution.py:383
  92.0 5.0 %input_grads.9 = (f32[512,512]{1,0:T(8,128)}, f32[1,512]{1,0:T(1,128)}) custom-call(f32[128,512]{1,0:T(8,128)S(1)} %get-tuple-element.176.refs_0_, bf16[512,512]{1,0:T(8,128)(2,1)S(1)} %get-tuple-element.177.refs_1_, bf16[16,512,512]{2,1,0:T(8,128)(2,1)} %get-tuple-element.178.refs_2_, f32[512,512]{1,0:T(8,128)S(1)} %input_grads.8.refs_3_, ...), custom_call_target="tpu_custom_call" | custom-call | flops 2147483648 | bytes 4194304 | tf_op jit(solution)/shard_map/input_grads/pallas_call | solution.py:262
  (87 shorter events, 10.7 us)
Async XLA Ops:
  4.2 9.9 %collective-permute-start.3 = (bf16[512,512]{1,0:T(8,128)(2,1)}, bf16[512,512]{1,0:T(8,128)(2,1)S(1)}, u32[]{:S(2)}, u32[]{:S(2)}) collective-permute-start(bf16[512,512]{1,0:T(8,128)(2,1)} %param.12), channel_id=1, source_target_pairs={{0,1},{1,0},{2,3},{3,2},{4,5},{5,4},{6,7},{7,6},{8,9},{9,8},{10,11... | collective-permute-start | bytes 1572872 | tf_op jit(solution)/shard_map/ppermute | solution.py:383
  4.7 6.5 %collective-permute-start.2 = (bf16[16,768]{1,0:T(8,128)(2,1)S(1)}, bf16[16,768]{1,0:T(8,128)(2,1)S(1)}, u32[]{:S(2)}, u32[]{:S(2)}) collective-permute-start(bf16[16,768]{1,0:T(8,128)(2,1)S(1)} %get-tuple-element.112), channel_id=1, source_target_pairs={{0,24},{1,25},{2,26},{3,27},{4,28},{5,29},{6,30},{7,31},{8,16},{9,... | collective-permute-start | bytes 73736 | tf_op jit(solution)/shard_map/ppermute | solution.py:383
  9.4 4.7 %collective-permute-start.1 = (bf16[16,768]{1,0:T(8,128)(2,1)S(1)}, bf16[16,768]{1,0:T(8,128)(2,1)S(1)}, u32[]{:S(2)}, u32[]{:S(2)}) collective-permute-start(bf16[16,768]{1,0:T(8,128)(2,1)S(1)} %get-tuple-element.112), channel_id=1, source_target_pairs={{0,16},{1,17},{2,18},{3,19},{4,20},{5,21},{6,22},{7,23},{8,24},{9,... | collective-permute-start | bytes 73736 | tf_op jit(solution)/shard_map/ppermute | solution.py:383
  9.4 4.7 %collective-permute-start = (bf16[16,768]{1,0:T(8,128)(2,1)S(1)}, bf16[16,768]{1,0:T(8,128)(2,1)S(1)}, u32[]{:S(2)}, u32[]{:S(2)}) collective-permute-start(bf16[16,768]{1,0:T(8,128)(2,1)S(1)} %get-tuple-element.112), channel_id=1, source_target_pairs={{0,8},{1,9},{2,10},{3,11},{4,12},{5,13},{6,14},{7,15},{8,0},{9,1},... | collective-permute-start | bytes 73736 | tf_op jit(solution)/shard_map/ppermute | solution.py:383
  14.2 6.0 %collective-permute-start.7 = (bf16[4,16,768]{2,1,0:T(8,128)(2,1)S(1)}, bf16[4,16,768]{2,1,0:T(8,128)(2,1)S(1)}, u32[]{:S(2)}, u32[]{:S(2)}) collective-permute-start(bf16[4,16,768]{2,1,0:T(8,128)(2,1)S(1)} %pad_maximum_fusion.3), channel_id=1, source_target_pairs={{0,6},{1,7},{2,4},{3,5},{4,2},{5,3},{6,0},{7,1},{8,14},{9,15},{10,... | collective-permute-start | bytes 294920 | tf_op jit(solution)/shard_map/ppermute | solution.py:383
  16.7 4.7 %collective-permute-start.6 = (bf16[4,16,768]{2,1,0:T(8,128)(2,1)S(1)}, bf16[4,16,768]{2,1,0:T(8,128)(2,1)S(1)}, u32[]{:S(2)}, u32[]{:S(2)}) collective-permute-start(bf16[4,16,768]{2,1,0:T(8,128)(2,1)S(1)} %pad_maximum_fusion.3), channel_id=1, source_target_pairs={{0,4},{1,5},{2,6},{3,7},{4,0},{5,1},{6,2},{7,3},{8,12},{9,13},{10,... | collective-permute-start | bytes 294920 | tf_op jit(solution)/shard_map/ppermute | solution.py:383
  17.2 4.6 %collective-permute-start.5 = (bf16[4,16,768]{2,1,0:T(8,128)(2,1)S(1)}, bf16[4,16,768]{2,1,0:T(8,128)(2,1)S(1)}, u32[]{:S(2)}, u32[]{:S(2)}) collective-permute-start(bf16[4,16,768]{2,1,0:T(8,128)(2,1)S(1)} %pad_maximum_fusion.3), channel_id=1, source_target_pairs={{0,2},{1,3},{2,0},{3,1},{4,6},{5,7},{6,4},{7,5},{8,10},{9,11},{10,... | collective-permute-start | bytes 294920 | tf_op jit(solution)/shard_map/ppermute | solution.py:383
  21.9 1.8 %collective-permute-start.8 = (bf16[4,4,16,768]{3,2,0,1:T(8,128)(2,1)S(1)}, bf16[4,4,16,768]{3,2,0,1:T(8,128)(2,1)S(1)}, u32[]{:S(2)}, u32[]{:S(2)}) collective-permute-start(bf16[4,4,16,768]{3,2,0,1:T(8,128)(2,1)S(1)} %pad_maximum_fusion.2), channel_id=1, source_target_pairs={{0,1},{1,0},{2,3},{3,2},{4,5},{5,4},{6,7},{7,6},{8,9},{9,8},{10,11... | collective-permute-start | bytes 1179656 | tf_op jit(solution)/shard_map/ppermute | solution.py:383
  58.7 2.6 %collective-permute-start.9 = (bf16[4,68,640]{2,1,0:T(8,128)(2,1)S(1)}, bf16[4,68,640]{2,1,0:T(8,128)(2,1)S(1)}, u32[]{:S(2)}, u32[]{:S(2)}) collective-permute-start(bf16[4,68,640]{2,1,0:T(8,128)(2,1)S(1)} %fusion.2), channel_id=1, source_target_pairs={{0,1},{1,0},{2,3},{3,2},{4,5},{5,4},{6,7},{7,6},{8,9},{9,8},{10,11... | collective-permute-start | bytes 1044488 | tf_op jit(solution)/shard_map/ppermute | solution.py:383
  58.9 2.4 %collective-permute-start.10 = (f32[1,512]{1,0:T(1,128)S(1)}, f32[1,512]{1,0:T(1,128)S(1)}, u32[]{:S(2)}, u32[]{:S(2)}) collective-permute-start(f32[1,512]{1,0:T(1,128)S(1)} %slice.12), channel_id=1, source_target_pairs={{0,1},{1,0},{2,3},{3,2},{4,5},{5,4},{6,7},{7,6},{8,9},{9,8},{10,11... | collective-permute-start | bytes 6152 | tf_op jit(solution)/shard_map/ppermute | solution.py:383
  61.4 7.6 %collective-permute-start.11 = (bf16[68,640]{1,0:T(8,128)(2,1)S(1)}, bf16[68,640]{1,0:T(8,128)(2,1)S(1)}, u32[]{:S(2)}, u32[]{:S(2)}) collective-permute-start(bf16[68,640]{1,0:T(8,128)(2,1)S(1)} %get-tuple-element.140), channel_id=1, source_target_pairs={{0,2},{1,3},{2,0},{3,1},{4,6},{5,7},{6,4},{7,5},{8,10},{9,11},{10,... | collective-permute-start | bytes 261128 | tf_op jit(solution)/shard_map/ppermute | solution.py:383
  62.4 6.6 %collective-permute-start.12 = (bf16[68,640]{1,0:T(8,128)(2,1)S(1)}, bf16[68,640]{1,0:T(8,128)(2,1)S(1)}, u32[]{:S(2)}, u32[]{:S(2)}) collective-permute-start(bf16[68,640]{1,0:T(8,128)(2,1)S(1)} %get-tuple-element.141), channel_id=1, source_target_pairs={{0,4},{1,5},{2,6},{3,7},{4,0},{5,1},{6,2},{7,3},{8,12},{9,13},{10,... | collective-permute-start | bytes 261128 | tf_op jit(solution)/shard_map/ppermute | solution.py:383
  63.6 5.6 %collective-permute-start.13 = (bf16[68,640]{1,0:T(8,128)(2,1)S(1)}, bf16[68,640]{1,0:T(8,128)(2,1)S(1)}, u32[]{:S(2)}, u32[]{:S(2)}) collective-permute-start(bf16[68,640]{1,0:T(8,128)(2,1)S(1)} %get-tuple-element.142), channel_id=1, source_target_pairs={{0,6},{1,7},{2,4},{3,5},{4,2},{5,3},{6,0},{7,1},{8,14},{9,15},{10,... | collective-permute-start | bytes 261128 | tf_op jit(solution)/shard_map/ppermute | solution.py:383
  69.4 7.8 %collective-permute-start.14 = (bf16[20,640]{1,0:T(8,128)(2,1)S(1)}, bf16[20,640]{1,0:T(8,128)(2,1)S(1)}, u32[]{:S(2)}, u32[]{:S(2)}) collective-permute-start(bf16[20,640]{1,0:T(8,128)(2,1)S(1)} %get-tuple-element.151), channel_id=1, source_target_pairs={{0,8},{1,9},{2,10},{3,11},{4,12},{5,13},{6,14},{7,15},{8,0},{9,1},... | collective-permute-start | bytes 76808 | tf_op jit(solution)/shard_map/ppermute | solution.py:383
  69.6 7.6 %collective-permute-start.15 = (bf16[20,640]{1,0:T(8,128)(2,1)S(1)}, bf16[20,640]{1,0:T(8,128)(2,1)S(1)}, u32[]{:S(2)}, u32[]{:S(2)}) collective-permute-start(bf16[20,640]{1,0:T(8,128)(2,1)S(1)} %get-tuple-element.152), channel_id=1, source_target_pairs={{0,16},{1,17},{2,18},{3,19},{4,20},{5,21},{6,22},{7,23},{8,24},{9,... | collective-permute-start | bytes 76808 | tf_op jit(solution)/shard_map/ppermute | solution.py:383
  71.7 5.7 %collective-permute-start.16 = (bf16[20,640]{1,0:T(8,128)(2,1)S(1)}, bf16[20,640]{1,0:T(8,128)(2,1)S(1)}, u32[]{:S(2)}, u32[]{:S(2)}) collective-permute-start(bf16[20,640]{1,0:T(8,128)(2,1)S(1)} %get-tuple-element.153), channel_id=1, source_target_pairs={{0,24},{1,25},{2,26},{3,27},{4,28},{5,29},{6,30},{7,31},{8,16},{9,... | collective-permute-start | bytes 76808 | tf_op jit(solution)/shard_map/ppermute | solution.py:383
  77.4 14.6 %collective-permute-start.24 = (f32[512,512]{1,0:T(8,128)S(1)}, f32[512,512]{1,0:T(8,128)S(1)}, u32[]{:S(2)}, u32[]{:S(2)}) collective-permute-start(f32[512,512]{1,0:T(8,128)S(1)} %input_grads.7), channel_id=1, source_target_pairs={{0,1},{1,0},{2,3},{3,2},{4,5},{5,4},{6,7},{7,6},{8,9},{9,8},{10,11... | collective-permute-start | bytes 3145736 | tf_op jit(solution)/shard_map/ppermute | solution.py:383
  78.2 1.9 %collective-permute-start.17 = (f32[16,128]{1,0:T(8,128)S(1)}, f32[16,128]{1,0:T(8,128)S(1)}, u32[]{:S(2)}, u32[]{:S(2)}) collective-permute-start(f32[16,128]{1,0:T(8,128)S(1)} %get-tuple-element.161), channel_id=1, source_target_pairs={{0,1},{1,0},{2,3},{3,2},{4,5},{5,4},{6,7},{7,6},{8,9},{9,8},{10,11... | collective-permute-start | bytes 24584 | tf_op jit(solution)/shard_map/ppermute | solution.py:383
  80.0 7.5 %collective-permute-start.18 = (f32[16,128]{1,0:T(8,128)S(1)}, f32[16,128]{1,0:T(8,128)S(1)}, u32[]{:S(2)}, u32[]{:S(2)}) collective-permute-start(f32[16,128]{1,0:T(8,128)S(1)} %add.94), channel_id=1, source_target_pairs={{0,2},{1,3},{2,0},{3,1},{4,6},{5,7},{6,4},{7,5},{8,10},{9,11},{10,... | collective-permute-start | bytes 24584 | tf_op jit(solution)/shard_map/ppermute | solution.py:383
  81.3 6.2 %collective-permute-start.19 = (f32[16,128]{1,0:T(8,128)S(1)}, f32[16,128]{1,0:T(8,128)S(1)}, u32[]{:S(2)}, u32[]{:S(2)}) collective-permute-start(f32[16,128]{1,0:T(8,128)S(1)} %add.94), channel_id=1, source_target_pairs={{0,4},{1,5},{2,6},{3,7},{4,0},{5,1},{6,2},{7,3},{8,12},{9,13},{10,... | collective-permute-start | bytes 24584 | tf_op jit(solution)/shard_map/ppermute | solution.py:383
  82.4 5.1 %collective-permute-start.20 = (f32[16,128]{1,0:T(8,128)S(1)}, f32[16,128]{1,0:T(8,128)S(1)}, u32[]{:S(2)}, u32[]{:S(2)}) collective-permute-start(f32[16,128]{1,0:T(8,128)S(1)} %add.94), channel_id=1, source_target_pairs={{0,6},{1,7},{2,4},{3,5},{4,2},{5,3},{6,0},{7,1},{8,14},{9,15},{10,... | collective-permute-start | bytes 24584 | tf_op jit(solution)/shard_map/ppermute | solution.py:383
  87.5 9.5 %collective-permute-start.21 = (f32[16,128]{1,0:T(8,128)S(1)}, f32[16,128]{1,0:T(8,128)S(1)}, u32[]{:S(2)}, u32[]{:S(2)}) collective-permute-start(f32[16,128]{1,0:T(8,128)S(1)} %add_add_fusion.refs_0_), channel_id=1, source_target_pairs={{0,8},{1,9},{2,10},{3,11},{4,12},{5,13},{6,14},{7,15},{8,0},{9,1},... | collective-permute-start | bytes 24584 | tf_op jit(solution)/shard_map/ppermute | solution.py:383
  87.7 9.4 %collective-permute-start.22 = (f32[16,128]{1,0:T(8,128)S(1)}, f32[16,128]{1,0:T(8,128)S(1)}, u32[]{:S(2)}, u32[]{:S(2)}) collective-permute-start(f32[16,128]{1,0:T(8,128)S(1)} %add_add_fusion.refs_0_), channel_id=1, source_target_pairs={{0,16},{1,17},{2,18},{3,19},{4,20},{5,21},{6,22},{7,23},{8,24},{9,... | collective-permute-start | bytes 24584 | tf_op jit(solution)/shard_map/ppermute | solution.py:383
  90.4 6.7 %collective-permute-start.23 = (f32[16,128]{1,0:T(8,128)S(1)}, f32[16,128]{1,0:T(8,128)S(1)}, u32[]{:S(2)}, u32[]{:S(2)}) collective-permute-start(f32[16,128]{1,0:T(8,128)S(1)} %add_add_fusion.refs_0_), channel_id=1, source_target_pairs={{0,24},{1,25},{2,26},{3,27},{4,28},{5,29},{6,30},{7,31},{8,16},{9,... | collective-permute-start | bytes 24584 | tf_op jit(solution)/shard_map/ppermute | solution.py:383
  (14 other events, 76.5 us)

commit v10 on v9

--- a/solution.py
+++ b/solution.py
@@ -55,7 +55,6 @@
         out_shape=(shape((own, D + LANES + L), BF16), shape(cot.shape)),
         in_specs=[SMEM, VMEM, VMEM, VMEM, VMEM],
         out_specs=(VMEM, VMEM),
-        compiler_params=SMALL,
         name="pack_weights",
     )(counts, matrix, adapters_t, heads, cot)
 
@@ -484,7 +483,7 @@
         wide, last, dp_groups[0][0] // n_member, states)
 
     rounds = [(1, 2)] + chip_groups[::-1] + dp_groups[::-1]
-    plan = {1: backward(0, 8), len(rounds) - 1: backward(8, 8, q=q_own, came=(ig_came, preds, pred_came, counts))}
+    plan = {0: backward(0, 2), 1: backward(2, 6), len(rounds) - 1: backward(8, 8, q=q_own, came=(ig_came, preds, pred_came, counts))}
     pending, acc = [sums], ()
     for step, (low, size) in enumerate(rounds):
         sums = pending[0]

time: 98.2 us -> 97.6 us (level)
  local copies, waits for them, and re-layouts: 3.2 us -> 0.34 us
  Pallas kernels: 54.5 us -> 57.1 us
  waiting for transfers between devices: 10.4 us -> 9.31 us
    unnamed x26 -> x20, local copies, waits for them, and re-layouts: 2.92 us -> 0.06 us
    pallas_call x1, Pallas kernels: 0.08 us -> 1.47 us  [pack_call(): pl.pallas_call(pack_kernel, out_shape=(shape((own, D + LANES + L), BF16),...]
    pallas_call x5 -> x6, Pallas kernels: 18.2 us -> 19.5 us  [back_call(): pl.pallas_call(functools.partial(back_kernel, start=start, first=acc is N...]
    ppermute x25, waiting for transfers between devices: 10.4 us -> 9.31 us  [swap(): return lax.ppermute(value, AXES, [(i, i ^ mask) for i in range(total)])]
  transfers between devices with their start and end apart: 25 -> 25, of which waited for: 9 -> 9; matrix products, arithmetic and copies ran while one was open for 1% -> 1% of each run, Pallas kernels for 19% -> 21%
where the time goes in v10:
time: 97.6 us; the launch traced here: 97.3 us
  Pallas kernels  57.1 us (59%)
  starting transfers between devices  26.4 us (27%)
  waiting for transfers between devices  9.31 us (10%)
  other arithmetic  2.32 us (2%)
  between operations  1.76 us (2%)
    pallas_call x1, Pallas kernels, grad_call(): pl.pallas_call(functools.partial(grad_kernel, own=own), grid=(members //...  34.7 us
    ppermute x25, starting transfers between devices, swap(): return lax.ppermute(value, AXES, [(i, i ^ mask) for i in range(total)])  26.4 us
    pallas_call x6, Pallas kernels, back_call(): pl.pallas_call(functools.partial(back_kernel, start=start, first=acc is N...  19.5 us
    ppermute x25, waiting for transfers between devices, swap(): return lax.ppermute(value, AXES, [(i, i ^ mask) for i in range(total)])  9.31 us
  transfers between devices with their start and end apart: 25, of which 9 were waited for; matrix products, arithmetic and copies ran while one was open for 1% of the time, Pallas kernels for 21%

profile of v10, /device:TPU:0, one launch (start us, length us, event | category | flops | bytes accessed | tf_op | source)
XLA Modules:
  0.0 97.3 jit_solution(11825877208498799028)
XLA Ops:
  1.3 1.5 %pack_weights.1 = (bf16[16,768]{1,0:T(8,128)(2,1)}, f32[1,512]{1,0:T(1,128)}) custom-call(s32[1]{0:T(128)S(6)} %copy.32.count_ref.refs_8_, f32[16,512]{1,0:T(8,128)} %refs_4_.3, f32[3,16,32]{2,1,0:T(8,128)} %bitcast.61, f32[4,512]{1,0:T(4,128)} %refs_6_.3, f32[1,512]{1,0:T(1,128)} %bitcast.68), custom_call_target="tpu_custom_call" | custom-call | tf_op jit(solution)/shard_map/pack_weights/pallas_call | solution.py:53
  3.2 4.7 %collective-permute-start.2 = (bf16[16,768]{1,0:T(8,128)(2,1)}, bf16[16,768]{1,0:T(8,128)(2,1)S(1)}, u32[]{:S(2)}, u32[]{:S(2)}) collective-permute-start(bf16[16,768]{1,0:T(8,128)(2,1)} %get-tuple-element.119), channel_id=1, source_target_pairs={{0,24},{1,25},{2,26},{3,27},{4,28},{5,29},{6,30},{7,31},{8,16},{9,... | collective-permute-start | bytes 73736 | tf_op jit(solution)/shard_map/ppermute | solution.py:382
  8.5 1.4 %collective-permute-done.4 = f32[1,512]{1,0:T(1,128)S(1)} collective-permute-done((f32[1,512]{1,0:T(1,128)}, f32[1,512]{1,0:T(1,128)S(1)}, u32[]{:S(2)}, u32[]{:S(2)}) %collective-permute-start.4) | collective-permute-done | bytes 2080 | tf_op jit(solution)/shard_map/ppermute | solution.py:382
  9.9 2.9 %collective-permute-done.1 = bf16[16,768]{1,0:T(8,128)(2,1)S(1)} collective-permute-done((bf16[16,768]{1,0:T(8,128)(2,1)}, bf16[16,768]{1,0:T(8,128)(2,1)S(1)}, u32[]{:S(2)}, u32[]{:S(2)}) %collective-permute-start.1) | collective-permute-done | bytes 24608 | tf_op jit(solution)/shard_map/ppermute | solution.py:382
  13.6 2.5 %collective-permute-start.7 = (bf16[4,16,768]{2,1,0:T(8,128)(2,1)S(1)}, bf16[4,16,768]{2,1,0:T(8,128)(2,1)S(1)}, u32[]{:S(2)}, u32[]{:S(2)}) collective-permute-start(bf16[4,16,768]{2,1,0:T(8,128)(2,1)S(1)} %pad_maximum_fusion.3), channel_id=1, source_target_pairs={{0,6},{1,7},{2,4},{3,5},{4,2},{5,3},{6,0},{7,1},{8,14},{9,15},{10,... | collective-permute-start | bytes 294920 | tf_op jit(solution)/shard_map/ppermute | solution.py:382
  17.2 1.1 %pad_maximum_fusion.x_ref = bf16[1024,512]{1,0:T(8,128)(2,1)S(1)} fusion(bf16[512,512]{1,0:T(8,128)(2,1)S(1)} %collective-permute-done.3, bf16[512,512]{1,0:T(8,128)(2,1)} %param.12), kind=kLoop, calls=%fused_computation | loop fusion | flops 2097152 | bytes 2097152 | tf_op jit(solution)/shard_map/concatenate | solution.py:395
  18.3 1.3 %collective-permute-done.7 = bf16[4,16,768]{2,1,0:T(8,128)(2,1)S(1)} collective-permute-done((bf16[4,16,768]{2,1,0:T(8,128)(2,1)S(1)}, bf16[4,16,768]{2,1,0:T(8,128)(2,1)S(1)}, u32[]{:S(2)}, u32[]{:S(2)}) %collective-permute-start.7) | collective-permute-done | bytes 98336 | tf_op jit(solution)/shard_map/ppermute | solution.py:382
  19.6 1.1 %collective-permute-done.6 = bf16[4,16,768]{2,1,0:T(8,128)(2,1)S(1)} collective-permute-done((bf16[4,16,768]{2,1,0:T(8,128)(2,1)S(1)}, bf16[4,16,768]{2,1,0:T(8,128)(2,1)S(1)}, u32[]{:S(2)}, u32[]{:S(2)}) %collective-permute-start.6) | collective-permute-done | bytes 98336 | tf_op jit(solution)/shard_map/ppermute | solution.py:382
  21.5 1.7 %collective-permute-done.8 = bf16[4,4,16,768]{3,2,0,1:T(8,128)(2,1)S(1)} collective-permute-done((bf16[4,4,16,768]{3,2,0,1:T(8,128)(2,1)S(1)}, bf16[4,4,16,768]{3,2,0,1:T(8,128)(2,1)S(1)}, u32[]{:S(2)}, u32[]{:S(2)}) %collective-permute-start.8) | collective-permute-done | bytes 393248 | tf_op jit(solution)/shard_map/ppermute | solution.py:382
  23.4 34.7 %member_grads.1 = (f32[256,640]{1,0:T(8,128)S(1)}, bf16[256,640]{1,0:T(8,128)(2,1)S(1)}, f32[32,512]{1,0:T(8,128)S(1)}, f32[2,512]{1,0:T(2,128)S(1)}, f32[128,51...) custom-call(bf16[1024,512]{1,0:T(8,128)(2,1)S(1)} %pad_maximum_fusio, ...), custom_call_target="tpu_custom_call" | custom-call | flops 34359738368 | bytes 16777216 | tf_op jit(solution)/shard_map/member_grads/pallas_call | solution.py:189
  58.8 1.9 %input_grads.6.refs_3_ = f32[512,512]{1,0:T(8,128)S(1)} custom-call(f32[128,512]{1,0:T(8,128)S(1)} %get-tuple-element.190.refs_0_, bf16[512,512]{1,0:T(8,128)(2,1)S(1)} %get-tuple-element.191.refs_1_, bf16[16,512,512]{2,1,0:T(8,128)(2,1)} %get-tuple-element.163.refs_2_), custom_call_target="tpu_custom_call" | custom-call | flops 536870912 | bytes 1048576 | tf_op jit(solution)/shard_map/input_grads/pallas_call | solution.py:261
  61.9 1.2 %collective-permute-start.12 = (bf16[68,640]{1,0:T(8,128)(2,1)S(1)}, bf16[68,640]{1,0:T(8,128)(2,1)S(1)}, u32[]{:S(2)}, u32[]{:S(2)}) collective-permute-start(bf16[68,640]{1,0:T(8,128)(2,1)S(1)} %get-tuple-element.148), channel_id=1, source_target_pairs={{0,4},{1,5},{2,6},{3,7},{4,0},{5,1},{6,2},{7,3},{8,12},{9,13},{10,... | collective-permute-start | bytes 261128 | tf_op jit(solution)/shard_map/ppermute | solution.py:382
  63.0 1.4 %collective-permute-start.13 = (bf16[68,640]{1,0:T(8,128)(2,1)S(1)}, bf16[68,640]{1,0:T(8,128)(2,1)S(1)}, u32[]{:S(2)}, u32[]{:S(2)}) collective-permute-start(bf16[68,640]{1,0:T(8,128)(2,1)S(1)} %get-tuple-element.149), channel_id=1, source_target_pairs={{0,6},{1,7},{2,4},{3,5},{4,2},{5,3},{6,0},{7,1},{8,14},{9,15},{10,... | collective-permute-start | bytes 261128 | tf_op jit(solution)/shard_map/ppermute | solution.py:382
  64.4 4.0 %input_grads.7.refs_3_ = f32[512,512]{1,0:T(8,128)S(1)} custom-call(f32[128,512]{1,0:T(8,128)S(1)} %get-tuple-element.190.refs_0_, bf16[512,512]{1,0:T(8,128)(2,1)S(1)} %get-tuple-element.191.refs_1_, bf16[16,512,512]{2,1,0:T(8,128)(2,1)} %get-tuple-element.163.refs_2_, f32[512,512]{1,0:T(8,128)S(1)} %input_grads.6.refs_3_), custom_call_target="tpu_custom_call" | custom-call | flops 2147483648 | bytes 4194304 | tf_op jit(solution)/shard_map/input_grads/pallas_call | solution.py:261
  69.1 2.0 %collective-permute-start.15 = (bf16[20,640]{1,0:T(8,128)(2,1)S(1)}, bf16[20,640]{1,0:T(8,128)(2,1)S(1)}, u32[]{:S(2)}, u32[]{:S(2)}) collective-permute-start(bf16[20,640]{1,0:T(8,128)(2,1)S(1)} %get-tuple-element.159), channel_id=1, source_target_pairs={{0,16},{1,17},{2,18},{3,19},{4,20},{5,21},{6,22},{7,23},{8,24},{9,... | collective-permute-start | bytes 76808 | tf_op jit(solution)/shard_map/ppermute | solution.py:382
  71.1 2.2 %collective-permute-start.16 = (bf16[20,640]{1,0:T(8,128)(2,1)S(1)}, bf16[20,640]{1,0:T(8,128)(2,1)S(1)}, u32[]{:S(2)}, u32[]{:S(2)}) collective-permute-start(bf16[20,640]{1,0:T(8,128)(2,1)S(1)} %get-tuple-element.160), channel_id=1, source_target_pairs={{0,24},{1,25},{2,26},{3,27},{4,28},{5,29},{6,30},{7,31},{8,16},{9,... | collective-permute-start | bytes 76808 | tf_op jit(solution)/shard_map/ppermute | solution.py:382
  73.3 3.3 %input_grads.8 = f32[512,512]{1,0:T(8,128)S(1)} custom-call(f32[128,512]{1,0:T(8,128)S(1)} %get-tuple-element.190.refs_0_, bf16[512,512]{1,0:T(8,128)(2,1)S(1)} %get-tuple-element.191.refs_1_, bf16[16,512,512]{2,1,0:T(8,128)(2,1)} %get-tuple-element.163.refs_2_, f32[512,512]{1,0:T(8,128)S(1)} %input_grads.7.refs_3_, f32[1,512]{1,0:T(1,128)S(1)} %slice.15.refs_4_), custom_call_target="tpu_custom_call" | custom-call | flops 1610612736 | bytes 3145728 | tf_op jit(solution)/shard_map/input_grads/pallas_call | solution.py:261
  78.1 1.9 %input_grads.9.refs_3_ = f32[512,512]{1,0:T(8,128)S(1)} custom-call(f32[128,512]{1,0:T(8,128)S(1)} %get-tuple-element.190.refs_0_, bf16[512,512]{1,0:T(8,128)(2,1)S(1)} %get-tuple-element.191.refs_1_, bf16[16,512,512]{2,1,0:T(8,128)(2,1)} %get-tuple-element.192.refs_2_), custom_call_target="tpu_custom_call" | custom-call | flops 536870912 | bytes 1048576 | tf_op jit(solution)/shard_map/input_grads/pallas_call | solution.py:261
  80.1 1.3 %collective-permute-start.18 = (f32[16,128]{1,0:T(8,128)S(1)}, f32[16,128]{1,0:T(8,128)S(1)}, u32[]{:S(2)}, u32[]{:S(2)}) collective-permute-start(f32[16,128]{1,0:T(8,128)S(1)} %add.94), channel_id=1, source_target_pairs={{0,2},{1,3},{2,0},{3,1},{4,6},{5,7},{6,4},{7,5},{8,10},{9,11},{10,... | collective-permute-start | bytes 24584 | tf_op jit(solution)/shard_map/ppermute | solution.py:382
  82.5 1.1 %collective-permute-start.20 = (f32[16,128]{1,0:T(8,128)S(1)}, f32[16,128]{1,0:T(8,128)S(1)}, u32[]{:S(2)}, u32[]{:S(2)}) collective-permute-start(f32[16,128]{1,0:T(8,128)S(1)} %add.94), channel_id=1, source_target_pairs={{0,6},{1,7},{2,4},{3,5},{4,2},{5,3},{6,0},{7,1},{8,14},{9,15},{10,... | collective-permute-start | bytes 24584 | tf_op jit(solution)/shard_map/ppermute | solution.py:382
  83.6 3.3 %input_grads.10.refs_3_ = f32[512,512]{1,0:T(8,128)S(1)} custom-call(f32[128,512]{1,0:T(8,128)S(1)} %get-tuple-element.190.refs_0_, bf16[512,512]{1,0:T(8,128)(2,1)S(1)} %get-tuple-element.191.refs_1_, bf16[16,512,512]{2,1,0:T(8,128)(2,1)} %get-tuple-element.192.refs_2_, f32[512,512]{1,0:T(8,128)S(1)} %input_grads.9.refs_3_), custom_call_target="tpu_custom_call" | custom-call | flops 1610612736 | bytes 3145728 | tf_op jit(solution)/shard_map/input_grads/pallas_call | solution.py:261
  87.2 2.7 %collective-permute-start.22 = (f32[16,128]{1,0:T(8,128)S(1)}, f32[16,128]{1,0:T(8,128)S(1)}, u32[]{:S(2)}, u32[]{:S(2)}) collective-permute-start(f32[16,128]{1,0:T(8,128)S(1)} %add_add_fusion.refs_0_), channel_id=1, source_target_pairs={{0,16},{1,17},{2,18},{3,19},{4,20},{5,21},{6,22},{7,23},{8,24},{9,... | collective-permute-start | bytes 24584 | tf_op jit(solution)/shard_map/ppermute | solution.py:382
  89.9 1.6 %collective-permute-start.23 = (f32[16,128]{1,0:T(8,128)S(1)}, f32[16,128]{1,0:T(8,128)S(1)}, u32[]{:S(2)}, u32[]{:S(2)}) collective-permute-start(f32[16,128]{1,0:T(8,128)S(1)} %add_add_fusion.refs_0_), channel_id=1, source_target_pairs={{0,24},{1,25},{2,26},{3,27},{4,28},{5,29},{6,30},{7,31},{8,16},{9,... | collective-permute-start | bytes 24584 | tf_op jit(solution)/shard_map/ppermute | solution.py:382
  91.4 5.0 %input_grads.11 = (f32[512,512]{1,0:T(8,128)}, f32[1,512]{1,0:T(1,128)}) custom-call(f32[128,512]{1,0:T(8,128)S(1)} %get-tuple-element.190.refs_0_, bf16[512,512]{1,0:T(8,128)(2,1)S(1)} %get-tuple-element.191.refs_1_, bf16[16,512,512]{2,1,0:T(8,128)(2,1)} %get-tuple-element.192.refs_2_, f32[512,512]{1,0:T(8,128)S(1)} %input_grads.10.refs_3_, ...), custom_call_target="tpu_custom_call" | custom-call | flops 2147483648 | bytes 4194304 | tf_op jit(solution)/shard_map/input_grads/pallas_call | solution.py:261
  (82 shorter events, 9.6 us)
Async XLA Ops:
  2.8 10.1 %collective-permute-start.3 = (bf16[512,512]{1,0:T(8,128)(2,1)}, bf16[512,512]{1,0:T(8,128)(2,1)S(1)}, u32[]{:S(2)}, u32[]{:S(2)}) collective-permute-start(bf16[512,512]{1,0:T(8,128)(2,1)} %param.12), channel_id=1, source_target_pairs={{0,1},{1,0},{2,3},{3,2},{4,5},{5,4},{6,7},{7,6},{8,9},{9,8},{10,11... | collective-permute-start | bytes 1572872 | tf_op jit(solution)/shard_map/ppermute | solution.py:382
  3.2 6.7 %collective-permute-start.2 = (bf16[16,768]{1,0:T(8,128)(2,1)}, bf16[16,768]{1,0:T(8,128)(2,1)S(1)}, u32[]{:S(2)}, u32[]{:S(2)}) collective-permute-start(bf16[16,768]{1,0:T(8,128)(2,1)} %get-tuple-element.119), channel_id=1, source_target_pairs={{0,24},{1,25},{2,26},{3,27},{4,28},{5,29},{6,30},{7,31},{8,16},{9,... | collective-permute-start | bytes 73736 | tf_op jit(solution)/shard_map/ppermute | solution.py:382
  7.9 4.9 %collective-permute-start.1 = (bf16[16,768]{1,0:T(8,128)(2,1)}, bf16[16,768]{1,0:T(8,128)(2,1)S(1)}, u32[]{:S(2)}, u32[]{:S(2)}) collective-permute-start(bf16[16,768]{1,0:T(8,128)(2,1)} %get-tuple-element.119), channel_id=1, source_target_pairs={{0,16},{1,17},{2,18},{3,19},{4,20},{5,21},{6,22},{7,23},{8,24},{9,... | collective-permute-start | bytes 73736 | tf_op jit(solution)/shard_map/ppermute | solution.py:382
  7.9 4.9 %collective-permute-start = (bf16[16,768]{1,0:T(8,128)(2,1)}, bf16[16,768]{1,0:T(8,128)(2,1)S(1)}, u32[]{:S(2)}, u32[]{:S(2)}) collective-permute-start(bf16[16,768]{1,0:T(8,128)(2,1)} %get-tuple-element.119), channel_id=1, source_target_pairs={{0,8},{1,9},{2,10},{3,11},{4,12},{5,13},{6,14},{7,15},{8,0},{9,1},... | collective-permute-start | bytes 73736 | tf_op jit(solution)/shard_map/ppermute | solution.py:382
  13.6 6.0 %collective-permute-start.7 = (bf16[4,16,768]{2,1,0:T(8,128)(2,1)S(1)}, bf16[4,16,768]{2,1,0:T(8,128)(2,1)S(1)}, u32[]{:S(2)}, u32[]{:S(2)}) collective-permute-start(bf16[4,16,768]{2,1,0:T(8,128)(2,1)S(1)} %pad_maximum_fusion.3), channel_id=1, source_target_pairs={{0,6},{1,7},{2,4},{3,5},{4,2},{5,3},{6,0},{7,1},{8,14},{9,15},{10,... | collective-permute-start | bytes 294920 | tf_op jit(solution)/shard_map/ppermute | solution.py:382
  16.1 4.7 %collective-permute-start.6 = (bf16[4,16,768]{2,1,0:T(8,128)(2,1)S(1)}, bf16[4,16,768]{2,1,0:T(8,128)(2,1)S(1)}, u32[]{:S(2)}, u32[]{:S(2)}) collective-permute-start(bf16[4,16,768]{2,1,0:T(8,128)(2,1)S(1)} %pad_maximum_fusion.3), channel_id=1, source_target_pairs={{0,4},{1,5},{2,6},{3,7},{4,0},{5,1},{6,2},{7,3},{8,12},{9,13},{10,... | collective-permute-start | bytes 294920 | tf_op jit(solution)/shard_map/ppermute | solution.py:382
  16.6 4.6 %collective-permute-start.5 = (bf16[4,16,768]{2,1,0:T(8,128)(2,1)S(1)}, bf16[4,16,768]{2,1,0:T(8,128)(2,1)S(1)}, u32[]{:S(2)}, u32[]{:S(2)}) collective-permute-start(bf16[4,16,768]{2,1,0:T(8,128)(2,1)S(1)} %pad_maximum_fusion.3), channel_id=1, source_target_pairs={{0,2},{1,3},{2,0},{3,1},{4,6},{5,7},{6,4},{7,5},{8,10},{9,11},{10,... | collective-permute-start | bytes 294920 | tf_op jit(solution)/shard_map/ppermute | solution.py:382
  21.4 1.8 %collective-permute-start.8 = (bf16[4,4,16,768]{3,2,0,1:T(8,128)(2,1)S(1)}, bf16[4,4,16,768]{3,2,0,1:T(8,128)(2,1)S(1)}, u32[]{:S(2)}, u32[]{:S(2)}) collective-permute-start(bf16[4,4,16,768]{3,2,0,1:T(8,128)(2,1)S(1)} %pad_maximum_fusion.2), channel_id=1, source_target_pairs={{0,1},{1,0},{2,3},{3,2},{4,5},{5,4},{6,7},{7,6},{8,9},{9,8},{10,11... | collective-permute-start | bytes 1179656 | tf_op jit(solution)/shard_map/ppermute | solution.py:382
  58.2 2.6 %collective-permute-start.9 = (bf16[4,68,640]{2,1,0:T(8,128)(2,1)S(1)}, bf16[4,68,640]{2,1,0:T(8,128)(2,1)S(1)}, u32[]{:S(2)}, u32[]{:S(2)}) collective-permute-start(bf16[4,68,640]{2,1,0:T(8,128)(2,1)S(1)} %fusion.2), channel_id=1, source_target_pairs={{0,1},{1,0},{2,3},{3,2},{4,5},{5,4},{6,7},{7,6},{8,9},{9,8},{10,11... | collective-permute-start | bytes 1044488 | tf_op jit(solution)/shard_map/ppermute | solution.py:382
  58.4 2.4 %collective-permute-start.10 = (f32[1,512]{1,0:T(1,128)S(1)}, f32[1,512]{1,0:T(1,128)S(1)}, u32[]{:S(2)}, u32[]{:S(2)}) collective-permute-start(f32[1,512]{1,0:T(1,128)S(1)} %slice.12), channel_id=1, source_target_pairs={{0,1},{1,0},{2,3},{3,2},{4,5},{5,4},{6,7},{7,6},{8,9},{9,8},{10,11... | collective-permute-start | bytes 6152 | tf_op jit(solution)/shard_map/ppermute | solution.py:382
  60.9 7.6 %collective-permute-start.11 = (bf16[68,640]{1,0:T(8,128)(2,1)S(1)}, bf16[68,640]{1,0:T(8,128)(2,1)S(1)}, u32[]{:S(2)}, u32[]{:S(2)}) collective-permute-start(bf16[68,640]{1,0:T(8,128)(2,1)S(1)} %get-tuple-element.147), channel_id=1, source_target_pairs={{0,2},{1,3},{2,0},{3,1},{4,6},{5,7},{6,4},{7,5},{8,10},{9,11},{10,... | collective-permute-start | bytes 261128 | tf_op jit(solution)/shard_map/ppermute | solution.py:382
  61.9 6.6 %collective-permute-start.12 = (bf16[68,640]{1,0:T(8,128)(2,1)S(1)}, bf16[68,640]{1,0:T(8,128)(2,1)S(1)}, u32[]{:S(2)}, u32[]{:S(2)}) collective-permute-start(bf16[68,640]{1,0:T(8,128)(2,1)S(1)} %get-tuple-element.148), channel_id=1, source_target_pairs={{0,4},{1,5},{2,6},{3,7},{4,0},{5,1},{6,2},{7,3},{8,12},{9,13},{10,... | collective-permute-start | bytes 261128 | tf_op jit(solution)/shard_map/ppermute | solution.py:382
  63.0 5.6 %collective-permute-start.13 = (bf16[68,640]{1,0:T(8,128)(2,1)S(1)}, bf16[68,640]{1,0:T(8,128)(2,1)S(1)}, u32[]{:S(2)}, u32[]{:S(2)}) collective-permute-start(bf16[68,640]{1,0:T(8,128)(2,1)S(1)} %get-tuple-element.149), channel_id=1, source_target_pairs={{0,6},{1,7},{2,4},{3,5},{4,2},{5,3},{6,0},{7,1},{8,14},{9,15},{10,... | collective-permute-start | bytes 261128 | tf_op jit(solution)/shard_map/ppermute | solution.py:382
  68.8 7.8 %collective-permute-start.14 = (bf16[20,640]{1,0:T(8,128)(2,1)S(1)}, bf16[20,640]{1,0:T(8,128)(2,1)S(1)}, u32[]{:S(2)}, u32[]{:S(2)}) collective-permute-start(bf16[20,640]{1,0:T(8,128)(2,1)S(1)} %get-tuple-element.158), channel_id=1, source_target_pairs={{0,8},{1,9},{2,10},{3,11},{4,12},{5,13},{6,14},{7,15},{8,0},{9,1},... | collective-permute-start | bytes 76808 | tf_op jit(solution)/shard_map/ppermute | solution.py:382
  69.1 7.6 %collective-permute-start.15 = (bf16[20,640]{1,0:T(8,128)(2,1)S(1)}, bf16[20,640]{1,0:T(8,128)(2,1)S(1)}, u32[]{:S(2)}, u32[]{:S(2)}) collective-permute-start(bf16[20,640]{1,0:T(8,128)(2,1)S(1)} %get-tuple-element.159), channel_id=1, source_target_pairs={{0,16},{1,17},{2,18},{3,19},{4,20},{5,21},{6,22},{7,23},{8,24},{9,... | collective-permute-start | bytes 76808 | tf_op jit(solution)/shard_map/ppermute | solution.py:382
  71.1 5.7 %collective-permute-start.16 = (bf16[20,640]{1,0:T(8,128)(2,1)S(1)}, bf16[20,640]{1,0:T(8,128)(2,1)S(1)}, u32[]{:S(2)}, u32[]{:S(2)}) collective-permute-start(bf16[20,640]{1,0:T(8,128)(2,1)S(1)} %get-tuple-element.160), channel_id=1, source_target_pairs={{0,24},{1,25},{2,26},{3,27},{4,28},{5,29},{6,30},{7,31},{8,16},{9,... | collective-permute-start | bytes 76808 | tf_op jit(solution)/shard_map/ppermute | solution.py:382
  76.8 14.6 %collective-permute-start.24 = (f32[512,512]{1,0:T(8,128)S(1)}, f32[512,512]{1,0:T(8,128)S(1)}, u32[]{:S(2)}, u32[]{:S(2)}) collective-permute-start(f32[512,512]{1,0:T(8,128)S(1)} %input_grads.8), channel_id=1, source_target_pairs={{0,1},{1,0},{2,3},{3,2},{4,5},{5,4},{6,7},{7,6},{8,9},{9,8},{10,11... | collective-permute-start | bytes 3145736 | tf_op jit(solution)/shard_map/ppermute | solution.py:382
  77.6 2.4 %collective-permute-start.17 = (f32[16,128]{1,0:T(8,128)S(1)}, f32[16,128]{1,0:T(8,128)S(1)}, u32[]{:S(2)}, u32[]{:S(2)}) collective-permute-start(f32[16,128]{1,0:T(8,128)S(1)} %get-tuple-element.170), channel_id=1, source_target_pairs={{0,1},{1,0},{2,3},{3,2},{4,5},{5,4},{6,7},{7,6},{8,9},{9,8},{10,11... | collective-permute-start | bytes 24584 | tf_op jit(solution)/shard_map/ppermute | solution.py:382
  80.1 6.9 %collective-permute-start.18 = (f32[16,128]{1,0:T(8,128)S(1)}, f32[16,128]{1,0:T(8,128)S(1)}, u32[]{:S(2)}, u32[]{:S(2)}) collective-permute-start(f32[16,128]{1,0:T(8,128)S(1)} %add.94), channel_id=1, source_target_pairs={{0,2},{1,3},{2,0},{3,1},{4,6},{5,7},{6,4},{7,5},{8,10},{9,11},{10,... | collective-permute-start | bytes 24584 | tf_op jit(solution)/shard_map/ppermute | solution.py:382
  81.4 5.5 %collective-permute-start.19 = (f32[16,128]{1,0:T(8,128)S(1)}, f32[16,128]{1,0:T(8,128)S(1)}, u32[]{:S(2)}, u32[]{:S(2)}) collective-permute-start(f32[16,128]{1,0:T(8,128)S(1)} %add.94), channel_id=1, source_target_pairs={{0,4},{1,5},{2,6},{3,7},{4,0},{5,1},{6,2},{7,3},{8,12},{9,13},{10,... | collective-permute-start | bytes 24584 | tf_op jit(solution)/shard_map/ppermute | solution.py:382
  82.5 4.5 %collective-permute-start.20 = (f32[16,128]{1,0:T(8,128)S(1)}, f32[16,128]{1,0:T(8,128)S(1)}, u32[]{:S(2)}, u32[]{:S(2)}) collective-permute-start(f32[16,128]{1,0:T(8,128)S(1)} %add.94), channel_id=1, source_target_pairs={{0,6},{1,7},{2,4},{3,5},{4,2},{5,3},{6,0},{7,1},{8,14},{9,15},{10,... | collective-permute-start | bytes 24584 | tf_op jit(solution)/shard_map/ppermute | solution.py:382
  87.0 9.4 %collective-permute-start.21 = (f32[16,128]{1,0:T(8,128)S(1)}, f32[16,128]{1,0:T(8,128)S(1)}, u32[]{:S(2)}, u32[]{:S(2)}) collective-permute-start(f32[16,128]{1,0:T(8,128)S(1)} %add_add_fusion.refs_0_), channel_id=1, source_target_pairs={{0,8},{1,9},{2,10},{3,11},{4,12},{5,13},{6,14},{7,15},{8,0},{9,1},... | collective-permute-start | bytes 24584 | tf_op jit(solution)/shard_map/ppermute | solution.py:382
  87.2 9.3 %collective-permute-start.22 = (f32[16,128]{1,0:T(8,128)S(1)}, f32[16,128]{1,0:T(8,128)S(1)}, u32[]{:S(2)}, u32[]{:S(2)}) collective-permute-start(f32[16,128]{1,0:T(8,128)S(1)} %add_add_fusion.refs_0_), channel_id=1, source_target_pairs={{0,16},{1,17},{2,18},{3,19},{4,20},{5,21},{6,22},{7,23},{8,24},{9,... | collective-permute-start | bytes 24584 | tf_op jit(solution)/shard_map/ppermute | solution.py:382
  89.9 6.6 %collective-permute-start.23 = (f32[16,128]{1,0:T(8,128)S(1)}, f32[16,128]{1,0:T(8,128)S(1)}, u32[]{:S(2)}, u32[]{:S(2)}) collective-permute-start(f32[16,128]{1,0:T(8,128)S(1)} %add_add_fusion.refs_0_), channel_id=1, source_target_pairs={{0,24},{1,25},{2,26},{3,27},{4,28},{5,29},{6,30},{7,31},{8,16},{9,... | collective-permute-start | bytes 24584 | tf_op jit(solution)/shard_map/ppermute | solution.py:382
  (11 other events, 89.3 us)

commit v11 on v10

--- a/solution.py
+++ b/solution.py
@@ -31,7 +31,7 @@
     return lax.rem(lax.axis_index("member"), 2)
 
 
-def pack_kernel(count_ref, matrix_ref, adapters_ref, heads_ref, cot_ref, packed_ref, q_ref):
+def pack_kernel(matrix_ref, adapters_ref, heads_ref, packed_ref):
     own, D = matrix_ref.shape
     K = adapters_ref.shape[2]
     packed_ref[:, :D] = matrix_ref[...].astype(BF16)
@@ -43,20 +43,18 @@
         h, c = divmod(t * L, D)
         rows.append(heads_ref[h:h + 1, c:c + L])
     packed_ref[:, D + LANES:] = jnp.concatenate(rows, axis=0).astype(BF16)
-    lane = lax.broadcasted_iota(jnp.int32, cot_ref.shape, 1)
-    q_ref[...] = jnp.where(lane < count_ref[0], cot_ref[...], 0.0) * (1.0 / K)
-
-
-def pack_call(counts, matrix, adapters_t, heads, cot):
+
+
+def pack_call(matrix, adapters_t, heads):
     own, D = matrix.shape
     L = heads.shape[0] * D // own
     return pl.pallas_call(
         pack_kernel,
-        out_shape=(shape((own, D + LANES + L), BF16), shape(cot.shape)),
-        in_specs=[SMEM, VMEM, VMEM, VMEM, VMEM],
-        out_specs=(VMEM, VMEM),
+        out_shape=shape((own, D + LANES + L), BF16),
+        in_specs=[VMEM] * 3,
+        out_specs=VMEM,
         name="pack_weights",
-    )(counts, matrix, adapters_t, heads, cot)
+    )(matrix, adapters_t, heads)
 
 
 def grad_kernel(
@@ -382,20 +380,25 @@
     return lax.ppermute(value, AXES, [(i, i ^ mask) for i in range(total)])
 
 
-def gather_groups(value, groups, total, index, objects, q):
-    value, objects, q = lax.optimization_barrier((value, objects, q))
-    rows = (objects, q)
+def gather_groups(value, groups, total, index, objects, counts, cot, members):
+    value, objects, cot = lax.optimization_barrier((value, objects, cot))
     for axis, (low, size) in enumerate(groups):
         place = (index // low) % size
         held = [value] + [swap(value, total, low * m) for m in reversed(range(1, size))][::-1]
         if axis == 0:
-            rows = rows + tuple(swap(v, total, 1) for v in rows)
-            held, rows = lax.optimization_barrier((held, rows))
+            x_other = swap(objects, total, 1)
+            held, x_other, objects = lax.optimization_barrier((held, x_other, objects))
         elif axis == 1:
-            rows = (jnp.concatenate([rows[0], rows[2]], axis=0), jnp.concatenate([rows[1], rows[3]], axis=1))
-            held, rows = lax.optimization_barrier((held, rows))
+            lane = lax.broadcasted_iota(jnp.int32, cot.shape, 1)
+            q = jnp.where(lane < counts[0], cot, 0.0) * (1.0 / members)
+            x = jnp.concatenate([objects, x_other], axis=0)
+            held, x, q = lax.optimization_barrier((held, x, q))
+        elif axis == len(groups) - 1:
+            q_other = swap(q, total, 1)
+            held, q_other = lax.optimization_barrier((held, q_other))
+            q = jnp.concatenate([q, q_other], axis=1)
         value = jnp.stack([lax.select_n(place ^ p, *held) for p in range(size)], axis=axis)
-    return (value,) + rows
+    return value, x, q
 
 
 def beside(sends, work, *inputs):
@@ -416,10 +419,11 @@
     chip_groups = member_groups[:-1]
     turned = [v.transpose(0, 2, 1) for v in (adapters, adapter_first, adapter_second)]
 
-    packed, q_own = pack_call(counts, matrix, turned[0], head_weights, cotangent.reshape(1, R))
-    full, x_both, q_both = gather_groups(packed, dp_groups + member_groups, total, index, objects, q_own)
+    packed = pack_call(matrix, turned[0], head_weights)
+    full, x_both, q_both = gather_groups(
+        packed, dp_groups + member_groups, total, index, objects, counts, cotangent.reshape(1, R), K)
     full = full.reshape(D, -1)
-    q_other = q_both[:, R:]
+    q_own, q_other = q_both[:, :R], q_both[:, R:]
     keep, sent, head_grads, preds, rows, wide_turned, back_own, back_other = grad_call(x_both, q_both, full, K, own)
 
     chips = [size for _, size in chip_groups]

time: 97.6 us -> 96.9 us (level)
  waiting for transfers between devices: 9.31 us -> 7.6 us
    ppermute x25, waiting for transfers between devices: 9.31 us -> 7.6 us  [swap(): return lax.ppermute(value, AXES, [(i, i ^ mask) for i in range(total)])]
  transfers between devices with their start and end apart: 25 -> 25, of which waited for: 9 -> 9; matrix products, arithmetic and copies ran while one was open for 1% -> 2% of each run, Pallas kernels for 21% -> 21%
where the time goes in v11:
time: 96.9 us; the launch traced here: 96.6 us
  Pallas kernels  57.1 us (59%)
  starting transfers between devices  26.8 us (28%)
  waiting for transfers between devices  7.6 us (8%)
  other arithmetic  3.01 us (3%)
  between operations  1.75 us (2%)
    pallas_call x1, Pallas kernels, grad_call(): pl.pallas_call(functools.partial(grad_kernel, own=own), grid=(members //...  34.7 us
    ppermute x25, starting transfers between devices, swap(): return lax.ppermute(value, AXES, [(i, i ^ mask) for i in range(total)])  26.8 us
    pallas_call x6, Pallas kernels, back_call(): pl.pallas_call(functools.partial(back_kernel, start=start, first=acc is N...  19.5 us
    ppermute x25, waiting for transfers between devices, swap(): return lax.ppermute(value, AXES, [(i, i ^ mask) for i in range(total)])  7.6 us
  transfers between devices with their start and end apart: 25, of which 9 were waited for; matrix products, arithmetic and copies ran while one was open for 2% of the time, Pallas kernels for 21%

profile of v11, /device:TPU:0, one launch (start us, length us, event | category | flops | bytes accessed | tf_op | source)
XLA Modules:
  0.0 96.6 jit_solution(530678122629844754)
XLA Ops:
  0.6 1.5 %pack_weights.1 = bf16[16,768]{1,0:T(8,128)(2,1)} custom-call(f32[16,512]{1,0:T(8,128)} %refs_4_.3, f32[3,16,32]{2,1,0:T(8,128)} %bitcast.63, f32[4,512]{1,0:T(4,128)} %refs_6_.3), custom_call_target="tpu_custom_call" | custom-call | tf_op jit(solution)/shard_map/pack_weights/pallas_call | solution.py:51
  2.6 4.6 %collective-permute-start.2 = (bf16[16,768]{1,0:T(8,128)(2,1)}, bf16[16,768]{1,0:T(8,128)(2,1)S(1)}, u32[]{:S(2)}, u32[]{:S(2)}) collective-permute-start(bf16[16,768]{1,0:T(8,128)(2,1)} %pack_weights.1), channel_id=1, source_target_pairs={{0,24},{1,25},{2,26},{3,27},{4,28},{5,29},{6,30},{7,31},{8,16},{9,... | collective-permute-start | bytes 73736 | tf_op jit(solution)/shard_map/ppermute | solution.py:380
  9.3 2.8 %collective-permute-done.1 = bf16[16,768]{1,0:T(8,128)(2,1)S(1)} collective-permute-done((bf16[16,768]{1,0:T(8,128)(2,1)}, bf16[16,768]{1,0:T(8,128)(2,1)S(1)}, u32[]{:S(2)}, u32[]{:S(2)}) %collective-permute-start.1) | collective-permute-done | bytes 24608 | tf_op jit(solution)/shard_map/ppermute | solution.py:380
  12.9 2.5 %collective-permute-start.6 = (bf16[4,16,768]{2,1,0:T(8,128)(2,1)S(1)}, bf16[4,16,768]{2,1,0:T(8,128)(2,1)S(1)}, u32[]{:S(2)}, u32[]{:S(2)}) collective-permute-start(bf16[4,16,768]{2,1,0:T(8,128)(2,1)S(1)} %pad_maximum_fusion.3), channel_id=1, source_target_pairs={{0,6},{1,7},{2,4},{3,5},{4,2},{5,3},{6,0},{7,1},{8,14},{9,15},{10,... | collective-permute-start | bytes 294920 | tf_op jit(solution)/shard_map/ppermute | solution.py:380
  16.4 1.1 %pad_maximum_fusion.x_ref = bf16[1024,512]{1,0:T(8,128)(2,1)S(1)} fusion(bf16[512,512]{1,0:T(8,128)(2,1)S(1)} %collective-permute-done.3, bf16[512,512]{1,0:T(8,128)(2,1)} %param.12), kind=kLoop, calls=%fused_computation | loop fusion | flops 2097152 | bytes 2097152 | tf_op jit(solution)/shard_map/concatenate | solution.py:394
  17.6 1.4 %collective-permute-done.6 = bf16[4,16,768]{2,1,0:T(8,128)(2,1)S(1)} collective-permute-done((bf16[4,16,768]{2,1,0:T(8,128)(2,1)S(1)}, bf16[4,16,768]{2,1,0:T(8,128)(2,1)S(1)}, u32[]{:S(2)}, u32[]{:S(2)}) %collective-permute-start.6) | collective-permute-done | bytes 98336 | tf_op jit(solution)/shard_map/ppermute | solution.py:380
  18.9 1.1 %collective-permute-done.5 = bf16[4,16,768]{2,1,0:T(8,128)(2,1)S(1)} collective-permute-done((bf16[4,16,768]{2,1,0:T(8,128)(2,1)S(1)}, bf16[4,16,768]{2,1,0:T(8,128)(2,1)S(1)}, u32[]{:S(2)}, u32[]{:S(2)}) %collective-permute-start.5) | collective-permute-done | bytes 98336 | tf_op jit(solution)/shard_map/ppermute | solution.py:380
  21.2 1.2 %collective-permute-done.8.refs_4_ = f32[1,512]{1,0:T(1,128)S(1)} collective-permute-done((f32[1,512]{1,0:T(1,128)S(1)}, f32[1,512]{1,0:T(1,128)S(1)}, u32[]{:S(2)}, u32[]{:S(2)}) %collective-permute-start.8) | collective-permute-done | bytes 2080 | tf_op jit(solution)/shard_map/ppermute | solution.py:380
  22.7 34.7 %member_grads.1 = (f32[256,640]{1,0:T(8,128)S(1)}, bf16[256,640]{1,0:T(8,128)(2,1)S(1)}, f32[32,512]{1,0:T(8,128)S(1)}, f32[2,512]{1,0:T(2,128)S(1)}, f32[128,51...) custom-call(bf16[1024,512]{1,0:T(8,128)(2,1)S(1)} %pad_maximum_fusio, ...), custom_call_target="tpu_custom_call" | custom-call | flops 34359738368 | bytes 16777216 | tf_op jit(solution)/shard_map/member_grads/pallas_call | solution.py:187
  58.0 1.9 %input_grads.6.refs_3_ = f32[512,512]{1,0:T(8,128)S(1)} custom-call(f32[128,512]{1,0:T(8,128)S(1)} %get-tuple-element.188.refs_0_, bf16[512,512]{1,0:T(8,128)(2,1)S(1)} %get-tuple-element.189.refs_1_, bf16[16,512,512]{2,1,0:T(8,128)(2,1)} %get-tuple-element.161.refs_2_), custom_call_target="tpu_custom_call" | custom-call | flops 536870912 | bytes 1048576 | tf_op jit(solution)/shard_map/input_grads/pallas_call | solution.py:259
  61.2 1.1 %collective-permute-start.12 = (bf16[68,640]{1,0:T(8,128)(2,1)S(1)}, bf16[68,640]{1,0:T(8,128)(2,1)S(1)}, u32[]{:S(2)}, u32[]{:S(2)}) collective-permute-start(bf16[68,640]{1,0:T(8,128)(2,1)S(1)} %get-tuple-element.146), channel_id=1, source_target_pairs={{0,4},{1,5},{2,6},{3,7},{4,0},{5,1},{6,2},{7,3},{8,12},{9,13},{10,... | collective-permute-start | bytes 261128 | tf_op jit(solution)/shard_map/ppermute | solution.py:380
  62.3 1.4 %collective-permute-start.13 = (bf16[68,640]{1,0:T(8,128)(2,1)S(1)}, bf16[68,640]{1,0:T(8,128)(2,1)S(1)}, u32[]{:S(2)}, u32[]{:S(2)}) collective-permute-start(bf16[68,640]{1,0:T(8,128)(2,1)S(1)} %get-tuple-element.147), channel_id=1, source_target_pairs={{0,6},{1,7},{2,4},{3,5},{4,2},{5,3},{6,0},{7,1},{8,14},{9,15},{10,... | collective-permute-start | bytes 261128 | tf_op jit(solution)/shard_map/ppermute | solution.py:380
  63.7 4.0 %input_grads.7.refs_3_ = f32[512,512]{1,0:T(8,128)S(1)} custom-call(f32[128,512]{1,0:T(8,128)S(1)} %get-tuple-element.188.refs_0_, bf16[512,512]{1,0:T(8,128)(2,1)S(1)} %get-tuple-element.189.refs_1_, bf16[16,512,512]{2,1,0:T(8,128)(2,1)} %get-tuple-element.161.refs_2_, f32[512,512]{1,0:T(8,128)S(1)} %input_grads.6.refs_3_), custom_call_target="tpu_custom_call" | custom-call | flops 2147483648 | bytes 4194304 | tf_op jit(solution)/shard_map/input_grads/pallas_call | solution.py:259
  68.5 1.8 %collective-permute-start.15 = (bf16[20,640]{1,0:T(8,128)(2,1)S(1)}, bf16[20,640]{1,0:T(8,128)(2,1)S(1)}, u32[]{:S(2)}, u32[]{:S(2)}) collective-permute-start(bf16[20,640]{1,0:T(8,128)(2,1)S(1)} %get-tuple-element.157), channel_id=1, source_target_pairs={{0,16},{1,17},{2,18},{3,19},{4,20},{5,21},{6,22},{7,23},{8,24},{9,... | collective-permute-start | bytes 76808 | tf_op jit(solution)/shard_map/ppermute | solution.py:380
  70.3 2.3 %collective-permute-start.16 = (bf16[20,640]{1,0:T(8,128)(2,1)S(1)}, bf16[20,640]{1,0:T(8,128)(2,1)S(1)}, u32[]{:S(2)}, u32[]{:S(2)}) collective-permute-start(bf16[20,640]{1,0:T(8,128)(2,1)S(1)} %get-tuple-element.158), channel_id=1, source_target_pairs={{0,24},{1,25},{2,26},{3,27},{4,28},{5,29},{6,30},{7,31},{8,16},{9,... | collective-permute-start | bytes 76808 | tf_op jit(solution)/shard_map/ppermute | solution.py:380
  72.6 3.3 %input_grads.8 = f32[512,512]{1,0:T(8,128)S(1)} custom-call(f32[128,512]{1,0:T(8,128)S(1)} %get-tuple-element.188.refs_0_, bf16[512,512]{1,0:T(8,128)(2,1)S(1)} %get-tuple-element.189.refs_1_, bf16[16,512,512]{2,1,0:T(8,128)(2,1)} %get-tuple-element.161.refs_2_, f32[512,512]{1,0:T(8,128)S(1)} %input_grads.7.refs_3_, f32[1,512]{1,0:T(1,128)S(1)} %collective-permute-done.8.refs_4_), custom_call_target="tpu_custom_call" | custom-call | flops 1610612736 | bytes 3145728 | tf_op jit(solution)/shard_map/input_grads/pallas_call | solution.py:259
  77.3 1.9 %input_grads.9.refs_3_ = f32[512,512]{1,0:T(8,128)S(1)} custom-call(f32[128,512]{1,0:T(8,128)S(1)} %get-tuple-element.188.refs_0_, bf16[512,512]{1,0:T(8,128)(2,1)S(1)} %get-tuple-element.189.refs_1_, bf16[16,512,512]{2,1,0:T(8,128)(2,1)} %get-tuple-element.190.refs_2_), custom_call_target="tpu_custom_call" | custom-call | flops 536870912 | bytes 1048576 | tf_op jit(solution)/shard_map/input_grads/pallas_call | solution.py:259
  79.3 1.4 %collective-permute-start.18 = (f32[16,128]{1,0:T(8,128)S(1)}, f32[16,128]{1,0:T(8,128)S(1)}, u32[]{:S(2)}, u32[]{:S(2)}) collective-permute-start(f32[16,128]{1,0:T(8,128)S(1)} %add.94), channel_id=1, source_target_pairs={{0,2},{1,3},{2,0},{3,1},{4,6},{5,7},{6,4},{7,5},{8,10},{9,11},{10,... | collective-permute-start | bytes 24584 | tf_op jit(solution)/shard_map/ppermute | solution.py:380
  80.7 1.1 %collective-permute-start.19 = (f32[16,128]{1,0:T(8,128)S(1)}, f32[16,128]{1,0:T(8,128)S(1)}, u32[]{:S(2)}, u32[]{:S(2)}) collective-permute-start(f32[16,128]{1,0:T(8,128)S(1)} %add.94), channel_id=1, source_target_pairs={{0,4},{1,5},{2,6},{3,7},{4,0},{5,1},{6,2},{7,3},{8,12},{9,13},{10,... | collective-permute-start | bytes 24584 | tf_op jit(solution)/shard_map/ppermute | solution.py:380
  81.8 1.1 %collective-permute-start.20 = (f32[16,128]{1,0:T(8,128)S(1)}, f32[16,128]{1,0:T(8,128)S(1)}, u32[]{:S(2)}, u32[]{:S(2)}) collective-permute-start(f32[16,128]{1,0:T(8,128)S(1)} %add.94), channel_id=1, source_target_pairs={{0,6},{1,7},{2,4},{3,5},{4,2},{5,3},{6,0},{7,1},{8,14},{9,15},{10,... | collective-permute-start | bytes 24584 | tf_op jit(solution)/shard_map/ppermute | solution.py:380
  82.8 3.3 %input_grads.10.refs_3_ = f32[512,512]{1,0:T(8,128)S(1)} custom-call(f32[128,512]{1,0:T(8,128)S(1)} %get-tuple-element.188.refs_0_, bf16[512,512]{1,0:T(8,128)(2,1)S(1)} %get-tuple-element.189.refs_1_, bf16[16,512,512]{2,1,0:T(8,128)(2,1)} %get-tuple-element.190.refs_2_, f32[512,512]{1,0:T(8,128)S(1)} %input_grads.9.refs_3_), custom_call_target="tpu_custom_call" | custom-call | flops 1610612736 | bytes 3145728 | tf_op jit(solution)/shard_map/input_grads/pallas_call | solution.py:259
  86.5 2.7 %collective-permute-start.22 = (f32[16,128]{1,0:T(8,128)S(1)}, f32[16,128]{1,0:T(8,128)S(1)}, u32[]{:S(2)}, u32[]{:S(2)}) collective-permute-start(f32[16,128]{1,0:T(8,128)S(1)} %add_add_fusion.refs_0_), channel_id=1, source_target_pairs={{0,16},{1,17},{2,18},{3,19},{4,20},{5,21},{6,22},{7,23},{8,24},{9,... | collective-permute-start | bytes 24584 | tf_op jit(solution)/shard_map/ppermute | solution.py:380
  89.1 1.6 %collective-permute-start.23 = (f32[16,128]{1,0:T(8,128)S(1)}, f32[16,128]{1,0:T(8,128)S(1)}, u32[]{:S(2)}, u32[]{:S(2)}) collective-permute-start(f32[16,128]{1,0:T(8,128)S(1)} %add_add_fusion.refs_0_), channel_id=1, source_target_pairs={{0,24},{1,25},{2,26},{3,27},{4,28},{5,29},{6,30},{7,31},{8,16},{9,... | collective-permute-start | bytes 24584 | tf_op jit(solution)/shard_map/ppermute | solution.py:380
  90.7 5.0 %input_grads.11 = (f32[512,512]{1,0:T(8,128)}, f32[1,512]{1,0:T(1,128)}) custom-call(f32[128,512]{1,0:T(8,128)S(1)} %get-tuple-element.188.refs_0_, bf16[512,512]{1,0:T(8,128)(2,1)S(1)} %get-tuple-element.189.refs_1_, bf16[16,512,512]{2,1,0:T(8,128)(2,1)} %get-tuple-element.190.refs_2_, f32[512,512]{1,0:T(8,128)S(1)} %input_grads.10.refs_3_, ...), custom_call_target="tpu_custom_call" | custom-call | flops 2147483648 | bytes 4194304 | tf_op jit(solution)/shard_map/input_grads/pallas_call | solution.py:259
  (80 shorter events, 9.9 us)
Async XLA Ops:
  2.1 10.0 %collective-permute-start.3 = (bf16[512,512]{1,0:T(8,128)(2,1)}, bf16[512,512]{1,0:T(8,128)(2,1)S(1)}, u32[]{:S(2)}, u32[]{:S(2)}) collective-permute-start(bf16[512,512]{1,0:T(8,128)(2,1)} %param.12), channel_id=1, source_target_pairs={{0,1},{1,0},{2,3},{3,2},{4,5},{5,4},{6,7},{7,6},{8,9},{9,8},{10,11... | collective-permute-start | bytes 1572872 | tf_op jit(solution)/shard_map/ppermute | solution.py:380
  2.6 6.7 %collective-permute-start.2 = (bf16[16,768]{1,0:T(8,128)(2,1)}, bf16[16,768]{1,0:T(8,128)(2,1)S(1)}, u32[]{:S(2)}, u32[]{:S(2)}) collective-permute-start(bf16[16,768]{1,0:T(8,128)(2,1)} %pack_weights.1), channel_id=1, source_target_pairs={{0,24},{1,25},{2,26},{3,27},{4,28},{5,29},{6,30},{7,31},{8,16},{9,... | collective-permute-start | bytes 73736 | tf_op jit(solution)/shard_map/ppermute | solution.py:380
  7.2 4.9 %collective-permute-start.1 = (bf16[16,768]{1,0:T(8,128)(2,1)}, bf16[16,768]{1,0:T(8,128)(2,1)S(1)}, u32[]{:S(2)}, u32[]{:S(2)}) collective-permute-start(bf16[16,768]{1,0:T(8,128)(2,1)} %pack_weights.1), channel_id=1, source_target_pairs={{0,16},{1,17},{2,18},{3,19},{4,20},{5,21},{6,22},{7,23},{8,24},{9,... | collective-permute-start | bytes 73736 | tf_op jit(solution)/shard_map/ppermute | solution.py:380
  7.2 4.9 %collective-permute-start = (bf16[16,768]{1,0:T(8,128)(2,1)}, bf16[16,768]{1,0:T(8,128)(2,1)S(1)}, u32[]{:S(2)}, u32[]{:S(2)}) collective-permute-start(bf16[16,768]{1,0:T(8,128)(2,1)} %pack_weights.1), channel_id=1, source_target_pairs={{0,8},{1,9},{2,10},{3,11},{4,12},{5,13},{6,14},{7,15},{8,0},{9,1},... | collective-permute-start | bytes 73736 | tf_op jit(solution)/shard_map/ppermute | solution.py:380
  12.9 6.0 %collective-permute-start.6 = (bf16[4,16,768]{2,1,0:T(8,128)(2,1)S(1)}, bf16[4,16,768]{2,1,0:T(8,128)(2,1)S(1)}, u32[]{:S(2)}, u32[]{:S(2)}) collective-permute-start(bf16[4,16,768]{2,1,0:T(8,128)(2,1)S(1)} %pad_maximum_fusion.3), channel_id=1, source_target_pairs={{0,6},{1,7},{2,4},{3,5},{4,2},{5,3},{6,0},{7,1},{8,14},{9,15},{10,... | collective-permute-start | bytes 294920 | tf_op jit(solution)/shard_map/ppermute | solution.py:380
  15.4 4.7 %collective-permute-start.5 = (bf16[4,16,768]{2,1,0:T(8,128)(2,1)S(1)}, bf16[4,16,768]{2,1,0:T(8,128)(2,1)S(1)}, u32[]{:S(2)}, u32[]{:S(2)}) collective-permute-start(bf16[4,16,768]{2,1,0:T(8,128)(2,1)S(1)} %pad_maximum_fusion.3), channel_id=1, source_target_pairs={{0,4},{1,5},{2,6},{3,7},{4,0},{5,1},{6,2},{7,3},{8,12},{9,13},{10,... | collective-permute-start | bytes 294920 | tf_op jit(solution)/shard_map/ppermute | solution.py:380
  15.9 4.6 %collective-permute-start.4 = (bf16[4,16,768]{2,1,0:T(8,128)(2,1)S(1)}, bf16[4,16,768]{2,1,0:T(8,128)(2,1)S(1)}, u32[]{:S(2)}, u32[]{:S(2)}) collective-permute-start(bf16[4,16,768]{2,1,0:T(8,128)(2,1)S(1)} %pad_maximum_fusion.3), channel_id=1, source_target_pairs={{0,2},{1,3},{2,0},{3,1},{4,6},{5,7},{6,4},{7,5},{8,10},{9,11},{10,... | collective-permute-start | bytes 294920 | tf_op jit(solution)/shard_map/ppermute | solution.py:380
  20.6 1.8 %collective-permute-start.7 = (bf16[4,4,16,768]{3,2,0,1:T(8,128)(2,1)S(1)}, bf16[4,4,16,768]{3,2,0,1:T(8,128)(2,1)S(1)}, u32[]{:S(2)}, u32[]{:S(2)}) collective-permute-start(bf16[4,4,16,768]{3,2,0,1:T(8,128)(2,1)S(1)} %pad_maximum_fusion.2), channel_id=1, source_target_pairs={{0,1},{1,0},{2,3},{3,2},{4,5},{5,4},{6,7},{7,6},{8,9},{9,8},{10,11... | collective-permute-start | bytes 1179656 | tf_op jit(solution)/shard_map/ppermute | solution.py:380
  57.5 2.6 %collective-permute-start.9 = (bf16[4,68,640]{2,1,0:T(8,128)(2,1)S(1)}, bf16[4,68,640]{2,1,0:T(8,128)(2,1)S(1)}, u32[]{:S(2)}, u32[]{:S(2)}) collective-permute-start(bf16[4,68,640]{2,1,0:T(8,128)(2,1)S(1)} %fusion.2), channel_id=1, source_target_pairs={{0,1},{1,0},{2,3},{3,2},{4,5},{5,4},{6,7},{7,6},{8,9},{9,8},{10,11... | collective-permute-start | bytes 1044488 | tf_op jit(solution)/shard_map/ppermute | solution.py:380
  57.7 2.4 %collective-permute-start.10 = (f32[1,512]{1,0:T(1,128)S(1)}, f32[1,512]{1,0:T(1,128)S(1)}, u32[]{:S(2)}, u32[]{:S(2)}) collective-permute-start(f32[1,512]{1,0:T(1,128)S(1)} %slice.9), channel_id=1, source_target_pairs={{0,1},{1,0},{2,3},{3,2},{4,5},{5,4},{6,7},{7,6},{8,9},{9,8},{10,11... | collective-permute-start | bytes 6152 | tf_op jit(solution)/shard_map/ppermute | solution.py:380
  60.2 7.6 %collective-permute-start.11 = (bf16[68,640]{1,0:T(8,128)(2,1)S(1)}, bf16[68,640]{1,0:T(8,128)(2,1)S(1)}, u32[]{:S(2)}, u32[]{:S(2)}) collective-permute-start(bf16[68,640]{1,0:T(8,128)(2,1)S(1)} %get-tuple-element.145), channel_id=1, source_target_pairs={{0,2},{1,3},{2,0},{3,1},{4,6},{5,7},{6,4},{7,5},{8,10},{9,11},{10,... | collective-permute-start | bytes 261128 | tf_op jit(solution)/shard_map/ppermute | solution.py:380
  61.2 6.6 %collective-permute-start.12 = (bf16[68,640]{1,0:T(8,128)(2,1)S(1)}, bf16[68,640]{1,0:T(8,128)(2,1)S(1)}, u32[]{:S(2)}, u32[]{:S(2)}) collective-permute-start(bf16[68,640]{1,0:T(8,128)(2,1)S(1)} %get-tuple-element.146), channel_id=1, source_target_pairs={{0,4},{1,5},{2,6},{3,7},{4,0},{5,1},{6,2},{7,3},{8,12},{9,13},{10,... | collective-permute-start | bytes 261128 | tf_op jit(solution)/shard_map/ppermute | solution.py:380
  62.3 5.6 %collective-permute-start.13 = (bf16[68,640]{1,0:T(8,128)(2,1)S(1)}, bf16[68,640]{1,0:T(8,128)(2,1)S(1)}, u32[]{:S(2)}, u32[]{:S(2)}) collective-permute-start(bf16[68,640]{1,0:T(8,128)(2,1)S(1)} %get-tuple-element.147), channel_id=1, source_target_pairs={{0,6},{1,7},{2,4},{3,5},{4,2},{5,3},{6,0},{7,1},{8,14},{9,15},{10,... | collective-permute-start | bytes 261128 | tf_op jit(solution)/shard_map/ppermute | solution.py:380
  68.1 7.8 %collective-permute-start.14 = (bf16[20,640]{1,0:T(8,128)(2,1)S(1)}, bf16[20,640]{1,0:T(8,128)(2,1)S(1)}, u32[]{:S(2)}, u32[]{:S(2)}) collective-permute-start(bf16[20,640]{1,0:T(8,128)(2,1)S(1)} %get-tuple-element.156), channel_id=1, source_target_pairs={{0,8},{1,9},{2,10},{3,11},{4,12},{5,13},{6,14},{7,15},{8,0},{9,1},... | collective-permute-start | bytes 76808 | tf_op jit(solution)/shard_map/ppermute | solution.py:380
  68.5 7.5 %collective-permute-start.15 = (bf16[20,640]{1,0:T(8,128)(2,1)S(1)}, bf16[20,640]{1,0:T(8,128)(2,1)S(1)}, u32[]{:S(2)}, u32[]{:S(2)}) collective-permute-start(bf16[20,640]{1,0:T(8,128)(2,1)S(1)} %get-tuple-element.157), channel_id=1, source_target_pairs={{0,16},{1,17},{2,18},{3,19},{4,20},{5,21},{6,22},{7,23},{8,24},{9,... | collective-permute-start | bytes 76808 | tf_op jit(solution)/shard_map/ppermute | solution.py:380
  70.3 5.7 %collective-permute-start.16 = (bf16[20,640]{1,0:T(8,128)(2,1)S(1)}, bf16[20,640]{1,0:T(8,128)(2,1)S(1)}, u32[]{:S(2)}, u32[]{:S(2)}) collective-permute-start(bf16[20,640]{1,0:T(8,128)(2,1)S(1)} %get-tuple-element.158), channel_id=1, source_target_pairs={{0,24},{1,25},{2,26},{3,27},{4,28},{5,29},{6,30},{7,31},{8,16},{9,... | collective-permute-start | bytes 76808 | tf_op jit(solution)/shard_map/ppermute | solution.py:380
  76.0 14.7 %collective-permute-start.24 = (f32[512,512]{1,0:T(8,128)S(1)}, f32[512,512]{1,0:T(8,128)S(1)}, u32[]{:S(2)}, u32[]{:S(2)}) collective-permute-start(f32[512,512]{1,0:T(8,128)S(1)} %input_grads.8), channel_id=1, source_target_pairs={{0,1},{1,0},{2,3},{3,2},{4,5},{5,4},{6,7},{7,6},{8,9},{9,8},{10,11... | collective-permute-start | bytes 3145736 | tf_op jit(solution)/shard_map/ppermute | solution.py:380
  76.8 2.4 %collective-permute-start.17 = (f32[16,128]{1,0:T(8,128)S(1)}, f32[16,128]{1,0:T(8,128)S(1)}, u32[]{:S(2)}, u32[]{:S(2)}) collective-permute-start(f32[16,128]{1,0:T(8,128)S(1)} %get-tuple-element.168), channel_id=1, source_target_pairs={{0,1},{1,0},{2,3},{3,2},{4,5},{5,4},{6,7},{7,6},{8,9},{9,8},{10,11... | collective-permute-start | bytes 24584 | tf_op jit(solution)/shard_map/ppermute | solution.py:380
  79.3 6.9 %collective-permute-start.18 = (f32[16,128]{1,0:T(8,128)S(1)}, f32[16,128]{1,0:T(8,128)S(1)}, u32[]{:S(2)}, u32[]{:S(2)}) collective-permute-start(f32[16,128]{1,0:T(8,128)S(1)} %add.94), channel_id=1, source_target_pairs={{0,2},{1,3},{2,0},{3,1},{4,6},{5,7},{6,4},{7,5},{8,10},{9,11},{10,... | collective-permute-start | bytes 24584 | tf_op jit(solution)/shard_map/ppermute | solution.py:380
  80.7 5.5 %collective-permute-start.19 = (f32[16,128]{1,0:T(8,128)S(1)}, f32[16,128]{1,0:T(8,128)S(1)}, u32[]{:S(2)}, u32[]{:S(2)}) collective-permute-start(f32[16,128]{1,0:T(8,128)S(1)} %add.94), channel_id=1, source_target_pairs={{0,4},{1,5},{2,6},{3,7},{4,0},{5,1},{6,2},{7,3},{8,12},{9,13},{10,... | collective-permute-start | bytes 24584 | tf_op jit(solution)/shard_map/ppermute | solution.py:380
  81.8 4.5 %collective-permute-start.20 = (f32[16,128]{1,0:T(8,128)S(1)}, f32[16,128]{1,0:T(8,128)S(1)}, u32[]{:S(2)}, u32[]{:S(2)}) collective-permute-start(f32[16,128]{1,0:T(8,128)S(1)} %add.94), channel_id=1, source_target_pairs={{0,6},{1,7},{2,4},{3,5},{4,2},{5,3},{6,0},{7,1},{8,14},{9,15},{10,... | collective-permute-start | bytes 24584 | tf_op jit(solution)/shard_map/ppermute | solution.py:380
  86.3 9.4 %collective-permute-start.21 = (f32[16,128]{1,0:T(8,128)S(1)}, f32[16,128]{1,0:T(8,128)S(1)}, u32[]{:S(2)}, u32[]{:S(2)}) collective-permute-start(f32[16,128]{1,0:T(8,128)S(1)} %add_add_fusion.refs_0_), channel_id=1, source_target_pairs={{0,8},{1,9},{2,10},{3,11},{4,12},{5,13},{6,14},{7,15},{8,0},{9,1},... | collective-permute-start | bytes 24584 | tf_op jit(solution)/shard_map/ppermute | solution.py:380
  86.5 9.3 %collective-permute-start.22 = (f32[16,128]{1,0:T(8,128)S(1)}, f32[16,128]{1,0:T(8,128)S(1)}, u32[]{:S(2)}, u32[]{:S(2)}) collective-permute-start(f32[16,128]{1,0:T(8,128)S(1)} %add_add_fusion.refs_0_), channel_id=1, source_target_pairs={{0,16},{1,17},{2,18},{3,19},{4,20},{5,21},{6,22},{7,23},{8,24},{9,... | collective-permute-start | bytes 24584 | tf_op jit(solution)/shard_map/ppermute | solution.py:380
  89.1 6.6 %collective-permute-start.23 = (f32[16,128]{1,0:T(8,128)S(1)}, f32[16,128]{1,0:T(8,128)S(1)}, u32[]{:S(2)}, u32[]{:S(2)}) collective-permute-start(f32[16,128]{1,0:T(8,128)S(1)} %add_add_fusion.refs_0_), channel_id=1, source_target_pairs={{0,24},{1,25},{2,26},{3,27},{4,28},{5,29},{6,30},{7,31},{8,16},{9,... | collective-permute-start | bytes 24584 | tf_op jit(solution)/shard_map/ppermute | solution.py:380
  (10 other events, 73.7 us)

commit v12 on v11

--- a/solution.py
+++ b/solution.py
@@ -128,21 +128,25 @@
         post_ref[...] = jnp.dot(xq_ref[...], gp_ref[...], preferred_element_type=F32)
 
     def spread(i, lo, hi, total):
-        s = rows_ref[pl.ds(K + base + i, 1), :]
-        step = 16
+        s_row = rows_ref[pl.ds(K + base + i, 1), :]
+        step, width = 16, 2 * LANES
         lane = lax.broadcasted_iota(jnp.int32, (step, LANES), 1)
-        for c in range(lo, hi, step):
-            g = post_ref[c:c + step, :]
-            r = jnp.sum(jnp.where(lane == base + i, cols_ref[c:c + step, :], 0.0), axis=1, keepdims=True)
-            t = g * weight_ref[c:c + step, :]
-            rt = t * r
-            part = sum(rt[j:j + 8] for j in range(0, step, 8))
-            total = part if total is None else total + part
-            st = t * s
-            fold = sum(st[:, l:l + LANES] for l in range(0, D, LANES))
-            gr_ref[c:c + step, :] += jnp.where(lane == base + i, jnp.sum(fold, axis=1, keepdims=True), 0.0)
-            grads_ref[c:c + step, :D] += (g * s) * r
-        return total
+        totals = []
+        for w in range(0, D, width):
+            s, total = s_row[:, w:w + width], None
+            for c in range(lo, hi, step):
+                g = post_ref[c:c + step, w:w + width]
+                r = jnp.sum(jnp.where(lane == base + i, cols_ref[c:c + step, :], 0.0), axis=1, keepdims=True)
+                t = g * weight_ref[c:c + step, w:w + width]
+                rt = t * r
+                part = sum(rt[j:j + 8] for j in range(0, step, 8))
+                total = part if total is None else total + part
+                st = t * s
+                fold = sum(st[:, l:l + LANES] for l in range(0, width, LANES))
+                gr_ref[c:c + step, :] += jnp.where(lane == base + i, jnp.sum(fold, axis=1, keepdims=True), 0.0)
+                grads_ref[c:c + step, w:w + width] += (g * s) * r
+            totals.append(total)
+        return jnp.concatenate(totals, axis=1)
 
     def finish(i, total):
         sums_ref[pl.ds(K + base + i, 1), :] = jnp.sum(total, axis=0, keepdims=True)

time: 96.9 us -> 96.8 us (level)
  transfers between devices with their start and end apart: 25 -> 25, of which waited for: 9 -> 8; matrix products, arithmetic and copies ran while one was open for 2% -> 2% of each run, Pallas kernels for 21% -> 21%
where the time goes in v12:
time: 96.8 us; the launch traced here: 96.4 us
  Pallas kernels  57 us (59%)
  starting transfers between devices  26.8 us (28%)
  waiting for transfers between devices  7.57 us (8%)
  other arithmetic  3.01 us (3%)
  between operations  1.75 us (2%)
    pallas_call x1, Pallas kernels, grad_call(): pl.pallas_call(functools.partial(grad_kernel, own=own), grid=(members //...  34.5 us
    ppermute x25, starting transfers between devices, swap(): return lax.ppermute(value, AXES, [(i, i ^ mask) for i in range(total)])  26.8 us
    pallas_call x6, Pallas kernels, back_call(): pl.pallas_call(functools.partial(back_kernel, start=start, first=acc is N...  19.5 us
    ppermute x25, waiting for transfers between devices, swap(): return lax.ppermute(value, AXES, [(i, i ^ mask) for i in range(total)])  7.57 us
  transfers between devices with their start and end apart: 25, of which 8 were waited for; matrix products, arithmetic and copies ran while one was open for 2% of the time, Pallas kernels for 21%

profile of v12, /device:TPU:0, one launch (start us, length us, event | category | flops | bytes accessed | tf_op | source)
XLA Modules:
  0.0 96.4 jit_solution(3369260043547929905)
XLA Ops:
  0.6 1.5 %pack_weights.1 = bf16[16,768]{1,0:T(8,128)(2,1)} custom-call(f32[16,512]{1,0:T(8,128)} %refs_4_.3, f32[3,16,32]{2,1,0:T(8,128)} %bitcast.63, f32[4,512]{1,0:T(4,128)} %refs_6_.3), custom_call_target="tpu_custom_call" | custom-call | tf_op jit(solution)/shard_map/pack_weights/pallas_call | solution.py:51
  2.6 4.6 %collective-permute-start.2 = (bf16[16,768]{1,0:T(8,128)(2,1)}, bf16[16,768]{1,0:T(8,128)(2,1)S(1)}, u32[]{:S(2)}, u32[]{:S(2)}) collective-permute-start(bf16[16,768]{1,0:T(8,128)(2,1)} %pack_weights.1), channel_id=1, source_target_pairs={{0,24},{1,25},{2,26},{3,27},{4,28},{5,29},{6,30},{7,31},{8,16},{9,... | collective-permute-start | bytes 73736 | tf_op jit(solution)/shard_map/ppermute | solution.py:384
  9.3 2.8 %collective-permute-done.1 = bf16[16,768]{1,0:T(8,128)(2,1)S(1)} collective-permute-done((bf16[16,768]{1,0:T(8,128)(2,1)}, bf16[16,768]{1,0:T(8,128)(2,1)S(1)}, u32[]{:S(2)}, u32[]{:S(2)}) %collective-permute-start.1) | collective-permute-done | bytes 24608 | tf_op jit(solution)/shard_map/ppermute | solution.py:384
  12.9 2.5 %collective-permute-start.6 = (bf16[4,16,768]{2,1,0:T(8,128)(2,1)S(1)}, bf16[4,16,768]{2,1,0:T(8,128)(2,1)S(1)}, u32[]{:S(2)}, u32[]{:S(2)}) collective-permute-start(bf16[4,16,768]{2,1,0:T(8,128)(2,1)S(1)} %pad_maximum_fusion.3), channel_id=1, source_target_pairs={{0,6},{1,7},{2,4},{3,5},{4,2},{5,3},{6,0},{7,1},{8,14},{9,15},{10,... | collective-permute-start | bytes 294920 | tf_op jit(solution)/shard_map/ppermute | solution.py:384
  16.4 1.1 %pad_maximum_fusion.x_ref = bf16[1024,512]{1,0:T(8,128)(2,1)S(1)} fusion(bf16[512,512]{1,0:T(8,128)(2,1)S(1)} %collective-permute-done.3, bf16[512,512]{1,0:T(8,128)(2,1)} %param.12), kind=kLoop, calls=%fused_computation | loop fusion | flops 2097152 | bytes 2097152 | tf_op jit(solution)/shard_map/concatenate | solution.py:398
  17.6 1.4 %collective-permute-done.6 = bf16[4,16,768]{2,1,0:T(8,128)(2,1)S(1)} collective-permute-done((bf16[4,16,768]{2,1,0:T(8,128)(2,1)S(1)}, bf16[4,16,768]{2,1,0:T(8,128)(2,1)S(1)}, u32[]{:S(2)}, u32[]{:S(2)}) %collective-permute-start.6) | collective-permute-done | bytes 98336 | tf_op jit(solution)/shard_map/ppermute | solution.py:384
  18.9 1.1 %collective-permute-done.5 = bf16[4,16,768]{2,1,0:T(8,128)(2,1)S(1)} collective-permute-done((bf16[4,16,768]{2,1,0:T(8,128)(2,1)S(1)}, bf16[4,16,768]{2,1,0:T(8,128)(2,1)S(1)}, u32[]{:S(2)}, u32[]{:S(2)}) %collective-permute-start.5) | collective-permute-done | bytes 98336 | tf_op jit(solution)/shard_map/ppermute | solution.py:384
  21.2 1.2 %collective-permute-done.8.refs_4_ = f32[1,512]{1,0:T(1,128)S(1)} collective-permute-done((f32[1,512]{1,0:T(1,128)S(1)}, f32[1,512]{1,0:T(1,128)S(1)}, u32[]{:S(2)}, u32[]{:S(2)}) %collective-permute-start.8) | collective-permute-done | bytes 2080 | tf_op jit(solution)/shard_map/ppermute | solution.py:384
  22.7 34.5 %member_grads.1 = (f32[256,640]{1,0:T(8,128)S(1)}, bf16[256,640]{1,0:T(8,128)(2,1)S(1)}, f32[32,512]{1,0:T(8,128)S(1)}, f32[2,512]{1,0:T(2,128)S(1)}, f32[128,51...) custom-call(bf16[1024,512]{1,0:T(8,128)(2,1)S(1)} %pad_maximum_fusio, ...), custom_call_target="tpu_custom_call" | custom-call | flops 34359738368 | bytes 16777216 | tf_op jit(solution)/shard_map/member_grads/pallas_call | solution.py:191
  57.9 1.9 %input_grads.6.refs_3_ = f32[512,512]{1,0:T(8,128)S(1)} custom-call(f32[128,512]{1,0:T(8,128)S(1)} %get-tuple-element.188.refs_0_, bf16[512,512]{1,0:T(8,128)(2,1)S(1)} %get-tuple-element.189.refs_1_, bf16[16,512,512]{2,1,0:T(8,128)(2,1)} %get-tuple-element.161.refs_2_), custom_call_target="tpu_custom_call" | custom-call | flops 536870912 | bytes 1048576 | tf_op jit(solution)/shard_map/input_grads/pallas_call | solution.py:263
  61.0 1.1 %collective-permute-start.12 = (bf16[68,640]{1,0:T(8,128)(2,1)S(1)}, bf16[68,640]{1,0:T(8,128)(2,1)S(1)}, u32[]{:S(2)}, u32[]{:S(2)}) collective-permute-start(bf16[68,640]{1,0:T(8,128)(2,1)S(1)} %get-tuple-element.146), channel_id=1, source_target_pairs={{0,4},{1,5},{2,6},{3,7},{4,0},{5,1},{6,2},{7,3},{8,12},{9,13},{10,... | collective-permute-start | bytes 261128 | tf_op jit(solution)/shard_map/ppermute | solution.py:384
  62.2 1.4 %collective-permute-start.13 = (bf16[68,640]{1,0:T(8,128)(2,1)S(1)}, bf16[68,640]{1,0:T(8,128)(2,1)S(1)}, u32[]{:S(2)}, u32[]{:S(2)}) collective-permute-start(bf16[68,640]{1,0:T(8,128)(2,1)S(1)} %get-tuple-element.147), channel_id=1, source_target_pairs={{0,6},{1,7},{2,4},{3,5},{4,2},{5,3},{6,0},{7,1},{8,14},{9,15},{10,... | collective-permute-start | bytes 261128 | tf_op jit(solution)/shard_map/ppermute | solution.py:384
  63.6 4.0 %input_grads.7.refs_3_ = f32[512,512]{1,0:T(8,128)S(1)} custom-call(f32[128,512]{1,0:T(8,128)S(1)} %get-tuple-element.188.refs_0_, bf16[512,512]{1,0:T(8,128)(2,1)S(1)} %get-tuple-element.189.refs_1_, bf16[16,512,512]{2,1,0:T(8,128)(2,1)} %get-tuple-element.161.refs_2_, f32[512,512]{1,0:T(8,128)S(1)} %input_grads.6.refs_3_), custom_call_target="tpu_custom_call" | custom-call | flops 2147483648 | bytes 4194304 | tf_op jit(solution)/shard_map/input_grads/pallas_call | solution.py:263
  68.4 1.8 %collective-permute-start.15 = (bf16[20,640]{1,0:T(8,128)(2,1)S(1)}, bf16[20,640]{1,0:T(8,128)(2,1)S(1)}, u32[]{:S(2)}, u32[]{:S(2)}) collective-permute-start(bf16[20,640]{1,0:T(8,128)(2,1)S(1)} %get-tuple-element.157), channel_id=1, source_target_pairs={{0,16},{1,17},{2,18},{3,19},{4,20},{5,21},{6,22},{7,23},{8,24},{9,... | collective-permute-start | bytes 76808 | tf_op jit(solution)/shard_map/ppermute | solution.py:384
  70.2 2.3 %collective-permute-start.16 = (bf16[20,640]{1,0:T(8,128)(2,1)S(1)}, bf16[20,640]{1,0:T(8,128)(2,1)S(1)}, u32[]{:S(2)}, u32[]{:S(2)}) collective-permute-start(bf16[20,640]{1,0:T(8,128)(2,1)S(1)} %get-tuple-element.158), channel_id=1, source_target_pairs={{0,24},{1,25},{2,26},{3,27},{4,28},{5,29},{6,30},{7,31},{8,16},{9,... | collective-permute-start | bytes 76808 | tf_op jit(solution)/shard_map/ppermute | solution.py:384
  72.5 3.3 %input_grads.8 = f32[512,512]{1,0:T(8,128)S(1)} custom-call(f32[128,512]{1,0:T(8,128)S(1)} %get-tuple-element.188.refs_0_, bf16[512,512]{1,0:T(8,128)(2,1)S(1)} %get-tuple-element.189.refs_1_, bf16[16,512,512]{2,1,0:T(8,128)(2,1)} %get-tuple-element.161.refs_2_, f32[512,512]{1,0:T(8,128)S(1)} %input_grads.7.refs_3_, f32[1,512]{1,0:T(1,128)S(1)} %collective-permute-done.8.refs_4_), custom_call_target="tpu_custom_call" | custom-call | flops 1610612736 | bytes 3145728 | tf_op jit(solution)/shard_map/input_grads/pallas_call | solution.py:263
  77.2 1.9 %input_grads.9.refs_3_ = f32[512,512]{1,0:T(8,128)S(1)} custom-call(f32[128,512]{1,0:T(8,128)S(1)} %get-tuple-element.188.refs_0_, bf16[512,512]{1,0:T(8,128)(2,1)S(1)} %get-tuple-element.189.refs_1_, bf16[16,512,512]{2,1,0:T(8,128)(2,1)} %get-tuple-element.190.refs_2_), custom_call_target="tpu_custom_call" | custom-call | flops 536870912 | bytes 1048576 | tf_op jit(solution)/shard_map/input_grads/pallas_call | solution.py:263
  79.2 1.4 %collective-permute-start.18 = (f32[16,128]{1,0:T(8,128)S(1)}, f32[16,128]{1,0:T(8,128)S(1)}, u32[]{:S(2)}, u32[]{:S(2)}) collective-permute-start(f32[16,128]{1,0:T(8,128)S(1)} %add.94), channel_id=1, source_target_pairs={{0,2},{1,3},{2,0},{3,1},{4,6},{5,7},{6,4},{7,5},{8,10},{9,11},{10,... | collective-permute-start | bytes 24584 | tf_op jit(solution)/shard_map/ppermute | solution.py:384
  80.6 1.1 %collective-permute-start.19 = (f32[16,128]{1,0:T(8,128)S(1)}, f32[16,128]{1,0:T(8,128)S(1)}, u32[]{:S(2)}, u32[]{:S(2)}) collective-permute-start(f32[16,128]{1,0:T(8,128)S(1)} %add.94), channel_id=1, source_target_pairs={{0,4},{1,5},{2,6},{3,7},{4,0},{5,1},{6,2},{7,3},{8,12},{9,13},{10,... | collective-permute-start | bytes 24584 | tf_op jit(solution)/shard_map/ppermute | solution.py:384
  81.7 1.1 %collective-permute-start.20 = (f32[16,128]{1,0:T(8,128)S(1)}, f32[16,128]{1,0:T(8,128)S(1)}, u32[]{:S(2)}, u32[]{:S(2)}) collective-permute-start(f32[16,128]{1,0:T(8,128)S(1)} %add.94), channel_id=1, source_target_pairs={{0,6},{1,7},{2,4},{3,5},{4,2},{5,3},{6,0},{7,1},{8,14},{9,15},{10,... | collective-permute-start | bytes 24584 | tf_op jit(solution)/shard_map/ppermute | solution.py:384
  82.7 3.3 %input_grads.10.refs_3_ = f32[512,512]{1,0:T(8,128)S(1)} custom-call(f32[128,512]{1,0:T(8,128)S(1)} %get-tuple-element.188.refs_0_, bf16[512,512]{1,0:T(8,128)(2,1)S(1)} %get-tuple-element.189.refs_1_, bf16[16,512,512]{2,1,0:T(8,128)(2,1)} %get-tuple-element.190.refs_2_, f32[512,512]{1,0:T(8,128)S(1)} %input_grads.9.refs_3_), custom_call_target="tpu_custom_call" | custom-call | flops 1610612736 | bytes 3145728 | tf_op jit(solution)/shard_map/input_grads/pallas_call | solution.py:263
  86.3 2.7 %collective-permute-start.22 = (f32[16,128]{1,0:T(8,128)S(1)}, f32[16,128]{1,0:T(8,128)S(1)}, u32[]{:S(2)}, u32[]{:S(2)}) collective-permute-start(f32[16,128]{1,0:T(8,128)S(1)} %add_add_fusion.refs_0_), channel_id=1, source_target_pairs={{0,16},{1,17},{2,18},{3,19},{4,20},{5,21},{6,22},{7,23},{8,24},{9,... | collective-permute-start | bytes 24584 | tf_op jit(solution)/shard_map/ppermute | solution.py:384
  89.0 1.6 %collective-permute-start.23 = (f32[16,128]{1,0:T(8,128)S(1)}, f32[16,128]{1,0:T(8,128)S(1)}, u32[]{:S(2)}, u32[]{:S(2)}) collective-permute-start(f32[16,128]{1,0:T(8,128)S(1)} %add_add_fusion.refs_0_), channel_id=1, source_target_pairs={{0,24},{1,25},{2,26},{3,27},{4,28},{5,29},{6,30},{7,31},{8,16},{9,... | collective-permute-start | bytes 24584 | tf_op jit(solution)/shard_map/ppermute | solution.py:384
  90.6 5.0 %input_grads.11 = (f32[512,512]{1,0:T(8,128)}, f32[1,512]{1,0:T(1,128)}) custom-call(f32[128,512]{1,0:T(8,128)S(1)} %get-tuple-element.188.refs_0_, bf16[512,512]{1,0:T(8,128)(2,1)S(1)} %get-tuple-element.189.refs_1_, bf16[16,512,512]{2,1,0:T(8,128)(2,1)} %get-tuple-element.190.refs_2_, f32[512,512]{1,0:T(8,128)S(1)} %input_grads.10.refs_3_, ...), custom_call_target="tpu_custom_call" | custom-call | flops 2147483648 | bytes 4194304 | tf_op jit(solution)/shard_map/input_grads/pallas_call | solution.py:263
  (80 shorter events, 9.9 us)
Async XLA Ops:
  2.1 10.0 %collective-permute-start.3 = (bf16[512,512]{1,0:T(8,128)(2,1)}, bf16[512,512]{1,0:T(8,128)(2,1)S(1)}, u32[]{:S(2)}, u32[]{:S(2)}) collective-permute-start(bf16[512,512]{1,0:T(8,128)(2,1)} %param.12), channel_id=1, source_target_pairs={{0,1},{1,0},{2,3},{3,2},{4,5},{5,4},{6,7},{7,6},{8,9},{9,8},{10,11... | collective-permute-start | bytes 1572872 | tf_op jit(solution)/shard_map/ppermute | solution.py:384
  2.6 6.7 %collective-permute-start.2 = (bf16[16,768]{1,0:T(8,128)(2,1)}, bf16[16,768]{1,0:T(8,128)(2,1)S(1)}, u32[]{:S(2)}, u32[]{:S(2)}) collective-permute-start(bf16[16,768]{1,0:T(8,128)(2,1)} %pack_weights.1), channel_id=1, source_target_pairs={{0,24},{1,25},{2,26},{3,27},{4,28},{5,29},{6,30},{7,31},{8,16},{9,... | collective-permute-start | bytes 73736 | tf_op jit(solution)/shard_map/ppermute | solution.py:384
  7.2 4.9 %collective-permute-start.1 = (bf16[16,768]{1,0:T(8,128)(2,1)}, bf16[16,768]{1,0:T(8,128)(2,1)S(1)}, u32[]{:S(2)}, u32[]{:S(2)}) collective-permute-start(bf16[16,768]{1,0:T(8,128)(2,1)} %pack_weights.1), channel_id=1, source_target_pairs={{0,16},{1,17},{2,18},{3,19},{4,20},{5,21},{6,22},{7,23},{8,24},{9,... | collective-permute-start | bytes 73736 | tf_op jit(solution)/shard_map/ppermute | solution.py:384
  7.2 4.9 %collective-permute-start = (bf16[16,768]{1,0:T(8,128)(2,1)}, bf16[16,768]{1,0:T(8,128)(2,1)S(1)}, u32[]{:S(2)}, u32[]{:S(2)}) collective-permute-start(bf16[16,768]{1,0:T(8,128)(2,1)} %pack_weights.1), channel_id=1, source_target_pairs={{0,8},{1,9},{2,10},{3,11},{4,12},{5,13},{6,14},{7,15},{8,0},{9,1},... | collective-permute-start | bytes 73736 | tf_op jit(solution)/shard_map/ppermute | solution.py:384
  12.9 6.0 %collective-permute-start.6 = (bf16[4,16,768]{2,1,0:T(8,128)(2,1)S(1)}, bf16[4,16,768]{2,1,0:T(8,128)(2,1)S(1)}, u32[]{:S(2)}, u32[]{:S(2)}) collective-permute-start(bf16[4,16,768]{2,1,0:T(8,128)(2,1)S(1)} %pad_maximum_fusion.3), channel_id=1, source_target_pairs={{0,6},{1,7},{2,4},{3,5},{4,2},{5,3},{6,0},{7,1},{8,14},{9,15},{10,... | collective-permute-start | bytes 294920 | tf_op jit(solution)/shard_map/ppermute | solution.py:384
  15.4 4.7 %collective-permute-start.5 = (bf16[4,16,768]{2,1,0:T(8,128)(2,1)S(1)}, bf16[4,16,768]{2,1,0:T(8,128)(2,1)S(1)}, u32[]{:S(2)}, u32[]{:S(2)}) collective-permute-start(bf16[4,16,768]{2,1,0:T(8,128)(2,1)S(1)} %pad_maximum_fusion.3), channel_id=1, source_target_pairs={{0,4},{1,5},{2,6},{3,7},{4,0},{5,1},{6,2},{7,3},{8,12},{9,13},{10,... | collective-permute-start | bytes 294920 | tf_op jit(solution)/shard_map/ppermute | solution.py:384
  15.9 4.6 %collective-permute-start.4 = (bf16[4,16,768]{2,1,0:T(8,128)(2,1)S(1)}, bf16[4,16,768]{2,1,0:T(8,128)(2,1)S(1)}, u32[]{:S(2)}, u32[]{:S(2)}) collective-permute-start(bf16[4,16,768]{2,1,0:T(8,128)(2,1)S(1)} %pad_maximum_fusion.3), channel_id=1, source_target_pairs={{0,2},{1,3},{2,0},{3,1},{4,6},{5,7},{6,4},{7,5},{8,10},{9,11},{10,... | collective-permute-start | bytes 294920 | tf_op jit(solution)/shard_map/ppermute | solution.py:384
  20.6 1.8 %collective-permute-start.7 = (bf16[4,4,16,768]{3,2,0,1:T(8,128)(2,1)S(1)}, bf16[4,4,16,768]{3,2,0,1:T(8,128)(2,1)S(1)}, u32[]{:S(2)}, u32[]{:S(2)}) collective-permute-start(bf16[4,4,16,768]{3,2,0,1:T(8,128)(2,1)S(1)} %pad_maximum_fusion.2), channel_id=1, source_target_pairs={{0,1},{1,0},{2,3},{3,2},{4,5},{5,4},{6,7},{7,6},{8,9},{9,8},{10,11... | collective-permute-start | bytes 1179656 | tf_op jit(solution)/shard_map/ppermute | solution.py:384
  57.4 2.6 %collective-permute-start.9 = (bf16[4,68,640]{2,1,0:T(8,128)(2,1)S(1)}, bf16[4,68,640]{2,1,0:T(8,128)(2,1)S(1)}, u32[]{:S(2)}, u32[]{:S(2)}) collective-permute-start(bf16[4,68,640]{2,1,0:T(8,128)(2,1)S(1)} %fusion.2), channel_id=1, source_target_pairs={{0,1},{1,0},{2,3},{3,2},{4,5},{5,4},{6,7},{7,6},{8,9},{9,8},{10,11... | collective-permute-start | bytes 1044488 | tf_op jit(solution)/shard_map/ppermute | solution.py:384
  57.6 2.4 %collective-permute-start.10 = (f32[1,512]{1,0:T(1,128)S(1)}, f32[1,512]{1,0:T(1,128)S(1)}, u32[]{:S(2)}, u32[]{:S(2)}) collective-permute-start(f32[1,512]{1,0:T(1,128)S(1)} %slice.9), channel_id=1, source_target_pairs={{0,1},{1,0},{2,3},{3,2},{4,5},{5,4},{6,7},{7,6},{8,9},{9,8},{10,11... | collective-permute-start | bytes 6152 | tf_op jit(solution)/shard_map/ppermute | solution.py:384
  60.1 7.6 %collective-permute-start.11 = (bf16[68,640]{1,0:T(8,128)(2,1)S(1)}, bf16[68,640]{1,0:T(8,128)(2,1)S(1)}, u32[]{:S(2)}, u32[]{:S(2)}) collective-permute-start(bf16[68,640]{1,0:T(8,128)(2,1)S(1)} %get-tuple-element.145), channel_id=1, source_target_pairs={{0,2},{1,3},{2,0},{3,1},{4,6},{5,7},{6,4},{7,5},{8,10},{9,11},{10,... | collective-permute-start | bytes 261128 | tf_op jit(solution)/shard_map/ppermute | solution.py:384
  61.0 6.6 %collective-permute-start.12 = (bf16[68,640]{1,0:T(8,128)(2,1)S(1)}, bf16[68,640]{1,0:T(8,128)(2,1)S(1)}, u32[]{:S(2)}, u32[]{:S(2)}) collective-permute-start(bf16[68,640]{1,0:T(8,128)(2,1)S(1)} %get-tuple-element.146), channel_id=1, source_target_pairs={{0,4},{1,5},{2,6},{3,7},{4,0},{5,1},{6,2},{7,3},{8,12},{9,13},{10,... | collective-permute-start | bytes 261128 | tf_op jit(solution)/shard_map/ppermute | solution.py:384
  62.2 5.6 %collective-permute-start.13 = (bf16[68,640]{1,0:T(8,128)(2,1)S(1)}, bf16[68,640]{1,0:T(8,128)(2,1)S(1)}, u32[]{:S(2)}, u32[]{:S(2)}) collective-permute-start(bf16[68,640]{1,0:T(8,128)(2,1)S(1)} %get-tuple-element.147), channel_id=1, source_target_pairs={{0,6},{1,7},{2,4},{3,5},{4,2},{5,3},{6,0},{7,1},{8,14},{9,15},{10,... | collective-permute-start | bytes 261128 | tf_op jit(solution)/shard_map/ppermute | solution.py:384
  68.0 7.8 %collective-permute-start.14 = (bf16[20,640]{1,0:T(8,128)(2,1)S(1)}, bf16[20,640]{1,0:T(8,128)(2,1)S(1)}, u32[]{:S(2)}, u32[]{:S(2)}) collective-permute-start(bf16[20,640]{1,0:T(8,128)(2,1)S(1)} %get-tuple-element.156), channel_id=1, source_target_pairs={{0,8},{1,9},{2,10},{3,11},{4,12},{5,13},{6,14},{7,15},{8,0},{9,1},... | collective-permute-start | bytes 76808 | tf_op jit(solution)/shard_map/ppermute | solution.py:384
  68.4 7.5 %collective-permute-start.15 = (bf16[20,640]{1,0:T(8,128)(2,1)S(1)}, bf16[20,640]{1,0:T(8,128)(2,1)S(1)}, u32[]{:S(2)}, u32[]{:S(2)}) collective-permute-start(bf16[20,640]{1,0:T(8,128)(2,1)S(1)} %get-tuple-element.157), channel_id=1, source_target_pairs={{0,16},{1,17},{2,18},{3,19},{4,20},{5,21},{6,22},{7,23},{8,24},{9,... | collective-permute-start | bytes 76808 | tf_op jit(solution)/shard_map/ppermute | solution.py:384
  70.2 5.7 %collective-permute-start.16 = (bf16[20,640]{1,0:T(8,128)(2,1)S(1)}, bf16[20,640]{1,0:T(8,128)(2,1)S(1)}, u32[]{:S(2)}, u32[]{:S(2)}) collective-permute-start(bf16[20,640]{1,0:T(8,128)(2,1)S(1)} %get-tuple-element.158), channel_id=1, source_target_pairs={{0,24},{1,25},{2,26},{3,27},{4,28},{5,29},{6,30},{7,31},{8,16},{9,... | collective-permute-start | bytes 76808 | tf_op jit(solution)/shard_map/ppermute | solution.py:384
  75.9 14.7 %collective-permute-start.24 = (f32[512,512]{1,0:T(8,128)S(1)}, f32[512,512]{1,0:T(8,128)S(1)}, u32[]{:S(2)}, u32[]{:S(2)}) collective-permute-start(f32[512,512]{1,0:T(8,128)S(1)} %input_grads.8), channel_id=1, source_target_pairs={{0,1},{1,0},{2,3},{3,2},{4,5},{5,4},{6,7},{7,6},{8,9},{9,8},{10,11... | collective-permute-start | bytes 3145736 | tf_op jit(solution)/shard_map/ppermute | solution.py:384
  76.7 2.4 %collective-permute-start.17 = (f32[16,128]{1,0:T(8,128)S(1)}, f32[16,128]{1,0:T(8,128)S(1)}, u32[]{:S(2)}, u32[]{:S(2)}) collective-permute-start(f32[16,128]{1,0:T(8,128)S(1)} %get-tuple-element.168), channel_id=1, source_target_pairs={{0,1},{1,0},{2,3},{3,2},{4,5},{5,4},{6,7},{7,6},{8,9},{9,8},{10,11... | collective-permute-start | bytes 24584 | tf_op jit(solution)/shard_map/ppermute | solution.py:384
  79.2 6.9 %collective-permute-start.18 = (f32[16,128]{1,0:T(8,128)S(1)}, f32[16,128]{1,0:T(8,128)S(1)}, u32[]{:S(2)}, u32[]{:S(2)}) collective-permute-start(f32[16,128]{1,0:T(8,128)S(1)} %add.94), channel_id=1, source_target_pairs={{0,2},{1,3},{2,0},{3,1},{4,6},{5,7},{6,4},{7,5},{8,10},{9,11},{10,... | collective-permute-start | bytes 24584 | tf_op jit(solution)/shard_map/ppermute | solution.py:384
  80.6 5.5 %collective-permute-start.19 = (f32[16,128]{1,0:T(8,128)S(1)}, f32[16,128]{1,0:T(8,128)S(1)}, u32[]{:S(2)}, u32[]{:S(2)}) collective-permute-start(f32[16,128]{1,0:T(8,128)S(1)} %add.94), channel_id=1, source_target_pairs={{0,4},{1,5},{2,6},{3,7},{4,0},{5,1},{6,2},{7,3},{8,12},{9,13},{10,... | collective-permute-start | bytes 24584 | tf_op jit(solution)/shard_map/ppermute | solution.py:384
  81.7 4.5 %collective-permute-start.20 = (f32[16,128]{1,0:T(8,128)S(1)}, f32[16,128]{1,0:T(8,128)S(1)}, u32[]{:S(2)}, u32[]{:S(2)}) collective-permute-start(f32[16,128]{1,0:T(8,128)S(1)} %add.94), channel_id=1, source_target_pairs={{0,6},{1,7},{2,4},{3,5},{4,2},{5,3},{6,0},{7,1},{8,14},{9,15},{10,... | collective-permute-start | bytes 24584 | tf_op jit(solution)/shard_map/ppermute | solution.py:384
  86.2 9.4 %collective-permute-start.21 = (f32[16,128]{1,0:T(8,128)S(1)}, f32[16,128]{1,0:T(8,128)S(1)}, u32[]{:S(2)}, u32[]{:S(2)}) collective-permute-start(f32[16,128]{1,0:T(8,128)S(1)} %add_add_fusion.refs_0_), channel_id=1, source_target_pairs={{0,8},{1,9},{2,10},{3,11},{4,12},{5,13},{6,14},{7,15},{8,0},{9,1},... | collective-permute-start | bytes 24584 | tf_op jit(solution)/shard_map/ppermute | solution.py:384
  86.3 9.3 %collective-permute-start.22 = (f32[16,128]{1,0:T(8,128)S(1)}, f32[16,128]{1,0:T(8,128)S(1)}, u32[]{:S(2)}, u32[]{:S(2)}) collective-permute-start(f32[16,128]{1,0:T(8,128)S(1)} %add_add_fusion.refs_0_), channel_id=1, source_target_pairs={{0,16},{1,17},{2,18},{3,19},{4,20},{5,21},{6,22},{7,23},{8,24},{9,... | collective-permute-start | bytes 24584 | tf_op jit(solution)/shard_map/ppermute | solution.py:384
  89.0 6.6 %collective-permute-start.23 = (f32[16,128]{1,0:T(8,128)S(1)}, f32[16,128]{1,0:T(8,128)S(1)}, u32[]{:S(2)}, u32[]{:S(2)}) collective-permute-start(f32[16,128]{1,0:T(8,128)S(1)} %add_add_fusion.refs_0_), channel_id=1, source_target_pairs={{0,24},{1,25},{2,26},{3,27},{4,28},{5,29},{6,30},{7,31},{8,16},{9,... | collective-permute-start | bytes 24584 | tf_op jit(solution)/shard_map/ppermute | solution.py:384
  (10 other events, 73.8 us)

commit v13 on v12

--- a/solution.py
+++ b/solution.py
@@ -170,8 +170,11 @@
 
     @pl.when(step_id == steps - 1)
     def _():
-        outer(gp_refs[1])
-        finish(members - 1, spread(members - 1, 0, D, None))
+        mid = D // 2
+        for lo, hi in ((0, mid), (mid, D + 16)):
+            post_ref[lo:hi, :] = jnp.dot(xq_ref[lo:hi, :], gp_refs[1][...], preferred_element_type=F32)
+        last = [spread(members - 1, lo, lo + mid, None) for lo in (0, mid)]
+        finish(members - 1, last[0] + last[1])
         for side in range(2):
             at = slice(side * half, (side + 1) * half)
             pred_ref[side:side + 1, :] = jnp.sum(pred_acc[at, :].T, axis=0, keepdims=True)

time: 96.8 us -> 96.8 us (level)
  no operation moved by 1% of the time
where the time goes in v13:
time: 96.8 us; the launch traced here: 96.5 us
  Pallas kernels  57 us (59%)
  starting transfers between devices  26.8 us (28%)
  waiting for transfers between devices  7.57 us (8%)
  other arithmetic  3.01 us (3%)
  between operations  1.75 us (2%)
    pallas_call x1, Pallas kernels, grad_call(): pl.pallas_call(functools.partial(grad_kernel, own=own), grid=(members //...  34.6 us
    ppermute x25, starting transfers between devices, swap(): return lax.ppermute(value, AXES, [(i, i ^ mask) for i in range(total)])  26.8 us
    pallas_call x6, Pallas kernels, back_call(): pl.pallas_call(functools.partial(back_kernel, start=start, first=acc is N...  19.5 us
    ppermute x25, waiting for transfers between devices, swap(): return lax.ppermute(value, AXES, [(i, i ^ mask) for i in range(total)])  7.57 us
  transfers between devices with their start and end apart: 25, of which 8 were waited for; matrix products, arithmetic and copies ran while one was open for 2% of the time, Pallas kernels for 21%

profile of v13, /device:TPU:0, one launch (start us, length us, event | category | flops | bytes accessed | tf_op | source)
XLA Modules:
  0.0 96.5 jit_solution(14996468283925294010)
XLA Ops:
  0.6 1.5 %pack_weights.1 = bf16[16,768]{1,0:T(8,128)(2,1)} custom-call(f32[16,512]{1,0:T(8,128)} %refs_4_.3, f32[3,16,32]{2,1,0:T(8,128)} %bitcast.63, f32[4,512]{1,0:T(4,128)} %refs_6_.3), custom_call_target="tpu_custom_call" | custom-call | tf_op jit(solution)/shard_map/pack_weights/pallas_call | solution.py:51
  2.6 4.6 %collective-permute-start.2 = (bf16[16,768]{1,0:T(8,128)(2,1)}, bf16[16,768]{1,0:T(8,128)(2,1)S(1)}, u32[]{:S(2)}, u32[]{:S(2)}) collective-permute-start(bf16[16,768]{1,0:T(8,128)(2,1)} %pack_weights.1), channel_id=1, source_target_pairs={{0,24},{1,25},{2,26},{3,27},{4,28},{5,29},{6,30},{7,31},{8,16},{9,... | collective-permute-start | bytes 73736 | tf_op jit(solution)/shard_map/ppermute | solution.py:387
  9.3 2.8 %collective-permute-done.1 = bf16[16,768]{1,0:T(8,128)(2,1)S(1)} collective-permute-done((bf16[16,768]{1,0:T(8,128)(2,1)}, bf16[16,768]{1,0:T(8,128)(2,1)S(1)}, u32[]{:S(2)}, u32[]{:S(2)}) %collective-permute-start.1) | collective-permute-done | bytes 24608 | tf_op jit(solution)/shard_map/ppermute | solution.py:387
  12.9 2.5 %collective-permute-start.6 = (bf16[4,16,768]{2,1,0:T(8,128)(2,1)S(1)}, bf16[4,16,768]{2,1,0:T(8,128)(2,1)S(1)}, u32[]{:S(2)}, u32[]{:S(2)}) collective-permute-start(bf16[4,16,768]{2,1,0:T(8,128)(2,1)S(1)} %pad_maximum_fusion.3), channel_id=1, source_target_pairs={{0,6},{1,7},{2,4},{3,5},{4,2},{5,3},{6,0},{7,1},{8,14},{9,15},{10,... | collective-permute-start | bytes 294920 | tf_op jit(solution)/shard_map/ppermute | solution.py:387
  16.4 1.1 %pad_maximum_fusion.x_ref = bf16[1024,512]{1,0:T(8,128)(2,1)S(1)} fusion(bf16[512,512]{1,0:T(8,128)(2,1)S(1)} %collective-permute-done.3, bf16[512,512]{1,0:T(8,128)(2,1)} %param.12), kind=kLoop, calls=%fused_computation | loop fusion | flops 2097152 | bytes 2097152 | tf_op jit(solution)/shard_map/concatenate | solution.py:401
  17.6 1.4 %collective-permute-done.6 = bf16[4,16,768]{2,1,0:T(8,128)(2,1)S(1)} collective-permute-done((bf16[4,16,768]{2,1,0:T(8,128)(2,1)S(1)}, bf16[4,16,768]{2,1,0:T(8,128)(2,1)S(1)}, u32[]{:S(2)}, u32[]{:S(2)}) %collective-permute-start.6) | collective-permute-done | bytes 98336 | tf_op jit(solution)/shard_map/ppermute | solution.py:387
  18.9 1.1 %collective-permute-done.5 = bf16[4,16,768]{2,1,0:T(8,128)(2,1)S(1)} collective-permute-done((bf16[4,16,768]{2,1,0:T(8,128)(2,1)S(1)}, bf16[4,16,768]{2,1,0:T(8,128)(2,1)S(1)}, u32[]{:S(2)}, u32[]{:S(2)}) %collective-permute-start.5) | collective-permute-done | bytes 98336 | tf_op jit(solution)/shard_map/ppermute | solution.py:387
  21.2 1.2 %collective-permute-done.8.refs_4_ = f32[1,512]{1,0:T(1,128)S(1)} collective-permute-done((f32[1,512]{1,0:T(1,128)S(1)}, f32[1,512]{1,0:T(1,128)S(1)}, u32[]{:S(2)}, u32[]{:S(2)}) %collective-permute-start.8) | collective-permute-done | bytes 2080 | tf_op jit(solution)/shard_map/ppermute | solution.py:387
  22.7 34.6 %member_grads.1 = (f32[256,640]{1,0:T(8,128)S(1)}, bf16[256,640]{1,0:T(8,128)(2,1)S(1)}, f32[32,512]{1,0:T(8,128)S(1)}, f32[2,512]{1,0:T(2,128)S(1)}, f32[128,51...) custom-call(bf16[1024,512]{1,0:T(8,128)(2,1)S(1)} %pad_maximum_fusio, ...), custom_call_target="tpu_custom_call" | custom-call | flops 34359738368 | bytes 16777216 | tf_op jit(solution)/shard_map/member_grads/pallas_call | solution.py:194
  58.0 1.9 %input_grads.6.refs_3_ = f32[512,512]{1,0:T(8,128)S(1)} custom-call(f32[128,512]{1,0:T(8,128)S(1)} %get-tuple-element.188.refs_0_, bf16[512,512]{1,0:T(8,128)(2,1)S(1)} %get-tuple-element.189.refs_1_, bf16[16,512,512]{2,1,0:T(8,128)(2,1)} %get-tuple-element.161.refs_2_), custom_call_target="tpu_custom_call" | custom-call | flops 536870912 | bytes 1048576 | tf_op jit(solution)/shard_map/input_grads/pallas_call | solution.py:266
  61.1 1.1 %collective-permute-start.12 = (bf16[68,640]{1,0:T(8,128)(2,1)S(1)}, bf16[68,640]{1,0:T(8,128)(2,1)S(1)}, u32[]{:S(2)}, u32[]{:S(2)}) collective-permute-start(bf16[68,640]{1,0:T(8,128)(2,1)S(1)} %get-tuple-element.146), channel_id=1, source_target_pairs={{0,4},{1,5},{2,6},{3,7},{4,0},{5,1},{6,2},{7,3},{8,12},{9,13},{10,... | collective-permute-start | bytes 261128 | tf_op jit(solution)/shard_map/ppermute | solution.py:387
  62.2 1.4 %collective-permute-start.13 = (bf16[68,640]{1,0:T(8,128)(2,1)S(1)}, bf16[68,640]{1,0:T(8,128)(2,1)S(1)}, u32[]{:S(2)}, u32[]{:S(2)}) collective-permute-start(bf16[68,640]{1,0:T(8,128)(2,1)S(1)} %get-tuple-element.147), channel_id=1, source_target_pairs={{0,6},{1,7},{2,4},{3,5},{4,2},{5,3},{6,0},{7,1},{8,14},{9,15},{10,... | collective-permute-start | bytes 261128 | tf_op jit(solution)/shard_map/ppermute | solution.py:387
  63.6 4.0 %input_grads.7.refs_3_ = f32[512,512]{1,0:T(8,128)S(1)} custom-call(f32[128,512]{1,0:T(8,128)S(1)} %get-tuple-element.188.refs_0_, bf16[512,512]{1,0:T(8,128)(2,1)S(1)} %get-tuple-element.189.refs_1_, bf16[16,512,512]{2,1,0:T(8,128)(2,1)} %get-tuple-element.161.refs_2_, f32[512,512]{1,0:T(8,128)S(1)} %input_grads.6.refs_3_), custom_call_target="tpu_custom_call" | custom-call | flops 2147483648 | bytes 4194304 | tf_op jit(solution)/shard_map/input_grads/pallas_call | solution.py:266
  68.4 1.8 %collective-permute-start.15 = (bf16[20,640]{1,0:T(8,128)(2,1)S(1)}, bf16[20,640]{1,0:T(8,128)(2,1)S(1)}, u32[]{:S(2)}, u32[]{:S(2)}) collective-permute-start(bf16[20,640]{1,0:T(8,128)(2,1)S(1)} %get-tuple-element.157), channel_id=1, source_target_pairs={{0,16},{1,17},{2,18},{3,19},{4,20},{5,21},{6,22},{7,23},{8,24},{9,... | collective-permute-start | bytes 76808 | tf_op jit(solution)/shard_map/ppermute | solution.py:387
  70.2 2.3 %collective-permute-start.16 = (bf16[20,640]{1,0:T(8,128)(2,1)S(1)}, bf16[20,640]{1,0:T(8,128)(2,1)S(1)}, u32[]{:S(2)}, u32[]{:S(2)}) collective-permute-start(bf16[20,640]{1,0:T(8,128)(2,1)S(1)} %get-tuple-element.158), channel_id=1, source_target_pairs={{0,24},{1,25},{2,26},{3,27},{4,28},{5,29},{6,30},{7,31},{8,16},{9,... | collective-permute-start | bytes 76808 | tf_op jit(solution)/shard_map/ppermute | solution.py:387
  72.5 3.3 %input_grads.8 = f32[512,512]{1,0:T(8,128)S(1)} custom-call(f32[128,512]{1,0:T(8,128)S(1)} %get-tuple-element.188.refs_0_, bf16[512,512]{1,0:T(8,128)(2,1)S(1)} %get-tuple-element.189.refs_1_, bf16[16,512,512]{2,1,0:T(8,128)(2,1)} %get-tuple-element.161.refs_2_, f32[512,512]{1,0:T(8,128)S(1)} %input_grads.7.refs_3_, f32[1,512]{1,0:T(1,128)S(1)} %collective-permute-done.8.refs_4_), custom_call_target="tpu_custom_call" | custom-call | flops 1610612736 | bytes 3145728 | tf_op jit(solution)/shard_map/input_grads/pallas_call | solution.py:266
  77.2 1.9 %input_grads.9.refs_3_ = f32[512,512]{1,0:T(8,128)S(1)} custom-call(f32[128,512]{1,0:T(8,128)S(1)} %get-tuple-element.188.refs_0_, bf16[512,512]{1,0:T(8,128)(2,1)S(1)} %get-tuple-element.189.refs_1_, bf16[16,512,512]{2,1,0:T(8,128)(2,1)} %get-tuple-element.190.refs_2_), custom_call_target="tpu_custom_call" | custom-call | flops 536870912 | bytes 1048576 | tf_op jit(solution)/shard_map/input_grads/pallas_call | solution.py:266
  79.2 1.4 %collective-permute-start.18 = (f32[16,128]{1,0:T(8,128)S(1)}, f32[16,128]{1,0:T(8,128)S(1)}, u32[]{:S(2)}, u32[]{:S(2)}) collective-permute-start(f32[16,128]{1,0:T(8,128)S(1)} %add.94), channel_id=1, source_target_pairs={{0,2},{1,3},{2,0},{3,1},{4,6},{5,7},{6,4},{7,5},{8,10},{9,11},{10,... | collective-permute-start | bytes 24584 | tf_op jit(solution)/shard_map/ppermute | solution.py:387
  80.6 1.1 %collective-permute-start.19 = (f32[16,128]{1,0:T(8,128)S(1)}, f32[16,128]{1,0:T(8,128)S(1)}, u32[]{:S(2)}, u32[]{:S(2)}) collective-permute-start(f32[16,128]{1,0:T(8,128)S(1)} %add.94), channel_id=1, source_target_pairs={{0,4},{1,5},{2,6},{3,7},{4,0},{5,1},{6,2},{7,3},{8,12},{9,13},{10,... | collective-permute-start | bytes 24584 | tf_op jit(solution)/shard_map/ppermute | solution.py:387
  81.7 1.1 %collective-permute-start.20 = (f32[16,128]{1,0:T(8,128)S(1)}, f32[16,128]{1,0:T(8,128)S(1)}, u32[]{:S(2)}, u32[]{:S(2)}) collective-permute-start(f32[16,128]{1,0:T(8,128)S(1)} %add.94), channel_id=1, source_target_pairs={{0,6},{1,7},{2,4},{3,5},{4,2},{5,3},{6,0},{7,1},{8,14},{9,15},{10,... | collective-permute-start | bytes 24584 | tf_op jit(solution)/shard_map/ppermute | solution.py:387
  82.7 3.3 %input_grads.10.refs_3_ = f32[512,512]{1,0:T(8,128)S(1)} custom-call(f32[128,512]{1,0:T(8,128)S(1)} %get-tuple-element.188.refs_0_, bf16[512,512]{1,0:T(8,128)(2,1)S(1)} %get-tuple-element.189.refs_1_, bf16[16,512,512]{2,1,0:T(8,128)(2,1)} %get-tuple-element.190.refs_2_, f32[512,512]{1,0:T(8,128)S(1)} %input_grads.9.refs_3_), custom_call_target="tpu_custom_call" | custom-call | flops 1610612736 | bytes 3145728 | tf_op jit(solution)/shard_map/input_grads/pallas_call | solution.py:266
  86.4 2.7 %collective-permute-start.22 = (f32[16,128]{1,0:T(8,128)S(1)}, f32[16,128]{1,0:T(8,128)S(1)}, u32[]{:S(2)}, u32[]{:S(2)}) collective-permute-start(f32[16,128]{1,0:T(8,128)S(1)} %add_add_fusion.refs_0_), channel_id=1, source_target_pairs={{0,16},{1,17},{2,18},{3,19},{4,20},{5,21},{6,22},{7,23},{8,24},{9,... | collective-permute-start | bytes 24584 | tf_op jit(solution)/shard_map/ppermute | solution.py:387
  89.0 1.6 %collective-permute-start.23 = (f32[16,128]{1,0:T(8,128)S(1)}, f32[16,128]{1,0:T(8,128)S(1)}, u32[]{:S(2)}, u32[]{:S(2)}) collective-permute-start(f32[16,128]{1,0:T(8,128)S(1)} %add_add_fusion.refs_0_), channel_id=1, source_target_pairs={{0,24},{1,25},{2,26},{3,27},{4,28},{5,29},{6,30},{7,31},{8,16},{9,... | collective-permute-start | bytes 24584 | tf_op jit(solution)/shard_map/ppermute | solution.py:387
  90.6 5.0 %input_grads.11 = (f32[512,512]{1,0:T(8,128)}, f32[1,512]{1,0:T(1,128)}) custom-call(f32[128,512]{1,0:T(8,128)S(1)} %get-tuple-element.188.refs_0_, bf16[512,512]{1,0:T(8,128)(2,1)S(1)} %get-tuple-element.189.refs_1_, bf16[16,512,512]{2,1,0:T(8,128)(2,1)} %get-tuple-element.190.refs_2_, f32[512,512]{1,0:T(8,128)S(1)} %input_grads.10.refs_3_, ...), custom_call_target="tpu_custom_call" | custom-call | flops 2147483648 | bytes 4194304 | tf_op jit(solution)/shard_map/input_grads/pallas_call | solution.py:266
  (80 shorter events, 9.9 us)
Async XLA Ops:
  2.1 10.0 %collective-permute-start.3 = (bf16[512,512]{1,0:T(8,128)(2,1)}, bf16[512,512]{1,0:T(8,128)(2,1)S(1)}, u32[]{:S(2)}, u32[]{:S(2)}) collective-permute-start(bf16[512,512]{1,0:T(8,128)(2,1)} %param.12), channel_id=1, source_target_pairs={{0,1},{1,0},{2,3},{3,2},{4,5},{5,4},{6,7},{7,6},{8,9},{9,8},{10,11... | collective-permute-start | bytes 1572872 | tf_op jit(solution)/shard_map/ppermute | solution.py:387
  2.6 6.7 %collective-permute-start.2 = (bf16[16,768]{1,0:T(8,128)(2,1)}, bf16[16,768]{1,0:T(8,128)(2,1)S(1)}, u32[]{:S(2)}, u32[]{:S(2)}) collective-permute-start(bf16[16,768]{1,0:T(8,128)(2,1)} %pack_weights.1), channel_id=1, source_target_pairs={{0,24},{1,25},{2,26},{3,27},{4,28},{5,29},{6,30},{7,31},{8,16},{9,... | collective-permute-start | bytes 73736 | tf_op jit(solution)/shard_map/ppermute | solution.py:387
  7.2 4.9 %collective-permute-start.1 = (bf16[16,768]{1,0:T(8,128)(2,1)}, bf16[16,768]{1,0:T(8,128)(2,1)S(1)}, u32[]{:S(2)}, u32[]{:S(2)}) collective-permute-start(bf16[16,768]{1,0:T(8,128)(2,1)} %pack_weights.1), channel_id=1, source_target_pairs={{0,16},{1,17},{2,18},{3,19},{4,20},{5,21},{6,22},{7,23},{8,24},{9,... | collective-permute-start | bytes 73736 | tf_op jit(solution)/shard_map/ppermute | solution.py:387
  7.2 4.9 %collective-permute-start = (bf16[16,768]{1,0:T(8,128)(2,1)}, bf16[16,768]{1,0:T(8,128)(2,1)S(1)}, u32[]{:S(2)}, u32[]{:S(2)}) collective-permute-start(bf16[16,768]{1,0:T(8,128)(2,1)} %pack_weights.1), channel_id=1, source_target_pairs={{0,8},{1,9},{2,10},{3,11},{4,12},{5,13},{6,14},{7,15},{8,0},{9,1},... | collective-permute-start | bytes 73736 | tf_op jit(solution)/shard_map/ppermute | solution.py:387
  12.9 6.0 %collective-permute-start.6 = (bf16[4,16,768]{2,1,0:T(8,128)(2,1)S(1)}, bf16[4,16,768]{2,1,0:T(8,128)(2,1)S(1)}, u32[]{:S(2)}, u32[]{:S(2)}) collective-permute-start(bf16[4,16,768]{2,1,0:T(8,128)(2,1)S(1)} %pad_maximum_fusion.3), channel_id=1, source_target_pairs={{0,6},{1,7},{2,4},{3,5},{4,2},{5,3},{6,0},{7,1},{8,14},{9,15},{10,... | collective-permute-start | bytes 294920 | tf_op jit(solution)/shard_map/ppermute | solution.py:387
  15.4 4.7 %collective-permute-start.5 = (bf16[4,16,768]{2,1,0:T(8,128)(2,1)S(1)}, bf16[4,16,768]{2,1,0:T(8,128)(2,1)S(1)}, u32[]{:S(2)}, u32[]{:S(2)}) collective-permute-start(bf16[4,16,768]{2,1,0:T(8,128)(2,1)S(1)} %pad_maximum_fusion.3), channel_id=1, source_target_pairs={{0,4},{1,5},{2,6},{3,7},{4,0},{5,1},{6,2},{7,3},{8,12},{9,13},{10,... | collective-permute-start | bytes 294920 | tf_op jit(solution)/shard_map/ppermute | solution.py:387
  15.9 4.6 %collective-permute-start.4 = (bf16[4,16,768]{2,1,0:T(8,128)(2,1)S(1)}, bf16[4,16,768]{2,1,0:T(8,128)(2,1)S(1)}, u32[]{:S(2)}, u32[]{:S(2)}) collective-permute-start(bf16[4,16,768]{2,1,0:T(8,128)(2,1)S(1)} %pad_maximum_fusion.3), channel_id=1, source_target_pairs={{0,2},{1,3},{2,0},{3,1},{4,6},{5,7},{6,4},{7,5},{8,10},{9,11},{10,... | collective-permute-start | bytes 294920 | tf_op jit(solution)/shard_map/ppermute | solution.py:387
  20.6 1.8 %collective-permute-start.7 = (bf16[4,4,16,768]{3,2,0,1:T(8,128)(2,1)S(1)}, bf16[4,4,16,768]{3,2,0,1:T(8,128)(2,1)S(1)}, u32[]{:S(2)}, u32[]{:S(2)}) collective-permute-start(bf16[4,4,16,768]{3,2,0,1:T(8,128)(2,1)S(1)} %pad_maximum_fusion.2), channel_id=1, source_target_pairs={{0,1},{1,0},{2,3},{3,2},{4,5},{5,4},{6,7},{7,6},{8,9},{9,8},{10,11... | collective-permute-start | bytes 1179656 | tf_op jit(solution)/shard_map/ppermute | solution.py:387
  57.4 2.6 %collective-permute-start.9 = (bf16[4,68,640]{2,1,0:T(8,128)(2,1)S(1)}, bf16[4,68,640]{2,1,0:T(8,128)(2,1)S(1)}, u32[]{:S(2)}, u32[]{:S(2)}) collective-permute-start(bf16[4,68,640]{2,1,0:T(8,128)(2,1)S(1)} %fusion.2), channel_id=1, source_target_pairs={{0,1},{1,0},{2,3},{3,2},{4,5},{5,4},{6,7},{7,6},{8,9},{9,8},{10,11... | collective-permute-start | bytes 1044488 | tf_op jit(solution)/shard_map/ppermute | solution.py:387
  57.6 2.4 %collective-permute-start.10 = (f32[1,512]{1,0:T(1,128)S(1)}, f32[1,512]{1,0:T(1,128)S(1)}, u32[]{:S(2)}, u32[]{:S(2)}) collective-permute-start(f32[1,512]{1,0:T(1,128)S(1)} %slice.9), channel_id=1, source_target_pairs={{0,1},{1,0},{2,3},{3,2},{4,5},{5,4},{6,7},{7,6},{8,9},{9,8},{10,11... | collective-permute-start | bytes 6152 | tf_op jit(solution)/shard_map/ppermute | solution.py:387
  60.1 7.6 %collective-permute-start.11 = (bf16[68,640]{1,0:T(8,128)(2,1)S(1)}, bf16[68,640]{1,0:T(8,128)(2,1)S(1)}, u32[]{:S(2)}, u32[]{:S(2)}) collective-permute-start(bf16[68,640]{1,0:T(8,128)(2,1)S(1)} %get-tuple-element.145), channel_id=1, source_target_pairs={{0,2},{1,3},{2,0},{3,1},{4,6},{5,7},{6,4},{7,5},{8,10},{9,11},{10,... | collective-permute-start | bytes 261128 | tf_op jit(solution)/shard_map/ppermute | solution.py:387
  61.1 6.6 %collective-permute-start.12 = (bf16[68,640]{1,0:T(8,128)(2,1)S(1)}, bf16[68,640]{1,0:T(8,128)(2,1)S(1)}, u32[]{:S(2)}, u32[]{:S(2)}) collective-permute-start(bf16[68,640]{1,0:T(8,128)(2,1)S(1)} %get-tuple-element.146), channel_id=1, source_target_pairs={{0,4},{1,5},{2,6},{3,7},{4,0},{5,1},{6,2},{7,3},{8,12},{9,13},{10,... | collective-permute-start | bytes 261128 | tf_op jit(solution)/shard_map/ppermute | solution.py:387
  62.2 5.6 %collective-permute-start.13 = (bf16[68,640]{1,0:T(8,128)(2,1)S(1)}, bf16[68,640]{1,0:T(8,128)(2,1)S(1)}, u32[]{:S(2)}, u32[]{:S(2)}) collective-permute-start(bf16[68,640]{1,0:T(8,128)(2,1)S(1)} %get-tuple-element.147), channel_id=1, source_target_pairs={{0,6},{1,7},{2,4},{3,5},{4,2},{5,3},{6,0},{7,1},{8,14},{9,15},{10,... | collective-permute-start | bytes 261128 | tf_op jit(solution)/shard_map/ppermute | solution.py:387
  68.0 7.8 %collective-permute-start.14 = (bf16[20,640]{1,0:T(8,128)(2,1)S(1)}, bf16[20,640]{1,0:T(8,128)(2,1)S(1)}, u32[]{:S(2)}, u32[]{:S(2)}) collective-permute-start(bf16[20,640]{1,0:T(8,128)(2,1)S(1)} %get-tuple-element.156), channel_id=1, source_target_pairs={{0,8},{1,9},{2,10},{3,11},{4,12},{5,13},{6,14},{7,15},{8,0},{9,1},... | collective-permute-start | bytes 76808 | tf_op jit(solution)/shard_map/ppermute | solution.py:387
  68.4 7.5 %collective-permute-start.15 = (bf16[20,640]{1,0:T(8,128)(2,1)S(1)}, bf16[20,640]{1,0:T(8,128)(2,1)S(1)}, u32[]{:S(2)}, u32[]{:S(2)}) collective-permute-start(bf16[20,640]{1,0:T(8,128)(2,1)S(1)} %get-tuple-element.157), channel_id=1, source_target_pairs={{0,16},{1,17},{2,18},{3,19},{4,20},{5,21},{6,22},{7,23},{8,24},{9,... | collective-permute-start | bytes 76808 | tf_op jit(solution)/shard_map/ppermute | solution.py:387
  70.2 5.7 %collective-permute-start.16 = (bf16[20,640]{1,0:T(8,128)(2,1)S(1)}, bf16[20,640]{1,0:T(8,128)(2,1)S(1)}, u32[]{:S(2)}, u32[]{:S(2)}) collective-permute-start(bf16[20,640]{1,0:T(8,128)(2,1)S(1)} %get-tuple-element.158), channel_id=1, source_target_pairs={{0,24},{1,25},{2,26},{3,27},{4,28},{5,29},{6,30},{7,31},{8,16},{9,... | collective-permute-start | bytes 76808 | tf_op jit(solution)/shard_map/ppermute | solution.py:387
  75.9 14.7 %collective-permute-start.24 = (f32[512,512]{1,0:T(8,128)S(1)}, f32[512,512]{1,0:T(8,128)S(1)}, u32[]{:S(2)}, u32[]{:S(2)}) collective-permute-start(f32[512,512]{1,0:T(8,128)S(1)} %input_grads.8), channel_id=1, source_target_pairs={{0,1},{1,0},{2,3},{3,2},{4,5},{5,4},{6,7},{7,6},{8,9},{9,8},{10,11... | collective-permute-start | bytes 3145736 | tf_op jit(solution)/shard_map/ppermute | solution.py:387
  76.8 2.4 %collective-permute-start.17 = (f32[16,128]{1,0:T(8,128)S(1)}, f32[16,128]{1,0:T(8,128)S(1)}, u32[]{:S(2)}, u32[]{:S(2)}) collective-permute-start(f32[16,128]{1,0:T(8,128)S(1)} %get-tuple-element.168), channel_id=1, source_target_pairs={{0,1},{1,0},{2,3},{3,2},{4,5},{5,4},{6,7},{7,6},{8,9},{9,8},{10,11... | collective-permute-start | bytes 24584 | tf_op jit(solution)/shard_map/ppermute | solution.py:387
  79.2 6.9 %collective-permute-start.18 = (f32[16,128]{1,0:T(8,128)S(1)}, f32[16,128]{1,0:T(8,128)S(1)}, u32[]{:S(2)}, u32[]{:S(2)}) collective-permute-start(f32[16,128]{1,0:T(8,128)S(1)} %add.94), channel_id=1, source_target_pairs={{0,2},{1,3},{2,0},{3,1},{4,6},{5,7},{6,4},{7,5},{8,10},{9,11},{10,... | collective-permute-start | bytes 24584 | tf_op jit(solution)/shard_map/ppermute | solution.py:387
  80.6 5.5 %collective-permute-start.19 = (f32[16,128]{1,0:T(8,128)S(1)}, f32[16,128]{1,0:T(8,128)S(1)}, u32[]{:S(2)}, u32[]{:S(2)}) collective-permute-start(f32[16,128]{1,0:T(8,128)S(1)} %add.94), channel_id=1, source_target_pairs={{0,4},{1,5},{2,6},{3,7},{4,0},{5,1},{6,2},{7,3},{8,12},{9,13},{10,... | collective-permute-start | bytes 24584 | tf_op jit(solution)/shard_map/ppermute | solution.py:387
  81.7 4.5 %collective-permute-start.20 = (f32[16,128]{1,0:T(8,128)S(1)}, f32[16,128]{1,0:T(8,128)S(1)}, u32[]{:S(2)}, u32[]{:S(2)}) collective-permute-start(f32[16,128]{1,0:T(8,128)S(1)} %add.94), channel_id=1, source_target_pairs={{0,6},{1,7},{2,4},{3,5},{4,2},{5,3},{6,0},{7,1},{8,14},{9,15},{10,... | collective-permute-start | bytes 24584 | tf_op jit(solution)/shard_map/ppermute | solution.py:387
  86.2 9.4 %collective-permute-start.21 = (f32[16,128]{1,0:T(8,128)S(1)}, f32[16,128]{1,0:T(8,128)S(1)}, u32[]{:S(2)}, u32[]{:S(2)}) collective-permute-start(f32[16,128]{1,0:T(8,128)S(1)} %add_add_fusion.refs_0_), channel_id=1, source_target_pairs={{0,8},{1,9},{2,10},{3,11},{4,12},{5,13},{6,14},{7,15},{8,0},{9,1},... | collective-permute-start | bytes 24584 | tf_op jit(solution)/shard_map/ppermute | solution.py:387
  86.4 9.3 %collective-permute-start.22 = (f32[16,128]{1,0:T(8,128)S(1)}, f32[16,128]{1,0:T(8,128)S(1)}, u32[]{:S(2)}, u32[]{:S(2)}) collective-permute-start(f32[16,128]{1,0:T(8,128)S(1)} %add_add_fusion.refs_0_), channel_id=1, source_target_pairs={{0,16},{1,17},{2,18},{3,19},{4,20},{5,21},{6,22},{7,23},{8,24},{9,... | collective-permute-start | bytes 24584 | tf_op jit(solution)/shard_map/ppermute | solution.py:387
  89.0 6.6 %collective-permute-start.23 = (f32[16,128]{1,0:T(8,128)S(1)}, f32[16,128]{1,0:T(8,128)S(1)}, u32[]{:S(2)}, u32[]{:S(2)}) collective-permute-start(f32[16,128]{1,0:T(8,128)S(1)} %add_add_fusion.refs_0_), channel_id=1, source_target_pairs={{0,24},{1,25},{2,26},{3,27},{4,28},{5,29},{6,30},{7,31},{8,16},{9,... | collective-permute-start | bytes 24584 | tf_op jit(solution)/shard_map/ppermute | solution.py:387
  (10 other events, 73.8 us)

commit v14 on v12

--- a/solution.py
+++ b/solution.py
@@ -449,8 +449,7 @@
     weights = (rows, wide_turned, back_other)
     other_heads = lax.dynamic_index_in_dim(head_grads, 1 - core, axis, keepdims=False)
     own_heads_grad = lax.dynamic_index_in_dim(head_grads, core, axis, keepdims=False)
-    (came, pred_came), acc = beside(
-        [(arrange(sent, other_heads.astype(BF16)), total, 1), (preds[1:2], total, 1)], backward(0, 2), *weights)
+    (came,), acc = beside([(arrange(sent, other_heads.astype(BF16)), total, 1)], backward(0, 2), *weights)
     wide = arrange(keep, own_heads_grad) + came.astype(F32)
     for axis in reversed(range(len(chips))):
         low, size = chip_groups[axis]
@@ -458,7 +457,8 @@
         part = [lax.dynamic_index_in_dim(wide, place ^ m, axis, keepdims=False) for m in range(size)]
         sends = [(part[m].astype(BF16), total, low * m) for m in range(1, size)]
         if axis == len(chips) - 1:
-            came, acc = beside(sends, backward(2, 8), *weights, acc)
+            came, acc = beside(sends + [(preds[1:2], total, 1)], backward(2, 8), *weights, acc)
+            *came, pred_came = came
         else:
             came = [swap(*send) for send in sends]
         wide = part[0]

time: 96.8 us -> 96.8 us (level)
  transfers between devices with their start and end apart: 25 -> 25, of which waited for: 8 -> 9; matrix products, arithmetic and copies ran while one was open for 2% -> 2% of each run, Pallas kernels for 21% -> 21%
where the time goes in v14:
time: 96.8 us; the launch traced here: 96.4 us
  Pallas kernels  57 us (59%)
  starting transfers between devices  26.8 us (28%)
  waiting for transfers between devices  7.57 us (8%)
  other arithmetic  2.99 us (3%)
  between operations  1.77 us (2%)
    pallas_call x1, Pallas kernels, grad_call(): pl.pallas_call(functools.partial(grad_kernel, own=own), grid=(members //...  34.5 us
    ppermute x25, starting transfers between devices, swap(): return lax.ppermute(value, AXES, [(i, i ^ mask) for i in range(total)])  26.8 us
    pallas_call x6, Pallas kernels, back_call(): pl.pallas_call(functools.partial(back_kernel, start=start, first=acc is N...  19.5 us
    ppermute x25, waiting for transfers between devices, swap(): return lax.ppermute(value, AXES, [(i, i ^ mask) for i in range(total)])  7.57 us
  transfers between devices with their start and end apart: 25, of which 9 were waited for; matrix products, arithmetic and copies ran while one was open for 2% of the time, Pallas kernels for 21%

profile of v14, /device:TPU:0, one launch (start us, length us, event | category | flops | bytes accessed | tf_op | source)
XLA Modules:
  0.0 96.4 jit_solution(14513949003220667030)
XLA Ops:
  0.6 1.5 %pack_weights.1 = bf16[16,768]{1,0:T(8,128)(2,1)} custom-call(f32[16,512]{1,0:T(8,128)} %refs_4_.3, f32[3,16,32]{2,1,0:T(8,128)} %bitcast.63, f32[4,512]{1,0:T(4,128)} %refs_6_.3), custom_call_target="tpu_custom_call" | custom-call | tf_op jit(solution)/shard_map/pack_weights/pallas_call | solution.py:51
  2.6 4.6 %collective-permute-start.2 = (bf16[16,768]{1,0:T(8,128)(2,1)}, bf16[16,768]{1,0:T(8,128)(2,1)S(1)}, u32[]{:S(2)}, u32[]{:S(2)}) collective-permute-start(bf16[16,768]{1,0:T(8,128)(2,1)} %pack_weights.1), channel_id=1, source_target_pairs={{0,24},{1,25},{2,26},{3,27},{4,28},{5,29},{6,30},{7,31},{8,16},{9,... | collective-permute-start | bytes 73736 | tf_op jit(solution)/shard_map/ppermute | solution.py:384
  9.3 2.8 %collective-permute-done.1 = bf16[16,768]{1,0:T(8,128)(2,1)S(1)} collective-permute-done((bf16[16,768]{1,0:T(8,128)(2,1)}, bf16[16,768]{1,0:T(8,128)(2,1)S(1)}, u32[]{:S(2)}, u32[]{:S(2)}) %collective-permute-start.1) | collective-permute-done | bytes 24608 | tf_op jit(solution)/shard_map/ppermute | solution.py:384
  12.9 2.5 %collective-permute-start.6 = (bf16[4,16,768]{2,1,0:T(8,128)(2,1)S(1)}, bf16[4,16,768]{2,1,0:T(8,128)(2,1)S(1)}, u32[]{:S(2)}, u32[]{:S(2)}) collective-permute-start(bf16[4,16,768]{2,1,0:T(8,128)(2,1)S(1)} %pad_maximum_fusion.3), channel_id=1, source_target_pairs={{0,6},{1,7},{2,4},{3,5},{4,2},{5,3},{6,0},{7,1},{8,14},{9,15},{10,... | collective-permute-start | bytes 294920 | tf_op jit(solution)/shard_map/ppermute | solution.py:384
  16.4 1.1 %pad_maximum_fusion.x_ref = bf16[1024,512]{1,0:T(8,128)(2,1)S(1)} fusion(bf16[512,512]{1,0:T(8,128)(2,1)S(1)} %collective-permute-done.3, bf16[512,512]{1,0:T(8,128)(2,1)} %param.12), kind=kLoop, calls=%fused_computation | loop fusion | flops 2097152 | bytes 2097152 | tf_op jit(solution)/shard_map/concatenate | solution.py:398
  17.6 1.4 %collective-permute-done.6 = bf16[4,16,768]{2,1,0:T(8,128)(2,1)S(1)} collective-permute-done((bf16[4,16,768]{2,1,0:T(8,128)(2,1)S(1)}, bf16[4,16,768]{2,1,0:T(8,128)(2,1)S(1)}, u32[]{:S(2)}, u32[]{:S(2)}) %collective-permute-start.6) | collective-permute-done | bytes 98336 | tf_op jit(solution)/shard_map/ppermute | solution.py:384
  18.9 1.1 %collective-permute-done.5 = bf16[4,16,768]{2,1,0:T(8,128)(2,1)S(1)} collective-permute-done((bf16[4,16,768]{2,1,0:T(8,128)(2,1)S(1)}, bf16[4,16,768]{2,1,0:T(8,128)(2,1)S(1)}, u32[]{:S(2)}, u32[]{:S(2)}) %collective-permute-start.5) | collective-permute-done | bytes 98336 | tf_op jit(solution)/shard_map/ppermute | solution.py:384
  21.2 1.2 %collective-permute-done.8.refs_4_ = f32[1,512]{1,0:T(1,128)S(1)} collective-permute-done((f32[1,512]{1,0:T(1,128)S(1)}, f32[1,512]{1,0:T(1,128)S(1)}, u32[]{:S(2)}, u32[]{:S(2)}) %collective-permute-start.8) | collective-permute-done | bytes 2080 | tf_op jit(solution)/shard_map/ppermute | solution.py:384
  22.7 34.5 %member_grads.1 = (f32[256,640]{1,0:T(8,128)S(1)}, bf16[256,640]{1,0:T(8,128)(2,1)S(1)}, f32[32,512]{1,0:T(8,128)S(1)}, f32[2,512]{1,0:T(2,128)S(1)}, f32[128,51...) custom-call(bf16[1024,512]{1,0:T(8,128)(2,1)S(1)} %pad_maximum_fusio, ...), custom_call_target="tpu_custom_call" | custom-call | flops 34359738368 | bytes 16777216 | tf_op jit(solution)/shard_map/member_grads/pallas_call | solution.py:191
  57.6 1.9 %input_grads.6.refs_3_ = f32[512,512]{1,0:T(8,128)S(1)} custom-call(f32[128,512]{1,0:T(8,128)S(1)} %get-tuple-element.188.refs_0_, bf16[512,512]{1,0:T(8,128)(2,1)S(1)} %get-tuple-element.189.refs_1_, bf16[16,512,512]{2,1,0:T(8,128)(2,1)} %get-tuple-element.161.refs_2_), custom_call_target="tpu_custom_call" | custom-call | flops 536870912 | bytes 1048576 | tf_op jit(solution)/shard_map/input_grads/pallas_call | solution.py:263
  61.0 1.1 %collective-permute-start.11 = (bf16[68,640]{1,0:T(8,128)(2,1)S(1)}, bf16[68,640]{1,0:T(8,128)(2,1)S(1)}, u32[]{:S(2)}, u32[]{:S(2)}) collective-permute-start(bf16[68,640]{1,0:T(8,128)(2,1)S(1)} %get-tuple-element.145), channel_id=1, source_target_pairs={{0,4},{1,5},{2,6},{3,7},{4,0},{5,1},{6,2},{7,3},{8,12},{9,13},{10,... | collective-permute-start | bytes 261128 | tf_op jit(solution)/shard_map/ppermute | solution.py:384
  62.2 1.4 %collective-permute-start.12 = (bf16[68,640]{1,0:T(8,128)(2,1)S(1)}, bf16[68,640]{1,0:T(8,128)(2,1)S(1)}, u32[]{:S(2)}, u32[]{:S(2)}) collective-permute-start(bf16[68,640]{1,0:T(8,128)(2,1)S(1)} %get-tuple-element.146), channel_id=1, source_target_pairs={{0,6},{1,7},{2,4},{3,5},{4,2},{5,3},{6,0},{7,1},{8,14},{9,15},{10,... | collective-permute-start | bytes 261128 | tf_op jit(solution)/shard_map/ppermute | solution.py:384
  63.6 4.0 %input_grads.7.refs_3_ = f32[512,512]{1,0:T(8,128)S(1)} custom-call(f32[128,512]{1,0:T(8,128)S(1)} %get-tuple-element.188.refs_0_, bf16[512,512]{1,0:T(8,128)(2,1)S(1)} %get-tuple-element.189.refs_1_, bf16[16,512,512]{2,1,0:T(8,128)(2,1)} %get-tuple-element.161.refs_2_, f32[512,512]{1,0:T(8,128)S(1)} %input_grads.6.refs_3_), custom_call_target="tpu_custom_call" | custom-call | flops 2147483648 | bytes 4194304 | tf_op jit(solution)/shard_map/input_grads/pallas_call | solution.py:263
  68.4 1.8 %collective-permute-start.15 = (bf16[20,640]{1,0:T(8,128)(2,1)S(1)}, bf16[20,640]{1,0:T(8,128)(2,1)S(1)}, u32[]{:S(2)}, u32[]{:S(2)}) collective-permute-start(bf16[20,640]{1,0:T(8,128)(2,1)S(1)} %get-tuple-element.157), channel_id=1, source_target_pairs={{0,16},{1,17},{2,18},{3,19},{4,20},{5,21},{6,22},{7,23},{8,24},{9,... | collective-permute-start | bytes 76808 | tf_op jit(solution)/shard_map/ppermute | solution.py:384
  70.2 2.3 %collective-permute-start.16 = (bf16[20,640]{1,0:T(8,128)(2,1)S(1)}, bf16[20,640]{1,0:T(8,128)(2,1)S(1)}, u32[]{:S(2)}, u32[]{:S(2)}) collective-permute-start(bf16[20,640]{1,0:T(8,128)(2,1)S(1)} %get-tuple-element.158), channel_id=1, source_target_pairs={{0,24},{1,25},{2,26},{3,27},{4,28},{5,29},{6,30},{7,31},{8,16},{9,... | collective-permute-start | bytes 76808 | tf_op jit(solution)/shard_map/ppermute | solution.py:384
  72.5 3.3 %input_grads.8 = f32[512,512]{1,0:T(8,128)S(1)} custom-call(f32[128,512]{1,0:T(8,128)S(1)} %get-tuple-element.188.refs_0_, bf16[512,512]{1,0:T(8,128)(2,1)S(1)} %get-tuple-element.189.refs_1_, bf16[16,512,512]{2,1,0:T(8,128)(2,1)} %get-tuple-element.161.refs_2_, f32[512,512]{1,0:T(8,128)S(1)} %input_grads.7.refs_3_, f32[1,512]{1,0:T(1,128)S(1)} %collective-permute-done.8.refs_4_), custom_call_target="tpu_custom_call" | custom-call | flops 1610612736 | bytes 3145728 | tf_op jit(solution)/shard_map/input_grads/pallas_call | solution.py:263
  77.2 1.9 %input_grads.9.refs_3_ = f32[512,512]{1,0:T(8,128)S(1)} custom-call(f32[128,512]{1,0:T(8,128)S(1)} %get-tuple-element.188.refs_0_, bf16[512,512]{1,0:T(8,128)(2,1)S(1)} %get-tuple-element.189.refs_1_, bf16[16,512,512]{2,1,0:T(8,128)(2,1)} %get-tuple-element.190.refs_2_), custom_call_target="tpu_custom_call" | custom-call | flops 536870912 | bytes 1048576 | tf_op jit(solution)/shard_map/input_grads/pallas_call | solution.py:263
  79.2 1.4 %collective-permute-start.18 = (f32[16,128]{1,0:T(8,128)S(1)}, f32[16,128]{1,0:T(8,128)S(1)}, u32[]{:S(2)}, u32[]{:S(2)}) collective-permute-start(f32[16,128]{1,0:T(8,128)S(1)} %add.94), channel_id=1, source_target_pairs={{0,2},{1,3},{2,0},{3,1},{4,6},{5,7},{6,4},{7,5},{8,10},{9,11},{10,... | collective-permute-start | bytes 24584 | tf_op jit(solution)/shard_map/ppermute | solution.py:384
  80.6 1.1 %collective-permute-start.19 = (f32[16,128]{1,0:T(8,128)S(1)}, f32[16,128]{1,0:T(8,128)S(1)}, u32[]{:S(2)}, u32[]{:S(2)}) collective-permute-start(f32[16,128]{1,0:T(8,128)S(1)} %add.94), channel_id=1, source_target_pairs={{0,4},{1,5},{2,6},{3,7},{4,0},{5,1},{6,2},{7,3},{8,12},{9,13},{10,... | collective-permute-start | bytes 24584 | tf_op jit(solution)/shard_map/ppermute | solution.py:384
  81.7 1.1 %collective-permute-start.20 = (f32[16,128]{1,0:T(8,128)S(1)}, f32[16,128]{1,0:T(8,128)S(1)}, u32[]{:S(2)}, u32[]{:S(2)}) collective-permute-start(f32[16,128]{1,0:T(8,128)S(1)} %add.94), channel_id=1, source_target_pairs={{0,6},{1,7},{2,4},{3,5},{4,2},{5,3},{6,0},{7,1},{8,14},{9,15},{10,... | collective-permute-start | bytes 24584 | tf_op jit(solution)/shard_map/ppermute | solution.py:384
  82.7 3.3 %input_grads.10.refs_3_ = f32[512,512]{1,0:T(8,128)S(1)} custom-call(f32[128,512]{1,0:T(8,128)S(1)} %get-tuple-element.188.refs_0_, bf16[512,512]{1,0:T(8,128)(2,1)S(1)} %get-tuple-element.189.refs_1_, bf16[16,512,512]{2,1,0:T(8,128)(2,1)} %get-tuple-element.190.refs_2_, f32[512,512]{1,0:T(8,128)S(1)} %input_grads.9.refs_3_), custom_call_target="tpu_custom_call" | custom-call | flops 1610612736 | bytes 3145728 | tf_op jit(solution)/shard_map/input_grads/pallas_call | solution.py:263
  86.3 2.7 %collective-permute-start.22 = (f32[16,128]{1,0:T(8,128)S(1)}, f32[16,128]{1,0:T(8,128)S(1)}, u32[]{:S(2)}, u32[]{:S(2)}) collective-permute-start(f32[16,128]{1,0:T(8,128)S(1)} %add_add_fusion.refs_0_), channel_id=1, source_target_pairs={{0,16},{1,17},{2,18},{3,19},{4,20},{5,21},{6,22},{7,23},{8,24},{9,... | collective-permute-start | bytes 24584 | tf_op jit(solution)/shard_map/ppermute | solution.py:384
  89.0 1.6 %collective-permute-start.23 = (f32[16,128]{1,0:T(8,128)S(1)}, f32[16,128]{1,0:T(8,128)S(1)}, u32[]{:S(2)}, u32[]{:S(2)}) collective-permute-start(f32[16,128]{1,0:T(8,128)S(1)} %add_add_fusion.refs_0_), channel_id=1, source_target_pairs={{0,24},{1,25},{2,26},{3,27},{4,28},{5,29},{6,30},{7,31},{8,16},{9,... | collective-permute-start | bytes 24584 | tf_op jit(solution)/shard_map/ppermute | solution.py:384
  90.6 5.0 %input_grads.11 = (f32[512,512]{1,0:T(8,128)}, f32[1,512]{1,0:T(1,128)}) custom-call(f32[128,512]{1,0:T(8,128)S(1)} %get-tuple-element.188.refs_0_, bf16[512,512]{1,0:T(8,128)(2,1)S(1)} %get-tuple-element.189.refs_1_, bf16[16,512,512]{2,1,0:T(8,128)(2,1)} %get-tuple-element.190.refs_2_, f32[512,512]{1,0:T(8,128)S(1)} %input_grads.10.refs_3_, ...), custom_call_target="tpu_custom_call" | custom-call | flops 2147483648 | bytes 4194304 | tf_op jit(solution)/shard_map/input_grads/pallas_call | solution.py:263
  (80 shorter events, 9.9 us)
Async XLA Ops:
  2.1 10.0 %collective-permute-start.3 = (bf16[512,512]{1,0:T(8,128)(2,1)}, bf16[512,512]{1,0:T(8,128)(2,1)S(1)}, u32[]{:S(2)}, u32[]{:S(2)}) collective-permute-start(bf16[512,512]{1,0:T(8,128)(2,1)} %param.12), channel_id=1, source_target_pairs={{0,1},{1,0},{2,3},{3,2},{4,5},{5,4},{6,7},{7,6},{8,9},{9,8},{10,11... | collective-permute-start | bytes 1572872 | tf_op jit(solution)/shard_map/ppermute | solution.py:384
  2.6 6.7 %collective-permute-start.2 = (bf16[16,768]{1,0:T(8,128)(2,1)}, bf16[16,768]{1,0:T(8,128)(2,1)S(1)}, u32[]{:S(2)}, u32[]{:S(2)}) collective-permute-start(bf16[16,768]{1,0:T(8,128)(2,1)} %pack_weights.1), channel_id=1, source_target_pairs={{0,24},{1,25},{2,26},{3,27},{4,28},{5,29},{6,30},{7,31},{8,16},{9,... | collective-permute-start | bytes 73736 | tf_op jit(solution)/shard_map/ppermute | solution.py:384
  7.2 4.9 %collective-permute-start.1 = (bf16[16,768]{1,0:T(8,128)(2,1)}, bf16[16,768]{1,0:T(8,128)(2,1)S(1)}, u32[]{:S(2)}, u32[]{:S(2)}) collective-permute-start(bf16[16,768]{1,0:T(8,128)(2,1)} %pack_weights.1), channel_id=1, source_target_pairs={{0,16},{1,17},{2,18},{3,19},{4,20},{5,21},{6,22},{7,23},{8,24},{9,... | collective-permute-start | bytes 73736 | tf_op jit(solution)/shard_map/ppermute | solution.py:384
  7.2 4.9 %collective-permute-start = (bf16[16,768]{1,0:T(8,128)(2,1)}, bf16[16,768]{1,0:T(8,128)(2,1)S(1)}, u32[]{:S(2)}, u32[]{:S(2)}) collective-permute-start(bf16[16,768]{1,0:T(8,128)(2,1)} %pack_weights.1), channel_id=1, source_target_pairs={{0,8},{1,9},{2,10},{3,11},{4,12},{5,13},{6,14},{7,15},{8,0},{9,1},... | collective-permute-start | bytes 73736 | tf_op jit(solution)/shard_map/ppermute | solution.py:384
  12.9 6.0 %collective-permute-start.6 = (bf16[4,16,768]{2,1,0:T(8,128)(2,1)S(1)}, bf16[4,16,768]{2,1,0:T(8,128)(2,1)S(1)}, u32[]{:S(2)}, u32[]{:S(2)}) collective-permute-start(bf16[4,16,768]{2,1,0:T(8,128)(2,1)S(1)} %pad_maximum_fusion.3), channel_id=1, source_target_pairs={{0,6},{1,7},{2,4},{3,5},{4,2},{5,3},{6,0},{7,1},{8,14},{9,15},{10,... | collective-permute-start | bytes 294920 | tf_op jit(solution)/shard_map/ppermute | solution.py:384
  15.4 4.7 %collective-permute-start.5 = (bf16[4,16,768]{2,1,0:T(8,128)(2,1)S(1)}, bf16[4,16,768]{2,1,0:T(8,128)(2,1)S(1)}, u32[]{:S(2)}, u32[]{:S(2)}) collective-permute-start(bf16[4,16,768]{2,1,0:T(8,128)(2,1)S(1)} %pad_maximum_fusion.3), channel_id=1, source_target_pairs={{0,4},{1,5},{2,6},{3,7},{4,0},{5,1},{6,2},{7,3},{8,12},{9,13},{10,... | collective-permute-start | bytes 294920 | tf_op jit(solution)/shard_map/ppermute | solution.py:384
  15.9 4.6 %collective-permute-start.4 = (bf16[4,16,768]{2,1,0:T(8,128)(2,1)S(1)}, bf16[4,16,768]{2,1,0:T(8,128)(2,1)S(1)}, u32[]{:S(2)}, u32[]{:S(2)}) collective-permute-start(bf16[4,16,768]{2,1,0:T(8,128)(2,1)S(1)} %pad_maximum_fusion.3), channel_id=1, source_target_pairs={{0,2},{1,3},{2,0},{3,1},{4,6},{5,7},{6,4},{7,5},{8,10},{9,11},{10,... | collective-permute-start | bytes 294920 | tf_op jit(solution)/shard_map/ppermute | solution.py:384
  20.6 1.8 %collective-permute-start.7 = (bf16[4,4,16,768]{3,2,0,1:T(8,128)(2,1)S(1)}, bf16[4,4,16,768]{3,2,0,1:T(8,128)(2,1)S(1)}, u32[]{:S(2)}, u32[]{:S(2)}) collective-permute-start(bf16[4,4,16,768]{3,2,0,1:T(8,128)(2,1)S(1)} %pad_maximum_fusion.2), channel_id=1, source_target_pairs={{0,1},{1,0},{2,3},{3,2},{4,5},{5,4},{6,7},{7,6},{8,9},{9,8},{10,11... | collective-permute-start | bytes 1179656 | tf_op jit(solution)/shard_map/ppermute | solution.py:384
  57.3 2.2 %collective-permute-start.9 = (bf16[4,68,640]{2,1,0:T(8,128)(2,1)S(1)}, bf16[4,68,640]{2,1,0:T(8,128)(2,1)S(1)}, u32[]{:S(2)}, u32[]{:S(2)}) collective-permute-start(bf16[4,68,640]{2,1,0:T(8,128)(2,1)S(1)} %fusion.2), channel_id=1, source_target_pairs={{0,1},{1,0},{2,3},{3,2},{4,5},{5,4},{6,7},{7,6},{8,9},{9,8},{10,11... | collective-permute-start | bytes 1044488 | tf_op jit(solution)/shard_map/ppermute | solution.py:384
  59.7 7.9 %collective-permute-start.13 = (f32[1,512]{1,0:T(1,128)S(1)}, f32[1,512]{1,0:T(1,128)S(1)}, u32[]{:S(2)}, u32[]{:S(2)}) collective-permute-start(f32[1,512]{1,0:T(1,128)S(1)} %slice.9), channel_id=1, source_target_pairs={{0,1},{1,0},{2,3},{3,2},{4,5},{5,4},{6,7},{7,6},{8,9},{9,8},{10,11... | collective-permute-start | bytes 6152 | tf_op jit(solution)/shard_map/ppermute | solution.py:384
  60.1 7.5 %collective-permute-start.10 = (bf16[68,640]{1,0:T(8,128)(2,1)S(1)}, bf16[68,640]{1,0:T(8,128)(2,1)S(1)}, u32[]{:S(2)}, u32[]{:S(2)}) collective-permute-start(bf16[68,640]{1,0:T(8,128)(2,1)S(1)} %get-tuple-element.144), channel_id=1, source_target_pairs={{0,2},{1,3},{2,0},{3,1},{4,6},{5,7},{6,4},{7,5},{8,10},{9,11},{10,... | collective-permute-start | bytes 261128 | tf_op jit(solution)/shard_map/ppermute | solution.py:384
  61.0 6.6 %collective-permute-start.11 = (bf16[68,640]{1,0:T(8,128)(2,1)S(1)}, bf16[68,640]{1,0:T(8,128)(2,1)S(1)}, u32[]{:S(2)}, u32[]{:S(2)}) collective-permute-start(bf16[68,640]{1,0:T(8,128)(2,1)S(1)} %get-tuple-element.145), channel_id=1, source_target_pairs={{0,4},{1,5},{2,6},{3,7},{4,0},{5,1},{6,2},{7,3},{8,12},{9,13},{10,... | collective-permute-start | bytes 261128 | tf_op jit(solution)/shard_map/ppermute | solution.py:384
  62.2 5.6 %collective-permute-start.12 = (bf16[68,640]{1,0:T(8,128)(2,1)S(1)}, bf16[68,640]{1,0:T(8,128)(2,1)S(1)}, u32[]{:S(2)}, u32[]{:S(2)}) collective-permute-start(bf16[68,640]{1,0:T(8,128)(2,1)S(1)} %get-tuple-element.146), channel_id=1, source_target_pairs={{0,6},{1,7},{2,4},{3,5},{4,2},{5,3},{6,0},{7,1},{8,14},{9,15},{10,... | collective-permute-start | bytes 261128 | tf_op jit(solution)/shard_map/ppermute | solution.py:384
  68.0 7.8 %collective-permute-start.14 = (bf16[20,640]{1,0:T(8,128)(2,1)S(1)}, bf16[20,640]{1,0:T(8,128)(2,1)S(1)}, u32[]{:S(2)}, u32[]{:S(2)}) collective-permute-start(bf16[20,640]{1,0:T(8,128)(2,1)S(1)} %get-tuple-element.156), channel_id=1, source_target_pairs={{0,8},{1,9},{2,10},{3,11},{4,12},{5,13},{6,14},{7,15},{8,0},{9,1},... | collective-permute-start | bytes 76808 | tf_op jit(solution)/shard_map/ppermute | solution.py:384
  68.4 7.5 %collective-permute-start.15 = (bf16[20,640]{1,0:T(8,128)(2,1)S(1)}, bf16[20,640]{1,0:T(8,128)(2,1)S(1)}, u32[]{:S(2)}, u32[]{:S(2)}) collective-permute-start(bf16[20,640]{1,0:T(8,128)(2,1)S(1)} %get-tuple-element.157), channel_id=1, source_target_pairs={{0,16},{1,17},{2,18},{3,19},{4,20},{5,21},{6,22},{7,23},{8,24},{9,... | collective-permute-start | bytes 76808 | tf_op jit(solution)/shard_map/ppermute | solution.py:384
  70.2 5.7 %collective-permute-start.16 = (bf16[20,640]{1,0:T(8,128)(2,1)S(1)}, bf16[20,640]{1,0:T(8,128)(2,1)S(1)}, u32[]{:S(2)}, u32[]{:S(2)}) collective-permute-start(bf16[20,640]{1,0:T(8,128)(2,1)S(1)} %get-tuple-element.158), channel_id=1, source_target_pairs={{0,24},{1,25},{2,26},{3,27},{4,28},{5,29},{6,30},{7,31},{8,16},{9,... | collective-permute-start | bytes 76808 | tf_op jit(solution)/shard_map/ppermute | solution.py:384
  75.9 14.7 %collective-permute-start.24 = (f32[512,512]{1,0:T(8,128)S(1)}, f32[512,512]{1,0:T(8,128)S(1)}, u32[]{:S(2)}, u32[]{:S(2)}) collective-permute-start(f32[512,512]{1,0:T(8,128)S(1)} %input_grads.8), channel_id=1, source_target_pairs={{0,1},{1,0},{2,3},{3,2},{4,5},{5,4},{6,7},{7,6},{8,9},{9,8},{10,11... | collective-permute-start | bytes 3145736 | tf_op jit(solution)/shard_map/ppermute | solution.py:384
  76.7 2.4 %collective-permute-start.17 = (f32[16,128]{1,0:T(8,128)S(1)}, f32[16,128]{1,0:T(8,128)S(1)}, u32[]{:S(2)}, u32[]{:S(2)}) collective-permute-start(f32[16,128]{1,0:T(8,128)S(1)} %get-tuple-element.168), channel_id=1, source_target_pairs={{0,1},{1,0},{2,3},{3,2},{4,5},{5,4},{6,7},{7,6},{8,9},{9,8},{10,11... | collective-permute-start | bytes 24584 | tf_op jit(solution)/shard_map/ppermute | solution.py:384
  79.2 6.9 %collective-permute-start.18 = (f32[16,128]{1,0:T(8,128)S(1)}, f32[16,128]{1,0:T(8,128)S(1)}, u32[]{:S(2)}, u32[]{:S(2)}) collective-permute-start(f32[16,128]{1,0:T(8,128)S(1)} %add.94), channel_id=1, source_target_pairs={{0,2},{1,3},{2,0},{3,1},{4,6},{5,7},{6,4},{7,5},{8,10},{9,11},{10,... | collective-permute-start | bytes 24584 | tf_op jit(solution)/shard_map/ppermute | solution.py:384
  80.6 5.5 %collective-permute-start.19 = (f32[16,128]{1,0:T(8,128)S(1)}, f32[16,128]{1,0:T(8,128)S(1)}, u32[]{:S(2)}, u32[]{:S(2)}) collective-permute-start(f32[16,128]{1,0:T(8,128)S(1)} %add.94), channel_id=1, source_target_pairs={{0,4},{1,5},{2,6},{3,7},{4,0},{5,1},{6,2},{7,3},{8,12},{9,13},{10,... | collective-permute-start | bytes 24584 | tf_op jit(solution)/shard_map/ppermute | solution.py:384
  81.7 4.5 %collective-permute-start.20 = (f32[16,128]{1,0:T(8,128)S(1)}, f32[16,128]{1,0:T(8,128)S(1)}, u32[]{:S(2)}, u32[]{:S(2)}) collective-permute-start(f32[16,128]{1,0:T(8,128)S(1)} %add.94), channel_id=1, source_target_pairs={{0,6},{1,7},{2,4},{3,5},{4,2},{5,3},{6,0},{7,1},{8,14},{9,15},{10,... | collective-permute-start | bytes 24584 | tf_op jit(solution)/shard_map/ppermute | solution.py:384
  86.2 9.4 %collective-permute-start.21 = (f32[16,128]{1,0:T(8,128)S(1)}, f32[16,128]{1,0:T(8,128)S(1)}, u32[]{:S(2)}, u32[]{:S(2)}) collective-permute-start(f32[16,128]{1,0:T(8,128)S(1)} %add_add_fusion.refs_0_), channel_id=1, source_target_pairs={{0,8},{1,9},{2,10},{3,11},{4,12},{5,13},{6,14},{7,15},{8,0},{9,1},... | collective-permute-start | bytes 24584 | tf_op jit(solution)/shard_map/ppermute | solution.py:384
  86.3 9.3 %collective-permute-start.22 = (f32[16,128]{1,0:T(8,128)S(1)}, f32[16,128]{1,0:T(8,128)S(1)}, u32[]{:S(2)}, u32[]{:S(2)}) collective-permute-start(f32[16,128]{1,0:T(8,128)S(1)} %add_add_fusion.refs_0_), channel_id=1, source_target_pairs={{0,16},{1,17},{2,18},{3,19},{4,20},{5,21},{6,22},{7,23},{8,24},{9,... | collective-permute-start | bytes 24584 | tf_op jit(solution)/shard_map/ppermute | solution.py:384
  89.0 6.6 %collective-permute-start.23 = (f32[16,128]{1,0:T(8,128)S(1)}, f32[16,128]{1,0:T(8,128)S(1)}, u32[]{:S(2)}, u32[]{:S(2)}) collective-permute-start(f32[16,128]{1,0:T(8,128)S(1)} %add_add_fusion.refs_0_), channel_id=1, source_target_pairs={{0,24},{1,25},{2,26},{3,27},{4,28},{5,29},{6,30},{7,31},{8,16},{9,... | collective-permute-start | bytes 24584 | tf_op jit(solution)/shard_map/ppermute | solution.py:384
  (10 other events, 73.7 us)
